TPU v7x, 32 devices: a whole 2x2x4 slice. The times are simulated.
32 devices in a mesh: sec: 2 (over core), grp: 4 (over z), tp: 4 (over y, x).
Axes of the slice: x: 2, y: 2, z: 4, core: 2. Of those that a mesh axis runs over, the one named last changes fastest.
Arguments:
- inputs: bfloat16 [2, 64, 2880], P(None, 'grp'), may hold values from -12.5 to 12.5
- attention_gain: float32 [2880], replicated, may hold values from 0.25 to 1.75
- w_query: bfloat16 [2880, 4096], P(None, ('sec', 'tp')), may hold values from -0.109375 to 0.109375
- key_value_weight: bfloat16 [2880, 8, 128], P(None, ('sec', 'tp')), may hold values from -0.109375 to 0.109375
- head_sink_logits: float32 [64], P(('sec', 'tp')), may hold values from 0 to 6
- w_output: bfloat16 [4096, 2880], P(('sec', 'tp')), may hold values from -0.09375 to 0.09375
- cache_pairs: bfloat16 [64, 256, 8, 128], P('grp', None, ('sec', 'tp')), may hold values from -600 to 600
- lengths: int32 [64], P('grp'), may hold values from 1 to 256, 8192 in all
- expert_gain: float32 [2880], replicated, may hold values from 0.25 to 1.75
- w_gate: bfloat16 [4, 2880, 1440], P('grp', None, ('sec', 'tp')), may hold values from -0.109375 to 0.109375
- w_up: bfloat16 [4, 2880, 1440], P('grp', None, ('sec', 'tp')), may hold values from -0.109375 to 0.109375
- w_down: bfloat16 [4, 1440, 2880], P('grp', ('sec', 'tp')), may hold values from -0.15625 to 0.15625
- routes: int32 [2, 64, 4], P(None, 'grp'), may hold values from 0 to 3, as said below
- gate_weights: float32 [2, 64, 4], P(None, 'grp'), may hold values from 0.2 to 1
Outputs:
- outputs: bfloat16 [2, 64, 2880], P(None, 'grp', ('sec', 'tp'))
Inputs may be any that keep to these rules, and one draw needn't show every extreme that they name: `routes`: A row names 4 different experts. In each step the 16 rows of one attention group (rows g * 16 to (g + 1) * 16 - 1) name each expert either 0 or 16 times in all, and in each step one expert is named 16 times by every group.
All inputs are finite; a program needn't handle non-finite values. No bound on the sum of `lengths` on one device may be relied on, other than what follows from the above.
Results may differ from a plain program's by a relative error of at most 0.012.
Values may be sent and summed in bfloat16 or wider, within the bound.
No kernel may reach another device: no remote copies, remote signals or barrier semaphores. Data moves between devices by JAX's collectives and lax.ppermute only.
A program may use at most 64 MiB of HBM per device.

v0:
```python
import jax
import jax.numpy as jnp
from jax import lax
from jax.sharding import PartitionSpec as P

HEAD_SIZE = 64
TOP = 4


def rms_norm(values, scale_row):
    widened = values.astype(jnp.float32)
    scale_factor = lax.rsqrt(jnp.mean(widened * widened, axis=-1, keepdims=True) + 1e-05)
    return (widened * scale_factor * scale_row).astype(jnp.bfloat16)


def rotate(vectors, position):
    half_size = vectors.shape[-1] // 2
    counter = jnp.arange(half_size).astype(jnp.float32)
    frequency = jnp.power(jnp.float32(150000.0), counter * (-2.0 / vectors.shape[-1]))
    angle_table = position * frequency
    cosine = jnp.cos(angle_table)
    sine_table = jnp.sin(angle_table)
    first_half = vectors[..., :half_size]
    second_half = vectors[..., half_size:]
    return jnp.concatenate(
        [
            first_half * cosine - second_half * sine_table,
            first_half * sine_table + second_half * cosine,
        ],
        axis=-1,
    )


def attend(
    normalized_input,
    w_query,
    key_value_weight,
    head_sink_logits,
    w_output,
    cache_pairs,
    lengths,
    step_index,
    fresh_keys,
    fresh_values,
):
    row_count = normalized_input.shape[0]
    kv_heads = key_value_weight.shape[1]
    query = jnp.dot(normalized_input, w_query, preferred_element_type=jnp.float32).reshape(
        row_count, -1, HEAD_SIZE
    )
    cache_entry_pairs = jnp.dot(
        normalized_input,
        key_value_weight.reshape(key_value_weight.shape[0], -1),
        preferred_element_type=jnp.float32,
    ).reshape(row_count, kv_heads, 2 * HEAD_SIZE)
    position = (lengths + step_index).astype(jnp.float32)[:, None, None]
    rotated_rows = rotate(query, position).astype(jnp.bfloat16)
    fresh_keys = fresh_keys + [
        rotate(cache_entry_pairs[..., :HEAD_SIZE], position).astype(jnp.bfloat16)
    ]
    fresh_values = fresh_values + [cache_entry_pairs[..., HEAD_SIZE:].astype(jnp.bfloat16)]
    grouped_queries = rotated_rows.reshape(row_count, kv_heads, -1, HEAD_SIZE)
    new_keys = jnp.stack(fresh_keys, 1)
    new_values = jnp.stack(fresh_values, 1)
    cached = (
        jnp.einsum(
            "rkgd,rjkd->rkgj",
            grouped_queries,
            cache_pairs[..., :HEAD_SIZE],
            preferred_element_type=jnp.float32,
        )
        * 0.125
    )
    valid = (jnp.arange(cache_pairs.shape[1])[None, :] < lengths[:, None])[:, None, None, :]
    cached = jnp.where(valid, cached, -jnp.inf)
    fresh = (
        jnp.einsum("rkgd,rikd->rkgi", grouped_queries, new_keys, preferred_element_type=jnp.float32)
        * 0.125
    )
    sink_row = head_sink_logits.reshape(kv_heads, -1)[None]
    largest = jnp.maximum(jnp.maximum(jnp.max(cached, axis=-1), jnp.max(fresh, axis=-1)), sink_row)
    cached_exp = jnp.exp(cached - largest[..., None])
    fresh_exp = jnp.exp(fresh - largest[..., None])
    denominator = (
        jnp.sum(cached_exp, axis=-1) + jnp.sum(fresh_exp, axis=-1) + jnp.exp(sink_row - largest)
    )
    cached_probs = (cached_exp / denominator[..., None]).astype(jnp.bfloat16)
    fresh_probs = (fresh_exp / denominator[..., None]).astype(jnp.bfloat16)
    mixed = jnp.einsum(
        "rkgj,rjkd->rkgd",
        cached_probs,
        cache_pairs[..., HEAD_SIZE:],
        preferred_element_type=jnp.float32,
    )
    mixed = mixed + jnp.einsum(
        "rkgi,rikd->rkgd", fresh_probs, new_values, preferred_element_type=jnp.float32
    )
    attention_mix = mixed.reshape(row_count, -1).astype(jnp.bfloat16)
    partial_sum = jnp.dot(attention_mix, w_output, preferred_element_type=jnp.float32)
    return (partial_sum, fresh_keys, fresh_values)


def body(
    inputs,
    attention_gain,
    w_query,
    key_value_weight,
    head_sink_logits,
    w_output,
    cache_pairs,
    lengths,
    expert_gain,
    w_gate,
    w_up,
    w_down,
    routes,
    gate_weights,
):
    shards = lax.axis_size(("sec", "tp"))
    shard_index = lax.axis_index(("sec", "tp"))
    experts = lax.axis_size("grp") * w_gate.shape[0]
    group_rows = inputs.shape[1]
    width = inputs.shape[2]
    part_width = width // shards
    chosen = max(TOP, experts // 2)
    capacity = group_rows * TOP // chosen
    slot_total = experts * capacity
    gate_matrix = w_gate[0]
    up_matrix = w_up[0]
    down_matrix = w_down[0]
    fresh_keys = []
    fresh_values = []
    results = []
    for step_index in range(inputs.shape[0]):
        normalized_input = rms_norm(inputs[step_index], attention_gain)
        partial_sum, fresh_keys, fresh_values = attend(
            normalized_input,
            w_query,
            key_value_weight,
            head_sink_logits,
            w_output,
            cache_pairs,
            lengths,
            step_index,
            fresh_keys,
            fresh_values,
        )
        summed = lax.psum(partial_sum[None], ("sec", "tp"))
        middle = (inputs[step_index][None].astype(jnp.float32) + summed).astype(jnp.bfloat16)
        route_rows = routes[step_index][None]
        step_count = middle.shape[0]
        expert_in = rms_norm(middle, expert_gain)
        flat_routes = route_rows.reshape(step_count, group_rows * TOP)
        onehot = (flat_routes[..., None] == jnp.arange(experts)[None, None, :]).astype(jnp.int32)
        earlier = jnp.cumsum(onehot, axis=1) - onehot
        slot_index = jnp.sum(earlier * onehot, axis=-1).reshape(step_count, group_rows, TOP)
        target = route_rows * capacity + slot_index
        placed = target[..., None] == jnp.arange(slot_total)[None, None, None, :]
        dispatch_table = jnp.sum(placed.astype(jnp.int32), axis=2).astype(jnp.bfloat16)
        combine_table = jnp.sum(
            jnp.where(placed, gate_weights[step_index][None][..., None], 0.0), axis=2
        )
        outgoing = jnp.einsum(
            "crm,crd->cmd", dispatch_table, expert_in, preferred_element_type=jnp.float32
        )
        outgoing = outgoing.astype(jnp.bfloat16).reshape(step_count, experts, capacity, width)
        arrived = lax.all_to_all(outgoing, "grp", split_axis=1, concat_axis=1, tiled=True)
        gate_h = jnp.einsum(
            "snpd,dh->snph", arrived, gate_matrix, preferred_element_type=jnp.float32
        )
        up_h = jnp.einsum("snpd,dh->snph", arrived, up_matrix, preferred_element_type=jnp.float32)
        act = ((up_h + 1.0) * gate_h * jax.nn.sigmoid(1.702 * gate_h)).astype(jnp.bfloat16)
        partial_out = jnp.einsum(
            "snph,hd->snpd", act, down_matrix, preferred_element_type=jnp.float32
        )
        reduced = lax.psum_scatter(
            partial_out, ("sec", "tp"), scatter_dimension=3, tiled=True
        ).astype(jnp.bfloat16)
        returned = lax.all_to_all(reduced, "grp", split_axis=1, concat_axis=1, tiled=True)
        returned_rows = returned.reshape(step_count, slot_total, part_width).astype(jnp.float32)
        weighted = jnp.einsum(
            "srm,smd->srd", combine_table, returned_rows, precision=lax.Precision.HIGHEST
        )
        own_middle = lax.dynamic_slice_in_dim(
            middle, shard_index * part_width, part_width, 2
        ).astype(jnp.float32)
        results.append((own_middle + weighted).astype(jnp.bfloat16)[0])
    return jnp.stack(results, 0)


def solution(mesh):
    placed = (
        P(None, "grp", None),
        P(),
        P(None, ("sec", "tp")),
        P(None, ("sec", "tp"), None),
        P(("sec", "tp")),
        P(("sec", "tp"), None),
        P("grp", None, ("sec", "tp"), None),
        P("grp"),
        P(),
        P("grp", None, ("sec", "tp")),
        P("grp", None, ("sec", "tp")),
        P("grp", ("sec", "tp"), None),
        P(None, "grp", None),
        P(None, "grp", None),
    )
    return jax.shard_map(
        body, mesh=mesh, in_specs=placed, out_specs=P(None, "grp", ("sec", "tp")), check_vma=False
    )
```

profile of v0, /device:TPU:0, one launch (start us, length us, event | category | flops | bytes accessed | tf_op | source)
XLA Modules:
  0.0 224.1 jit_solution(3676960205089797589)
XLA Ops:
  8.2 1.1 fusion.47
  9.3 1.5 convolution_bitcast_fusion.6
  12.2 4.6 %copy.68 = bf16[2880,512]{0,1:T(8,128)(2,1)} copy(bf16[2880,512]{1,0:T(8,128)(2,1)} %param.16) | data formatting | bytes 5898240 | tf_op args[2]
  16.8 3.3 %fusion.61 = f32[16,8,64]{2,0,1:T(8,128)S(1)} fusion(bf16[8,64,2880]{2,1,0:T(8,128)(2,1)} %bitcast.156, f32[16]{0:T(128)S(1)} %get-tuple-element.52, f32[2880]{0:T(1024)S(1)} %copy-done.5, bf16[2,16,2880]{2,1,0:T(8,128)(2,1)S(1)} %copy-done.3), kind=kOutput, calls=%fused_computation.88 | convolution fusion | flops 47370240 | bytes 3088896 | tf_op jit(solution)/shard_map/dot_general | solution.py:48
  20.2 1.3 fusion.64
  24.4 1.7 fusion.24
  26.4 1.6 convolution_bitcast_fusion.2
  28.0 1.6 convolution_bitcast_fusion.3
  31.1 55.6 %all-reduce.7.cloned.1.call-done = (f32[1,16,2880]{2,1,0:T(8,128)}, f32[1,16,2880]{2,1,0:T(8,128)}) async-done(((f32[1,16,2880]{2,1,0:T(8,128)}, f32[1,16,2880]{2,1,0:T(8,128)}), (f32[1,16,2880]{2,1,0:T(8,128)}, f32[1,16,2880]{2,1,0:T(8,128)})) %all-reduce.7.cloned.1.call-update) | async-done | bytes 368656 | tf_op jit(solution)/shard_map/psum | solution.py:148
  86.7 1.2 fusion.41
  88.9 4.7 %all-to-all-start.2 = ((bf16[1,4,16,2880]{3,2,0,1:T(8,128)(2,1)}), bf16[1,4,16,2880]{3,2,0,1:T(8,128)(2,1)S(1)}, u32[]{:S(2)}, u32[]{:S(2)}) async-start(bf16[1,4,16,2880]{3,2,0,1:T(8,128)(2,1)} %bitcast.159), calls=%async_computation.2 | async-start | bytes 753664 | tf_op jit(solution)/shard_map/all_to_all | solution.py:167
  94.7 9.4 %all-to-all-done.2 = bf16[1,4,16,2880]{3,2,0,1:T(8,128)(2,1)S(1)} async-done(((bf16[1,4,16,2880]{3,2,0,1:T(8,128)(2,1)}), bf16[1,4,16,2880]{3,2,0,1:T(8,128)(2,1)S(1)}, u32[]{:S(2)}, u32[]{:S(2)}) %all-to-all-start.2) | async-done | bytes 368672 | tf_op jit(solution)/shard_map/all_to_all | solution.py:167
  104.2 4.1 %all-to-all-start = ((bf16[1,4,16,2880]{3,2,0,1:T(8,128)(2,1)}), bf16[1,4,16,2880]{3,2,0,1:T(8,128)(2,1)}, u32[]{:S(2)}, u32[]{:S(2)}) async-start(bf16[1,4,16,2880]{3,2,0,1:T(8,128)(2,1)} %bitcast.158), calls=%async_computation | async-start | bytes 753664 | tf_op jit(solution)/shard_map/all_to_all | solution.py:167
  109.6 2.3 %fusion.16 = f32[4,16,180]{2,1,0:T(8,128)} fusion(bf16[1,2880,180]{1,2,0:T(8,128)(2,1)} %param.23, bf16[1,4,16,2880]{3,2,0,1:T(8,128)(2,1)S(1)} %all-to-all-done.2), kind=kOutput, calls=%fused_computation.33 | convolution fusion | flops 66355200 | bytes 1451520 | tf_op jit(solution)/shard_map/snpd,dh->snph/dot_general | solution.py:168
  112.0 3.4 %convolution_bitcast_fusion = f32[1,4,16,2880]{3,2,1,0:T(8,128)} fusion(bf16[1,180,2880]{2,1,0:T(8,128)(2,1)} %param.25, f32[4,16,180]{2,1,0:T(8,128)} %fusion.16, bf16[1,2880,180]{1,2,0:T(8,128)(2,1)} %param.24, bf16[1,4,16,2880]{3,2,0,1:T(8,128)(2,1)S(1)} %all-to-all-done.2), kind=kOutput, calls=%fused_computation | convolution fusion | flops 132802560 | bytes 3225600 | tf_op jit(solution)/shard_map/snph,hd->snpd/dot_general | solution.py:173
  115.4 2.2 %all-to-all-done = bf16[1,4,16,2880]{3,2,0,1:T(8,128)(2,1)} async-done(((bf16[1,4,16,2880]{3,2,0,1:T(8,128)(2,1)}), bf16[1,4,16,2880]{3,2,0,1:T(8,128)(2,1)}, u32[]{:S(2)}, u32[]{:S(2)}) %all-to-all-start) | async-done | bytes 368672 | tf_op jit(solution)/shard_map/all_to_all | solution.py:167
  117.7 1.8 fusion.18
  119.5 3.5 %convolution_bitcast_fusion.1 = f32[1,4,16,2880]{3,2,1,0:T(8,128)} fusion(bf16[1,180,2880]{2,1,0:T(8,128)(2,1)} %param.25, f32[4,16,180]{2,1,0:T(8,128)S(1)} %fusion.18, bf16[1,2880,180]{1,2,0:T(8,128)(2,1)} %param.24, bf16[1,4,16,2880]{3,2,0,1:T(8,128)(2,1)} %all-to-all-done), kind=kOutput, calls=%fused_computation.1 | convolution fusion | flops 132802560 | bytes 3225600 | tf_op jit(solution)/shard_map/snph,hd->snpd/dot_general | solution.py:173
  123.0 74.9 %all-reduce.8 = (bf16[1,4,16,2880]{3,2,1,0:T(8,128)(2,1)}, bf16[1,4,16,2880]{3,2,1,0:T(8,128)(2,1)S(1)}) all-reduce(f32[1,4,16,2880]{3,2,1,0:T(8,128)} %convolution_bitcast_fusion, f32[1,4,16,2880]{3,2,1,0:T(8,128)} %convolution_bitcast_fusion.1), channel_id=3, replica_groups=mesh['sec'=2,'grp'=4,'tp'=4] {'sec','tp'}, use_global_device_ids=true, to_apply=%region_21.22.clone | all-reduce | flops 368640 | bytes 2211840
  198.6 3.3 %all-to-all-start.1 = ((bf16[1,4,16,360]{3,2,0,1:T(8,128)(2,1)}), bf16[1,4,16,360]{3,2,0,1:T(8,128)(2,1)S(1)}, u32[]{:S(2)}, u32[]{:S(2)}) async-start(bf16[1,4,16,360]{3,2,0,1:T(8,128)(2,1)} %fusion.85), calls=%async_computation.1 | async-start | bytes 98304 | tf_op jit(solution)/shard_map/all_to_all | solution.py:179
  201.9 1.6 fusion.86
  203.4 4.1 %all-to-all-done.1 = bf16[1,4,16,360]{3,2,0,1:T(8,128)(2,1)S(1)} async-done(((bf16[1,4,16,360]{3,2,0,1:T(8,128)(2,1)}), bf16[1,4,16,360]{3,2,0,1:T(8,128)(2,1)S(1)}, u32[]{:S(2)}, u32[]{:S(2)}) %all-to-all-start.1) | async-done | bytes 46112 | tf_op jit(solution)/shard_map/all_to_all | solution.py:179
  207.6 3.3 %all-to-all-start.3 = ((bf16[1,4,16,360]{3,2,0,1:T(8,128)(2,1)}), bf16[1,4,16,360]{3,2,0,1:T(8,128)(2,1)S(1)}, u32[]{:S(2)}, u32[]{:S(2)}) async-start(bf16[1,4,16,360]{3,2,0,1:T(8,128)(2,1)} %fusion.86), calls=%async_computation.3 | async-start | bytes 98304 | tf_op jit(solution)/shard_map/all_to_all | solution.py:179
  211.0 5.5 %all-to-all-done.3 = bf16[1,4,16,360]{3,2,0,1:T(8,128)(2,1)S(1)} async-done(((bf16[1,4,16,360]{3,2,0,1:T(8,128)(2,1)}), bf16[1,4,16,360]{3,2,0,1:T(8,128)(2,1)S(1)}, u32[]{:S(2)}, u32[]{:S(2)}) %all-to-all-start.3) | async-done | bytes 46112 | tf_op jit(solution)/shard_map/all_to_all | solution.py:179
  (84 shorter events, 12.2 us)
Async XLA Ops:
  6.5 19.9 %copy-start = (bf16[512,2880]{0,1:T(8,128)(2,1)S(1)}, bf16[512,2880]{0,1:T(8,128)(2,1)}, u32[]{:S(2)}) copy-start(bf16[512,2880]{0,1:T(8,128)(2,1)} %param.19) | copy-start | bytes 8847364
  6.5 4.3 %copy-start.3 = (bf16[2,16,2880]{2,1,0:T(8,128)(2,1)S(1)}, bf16[2,16,2880]{2,1,0:T(8,128)(2,1)}, u32[]{:S(2)}) copy-start(bf16[2,16,2880]{2,1,0:T(8,128)(2,1)} %param.14) | copy-start | bytes 552964
  6.5 80.2 %all-reduce.7.cloned.1.call-start = ((), (), s32[]{:S(2)}) async-start(), calls=%async_computation.4 | async-start | bytes 753664 | tf_op jit(solution)/shard_map/psum | solution.py:148
  6.5 4.3 %copy-start.4 = (bf16[2880,1,128]{2,0,1:T(8,128)(2,1)S(1)}, bf16[2880,1,128]{2,0,1:T(8,128)(2,1)}, u32[]{:S(2)}) copy-start(bf16[2880,1,128]{2,0,1:T(8,128)(2,1)} %param.17) | copy-start | bytes 2211844
  12.2 4.6 %copy-start.5 = (f32[2880]{0:T(1024)S(1)}, f32[2880]{0:T(1024)}, u32[]{:S(2)}) copy-start(f32[2880]{0:T(1024)} %param.15) | copy-start | bytes 34564
  16.8 3.3 %copy-start.1 = (bf16[2880,512]{0,1:T(8,128)(2,1)S(1)}, bf16[2880,512]{0,1:T(8,128)(2,1)}, u32[]{:S(2)}) copy-start(bf16[2880,512]{0,1:T(8,128)(2,1)} %copy.68) | copy-start | bytes 8847364
  20.2 2.0 copy-start.2
  22.1 1.2 copy-start.7
  28.0 1.6 copy-start.8
  28.0 3.1 %copy-start.9 = (f32[2,16,4]{1,2,0:T(4,128)S(1)}, f32[2,16,4]{1,2,0:T(4,128)}, u32[]{:S(2)}) copy-start(f32[2,16,4]{1,2,0:T(4,128)} %param.27) | copy-start | bytes 1540
  29.6 58.3 %copy-start.6 = (f32[2880]{0:T(1024)S(1)}, f32[2880]{0:T(1024)}, u32[]{:S(2)}) copy-start(f32[2880]{0:T(1024)} %param.22) | copy-start | bytes 34564
  88.9 19.5 %copy-start.10 = (u32[32]{0:T(128)S(1)}, u32[32]{0:T(128)}, u32[]{:S(2)}) copy-start(u32[32]{0:T(128)} %constant.61) | copy-start | bytes 388
  88.9 15.2 %all-to-all-start.2 = ((bf16[1,4,16,2880]{3,2,0,1:T(8,128)(2,1)}), bf16[1,4,16,2880]{3,2,0,1:T(8,128)(2,1)S(1)}, u32[]{:S(2)}, u32[]{:S(2)}) async-start(bf16[1,4,16,2880]{3,2,0,1:T(8,128)(2,1)} %bitcast.159), calls=%async_computation.2 | async-start | bytes 753664 | tf_op jit(solution)/shard_map/all_to_all | solution.py:167
  104.2 13.5 %all-to-all-start = ((bf16[1,4,16,2880]{3,2,0,1:T(8,128)(2,1)}), bf16[1,4,16,2880]{3,2,0,1:T(8,128)(2,1)}, u32[]{:S(2)}, u32[]{:S(2)}) async-start(bf16[1,4,16,2880]{3,2,0,1:T(8,128)(2,1)} %bitcast.158), calls=%async_computation | async-start | bytes 753664 | tf_op jit(solution)/shard_map/all_to_all | solution.py:167
  198.6 8.9 %all-to-all-start.1 = ((bf16[1,4,16,360]{3,2,0,1:T(8,128)(2,1)}), bf16[1,4,16,360]{3,2,0,1:T(8,128)(2,1)S(1)}, u32[]{:S(2)}, u32[]{:S(2)}) async-start(bf16[1,4,16,360]{3,2,0,1:T(8,128)(2,1)} %fusion.85), calls=%async_computation.1 | async-start | bytes 98304 | tf_op jit(solution)/shard_map/all_to_all | solution.py:179
  207.6 8.9 %all-to-all-start.3 = ((bf16[1,4,16,360]{3,2,0,1:T(8,128)(2,1)}), bf16[1,4,16,360]{3,2,0,1:T(8,128)(2,1)S(1)}, u32[]{:S(2)}, u32[]{:S(2)}) async-start(bf16[1,4,16,360]{3,2,0,1:T(8,128)(2,1)} %fusion.86), calls=%async_computation.3 | async-start | bytes 98304 | tf_op jit(solution)/shard_map/all_to_all | solution.py:179
Sparse Core Ops, SparseCore 0:
  29.7 56.9 all-reduce.6
where the time goes:
time: 225 us; the launch traced here: 224 us
  waiting for transfers between devices  76.9 us (34%)
  blocking collectives  74.9 us (33%)
  matrix products  27.4 us (12%)
  starting transfers between devices  15.3 us (7%)
  between operations  14.4 us (6%)
  local copies, waits for them, and re-layouts  8.41 us (4%)
  other arithmetic  6.86 us (3%)
    unnamed x1, blocking collectives  74.9 us
    psum x1, waiting for transfers between devices, body(): summed = lax.psum(partial_sum[None], ('sec', 'tp'))  55.6 us
    all_to_all x2, waiting for transfers between devices, body(): lax.all_to_all(outgoing, 'grp', split_axis=1, concat_axis=1, tiled=True)  11.7 us
    all_to_all x2, waiting for transfers between devices, body(): lax.all_to_all(reduced, 'grp', split_axis=1, concat_axis=1, tiled=True)  9.63 us
    all_to_all x2, starting transfers between devices, body(): lax.all_to_all(outgoing, 'grp', split_axis=1, concat_axis=1, tiled=True)  8.77 us
    dot_general x2, matrix products, body(): jnp.einsum('snph,hd->snpd', act, down_matrix, preferred_element_type=jnp....  6.99 us
    all_to_all x2, starting transfers between devices, body(): lax.all_to_all(reduced, 'grp', split_axis=1, concat_axis=1, tiled=True)  6.55 us
    unnamed x26, local copies, waits for them, and re-layouts  5.37 us
  transfers between devices with their start and end apart: 5, of which 5 were waited for; matrix products, arithmetic and copies ran while one was open for 5% of the time, Pallas kernels for 0%

commit v1 on v0

--- a/solution.py
+++ b/solution.py
@@ -29,6 +29,98 @@
         ],
         axis=-1,
     )
+
+
+def attention_partial(normed, w_query, key_value_weight, head_sink_logits, w_output, cache_pairs, lengths, steps):
+    rows = lengths.shape[0]
+    query = jnp.dot(normed, w_query, preferred_element_type=jnp.float32)
+    pairs = jnp.dot(normed, key_value_weight, preferred_element_type=jnp.float32)
+    heads = query.shape[1] // HEAD_SIZE
+    position = (lengths[None, :] + jnp.arange(steps)[:, None]).astype(jnp.float32)[..., None]
+    turned = rotate(query.reshape(steps, rows, heads, HEAD_SIZE), position[..., None]).astype(jnp.bfloat16)
+    pairs = pairs.reshape(steps, rows, 2 * HEAD_SIZE)
+    new_key = rotate(pairs[..., :HEAD_SIZE], position).astype(jnp.bfloat16)
+    new_value = pairs[..., HEAD_SIZE:].astype(jnp.bfloat16)
+    cached = jnp.einsum("srgd,rjd->rsgj", turned, cache_pairs[..., :HEAD_SIZE], preferred_element_type=jnp.float32) * 0.125
+    valid = (jnp.arange(cache_pairs.shape[1])[None, :] < lengths[:, None])[:, None, None, :]
+    cached = jnp.where(valid, cached, -jnp.inf)
+    fresh = jnp.einsum("srgd,ird->rsgi", turned, new_key, preferred_element_type=jnp.float32) * 0.125
+    seen = (jnp.arange(steps)[None, :] <= jnp.arange(steps)[:, None])[None, :, None, :]
+    fresh = jnp.where(seen, fresh, -jnp.inf)
+    sink = head_sink_logits[None, None, :]
+    largest = jnp.maximum(jnp.maximum(jnp.max(cached, -1), jnp.max(fresh, -1)), sink)
+    cached_exp = jnp.exp(cached - largest[..., None])
+    fresh_exp = jnp.exp(fresh - largest[..., None])
+    total = jnp.sum(cached_exp, -1) + jnp.sum(fresh_exp, -1) + jnp.exp(sink - largest)
+    cached_probs = (cached_exp / total[..., None]).astype(jnp.bfloat16)
+    fresh_probs = (fresh_exp / total[..., None]).astype(jnp.bfloat16)
+    mixed = jnp.einsum("rsgj,rjd->srgd", cached_probs, cache_pairs[..., HEAD_SIZE:], preferred_element_type=jnp.float32)
+    mixed = mixed + jnp.einsum("rsgi,ird->srgd", fresh_probs, new_value, preferred_element_type=jnp.float32)
+    mixed = mixed.reshape(steps * rows, heads * HEAD_SIZE).astype(jnp.bfloat16)
+    return jnp.dot(mixed, w_output, preferred_element_type=jnp.float32)
+
+
+def swap(value, axes, mask):
+    size = lax.axis_size(axes)
+    return lax.ppermute(value, axes, [(i, i ^ mask) for i in range(size)])
+
+
+def every_expert_body(inputs, attention_gain, w_query, key_value_weight, head_sink_logits, w_output, cache_pairs, lengths,
+                      expert_gain, w_gate, w_up, w_down, routes, gate_weights):
+    shards = lax.axis_size(("sec", "tp"))
+    mine = lax.axis_index(("sec", "tp"))
+    sec, tp, grp = lax.axis_index("sec"), lax.axis_index("tp"), lax.axis_index("grp")
+    secs, tps, groups = lax.axis_size("sec"), lax.axis_size("tp"), lax.axis_size("grp")
+    steps, rows, width = inputs.shape
+    part = width // shards
+    flat = inputs.reshape(steps * rows, width)
+    normed = rms_norm(flat, attention_gain)
+    partial = attention_partial(normed, w_query, key_value_weight[:, 0], head_sink_logits, w_output,
+                                cache_pairs[:, :, 0], lengths, steps)
+    chunks = partial.reshape(steps * rows, shards, part).swapaxes(0, 1)
+    own = lax.dynamic_index_in_dim(chunks, mine, 0, False)
+    chunks = chunks.astype(jnp.bfloat16)
+    arrived = [swap(lax.dynamic_index_in_dim(chunks, mine ^ m, 0, False), ("sec", "tp"), m) for m in range(1, shards)]
+    own_input = lax.dynamic_slice_in_dim(flat, mine * part, part, 1).astype(jnp.float32)
+    for piece in arrived:
+        own = own + piece.astype(jnp.float32)
+    middle = (own_input + own).astype(jnp.bfloat16)
+    grouped = jnp.stack([middle] + [swap(middle, "grp", m) for m in range(1, groups)])
+    grouped = jnp.stack([grouped] + [swap(grouped, "tp", m) for m in range(1, tps)])
+    grouped = jnp.stack([grouped] + [swap(grouped, "sec", m) for m in range(1, secs)])
+    grouped = jnp.take(grouped, jnp.arange(secs) ^ sec, axis=0)
+    grouped = jnp.take(grouped, jnp.arange(tps) ^ tp, axis=1)
+    everyone = grouped.transpose(2, 3, 0, 1, 4).reshape(groups * steps * rows, width)
+    expert_in = rms_norm(everyone, expert_gain)
+    gate_h = jnp.dot(expert_in, w_gate[0], preferred_element_type=jnp.float32)
+    up_h = jnp.dot(expert_in, w_up[0], preferred_element_type=jnp.float32)
+    act = ((up_h + 1.0) * gate_h * jax.nn.sigmoid(1.702 * gate_h)).astype(jnp.bfloat16)
+    out = jnp.dot(act, w_down[0], preferred_element_type=jnp.float32)
+    halves = out.reshape(-1, secs, tps * part).swapaxes(0, 1)
+    held = lax.dynamic_index_in_dim(halves, sec, 0, False)
+    for m in range(1, secs):
+        held = held + swap(lax.dynamic_index_in_dim(halves, sec ^ m, 0, False).astype(jnp.bfloat16), "sec", m).astype(jnp.float32)
+    quarters = held.reshape(-1, tps, part).swapaxes(0, 1)
+    held = lax.dynamic_index_in_dim(quarters, tp, 0, False)
+    quarters = quarters.astype(jnp.bfloat16)
+    come = [swap(lax.dynamic_index_in_dim(quarters, tp ^ m, 0, False), "tp", m) for m in range(1, tps)]
+    for piece in come:
+        held = held + piece.astype(jnp.float32)
+    held = held.astype(jnp.bfloat16).reshape(groups, steps * rows, part)
+    back = [held[0]] + [swap(held[m], "grp", m) for m in range(1, groups)]
+    weights = gate_weights.reshape(steps * rows, TOP)
+    named = routes.reshape(steps * rows, TOP)
+    result = middle.astype(jnp.float32)
+    for m in range(groups):
+        weight = jnp.sum(jnp.where(named == (grp ^ m), weights, 0.0), axis=1, keepdims=True)
+        result = result + weight * back[m].astype(jnp.float32)
+    return result.astype(jnp.bfloat16).reshape(steps, rows, part)
+
+
+def body(*args):
+    if lax.axis_size("grp") * args[9].shape[0] == TOP and args[9].shape[0] == 1:
+        return every_expert_body(*args)
+    return general_body(*args)
 
 
 def attend(
@@ -100,7 +192,7 @@
     return (partial_sum, fresh_keys, fresh_values)
 
 
-def body(
+def general_body(
     inputs,
     attention_gain,
     w_query,

time: 225 us -> 103 us (0.46)
  blocking collectives: 74.9 us -> 0 us
  waiting for transfers between devices: 76.9 us -> 19.7 us
  local copies, waits for them, and re-layouts: 8.41 us -> 27.1 us
  between operations: 14.4 us -> 0.27 us
  matrix products: 27.4 us -> 14.6 us
  starting transfers between devices: 15.3 us -> 24.7 us
  other arithmetic: 6.86 us -> 15.5 us
    unnamed x1 -> x0, blocking collectives: 74.9 us -> none
    psum x1 -> x0, waiting for transfers between devices: 55.6 us -> none  [body(): summed = lax.psum(partial_sum[None], ('sec', 'tp'))]
    ppermute x0 -> x21, starting transfers between devices: none -> 24.7 us  [swap(): return lax.ppermute(value, axes, [(i, i ^ mask) for i in range(size)])]
    all_to_all x4 -> x0, waiting for transfers between devices: 21.3 us -> none  [the longest x2 11.7 us: body(): lax.all_to_all(outgoing, 'grp', split_axis=1, concat_axis=1, tiled=True)]
    ppermute x0 -> x21, waiting for transfers between devices: none -> 19.7 us  [swap(): return lax.ppermute(value, axes, [(i, i ^ mask) for i in range(size)])]
    all_to_all x4 -> x0, starting transfers between devices: 15.3 us -> none  [the longest x2 8.77 us: body(): lax.all_to_all(outgoing, 'grp', split_axis=1, concat_axis=1, tiled=True)]
    dot_general x21 -> x9, matrix products: 27.4 us -> 14.6 us  [the longest x1 3.91 us: every_expert_body(): out = jnp.dot(act, w_down[0], preferred_element_type=jnp.float32)]
    gather x0 -> x2, local copies, waits for them, and re-layouts: none -> 5.43 us  [the longest x1 2.73 us: every_expert_body(): grouped = jnp.take(grouped, jnp.arange(secs) ^ sec, axis=0)]
  transfers between devices with their start and end apart: 5 -> 21, of which waited for: 5 -> 13; matrix products, arithmetic and copies ran while one was open for 5% -> 7% of each run, Pallas kernels for 0% -> 0%
where the time goes in v1:
time: 103 us; the launch traced here: 102 us
  local copies, waits for them, and re-layouts  27.1 us (26%)
  starting transfers between devices  24.7 us (24%)
  waiting for transfers between devices  19.7 us (19%)
  other arithmetic  15.5 us (15%)
  matrix products  14.6 us (14%)
    ppermute x21, starting transfers between devices, swap(): return lax.ppermute(value, axes, [(i, i ^ mask) for i in range(size)])  24.7 us
    ppermute x21, waiting for transfers between devices, swap(): return lax.ppermute(value, axes, [(i, i ^ mask) for i in range(size)])  19.7 us
    unnamed x20, local copies, waits for them, and re-layouts  7.83 us
    dot_general x1, local copies, waits for them, and re-layouts, every_expert_body(): out = jnp.dot(act, w_down[0], preferred_element_type=jnp.float32)  4.53 us
    dot_general x1, matrix products, every_expert_body(): out = jnp.dot(act, w_down[0], preferred_element_type=jnp.float32)  3.91 us
    dot_general x1, matrix products, attention_partial(): query = jnp.dot(normed, w_query, preferred_element_type=jnp.float32)  3.38 us
    another operation x6, local copies, waits for them, and re-layouts  3.37 us
    another operation x2, other arithmetic, every_expert_body(): jnp.stack([grouped] + [swap(grouped, 'sec', m) for m in range(1, secs)])  2.91 us
  transfers between devices with their start and end apart: 21, of which 13 were waited for; matrix products, arithmetic and copies ran while one was open for 7% of the time, Pallas kernels for 0%

profile of v1, /device:TPU:0, one launch (start us, length us, event | category | flops | bytes accessed | tf_op | source)
XLA Modules:
  0.0 101.9 jit_solution(2776063096503877532)
XLA Ops:
  2.7 4.6 %copy.38 = bf16[2880,512]{0,1:T(8,128)(2,1)} copy(bf16[2880,512]{1,0:T(8,128)(2,1)} %param.16) | data formatting | bytes 5898240 | tf_op args[2]
  8.8 3.4 %fusion.30 = f32[2,16,8,64]{3,1,2,0:T(8,128)S(1)} fusion(bf16[8,64,2880,1]{2,1,0,3:T(8,128)(2,1)} %bitcast.143, bf16[2,16,2880]{2,1,0:T(8,128)(2,1)S(1)} %copy-done.3, f32[2880]{0:T(1024)S(1)} %copy-done.4, f32[2,16]{1,0:T(2,128)S(1)} %add_rsqrt_fusion.1), kind=kOutput, calls=%fused_computation.50 | convolution fusion | flops 94740480 | bytes 3210624 | tf_op jit(solution)/shard_map/dot_general | solution.py:36
  12.2 2.3 %copy.39 = bf16[16,256,1,128]{1,3,0,2:T(8,128)(2,1)} copy(bf16[16,256,1,128]{3,1,2,0:T(8,128)(2,1)} %param.20) | data formatting | bytes 2097152 | tf_op args[6]
  17.7 1.7 %fusion.68 = (bf16[32,8,360]{2,0,1:T(8,128)(2,1)S(1)}, f32[32,8,360]{2,0,1:T(8,128)}) fusion(bf16[32,512,1]{1,0,2:T(8,128)(2,1)S(1)} %reshape.311, bf16[8,360,512]{2,1,0:T(8,128)(2,1)S(1)} %bitcast.142), kind=kOutput, calls=%fused_computation.131 | convolution fusion | flops 94464000 | bytes 3534848 | tf_op jit(solution)/shard_map/dot_general | solution.py:60
  19.5 3.0 %collective-permute-start = (bf16[32,360]{1,0:T(8,128)(2,1)S(1)}, bf16[32,360]{1,0:T(8,128)(2,1)S(1)}, u32[]{:S(2)}, u32[]{:S(2)}) collective-permute-start(bf16[32,360]{1,0:T(8,128)(2,1)S(1)} %get-tuple-element.14), channel_id=1, source_target_pairs={{0,1},{1,0},{2,3},{3,2},{16,17},{17,16},{18,19},{19,18},{4,5},{5,4... | collective-permute-start | bytes 69128 | tf_op jit(solution)/shard_map/ppermute | solution.py:65
  24.0 2.1 %collective-permute-start.4 = (bf16[32,360]{1,0:T(8,128)(2,1)S(1)}, bf16[32,360]{1,0:T(8,128)(2,1)S(1)}, u32[]{:S(2)}, u32[]{:S(2)}) collective-permute-start(bf16[32,360]{1,0:T(8,128)(2,1)S(1)} %get-tuple-element.17), channel_id=1, source_target_pairs={{0,17},{1,16},{2,19},{3,18},{16,1},{17,0},{18,3},{19,2},{4,21},{5,... | collective-permute-start | bytes 69128 | tf_op jit(solution)/shard_map/ppermute | solution.py:65
  29.4 2.0 %collective-permute-done.6 = bf16[32,360]{1,0:T(8,128)(2,1)S(1)} collective-permute-done((bf16[32,360]{1,0:T(8,128)(2,1)S(1)}, bf16[32,360]{1,0:T(8,128)(2,1)S(1)}, u32[]{:S(2)}, u32[]{:S(2)}) %collective-permute-start.6) | collective-permute-done | bytes 23072 | tf_op jit(solution)/shard_map/ppermute | solution.py:65
  32.3 1.6 %collective-permute-start.7 = (bf16[32,360]{1,0:T(8,128)(2,1)S(1)}, bf16[32,360]{1,0:T(8,128)(2,1)S(1)}, u32[]{:S(2)}, u32[]{:S(2)}) collective-permute-start(bf16[32,360]{1,0:T(8,128)(2,1)S(1)} %fusion.50), channel_id=1, source_target_pairs={{0,4},{4,0},{8,12},{12,8},{1,5},{5,1},{9,13},{13,9},{2,6},{6,2},{1... | collective-permute-start | bytes 69128 | tf_op jit(solution)/shard_map/ppermute | solution.py:65
  33.9 2.6 %collective-permute-start.8 = (bf16[32,360]{1,0:T(8,128)(2,1)S(1)}, bf16[32,360]{1,0:T(8,128)(2,1)S(1)}, u32[]{:S(2)}, u32[]{:S(2)}) collective-permute-start(bf16[32,360]{1,0:T(8,128)(2,1)S(1)} %fusion.50), channel_id=1, source_target_pairs={{0,8},{4,12},{8,0},{12,4},{1,9},{5,13},{9,1},{13,5},{2,10},{6,14},... | collective-permute-start | bytes 69128 | tf_op jit(solution)/shard_map/ppermute | solution.py:65
  36.7 2.1 %collective-permute-done.8 = bf16[32,360]{1,0:T(8,128)(2,1)S(1)} collective-permute-done((bf16[32,360]{1,0:T(8,128)(2,1)S(1)}, bf16[32,360]{1,0:T(8,128)(2,1)S(1)}, u32[]{:S(2)}, u32[]{:S(2)}) %collective-permute-start.8) | collective-permute-done | bytes 23072 | tf_op jit(solution)/shard_map/ppermute | solution.py:65
  38.8 3.3 %collective-permute-done.9 = bf16[32,360]{1,0:T(8,128)(2,1)S(1)} collective-permute-done((bf16[32,360]{1,0:T(8,128)(2,1)S(1)}, bf16[32,360]{1,0:T(8,128)(2,1)S(1)}, u32[]{:S(2)}, u32[]{:S(2)}) %collective-permute-start.9) | collective-permute-done | bytes 23072 | tf_op jit(solution)/shard_map/ppermute | solution.py:65
  43.3 2.4 %collective-permute-start.12 = (bf16[4,32,360]{2,1,0:T(8,128)(2,1)S(1)}, bf16[4,32,360]{2,1,0:T(8,128)(2,1)S(1)}, u32[]{:S(2)}, u32[]{:S(2)}) collective-permute-start(bf16[4,32,360]{2,1,0:T(8,128)(2,1)S(1)} %get-tuple-element.27), channel_id=1, source_target_pairs={{0,3},{1,2},{2,1},{3,0},{4,7},{5,6},{6,5},{7,4},{8,11},{9,10},{10,... | collective-permute-start | bytes 276488 | tf_op jit(solution)/shard_map/ppermute | solution.py:65
  49.8 4.5 %dot_general.56 = bf16[2,1440,180]{1,0,2:T(2,128)(2,1)} reshape(bf16[2880,180]{0,1:T(8,128)(2,1)} %bitcast.149) | data formatting | bytes 2073600 | tf_op jit(solution)/shard_map/dot_general | solution.py:98
  54.4 2.1 %pad_maximum_fusion = bf16[2,4,4,32,360]{4,3,2,1,0:T(8,128)(2,1)} fusion(bf16[1,4,4,32,360]{4,3,2,1,0:T(8,128)(2,1)} %bitcast.36, bf16[1,4,4,32,360]{4,3,2,1,0:T(8,128)(2,1)S(1)} %get-tuple-element.9), kind=kLoop, calls=%fused_computation.27 | loop fusion | flops 368640 | bytes 1474560 | tf_op jit(solution)/shard_map/stack | solution.py:90
  56.5 2.7 %gather_fusion = bf16[2,4,4,32,360]{4,3,2,1,0:T(8,128)(2,1)} fusion(bf16[2,4,4,32,360]{4,3,2,1,0:T(8,128)(2,1)} %pad_maximum_fusion, s32[1024]{0:T(1024)S(1)} %pad_clamp_fusion.1), kind=kCustom, calls=%fused_computation | custom fusion | bytes 1474568 | tf_op jit(solution)/shard_map/jit(_take)/gather | solution.py:91
  59.2 2.2 %broadcast_select_fusion.1 = bf16[2,4,4,32,360]{4,3,2,1,0:T(8,128)(2,1)} fusion(bf16[2,4,4,32,360]{4,3,2,1,0:T(8,128)(2,1)} %gather_fusion, pred[2]{0:T(512)(128)(4,1)S(1)} %compare_and_fusion), kind=kLoop, calls=%fused_computation.29 | loop fusion | flops 368640 | bytes 1474562 | tf_op jit(solution)/shard_map/jit(_take)/select_n | solution.py:91
  61.4 2.7 %gather_fusion.1 = bf16[4,2,4,32,360]{4,3,2,1,0:T(8,128)(2,1)} fusion(bf16[2,4,4,32,360]{4,3,2,1,0:T(8,128)(2,1)} %broadcast_select_fusion.1, s32[1024]{0:T(1024)S(1)} %pad_clamp_fusion), kind=kCustom, calls=%fused_computation.1 | custom fusion | bytes 1474576 | tf_op jit(solution)/shard_map/jit(_take)/gather | solution.py:92
  67.1 1.5 %copy.46 = bf16[4,32,2,4,360]{4,3,2,1,0:T(4,128)(2,1)} copy(bf16[4,32,2,4,360]{4,1,0,2,3:T(8,128)(2,1)S(1)} %fusion.17) | data formatting | bytes 1474560 | tf_op jit(solution)/shard_map/mul | solution.py:13
  68.7 2.6 %convert_element_type.158 = bf16[128,2880]{1,0:T(8,128)(2,1)} reshape(bf16[4,32,2,4,360]{4,3,2,1,0:T(4,128)(2,1)} %copy.46) | data formatting | bytes 1474560 | tf_op jit(solution)/shard_map/convert_element_type | solution.py:13
  71.3 1.9 %fusion.14 = f32[128,180]{0,1:T(8,128)S(1)} fusion(bf16[128,2880]{1,0:T(8,128)(2,1)} %convert_element_type.158, bf16[1,2880,180]{1,2,0:T(8,128)(2,1)} %param.23), kind=kOutput, calls=%fused_computation.23 | convolution fusion | flops 132710400 | bytes 1866240 | tf_op jit(solution)/shard_map/dot_general | solution.py:95
  73.2 3.9 %fusion.6 = f32[128,2,1440]{0,2,1:T(8,128)} fusion(bf16[2,1440,180]{1,0,2:T(2,128)(2,1)} %dot_general.56, f32[128,180]{0,1:T(8,128)S(1)} %fusion.14, bf16[128,2880]{1,0:T(8,128)(2,1)} %convert_element_type.158, bf16[1,2880,180]{1,2,0:T(8,128)(2,1)} %param.24), kind=kOutput, calls=%fused_computation.13 | convolution fusion | flops 265605120 | bytes 4377600 | tf_op jit(solution)/shard_map/dot_general | solution.py:98
  90.7 2.9 %collective-permute-done.17 = bf16[128,360]{1,0:T(8,128)(2,1)} collective-permute-done((bf16[128,360]{1,0:T(8,128)(2,1)}, bf16[128,360]{1,0:T(8,128)(2,1)}, u32[]{:S(2)}, u32[]{:S(2)}) %collective-permute-start.17) | collective-permute-done | bytes 92192 | tf_op jit(solution)/shard_map/ppermute | solution.py:65
  95.6 3.5 %collective-permute-start.20 = (bf16[32,360]{1,0:T(8,128)(2,1)S(1)}, bf16[32,360]{1,0:T(8,128)(2,1)S(1)}, u32[]{:S(2)}, u32[]{:S(2)}) collective-permute-start(bf16[32,360]{1,0:T(8,128)(2,1)S(1)} %get-tuple-element.24), channel_id=1, source_target_pairs={{0,12},{4,8},{8,4},{12,0},{1,13},{5,9},{9,5},{13,1},{2,14},{6,10},... | collective-permute-start | bytes 69128 | tf_op jit(solution)/shard_map/ppermute | solution.py:65
  99.5 1.7 %collective-permute-done.20 = bf16[32,360]{1,0:T(8,128)(2,1)S(1)} collective-permute-done((bf16[32,360]{1,0:T(8,128)(2,1)S(1)}, bf16[32,360]{1,0:T(8,128)(2,1)S(1)}, u32[]{:S(2)}, u32[]{:S(2)}) %collective-permute-start.20) | collective-permute-done | bytes 23072 | tf_op jit(solution)/shard_map/ppermute | solution.py:65
  (103 shorter events, 38.3 us)
Async XLA Ops:
  0.0 17.7 %copy-start = (bf16[512,2880]{0,1:T(8,128)(2,1)S(1)}, bf16[512,2880]{0,1:T(8,128)(2,1)}, u32[]{:S(2)}) copy-start(bf16[512,2880]{0,1:T(8,128)(2,1)} %param.19) | copy-start | bytes 8847364
  19.4 30.3 %copy-start.5 = (f32[2880]{0:T(1024)S(1)}, f32[2880]{0:T(1024)}, u32[]{:S(2)}) copy-start(f32[2880]{0:T(1024)} %param.22) | copy-start | bytes 34564
  19.5 6.6 %collective-permute-start = (bf16[32,360]{1,0:T(8,128)(2,1)S(1)}, bf16[32,360]{1,0:T(8,128)(2,1)S(1)}, u32[]{:S(2)}, u32[]{:S(2)}) collective-permute-start(bf16[32,360]{1,0:T(8,128)(2,1)S(1)} %get-tuple-element.14), channel_id=1, source_target_pairs={{0,1},{1,0},{2,3},{3,2},{16,17},{17,16},{18,19},{19,18},{4,5},{5,4... | collective-permute-start | bytes 69128 | tf_op jit(solution)/shard_map/ppermute | solution.py:65
  22.5 4.7 %collective-permute-start.1 = (bf16[32,360]{1,0:T(8,128)(2,1)S(1)}, bf16[32,360]{1,0:T(8,128)(2,1)S(1)}, u32[]{:S(2)}, u32[]{:S(2)}) collective-permute-start(bf16[32,360]{1,0:T(8,128)(2,1)S(1)} %get-tuple-element.20), channel_id=1, source_target_pairs={{0,2},{1,3},{2,0},{3,1},{16,18},{17,19},{18,16},{19,17},{4,6},{5,7... | collective-permute-start | bytes 69128 | tf_op jit(solution)/shard_map/ppermute | solution.py:65
  24.0 5.0 %collective-permute-start.2 = (bf16[32,360]{1,0:T(8,128)(2,1)S(1)}, bf16[32,360]{1,0:T(8,128)(2,1)S(1)}, u32[]{:S(2)}, u32[]{:S(2)}) collective-permute-start(bf16[32,360]{1,0:T(8,128)(2,1)S(1)} %get-tuple-element.19), channel_id=1, source_target_pairs={{0,3},{1,2},{2,1},{3,0},{16,19},{17,18},{18,17},{19,16},{4,7},{5,6... | collective-permute-start | bytes 69128 | tf_op jit(solution)/shard_map/ppermute | solution.py:65
  24.0 4.9 %collective-permute-start.3 = (bf16[32,360]{1,0:T(8,128)(2,1)S(1)}, bf16[32,360]{1,0:T(8,128)(2,1)S(1)}, u32[]{:S(2)}, u32[]{:S(2)}) collective-permute-start(bf16[32,360]{1,0:T(8,128)(2,1)S(1)} %get-tuple-element.18), channel_id=1, source_target_pairs={{0,16},{1,17},{2,18},{3,19},{16,0},{17,1},{18,2},{19,3},{4,20},{5,... | collective-permute-start | bytes 69128 | tf_op jit(solution)/shard_map/ppermute | solution.py:65
  24.0 4.9 %collective-permute-start.4 = (bf16[32,360]{1,0:T(8,128)(2,1)S(1)}, bf16[32,360]{1,0:T(8,128)(2,1)S(1)}, u32[]{:S(2)}, u32[]{:S(2)}) collective-permute-start(bf16[32,360]{1,0:T(8,128)(2,1)S(1)} %get-tuple-element.17), channel_id=1, source_target_pairs={{0,17},{1,16},{2,19},{3,18},{16,1},{17,0},{18,3},{19,2},{4,21},{5,... | collective-permute-start | bytes 69128 | tf_op jit(solution)/shard_map/ppermute | solution.py:65
  26.1 3.3 %collective-permute-start.5 = (bf16[32,360]{1,0:T(8,128)(2,1)S(1)}, bf16[32,360]{1,0:T(8,128)(2,1)S(1)}, u32[]{:S(2)}, u32[]{:S(2)}) collective-permute-start(bf16[32,360]{1,0:T(8,128)(2,1)S(1)} %get-tuple-element.16), channel_id=1, source_target_pairs={{0,18},{1,19},{2,16},{3,17},{16,2},{17,3},{18,0},{19,1},{4,22},{5,... | collective-permute-start | bytes 69128 | tf_op jit(solution)/shard_map/ppermute | solution.py:65
  27.2 4.2 %collective-permute-start.6 = (bf16[32,360]{1,0:T(8,128)(2,1)S(1)}, bf16[32,360]{1,0:T(8,128)(2,1)S(1)}, u32[]{:S(2)}, u32[]{:S(2)}) collective-permute-start(bf16[32,360]{1,0:T(8,128)(2,1)S(1)} %get-tuple-element.15), channel_id=1, source_target_pairs={{0,19},{1,18},{2,17},{3,16},{16,3},{17,2},{18,1},{19,0},{4,23},{5,... | collective-permute-start | bytes 69128 | tf_op jit(solution)/shard_map/ppermute | solution.py:65
  32.3 4.5 %collective-permute-start.7 = (bf16[32,360]{1,0:T(8,128)(2,1)S(1)}, bf16[32,360]{1,0:T(8,128)(2,1)S(1)}, u32[]{:S(2)}, u32[]{:S(2)}) collective-permute-start(bf16[32,360]{1,0:T(8,128)(2,1)S(1)} %fusion.50), channel_id=1, source_target_pairs={{0,4},{4,0},{8,12},{12,8},{1,5},{5,1},{9,13},{13,9},{2,6},{6,2},{1... | collective-permute-start | bytes 69128 | tf_op jit(solution)/shard_map/ppermute | solution.py:65
  33.9 4.9 %collective-permute-start.8 = (bf16[32,360]{1,0:T(8,128)(2,1)S(1)}, bf16[32,360]{1,0:T(8,128)(2,1)S(1)}, u32[]{:S(2)}, u32[]{:S(2)}) collective-permute-start(bf16[32,360]{1,0:T(8,128)(2,1)S(1)} %fusion.50), channel_id=1, source_target_pairs={{0,8},{4,12},{8,0},{12,4},{1,9},{5,13},{9,1},{13,5},{2,10},{6,14},... | collective-permute-start | bytes 69128 | tf_op jit(solution)/shard_map/ppermute | solution.py:65
  36.5 5.6 %collective-permute-start.9 = (bf16[32,360]{1,0:T(8,128)(2,1)S(1)}, bf16[32,360]{1,0:T(8,128)(2,1)S(1)}, u32[]{:S(2)}, u32[]{:S(2)}) collective-permute-start(bf16[32,360]{1,0:T(8,128)(2,1)S(1)} %fusion.50), channel_id=1, source_target_pairs={{0,12},{4,8},{8,4},{12,0},{1,13},{5,9},{9,5},{13,1},{2,14},{6,10},... | collective-permute-start | bytes 69128 | tf_op jit(solution)/shard_map/ppermute | solution.py:65
  42.1 5.0 %collective-permute-start.10 = (bf16[4,32,360]{2,1,0:T(8,128)(2,1)S(1)}, bf16[4,32,360]{2,1,0:T(8,128)(2,1)S(1)}, u32[]{:S(2)}, u32[]{:S(2)}) collective-permute-start(bf16[4,32,360]{2,1,0:T(8,128)(2,1)S(1)} %get-tuple-element.27), channel_id=1, source_target_pairs={{0,1},{1,0},{2,3},{3,2},{4,5},{5,4},{6,7},{7,6},{8,9},{9,8},{10,11... | collective-permute-start | bytes 276488 | tf_op jit(solution)/shard_map/ppermute | solution.py:65
  42.7 4.6 %collective-permute-start.11 = (bf16[4,32,360]{2,1,0:T(8,128)(2,1)S(1)}, bf16[4,32,360]{2,1,0:T(8,128)(2,1)S(1)}, u32[]{:S(2)}, u32[]{:S(2)}) collective-permute-start(bf16[4,32,360]{2,1,0:T(8,128)(2,1)S(1)} %get-tuple-element.27), channel_id=1, source_target_pairs={{0,2},{1,3},{2,0},{3,1},{4,6},{5,7},{6,4},{7,5},{8,10},{9,11},{10,... | collective-permute-start | bytes 276488 | tf_op jit(solution)/shard_map/ppermute | solution.py:65
  43.3 5.5 %collective-permute-start.12 = (bf16[4,32,360]{2,1,0:T(8,128)(2,1)S(1)}, bf16[4,32,360]{2,1,0:T(8,128)(2,1)S(1)}, u32[]{:S(2)}, u32[]{:S(2)}) collective-permute-start(bf16[4,32,360]{2,1,0:T(8,128)(2,1)S(1)} %get-tuple-element.27), channel_id=1, source_target_pairs={{0,3},{1,2},{2,1},{3,0},{4,7},{5,6},{6,5},{7,4},{8,11},{9,10},{10,... | collective-permute-start | bytes 276488 | tf_op jit(solution)/shard_map/ppermute | solution.py:65
  49.7 4.7 %collective-permute-start.13 = (bf16[4,4,32,360]{3,2,1,0:T(8,128)(2,1)}, bf16[4,4,32,360]{3,2,1,0:T(8,128)(2,1)}, u32[]{:S(2)}, u32[]{:S(2)}) collective-permute-start(bf16[4,4,32,360]{3,2,1,0:T(8,128)(2,1)} %get-tuple-element.10), channel_id=1, source_target_pairs={{0,16},{16,0},{1,17},{17,1},{2,18},{18,2},{3,19},{19,3},{4,20},{20... | collective-permute-start | bytes 1105928 | tf_op jit(solution)/shard_map/ppermute | solution.py:65
  78.2 2.0 %collective-permute-start.14 = (bf16[128,1440]{0,1:T(8,128)(2,1)S(1)}, bf16[128,1440]{0,1:T(8,128)(2,1)}, u32[]{:S(2)}, u32[]{:S(2)}) collective-permute-start(bf16[128,1440]{0,1:T(8,128)(2,1)S(1)} %fusion.25), channel_id=1, source_target_pairs={{0,16},{16,0},{1,17},{17,1},{2,18},{18,2},{3,19},{19,3},{4,20},{20... | collective-permute-start | bytes 1105928 | tf_op jit(solution)/shard_map/ppermute | solution.py:65
  82.5 16.6 %copy-start.6 = (f32[2,16,4]{1,2,0:T(4,128)S(1)}, f32[2,16,4]{1,2,0:T(4,128)}, u32[]{:S(2)}) copy-start(f32[2,16,4]{1,2,0:T(4,128)} %param.27) | copy-start | bytes 1540
  83.3 6.1 %collective-permute-start.15 = (bf16[128,360]{1,0:T(8,128)(2,1)}, bf16[128,360]{1,0:T(8,128)(2,1)S(1)}, u32[]{:S(2)}, u32[]{:S(2)}) collective-permute-start(bf16[128,360]{1,0:T(8,128)(2,1)} %bitcast.50), channel_id=1, source_target_pairs={{0,1},{1,0},{2,3},{3,2},{4,5},{5,4},{6,7},{7,6},{8,9},{9,8},{10,11... | collective-permute-start | bytes 276488 | tf_op jit(solution)/shard_map/ppermute | solution.py:65
  85.6 5.1 %collective-permute-start.16 = (bf16[128,360]{1,0:T(8,128)(2,1)}, bf16[128,360]{1,0:T(8,128)(2,1)}, u32[]{:S(2)}, u32[]{:S(2)}) collective-permute-start(bf16[128,360]{1,0:T(8,128)(2,1)} %bitcast.51), channel_id=1, source_target_pairs={{0,2},{1,3},{2,0},{3,1},{4,6},{5,7},{6,4},{7,5},{8,10},{9,11},{10,... | collective-permute-start | bytes 276488 | tf_op jit(solution)/shard_map/ppermute | solution.py:65
  87.8 5.8 %collective-permute-start.17 = (bf16[128,360]{1,0:T(8,128)(2,1)}, bf16[128,360]{1,0:T(8,128)(2,1)}, u32[]{:S(2)}, u32[]{:S(2)}) collective-permute-start(bf16[128,360]{1,0:T(8,128)(2,1)} %bitcast.52), channel_id=1, source_target_pairs={{0,3},{1,2},{2,1},{3,0},{4,7},{5,6},{6,5},{7,4},{8,11},{9,10},{10,... | collective-permute-start | bytes 276488 | tf_op jit(solution)/shard_map/ppermute | solution.py:65
  94.6 4.8 %collective-permute-start.18 = (bf16[32,360]{1,0:T(8,128)(2,1)S(1)}, bf16[32,360]{1,0:T(8,128)(2,1)S(1)}, u32[]{:S(2)}, u32[]{:S(2)}) collective-permute-start(bf16[32,360]{1,0:T(8,128)(2,1)S(1)} %get-tuple-element.23), channel_id=1, source_target_pairs={{0,4},{4,0},{8,12},{12,8},{1,5},{5,1},{9,13},{13,9},{2,6},{6,2},{1... | collective-permute-start | bytes 69128 | tf_op jit(solution)/shard_map/ppermute | solution.py:65
  94.7 4.8 %collective-permute-start.19 = (bf16[32,360]{1,0:T(8,128)(2,1)S(1)}, bf16[32,360]{1,0:T(8,128)(2,1)S(1)}, u32[]{:S(2)}, u32[]{:S(2)}) collective-permute-start(bf16[32,360]{1,0:T(8,128)(2,1)S(1)} %get-tuple-element.25), channel_id=1, source_target_pairs={{0,8},{4,12},{8,0},{12,4},{1,9},{5,13},{9,1},{13,5},{2,10},{6,14},... | collective-permute-start | bytes 69128 | tf_op jit(solution)/shard_map/ppermute | solution.py:65
  95.6 5.6 %collective-permute-start.20 = (bf16[32,360]{1,0:T(8,128)(2,1)S(1)}, bf16[32,360]{1,0:T(8,128)(2,1)S(1)}, u32[]{:S(2)}, u32[]{:S(2)}) collective-permute-start(bf16[32,360]{1,0:T(8,128)(2,1)S(1)} %get-tuple-element.24), channel_id=1, source_target_pairs={{0,12},{4,8},{8,4},{12,0},{1,13},{5,9},{9,5},{13,1},{2,14},{6,10},... | collective-permute-start | bytes 69128 | tf_op jit(solution)/shard_map/ppermute | solution.py:65
  (6 other events, 34.2 us)

commit v2 on v0

--- a/solution.py
+++ b/solution.py
@@ -1,6 +1,11 @@
+import functools
+
 import jax
 import jax.numpy as jnp
+import numpy as np
 from jax import lax
+from jax.experimental import pallas as pl
+from jax.experimental.pallas import tpu as pltpu
 from jax.sharding import PartitionSpec as P
 
 HEAD_SIZE = 64
@@ -100,7 +105,7 @@
     return (partial_sum, fresh_keys, fresh_values)
 
 
-def body(
+def general_body(
     inputs,
     attention_gain,
     w_query,
@@ -188,6 +193,349 @@
     return jnp.stack(results, 0)
 
 
+LANES = 384
+BASE = 150000.0
+MIB = 1 << 20
+
+
+def shape_of(shape, dtype=jnp.bfloat16):
+    return jax.ShapeDtypeStruct(shape, dtype)
+
+
+def vmem():
+    return pl.BlockSpec(memory_space=pltpu.VMEM)
+
+
+def smem():
+    return pl.BlockSpec(memory_space=pltpu.SMEM)
+
+
+def outside():
+    return pl.BlockSpec(memory_space=pltpu.HBM)
+
+
+def dot_last(left, right):
+    return lax.dot_general(left, right, (((1,), (1,)), ((), ())), preferred_element_type=jnp.float32)
+
+
+def swap(value, axes, mask):
+    size = lax.axis_size(axes)
+    return lax.ppermute(value, axes, [(i, i ^ mask) for i in range(size)])
+
+
+def split_width(width):
+    cuts = list(range(0, width, 768)) + [width]
+    return list(zip(cuts[:-1], cuts[1:]))
+
+
+def attention_kernel(lengths_ref, sinks_ref, gain_ref, x_hbm, wq_hbm, wkv_hbm, cache_hbm, wo_hbm,
+                     other_ref, mine_ref, own_x_ref,
+                     x_ref, wq_ref, wkv_ref, cache_ref, wo_ref, xs_ref, turned_ref, mixed_ref, chunk_ref, sems):
+    total_rows, width = x_ref.shape
+    rows, slots, pair = cache_ref.shape
+    steps = total_rows // rows
+    heads = wq_ref.shape[1] // HEAD_SIZE
+    per_row = heads * steps
+    tps = mine_ref.shape[0]
+    secs = chunk_ref.shape[0] // tps
+    cuts = split_width(width)
+    copies = [pltpu.make_async_copy(x_hbm, x_ref, sems.at[0]), pltpu.make_async_copy(wkv_hbm, wkv_ref, sems.at[1])]
+    for n, (low, high) in enumerate(cuts):
+        part = pl.ds(low, high - low)
+        copies.append(pltpu.make_async_copy(wq_hbm.at[part], wq_ref.at[part], sems.at[4 + n]))
+    copies.append(pltpu.make_async_copy(cache_hbm, cache_ref, sems.at[2]))
+    copies.append(pltpu.make_async_copy(wo_hbm, wo_ref, sems.at[3]))
+    for copy in copies:
+        copy.start()
+
+    lane = lax.broadcasted_iota(jnp.int32, (total_rows, pair), 1)
+    line = lax.broadcasted_iota(jnp.int32, (total_rows, pair), 0)
+    position = jnp.zeros((total_rows, pair), jnp.int32)
+    for r in range(rows):
+        for s in range(steps):
+            position = jnp.where(line == s * rows + r, lengths_ref[r] + s, position)
+    half = HEAD_SIZE // 2
+    counter = jnp.bitwise_and(lane, half - 1).astype(jnp.float32)
+    frequency = jnp.exp(counter * jnp.float32(-2.0 / HEAD_SIZE * np.log(BASE)))
+    angle = position.astype(jnp.float32) * frequency
+    cosine, sine = jnp.cos(angle), jnp.sin(angle)
+    low_half = jnp.bitwise_and(lane, HEAD_SIZE - 1) < half
+    sine = jnp.where(low_half, -sine, sine)
+
+    def turn(two):
+        return two * cosine + jnp.where(low_half, pltpu.roll(two, pair - half, 1), pltpu.roll(two, half, 1)) * sine
+
+    copies[0].wait()
+    x = x_ref[...].astype(jnp.float32)
+    xs_ref[...] = jnp.concatenate([x, jnp.zeros((total_rows, xs_ref.shape[1] - width), jnp.float32)], axis=1)
+    own = (lax.axis_index("sec") * tps + lax.axis_index("tp")) * LANES
+    own_x_ref[...] = xs_ref[:, pl.ds(pl.multiple_of(own, LANES), LANES)]
+    scale = lax.rsqrt(jnp.mean(x * x, axis=-1, keepdims=True) + 1e-05)
+    normed = (x * scale * gain_ref[...]).astype(jnp.bfloat16)
+    copies[1].wait()
+    pairs = jnp.dot(normed, wkv_ref[...], preferred_element_type=jnp.float32)
+    query = None
+    for n, (low, high) in enumerate(cuts):
+        copies[2 + n].wait()
+        term = jnp.dot(normed[:, low:high], wq_ref[low:high, :], preferred_element_type=jnp.float32)
+        query = term if query is None else query + term
+
+    is_key = lane < HEAD_SIZE
+    fresh = jnp.where(is_key, turn(pairs), pairs).astype(jnp.bfloat16)
+    for m in range(heads // 2):
+        two = turn(query[:, m * pair:(m + 1) * pair])
+        for odd in range(2):
+            one = two if odd == 0 else pltpu.roll(two, HEAD_SIZE, 1)
+            one = jnp.where(is_key, one, 0.0)
+            for s in range(steps):
+                slot = (2 * m + odd) * steps + s
+                turned_ref[pl.ds(slot, rows, stride=per_row), :] = one[s * rows:(s + 1) * rows]
+    turned = turned_ref[...].astype(jnp.bfloat16)
+
+    copies[-2].wait()
+    place = lax.broadcasted_iota(jnp.int32, (per_row, slots), 1)
+    scores = []
+    for r in range(rows):
+        score = dot_last(turned[r * per_row:(r + 1) * per_row], cache_ref[r]) * 0.125
+        scores.append(jnp.where(place < lengths_ref[r], score, -jnp.inf))
+    cached = jnp.concatenate(scores, axis=0)
+    row_at = lax.broadcasted_iota(jnp.int32, (rows * per_row, total_rows), 0)
+    fresh_at = lax.broadcasted_iota(jnp.int32, (rows * per_row, total_rows), 1)
+    seen = (row_at // per_row == fresh_at % rows) & (fresh_at // rows <= row_at % steps)
+    new = jnp.where(seen, dot_last(turned, fresh) * 0.125, -jnp.inf)
+    head_at = lax.broadcasted_iota(jnp.int32, (rows * per_row, 1), 0) % per_row // steps
+    sink = jnp.zeros((rows * per_row, 1), jnp.float32)
+    for h in range(heads):
+        sink = jnp.where(head_at == h, sinks_ref[h], sink)
+    largest = jnp.maximum(jnp.maximum(jnp.max(cached, axis=-1, keepdims=True), jnp.max(new, axis=-1, keepdims=True)), sink)
+    cached = jnp.exp(cached - largest)
+    new = jnp.exp(new - largest)
+    total = jnp.sum(cached, axis=-1, keepdims=True) + jnp.sum(new, axis=-1, keepdims=True) + jnp.exp(sink - largest)
+    share = 1.0 / total
+    cached = (cached * share).astype(jnp.bfloat16)
+    new = (new * share).astype(jnp.bfloat16)
+    mixed = []
+    for r in range(rows):
+        mixed.append(jnp.dot(cached[r * per_row:(r + 1) * per_row], cache_ref[r], preferred_element_type=jnp.float32))
+    mixed_ref[...] = jnp.concatenate(mixed, axis=0) + jnp.dot(new, fresh, preferred_element_type=jnp.float32)
+
+    def head(h):
+        return jnp.concatenate([mixed_ref[pl.ds(h * steps + s, rows, stride=per_row), :] for s in range(steps)], axis=0)
+
+    mix = jnp.concatenate(
+        [jnp.where(is_key, pltpu.roll(head(2 * m), HEAD_SIZE, 1), head(2 * m + 1)) for m in range(heads // 2)], axis=1
+    ).astype(jnp.bfloat16)
+    copies[-1].wait()
+    partial = dot_last(mix, wo_ref[...])
+    for c in range(secs * tps):
+        low, high = c * LANES, min((c + 1) * LANES, width)
+        piece = partial[:, low:high]
+        if high - low < LANES:
+            piece = jnp.concatenate([piece, jnp.zeros((total_rows, LANES - (high - low)), jnp.float32)], axis=1)
+        chunk_ref[c] = piece
+    sec = lax.axis_index("sec")
+    for t in range(tps):
+        other_ref[t] = chunk_ref[(1 - sec) * tps + t].astype(jnp.bfloat16)
+        mine_ref[t] = chunk_ref[sec * tps + t]
+
+
+def attention_partial(flat, gain, w_query, key_value, sinks, w_output, cache, lengths, secs, tps):
+    total_rows, width = flat.shape
+    rows, slots, pair = cache.shape
+    per_row = w_query.shape[1] // HEAD_SIZE * (total_rows // rows)
+    shards = secs * tps
+    return pl.pallas_call(
+        attention_kernel,
+        name="attention",
+        out_shape=[shape_of((tps, total_rows, LANES)), shape_of((tps, total_rows, LANES), jnp.float32),
+                   shape_of((total_rows, LANES), jnp.float32)],
+        in_specs=[smem(), smem(), vmem(), outside(), outside(), outside(), outside(), outside()],
+        out_specs=[vmem()] * 3,
+        scratch_shapes=[
+            pltpu.VMEM((total_rows, width), jnp.bfloat16),
+            pltpu.VMEM(w_query.shape, jnp.bfloat16),
+            pltpu.VMEM(key_value.shape, jnp.bfloat16),
+            pltpu.VMEM(cache.shape, jnp.bfloat16),
+            pltpu.VMEM((width, w_output.shape[0]), jnp.bfloat16),
+            pltpu.VMEM((total_rows, shards * LANES), jnp.float32),
+            pltpu.VMEM((rows * per_row, pair), jnp.float32),
+            pltpu.VMEM((rows * per_row, pair), jnp.float32),
+            pltpu.VMEM((shards, total_rows, LANES), jnp.float32),
+            pltpu.SemaphoreType.DMA((4 + len(split_width(width)),)),
+        ],
+        compiler_params=pltpu.CompilerParams(vmem_limit_bytes=20 * MIB),
+    )(lengths, sinks, gain.reshape(1, -1), flat, w_query, key_value, cache, w_output.swapaxes(0, 1))
+
+
+def add_and_split_kernel(mine_ref, come_ref, *refs, with_extra):
+    extra_ref, refs = (refs[0], refs[1:]) if with_extra else (None, refs)
+    tp = lax.axis_index("tp")
+    own = mine_ref[tp] + come_ref[tp].astype(jnp.float32)
+    refs[0][...] = own if extra_ref is None else own + extra_ref[...]
+    for m in range(1, mine_ref.shape[0]):
+        to = jnp.bitwise_xor(tp, m)
+        refs[m][...] = (mine_ref[to] + come_ref[to].astype(jnp.float32)).astype(jnp.bfloat16)
+
+
+def add_and_split(mine, come, extra=None):
+    tps = mine.shape[0]
+    shape = mine.shape[1:]
+    return pl.pallas_call(
+        functools.partial(add_and_split_kernel, with_extra=extra is not None),
+        name="add_and_split",
+        out_shape=[shape_of(shape, jnp.float32)] + [shape_of(shape)] * (tps - 1),
+        in_specs=[vmem()] * (2 if extra is None else 3),
+        out_specs=[vmem()] * tps,
+        compiler_params=pltpu.CompilerParams(vmem_limit_bytes=8 * MIB),
+    )(*((mine, come) if extra is None else (mine, come, extra)))
+
+
+def sum_kernel(own_ref, *refs):
+    come, out = refs[:-1], refs[-1]
+    total = own_ref[...]
+    for ref in come:
+        total = total + ref[...].astype(jnp.float32)
+    out[...] = total.astype(jnp.bfloat16).reshape(out.shape)
+
+
+def sum_pieces(own, come, shape):
+    return pl.pallas_call(
+        sum_kernel,
+        name="sum_pieces",
+        out_shape=shape_of(shape),
+        in_specs=[vmem()] * (1 + len(come)),
+        out_specs=vmem(),
+        compiler_params=pltpu.CompilerParams(vmem_limit_bytes=4 * MIB),
+    )(own, *come)
+
+
+def expert_kernel(gain_ref, gate_ref, up_ref, down_ref, *refs, secs, tps):
+    pieces, (other_ref, mine_ref, middle_ref, x_ref, chunk_ref, row_ref) = refs[:secs * tps], refs[secs * tps:]
+    groups, total_rows, _ = pieces[0].shape
+    width = gain_ref.shape[1]
+    part = mine_ref.shape[2]
+    sec, tp = lax.axis_index("sec"), lax.axis_index("tp")
+    for n, piece in enumerate(pieces):
+        at = jnp.bitwise_xor(sec, n // tps) * tps + jnp.bitwise_xor(tp, n % tps)
+        x_ref[:, pl.ds(pl.multiple_of(at * LANES, LANES), LANES)] = piece[...].reshape(groups * total_rows, LANES)
+    x = x_ref[:, :width].astype(jnp.float32)
+    for c in range(secs * tps):
+        row_ref[c] = x[:total_rows, c * part:(c + 1) * part]
+    middle_ref[...] = row_ref[sec * tps + tp]
+    scale = lax.rsqrt(jnp.mean(x * x, axis=-1, keepdims=True) + 1e-05)
+    expert_in = (x * scale * gain_ref[...]).astype(jnp.bfloat16)
+    gate_h = dot_last(expert_in, gate_ref[...])
+    up_h = dot_last(expert_in, up_ref[...])
+    act = ((up_h + 1.0) * gate_h * jax.nn.sigmoid(1.702 * gate_h)).astype(jnp.bfloat16)
+    out = jnp.dot(act, down_ref[...], preferred_element_type=jnp.float32)
+    for c in range(secs * tps):
+        chunk_ref[c] = out[:, c * part:(c + 1) * part]
+    for t in range(tps):
+        other_ref[t] = chunk_ref[(1 - sec) * tps + t].astype(jnp.bfloat16)
+        mine_ref[t] = chunk_ref[sec * tps + t]
+
+
+def expert_partial(gain, w_gate, w_up, w_down, pieces, secs, tps):
+    groups, total_rows, _ = pieces[0].shape
+    width = gain.shape[0]
+    shards = secs * tps
+    part = width // shards
+    lines = groups * total_rows
+    return pl.pallas_call(
+        functools.partial(expert_kernel, secs=secs, tps=tps),
+        name="expert",
+        out_shape=[shape_of((tps, lines, part)), shape_of((tps, lines, part), jnp.float32),
+                   shape_of((total_rows, part), jnp.float32)],
+        in_specs=[vmem()] * (4 + shards),
+        out_specs=[vmem()] * 3,
+        scratch_shapes=[
+            pltpu.VMEM((lines, shards * LANES), jnp.bfloat16),
+            pltpu.VMEM((shards, lines, part), jnp.float32),
+            pltpu.VMEM((shards, total_rows, part), jnp.float32),
+        ],
+        compiler_params=pltpu.CompilerParams(vmem_limit_bytes=20 * MIB),
+    )(gain.reshape(1, -1), w_gate.swapaxes(0, 1), w_up.swapaxes(0, 1), w_down, *pieces)
+
+
+def combine_kernel(routes_ref, weights_ref, middle_ref, *refs):
+    come, out_ref = refs[:-1], refs[-1]
+    steps, rows, part = out_ref.shape
+    grp = lax.axis_index("grp")
+    corner = lax.broadcasted_iota(jnp.int32, (rows, rows), 0) == lax.broadcasted_iota(jnp.int32, (rows, rows), 1)
+    for s in range(steps):
+        at = pl.ds(s * rows, rows)
+        total = middle_ref[at, :]
+        for m, ref in enumerate(come):
+            named = routes_ref[s] == jnp.bitwise_xor(grp, m)
+            line = jnp.sum(jnp.where(named, weights_ref[s], 0.0), axis=0, keepdims=True)
+            column = jnp.sum(jnp.where(corner, line, 0.0), axis=1, keepdims=True)
+            total = total + column * ref[at, :].astype(jnp.float32)
+        out_ref[s] = total.astype(jnp.bfloat16)
+
+
+def combine(routes, weights, middle, come, steps):
+    total_rows, part = middle.shape
+    return pl.pallas_call(
+        combine_kernel,
+        name="combine",
+        out_shape=shape_of((steps, total_rows // steps, part)),
+        in_specs=[vmem()] * (3 + len(come)),
+        out_specs=vmem(),
+        compiler_params=pltpu.CompilerParams(vmem_limit_bytes=4 * MIB),
+    )(routes.swapaxes(1, 2), weights.swapaxes(1, 2), middle, *come)
+
+
+def unstack_kernel(own_ref, *refs, groups):
+    come, outs = refs[:-groups], refs[-groups:]
+    total = own_ref[...]
+    for ref in come:
+        total = total + ref[...].astype(jnp.float32)
+    lines = outs[0].shape[0]
+    for m, out in enumerate(outs):
+        out[...] = total[m * lines:(m + 1) * lines].astype(jnp.bfloat16)
+
+
+def sum_and_unstack(own, come, groups):
+    lines, part = own.shape
+    return pl.pallas_call(
+        functools.partial(unstack_kernel, groups=groups),
+        name="sum_and_unstack",
+        out_shape=[shape_of((lines // groups, part))] * groups,
+        in_specs=[vmem()] * (1 + len(come)),
+        out_specs=[vmem()] * groups,
+        compiler_params=pltpu.CompilerParams(vmem_limit_bytes=4 * MIB),
+    )(own, *come)
+
+
+def every_expert_body(inputs, attention_gain, w_query, key_value_weight, head_sink_logits, w_output, cache_pairs, lengths,
+                      expert_gain, w_gate, w_up, w_down, routes, gate_weights):
+    secs, tps, groups = lax.axis_size("sec"), lax.axis_size("tp"), lax.axis_size("grp")
+    steps, rows, width = inputs.shape
+    flat = inputs.reshape(steps * rows, width)
+    other, mine, own_x = attention_partial(flat, attention_gain, w_query, key_value_weight[:, 0], head_sink_logits, w_output,
+                                           cache_pairs[:, :, 0], lengths, secs, tps)
+    own, *parts = add_and_split(mine, swap(other, "sec", 1), own_x)
+    come = [swap(parts[m - 1], "tp", m) for m in reversed(range(1, tps))]
+    middle = sum_pieces(own, come, own.shape)
+    come = {m: swap(middle, "grp", m) for m in reversed(range(1, groups))}
+    stacked = jnp.stack([middle] + [come[m] for m in range(1, groups)])
+    come = {m: swap(stacked, "tp", m) for m in reversed(range(1, tps))}
+    pieces = [stacked] + [come[m] for m in range(1, tps)]
+    pieces = pieces + [swap(piece, "sec", 1) for piece in pieces]
+    other, mine, own_middle = expert_partial(expert_gain, w_gate[0], w_up[0], w_down[0], pieces, secs, tps)
+    own, *parts = add_and_split(mine, swap(other, "sec", 1))
+    come = [swap(parts[m - 1], "tp", m) for m in reversed(range(1, tps))]
+    held = sum_and_unstack(own, come, groups)
+    come = {m: swap(held[m], "grp", m) for m in reversed(range(1, groups))}
+    return combine(routes, gate_weights, own_middle, [held[0]] + [come[m] for m in range(1, groups)], steps)
+
+
+def body(*args):
+    if lax.axis_size("grp") * args[9].shape[0] == TOP and args[9].shape[0] == 1:
+        return every_expert_body(*args)
+    return general_body(*args)
+
+
 def solution(mesh):
     placed = (
         P(None, "grp", None),

time: 225 us -> 61.4 us (0.27)
  blocking collectives: 74.9 us -> 0 us
  waiting for transfers between devices: 76.9 us -> 22 us
  matrix products: 27.4 us -> 0 us
  between operations: 14.4 us -> 0.11 us
  Pallas kernels: 0 us -> 8.1 us
  other arithmetic: 6.86 us -> 0.02 us
  starting transfers between devices: 15.3 us -> 21.8 us
    unnamed x1 -> x0, blocking collectives: 74.9 us -> none
    psum x1 -> x0, waiting for transfers between devices: 55.6 us -> none  [body(): summed = lax.psum(partial_sum[None], ('sec', 'tp'))]
    dot_general x21 -> x0, matrix products: 27.4 us -> none  [the longest x2 6.99 us: body(): jnp.einsum('snph,hd->snpd', act, down_matrix, preferred_element_type=jnp....]
    ppermute x0 -> x21, waiting for transfers between devices: none -> 22 us  [swap(): return lax.ppermute(value, axes, [(i, i ^ mask) for i in range(size)])]
    ppermute x0 -> x21, starting transfers between devices: none -> 21.8 us  [swap(): return lax.ppermute(value, axes, [(i, i ^ mask) for i in range(size)])]
    all_to_all x4 -> x0, waiting for transfers between devices: 21.3 us -> none  [the longest x2 11.7 us: body(): lax.all_to_all(outgoing, 'grp', split_axis=1, concat_axis=1, tiled=True)]
    all_to_all x4 -> x0, starting transfers between devices: 15.3 us -> none  [the longest x2 8.77 us: body(): lax.all_to_all(outgoing, 'grp', split_axis=1, concat_axis=1, tiled=True)]
    pallas_call x0 -> x7, Pallas kernels: none -> 8.1 us  [the longest x1 5.18 us: attention_partial(): pl.pallas_call(attention_kernel, name='attention', out_shape=[shape_of((t...]
  transfers between devices with their start and end apart: 5 -> 21, of which waited for: 5 -> 16; matrix products, arithmetic and copies ran while one was open for 5% -> 0% of each run, Pallas kernels for 0% -> 0%
where the time goes in v2:
time: 61.4 us; the launch traced here: 61 us
  waiting for transfers between devices  22 us (36%)
  starting transfers between devices  21.8 us (36%)
  local copies, waits for them, and re-layouts  8.98 us (15%)
  Pallas kernels  8.1 us (13%)
    ppermute x21, waiting for transfers between devices, swap(): return lax.ppermute(value, axes, [(i, i ^ mask) for i in range(size)])  22 us
    ppermute x21, starting transfers between devices, swap(): return lax.ppermute(value, axes, [(i, i ^ mask) for i in range(size)])  21.8 us
    unnamed x26, local copies, waits for them, and re-layouts  8.26 us
    pallas_call x1, Pallas kernels, attention_partial(): pl.pallas_call(attention_kernel, name='attention', out_shape=[shape_of((t...  5.18 us
    pallas_call x1, Pallas kernels, expert_partial(): pl.pallas_call(functools.partial(expert_kernel, secs=secs, tps=tps), name...  2.02 us
  transfers between devices with their start and end apart: 21, of which 16 were waited for; matrix products, arithmetic and copies ran while one was open for 0% of the time, Pallas kernels for 0%

profile of v2, /device:TPU:0, one launch (start us, length us, event | category | flops | bytes accessed | tf_op | source)
XLA Modules:
  0.0 61.0 jit_solution(7860227824134780570)
XLA Ops:
  0.7 1.8 %copy-done = bf16[2880,512]{1,0:T(8,128)(2,1)S(1)} copy-done((bf16[2880,512]{1,0:T(8,128)(2,1)S(1)}, bf16[2880,512]{1,0:T(8,128)(2,1)}, u32[]{:S(2)}) %copy-start) | copy-done | bytes 2949144
  2.6 1.8 %copy-done.1 = bf16[512,2880]{0,1:T(8,128)(2,1)S(1)} copy-done((bf16[512,2880]{0,1:T(8,128)(2,1)S(1)}, bf16[512,2880]{0,1:T(8,128)(2,1)}, u32[]{:S(2)}) %copy-start.1) | copy-done | bytes 2949144
  4.4 1.2 %copy-done.5 = bf16[16,256,1,128]{3,1,2,0:T(8,128)(2,1)S(1)} copy-done((bf16[16,256,1,128]{3,1,2,0:T(8,128)(2,1)S(1)}, bf16[16,256,1,128]{3,1,2,0:T(8,128)(2,1)}, u32[]{:S(2)}) %copy-start.5) | copy-done | bytes 1048600
  5.6 1.1 %copy-done.6 = bf16[2880,1,128]{2,0,1:T(8,128)(2,1)S(1)} copy-done((bf16[2880,1,128]{2,0,1:T(8,128)(2,1)S(1)}, bf16[2880,1,128]{2,0,1:T(8,128)(2,1)}, u32[]{:S(2)}) %copy-start.6) | copy-done | bytes 737304
  9.0 5.2 %attention.1 = (bf16[4,32,384]{2,1,0:T(8,128)(2,1)S(1)}, f32[4,32,384]{2,1,0:T(8,128)S(1)}, f32[32,384]{1,0:T(8,128)S(1)}) custom-call(s32[16]{0:T(128)S(1)} %copy-done.10, f32[8]{0:T(128)S(1)} %copy-done.11, f32[1,2880]{1,0:T(1,128)S(1)} %reshape.10.gain_ref, bf16[32,2880]{1,0:T(8,128)(2,1)S(1)} %bitcast.23, bf16[2880,512]{1,0:T(8,128)(2,1)S(1)} %copy-done, ...), custom_call_target="tpu_custom_call" | custom-call | tf_op jit(solution)/shard_map/attention/pallas_call | solution.py:347
  14.7 0.9 %collective-permute-done.come_ref = bf16[4,32,384]{2,1,0:T(8,128)(2,1)S(1)} collective-permute-done((bf16[4,32,384]{2,1,0:T(8,128)(2,1)S(1)}, bf16[4,32,384]{2,1,0:T(8,128)(2,1)S(1)}, u32[]{:S(2)}, u32[]{:S(2)}) %collective-permute-start) | collective-permute-done | bytes 98336 | tf_op jit(solution)/shard_map/ppermute | solution.py:223
  15.7 3.9 %collective-permute-start.1 = (bf16[32,384]{1,0:T(8,128)(2,1)S(1)}, bf16[32,384]{1,0:T(8,128)(2,1)S(1)}, u32[]{:S(2)}, u32[]{:S(2)}) collective-permute-start(bf16[32,384]{1,0:T(8,128)(2,1)S(1)} %get-tuple-element.27), channel_id=1, source_target_pairs={{0,3},{1,2},{2,1},{3,0},{4,7},{5,6},{6,5},{7,4},{8,11},{9,10},{10,... | collective-permute-start | bytes 73736 | tf_op jit(solution)/shard_map/ppermute | solution.py:223
  20.2 1.2 %collective-permute-done.1.refs_0_ = bf16[32,384]{1,0:T(8,128)(2,1)S(1)} collective-permute-done((bf16[32,384]{1,0:T(8,128)(2,1)S(1)}, bf16[32,384]{1,0:T(8,128)(2,1)S(1)}, u32[]{:S(2)}, u32[]{:S(2)}) %collective-permute-start.1) | collective-permute-done | bytes 24608 | tf_op jit(solution)/shard_map/ppermute | solution.py:223
  21.3 2.0 %collective-permute-done.2.refs_1_ = bf16[32,384]{1,0:T(8,128)(2,1)S(1)} collective-permute-done((bf16[32,384]{1,0:T(8,128)(2,1)S(1)}, bf16[32,384]{1,0:T(8,128)(2,1)S(1)}, u32[]{:S(2)}, u32[]{:S(2)}) %collective-permute-start.2) | collective-permute-done | bytes 24608 | tf_op jit(solution)/shard_map/ppermute | solution.py:223
  23.9 3.7 %collective-permute-start.6 = (bf16[32,384]{1,0:T(8,128)(2,1)S(1)}, bf16[32,384]{1,0:T(8,128)(2,1)S(1)}, u32[]{:S(2)}, u32[]{:S(2)}) collective-permute-start(bf16[32,384]{1,0:T(8,128)(2,1)S(1)} %sum_pieces.1), channel_id=1, source_target_pairs={{0,12},{4,8},{8,4},{12,0},{1,13},{5,9},{9,5},{13,1},{2,14},{6,10},... | collective-permute-start | bytes 73736 | tf_op jit(solution)/shard_map/ppermute | solution.py:223
  28.3 1.3 %collective-permute-done.6 = bf16[32,384]{1,0:T(8,128)(2,1)S(1)} collective-permute-done((bf16[32,384]{1,0:T(8,128)(2,1)S(1)}, bf16[32,384]{1,0:T(8,128)(2,1)S(1)}, u32[]{:S(2)}, u32[]{:S(2)}) %collective-permute-start.6) | collective-permute-done | bytes 24608 | tf_op jit(solution)/shard_map/ppermute | solution.py:223
  29.7 2.6 %collective-permute-done.5 = bf16[32,384]{1,0:T(8,128)(2,1)S(1)} collective-permute-done((bf16[32,384]{1,0:T(8,128)(2,1)S(1)}, bf16[32,384]{1,0:T(8,128)(2,1)S(1)}, u32[]{:S(2)}, u32[]{:S(2)}) %collective-permute-start.5) | collective-permute-done | bytes 24608 | tf_op jit(solution)/shard_map/ppermute | solution.py:223
  32.3 1.6 %collective-permute-start.9 = (bf16[4,32,384]{2,1,0:T(8,128)(2,1)S(1)}, bf16[4,32,384]{2,1,0:T(8,128)(2,1)S(1)}, u32[]{:S(2)}, u32[]{:S(2)}) collective-permute-start(bf16[4,32,384]{2,1,0:T(8,128)(2,1)S(1)} %pad_maximum_fusion.refs_0_), channel_id=1, source_target_pairs={{0,3},{1,2},{2,1},{3,0},{4,7},{5,6},{6,5},{7,4},{8,11},{9,10},{10,... | collective-permute-start | bytes 294920 | tf_op jit(solution)/shard_map/ppermute | solution.py:223
  34.4 1.5 %collective-permute-start.7 = (bf16[4,32,384]{2,1,0:T(8,128)(2,1)S(1)}, bf16[4,32,384]{2,1,0:T(8,128)(2,1)S(1)}, u32[]{:S(2)}, u32[]{:S(2)}) collective-permute-start(bf16[4,32,384]{2,1,0:T(8,128)(2,1)S(1)} %pad_maximum_fusion.refs_0_), channel_id=1, source_target_pairs={{0,1},{1,0},{2,3},{3,2},{4,5},{5,4},{6,7},{7,6},{8,9},{9,8},{10,11... | collective-permute-start | bytes 294920 | tf_op jit(solution)/shard_map/ppermute | solution.py:223
  35.9 2.1 %collective-permute-done.9.refs_3_ = bf16[4,32,384]{2,1,0:T(8,128)(2,1)S(1)} collective-permute-done((bf16[4,32,384]{2,1,0:T(8,128)(2,1)S(1)}, bf16[4,32,384]{2,1,0:T(8,128)(2,1)S(1)}, u32[]{:S(2)}, u32[]{:S(2)}) %collective-permute-start.9) | collective-permute-done | bytes 98336 | tf_op jit(solution)/shard_map/ppermute | solution.py:223
  37.9 1.0 %collective-permute-done.8.refs_2_ = bf16[4,32,384]{2,1,0:T(8,128)(2,1)S(1)} collective-permute-done((bf16[4,32,384]{2,1,0:T(8,128)(2,1)S(1)}, bf16[4,32,384]{2,1,0:T(8,128)(2,1)S(1)}, u32[]{:S(2)}, u32[]{:S(2)}) %collective-permute-start.8) | collective-permute-done | bytes 98336 | tf_op jit(solution)/shard_map/ppermute | solution.py:223
  40.4 2.0 %expert.1 = (bf16[4,128,360]{2,1,0:T(8,128)(2,1)S(1)}, f32[4,128,360]{2,1,0:T(8,128)S(1)}, f32[32,360]{1,0:T(8,128)S(1)}) custom-call(f32[1,2880]{1,0:T(1,128)S(1)} %reshape.9.gain_ref, bf16[180,2880]{1,0:T(8,128)(2,1)S(1)} %bitcast.18, bf16[180,2880]{1,0:T(8,128)(2,1)S(1)} %bitcast.19, bf16[180,2880]{1,0:T(8,128)(2,1)S(1)} %bitcast.20, ...), custom_call_target="tpu_custom_call" | custom-call | tf_op jit(solution)/shard_map/expert/pallas_call | solution.py:444
  42.8 1.4 %collective-permute-done.14.come_ref = bf16[4,128,360]{2,1,0:T(8,128)(2,1)S(1)} collective-permute-done((bf16[4,128,360]{2,1,0:T(8,128)(2,1)S(1)}, bf16[4,128,360]{2,1,0:T(8,128)(2,1)S(1)}, u32[]{:S(2)}, u32[]{:S(2)}) %collective-permute-start.14) | collective-permute-done | bytes 368672 | tf_op jit(solution)/shard_map/ppermute | solution.py:223
  44.3 2.4 %collective-permute-start.15 = (bf16[128,360]{1,0:T(8,128)(2,1)S(1)}, bf16[128,360]{1,0:T(8,128)(2,1)S(1)}, u32[]{:S(2)}, u32[]{:S(2)}) collective-permute-start(bf16[128,360]{1,0:T(8,128)(2,1)S(1)} %get-tuple-element.34), channel_id=1, source_target_pairs={{0,3},{1,2},{2,1},{3,0},{4,7},{5,6},{6,5},{7,4},{8,11},{9,10},{10,... | collective-permute-start | bytes 276488 | tf_op jit(solution)/shard_map/ppermute | solution.py:223
  47.9 2.5 %collective-permute-done.15.refs_0_ = bf16[128,360]{1,0:T(8,128)(2,1)S(1)} collective-permute-done((bf16[128,360]{1,0:T(8,128)(2,1)S(1)}, bf16[128,360]{1,0:T(8,128)(2,1)S(1)}, u32[]{:S(2)}, u32[]{:S(2)}) %collective-permute-start.15) | collective-permute-done | bytes 92192 | tf_op jit(solution)/shard_map/ppermute | solution.py:223
  50.4 2.0 %collective-permute-done.16.refs_1_ = bf16[128,360]{1,0:T(8,128)(2,1)S(1)} collective-permute-done((bf16[128,360]{1,0:T(8,128)(2,1)S(1)}, bf16[128,360]{1,0:T(8,128)(2,1)S(1)}, u32[]{:S(2)}, u32[]{:S(2)}) %collective-permute-start.16) | collective-permute-done | bytes 92192 | tf_op jit(solution)/shard_map/ppermute | solution.py:223
  52.6 2.1 %collective-permute-start.19 = (bf16[32,360]{1,0:T(8,128)(2,1)S(1)}, bf16[32,360]{1,0:T(8,128)(2,1)S(1)}, u32[]{:S(2)}, u32[]{:S(2)}) collective-permute-start(bf16[32,360]{1,0:T(8,128)(2,1)S(1)} %get-tuple-element.39), channel_id=1, source_target_pairs={{0,8},{4,12},{8,0},{12,4},{1,9},{5,13},{9,1},{13,5},{2,10},{6,14},... | collective-permute-start | bytes 69128 | tf_op jit(solution)/shard_map/ppermute | solution.py:223
  54.7 2.3 %collective-permute-start.20 = (bf16[32,360]{1,0:T(8,128)(2,1)S(1)}, bf16[32,360]{1,0:T(8,128)(2,1)S(1)}, u32[]{:S(2)}, u32[]{:S(2)}) collective-permute-start(bf16[32,360]{1,0:T(8,128)(2,1)S(1)} %get-tuple-element.40), channel_id=1, source_target_pairs={{0,12},{4,8},{8,4},{12,0},{1,13},{5,9},{9,5},{13,1},{2,14},{6,10},... | collective-permute-start | bytes 69128 | tf_op jit(solution)/shard_map/ppermute | solution.py:223
  57.6 2.7 %collective-permute-done.20.refs_3_ = bf16[32,360]{1,0:T(8,128)(2,1)S(1)} collective-permute-done((bf16[32,360]{1,0:T(8,128)(2,1)S(1)}, bf16[32,360]{1,0:T(8,128)(2,1)S(1)}, u32[]{:S(2)}, u32[]{:S(2)}) %collective-permute-start.20) | collective-permute-done | bytes 23072 | tf_op jit(solution)/shard_map/ppermute | solution.py:223
  (54 shorter events, 10.6 us)
Async XLA Ops:
  9.0 31.4 %copy-start.2 = (bf16[1,2880,180]{1,2,0:T(8,128)(2,1)S(1)}, bf16[1,2880,180]{1,2,0:T(8,128)(2,1)}, u32[]{:S(2)}) copy-start(bf16[1,2880,180]{1,2,0:T(8,128)(2,1)} %param.23) | copy-start | bytes 3110404
  9.0 31.4 %copy-start.3 = (bf16[1,2880,180]{1,2,0:T(8,128)(2,1)S(1)}, bf16[1,2880,180]{1,2,0:T(8,128)(2,1)}, u32[]{:S(2)}) copy-start(bf16[1,2880,180]{1,2,0:T(8,128)(2,1)} %param.24) | copy-start | bytes 3110404
  9.0 31.4 %copy-start.4 = (bf16[1,180,2880]{2,1,0:T(8,128)(2,1)S(1)}, bf16[1,180,2880]{2,1,0:T(8,128)(2,1)}, u32[]{:S(2)}) copy-start(bf16[1,180,2880]{2,1,0:T(8,128)(2,1)} %param.25) | copy-start | bytes 3110404
  14.2 1.5 %collective-permute-start = (bf16[4,32,384]{2,1,0:T(8,128)(2,1)S(1)}, bf16[4,32,384]{2,1,0:T(8,128)(2,1)S(1)}, u32[]{:S(2)}, u32[]{:S(2)}) collective-permute-start(bf16[4,32,384]{2,1,0:T(8,128)(2,1)S(1)} %get-tuple-element.24), channel_id=1, source_target_pairs={{0,16},{16,0},{1,17},{17,1},{2,18},{18,2},{3,19},{19,3},{4,20},{20... | collective-permute-start | bytes 294920 | tf_op jit(solution)/shard_map/ppermute | solution.py:223
  15.7 5.7 %collective-permute-start.1 = (bf16[32,384]{1,0:T(8,128)(2,1)S(1)}, bf16[32,384]{1,0:T(8,128)(2,1)S(1)}, u32[]{:S(2)}, u32[]{:S(2)}) collective-permute-start(bf16[32,384]{1,0:T(8,128)(2,1)S(1)} %get-tuple-element.27), channel_id=1, source_target_pairs={{0,3},{1,2},{2,1},{3,0},{4,7},{5,6},{6,5},{7,4},{8,11},{9,10},{10,... | collective-permute-start | bytes 73736 | tf_op jit(solution)/shard_map/ppermute | solution.py:223
  19.5 3.8 %collective-permute-start.2 = (bf16[32,384]{1,0:T(8,128)(2,1)S(1)}, bf16[32,384]{1,0:T(8,128)(2,1)S(1)}, u32[]{:S(2)}, u32[]{:S(2)}) collective-permute-start(bf16[32,384]{1,0:T(8,128)(2,1)S(1)} %get-tuple-element.28), channel_id=1, source_target_pairs={{0,2},{1,3},{2,0},{3,1},{4,6},{5,7},{6,4},{7,5},{8,10},{9,11},{10,... | collective-permute-start | bytes 73736 | tf_op jit(solution)/shard_map/ppermute | solution.py:223
  20.0 3.8 %collective-permute-start.3 = (bf16[32,384]{1,0:T(8,128)(2,1)S(1)}, bf16[32,384]{1,0:T(8,128)(2,1)S(1)}, u32[]{:S(2)}, u32[]{:S(2)}) collective-permute-start(bf16[32,384]{1,0:T(8,128)(2,1)S(1)} %get-tuple-element.29), channel_id=1, source_target_pairs={{0,1},{1,0},{2,3},{3,2},{4,5},{5,4},{6,7},{7,6},{8,9},{9,8},{10,11... | collective-permute-start | bytes 73736 | tf_op jit(solution)/shard_map/ppermute | solution.py:223
  23.9 5.8 %collective-permute-start.6 = (bf16[32,384]{1,0:T(8,128)(2,1)S(1)}, bf16[32,384]{1,0:T(8,128)(2,1)S(1)}, u32[]{:S(2)}, u32[]{:S(2)}) collective-permute-start(bf16[32,384]{1,0:T(8,128)(2,1)S(1)} %sum_pieces.1), channel_id=1, source_target_pairs={{0,12},{4,8},{8,4},{12,0},{1,13},{5,9},{9,5},{13,1},{2,14},{6,10},... | collective-permute-start | bytes 73736 | tf_op jit(solution)/shard_map/ppermute | solution.py:223
  27.5 4.7 %collective-permute-start.5 = (bf16[32,384]{1,0:T(8,128)(2,1)S(1)}, bf16[32,384]{1,0:T(8,128)(2,1)S(1)}, u32[]{:S(2)}, u32[]{:S(2)}) collective-permute-start(bf16[32,384]{1,0:T(8,128)(2,1)S(1)} %sum_pieces.1), channel_id=1, source_target_pairs={{0,8},{4,12},{8,0},{12,4},{1,9},{5,13},{9,1},{13,5},{2,10},{6,14},... | collective-permute-start | bytes 73736 | tf_op jit(solution)/shard_map/ppermute | solution.py:223
  27.5 4.7 %collective-permute-start.4 = (bf16[32,384]{1,0:T(8,128)(2,1)S(1)}, bf16[32,384]{1,0:T(8,128)(2,1)S(1)}, u32[]{:S(2)}, u32[]{:S(2)}) collective-permute-start(bf16[32,384]{1,0:T(8,128)(2,1)S(1)} %sum_pieces.1), channel_id=1, source_target_pairs={{0,4},{4,0},{8,12},{12,8},{1,5},{5,1},{9,13},{13,9},{2,6},{6,2},{1... | collective-permute-start | bytes 73736 | tf_op jit(solution)/shard_map/ppermute | solution.py:223
  32.3 5.6 %collective-permute-start.9 = (bf16[4,32,384]{2,1,0:T(8,128)(2,1)S(1)}, bf16[4,32,384]{2,1,0:T(8,128)(2,1)S(1)}, u32[]{:S(2)}, u32[]{:S(2)}) collective-permute-start(bf16[4,32,384]{2,1,0:T(8,128)(2,1)S(1)} %pad_maximum_fusion.refs_0_), channel_id=1, source_target_pairs={{0,3},{1,2},{2,1},{3,0},{4,7},{5,6},{6,5},{7,4},{8,11},{9,10},{10,... | collective-permute-start | bytes 294920 | tf_op jit(solution)/shard_map/ppermute | solution.py:223
  33.9 5.1 %collective-permute-start.8 = (bf16[4,32,384]{2,1,0:T(8,128)(2,1)S(1)}, bf16[4,32,384]{2,1,0:T(8,128)(2,1)S(1)}, u32[]{:S(2)}, u32[]{:S(2)}) collective-permute-start(bf16[4,32,384]{2,1,0:T(8,128)(2,1)S(1)} %pad_maximum_fusion.refs_0_), channel_id=1, source_target_pairs={{0,2},{1,3},{2,0},{3,1},{4,6},{5,7},{6,4},{7,5},{8,10},{9,11},{10,... | collective-permute-start | bytes 294920 | tf_op jit(solution)/shard_map/ppermute | solution.py:223
  34.4 4.7 %collective-permute-start.7 = (bf16[4,32,384]{2,1,0:T(8,128)(2,1)S(1)}, bf16[4,32,384]{2,1,0:T(8,128)(2,1)S(1)}, u32[]{:S(2)}, u32[]{:S(2)}) collective-permute-start(bf16[4,32,384]{2,1,0:T(8,128)(2,1)S(1)} %pad_maximum_fusion.refs_0_), channel_id=1, source_target_pairs={{0,1},{1,0},{2,3},{3,2},{4,5},{5,4},{6,7},{7,6},{8,9},{9,8},{10,11... | collective-permute-start | bytes 294920 | tf_op jit(solution)/shard_map/ppermute | solution.py:223
  35.8 3.6 %collective-permute-start.10 = (bf16[4,32,384]{2,1,0:T(8,128)(2,1)S(1)}, bf16[4,32,384]{2,1,0:T(8,128)(2,1)S(1)}, u32[]{:S(2)}, u32[]{:S(2)}) collective-permute-start(bf16[4,32,384]{2,1,0:T(8,128)(2,1)S(1)} %pad_maximum_fusion.refs_0_), channel_id=1, source_target_pairs={{0,16},{16,0},{1,17},{17,1},{2,18},{18,2},{3,19},{19,3},{4,20},{20... | collective-permute-start | bytes 294920 | tf_op jit(solution)/shard_map/ppermute | solution.py:223
  37.9 1.5 %collective-permute-start.13 = (bf16[4,32,384]{2,1,0:T(8,128)(2,1)S(1)}, bf16[4,32,384]{2,1,0:T(8,128)(2,1)S(1)}, u32[]{:S(2)}, u32[]{:S(2)}) collective-permute-start(bf16[4,32,384]{2,1,0:T(8,128)(2,1)S(1)} %collective-permute-done.9.refs_3_), channel_id=1, source_target_pairs={{0,16},{16,0},{1,17},{17,1},{2,18},{18,2},{3,19},{19,3},{4,20},{20... | collective-permute-start | bytes 294920 | tf_op jit(solution)/shard_map/ppermute | solution.py:223
  38.9 1.3 %collective-permute-start.12 = (bf16[4,32,384]{2,1,0:T(8,128)(2,1)S(1)}, bf16[4,32,384]{2,1,0:T(8,128)(2,1)S(1)}, u32[]{:S(2)}, u32[]{:S(2)}) collective-permute-start(bf16[4,32,384]{2,1,0:T(8,128)(2,1)S(1)} %collective-permute-done.8.refs_2_), channel_id=1, source_target_pairs={{0,16},{16,0},{1,17},{17,1},{2,18},{18,2},{3,19},{19,3},{4,20},{20... | collective-permute-start | bytes 294920 | tf_op jit(solution)/shard_map/ppermute | solution.py:223
  39.0 1.4 %collective-permute-start.11 = (bf16[4,32,384]{2,1,0:T(8,128)(2,1)S(1)}, bf16[4,32,384]{2,1,0:T(8,128)(2,1)S(1)}, u32[]{:S(2)}, u32[]{:S(2)}) collective-permute-start(bf16[4,32,384]{2,1,0:T(8,128)(2,1)S(1)} %collective-permute-done.7.refs_1_), channel_id=1, source_target_pairs={{0,16},{16,0},{1,17},{17,1},{2,18},{18,2},{3,19},{19,3},{4,20},{20... | collective-permute-start | bytes 294920 | tf_op jit(solution)/shard_map/ppermute | solution.py:223
  42.4 1.8 %collective-permute-start.14 = (bf16[4,128,360]{2,1,0:T(8,128)(2,1)S(1)}, bf16[4,128,360]{2,1,0:T(8,128)(2,1)S(1)}, u32[]{:S(2)}, u32[]{:S(2)}) collective-permute-start(bf16[4,128,360]{2,1,0:T(8,128)(2,1)S(1)} %get-tuple-element.32), channel_id=1, source_target_pairs={{0,16},{16,0},{1,17},{17,1},{2,18},{18,2},{3,19},{19,3},{4,20},{20... | collective-permute-start | bytes 1105928 | tf_op jit(solution)/shard_map/ppermute | solution.py:223
  44.3 6.1 %collective-permute-start.15 = (bf16[128,360]{1,0:T(8,128)(2,1)S(1)}, bf16[128,360]{1,0:T(8,128)(2,1)S(1)}, u32[]{:S(2)}, u32[]{:S(2)}) collective-permute-start(bf16[128,360]{1,0:T(8,128)(2,1)S(1)} %get-tuple-element.34), channel_id=1, source_target_pairs={{0,3},{1,2},{2,1},{3,0},{4,7},{5,6},{6,5},{7,4},{8,11},{9,10},{10,... | collective-permute-start | bytes 276488 | tf_op jit(solution)/shard_map/ppermute | solution.py:223
  46.7 5.7 %collective-permute-start.16 = (bf16[128,360]{1,0:T(8,128)(2,1)S(1)}, bf16[128,360]{1,0:T(8,128)(2,1)S(1)}, u32[]{:S(2)}, u32[]{:S(2)}) collective-permute-start(bf16[128,360]{1,0:T(8,128)(2,1)S(1)} %get-tuple-element.35), channel_id=1, source_target_pairs={{0,2},{1,3},{2,0},{3,1},{4,6},{5,7},{6,4},{7,5},{8,10},{9,11},{10,... | collective-permute-start | bytes 276488 | tf_op jit(solution)/shard_map/ppermute | solution.py:223
  47.2 5.2 %collective-permute-start.17 = (bf16[128,360]{1,0:T(8,128)(2,1)S(1)}, bf16[128,360]{1,0:T(8,128)(2,1)S(1)}, u32[]{:S(2)}, u32[]{:S(2)}) collective-permute-start(bf16[128,360]{1,0:T(8,128)(2,1)S(1)} %get-tuple-element.36), channel_id=1, source_target_pairs={{0,1},{1,0},{2,3},{3,2},{4,5},{5,4},{6,7},{7,6},{8,9},{9,8},{10,11... | collective-permute-start | bytes 276488 | tf_op jit(solution)/shard_map/ppermute | solution.py:223
  52.5 4.5 %collective-permute-start.18 = (bf16[32,360]{1,0:T(8,128)(2,1)S(1)}, bf16[32,360]{1,0:T(8,128)(2,1)S(1)}, u32[]{:S(2)}, u32[]{:S(2)}) collective-permute-start(bf16[32,360]{1,0:T(8,128)(2,1)S(1)} %get-tuple-element.38), channel_id=1, source_target_pairs={{0,4},{4,0},{8,12},{12,8},{1,5},{5,1},{9,13},{13,9},{2,6},{6,2},{1... | collective-permute-start | bytes 69128 | tf_op jit(solution)/shard_map/ppermute | solution.py:223
  52.6 5.1 %collective-permute-start.19 = (bf16[32,360]{1,0:T(8,128)(2,1)S(1)}, bf16[32,360]{1,0:T(8,128)(2,1)S(1)}, u32[]{:S(2)}, u32[]{:S(2)}) collective-permute-start(bf16[32,360]{1,0:T(8,128)(2,1)S(1)} %get-tuple-element.39), channel_id=1, source_target_pairs={{0,8},{4,12},{8,0},{12,4},{1,9},{5,13},{9,1},{13,5},{2,10},{6,14},... | collective-permute-start | bytes 69128 | tf_op jit(solution)/shard_map/ppermute | solution.py:223
  54.7 5.6 %collective-permute-start.20 = (bf16[32,360]{1,0:T(8,128)(2,1)S(1)}, bf16[32,360]{1,0:T(8,128)(2,1)S(1)}, u32[]{:S(2)}, u32[]{:S(2)}) collective-permute-start(bf16[32,360]{1,0:T(8,128)(2,1)S(1)} %get-tuple-element.40), channel_id=1, source_target_pairs={{0,12},{4,8},{8,4},{12,0},{1,13},{5,9},{9,5},{13,1},{2,14},{6,10},... | collective-permute-start | bytes 69128 | tf_op jit(solution)/shard_map/ppermute | solution.py:223
  (10 other events, 74.5 us)

commit v3 on v2

--- a/solution.py
+++ b/solution.py
@@ -223,14 +223,27 @@
     return lax.ppermute(value, axes, [(i, i ^ mask) for i in range(size)])
 
 
+def swap_by_core(value, axis, first):
+    size = lax.axis_size(axis)
+    masks = (1, 2) if first else (2, 1)
+    pairs = [(s * size + i, s * size + (i ^ masks[s])) for s in range(2) for i in range(size)]
+    return lax.ppermute(value, ("sec", axis), pairs)
+
+
+def masks_by_core():
+    sec = lax.axis_index("sec")
+    return 1 + sec, 2 - sec
+
+
 def split_width(width):
     cuts = list(range(0, width, 768)) + [width]
     return list(zip(cuts[:-1], cuts[1:]))
 
 
-def attention_kernel(lengths_ref, sinks_ref, gain_ref, x_hbm, wq_hbm, wkv_hbm, cache_hbm, wo_hbm,
+def attention_kernel(lengths_hbm, sinks_hbm, routes_hbm, weights_hbm, gain_hbm, x_hbm, wq_hbm, wkv_hbm, cache_hbm, wo_hbm,
                      other_ref, mine_ref, own_x_ref,
-                     x_ref, wq_ref, wkv_ref, cache_ref, wo_ref, xs_ref, turned_ref, mixed_ref, chunk_ref, sems):
+                     lengths_ref, sinks_ref, routes_ref, weights_ref, gain_ref, x_ref, wq_ref, wkv_ref, cache_ref, wo_ref,
+                     xs_ref, turned_ref, mixed_ref, chunk_ref, sems):
     total_rows, width = x_ref.shape
     rows, slots, pair = cache_ref.shape
     steps = total_rows // rows
@@ -239,14 +252,18 @@
     tps = mine_ref.shape[0]
     secs = chunk_ref.shape[0] // tps
     cuts = split_width(width)
-    copies = [pltpu.make_async_copy(x_hbm, x_ref, sems.at[0]), pltpu.make_async_copy(wkv_hbm, wkv_ref, sems.at[1])]
+    small = [(lengths_hbm, lengths_ref), (x_hbm, x_ref), (gain_hbm, gain_ref), (routes_hbm, routes_ref), (weights_hbm, weights_ref),
+             (sinks_hbm, sinks_ref)]
+    small = [pltpu.make_async_copy(source, target, sems.at[n]) for n, (source, target) in enumerate(small)]
+    copies = [pltpu.make_async_copy(wkv_hbm, wkv_ref, sems.at[6])]
     for n, (low, high) in enumerate(cuts):
         part = pl.ds(low, high - low)
-        copies.append(pltpu.make_async_copy(wq_hbm.at[part], wq_ref.at[part], sems.at[4 + n]))
-    copies.append(pltpu.make_async_copy(cache_hbm, cache_ref, sems.at[2]))
-    copies.append(pltpu.make_async_copy(wo_hbm, wo_ref, sems.at[3]))
-    for copy in copies:
+        copies.append(pltpu.make_async_copy(wq_hbm.at[part], wq_ref.at[part], sems.at[9 + n]))
+    copies.append(pltpu.make_async_copy(cache_hbm, cache_ref, sems.at[7]))
+    copies.append(pltpu.make_async_copy(wo_hbm, wo_ref, sems.at[8]))
+    for copy in small + copies:
         copy.start()
+    small[0].wait()
 
     lane = lax.broadcasted_iota(jnp.int32, (total_rows, pair), 1)
     line = lax.broadcasted_iota(jnp.int32, (total_rows, pair), 0)
@@ -265,18 +282,31 @@
     def turn(two):
         return two * cosine + jnp.where(low_half, pltpu.roll(two, pair - half, 1), pltpu.roll(two, half, 1)) * sine
 
-    copies[0].wait()
+    for copy in small[1:]:
+        copy.wait()
+    spare = xs_ref.shape[1] - width
+    spare_at = lax.broadcasted_iota(jnp.int32, (rows, spare), 1)
+    corner = lax.broadcasted_iota(jnp.int32, (rows, rows), 0) == lax.broadcasted_iota(jnp.int32, (rows, rows), 1)
+    tables = []
+    for s in range(steps):
+        table = jnp.zeros((rows, spare), jnp.float32)
+        for e in range(TOP):
+            across = jnp.sum(jnp.where(routes_ref[s] == e, weights_ref[s], 0.0), axis=0, keepdims=True)
+            column = jnp.sum(jnp.where(corner, across, 0.0), axis=1, keepdims=True)
+            high_part = column.astype(jnp.bfloat16).astype(jnp.float32)
+            table = jnp.where(spare_at == 2 * e, high_part, jnp.where(spare_at == 2 * e + 1, column - high_part, table))
+        tables.append(table)
     x = x_ref[...].astype(jnp.float32)
-    xs_ref[...] = jnp.concatenate([x, jnp.zeros((total_rows, xs_ref.shape[1] - width), jnp.float32)], axis=1)
+    xs_ref[...] = jnp.concatenate([x, jnp.concatenate(tables, axis=0)], axis=1)
     own = (lax.axis_index("sec") * tps + lax.axis_index("tp")) * LANES
     own_x_ref[...] = xs_ref[:, pl.ds(pl.multiple_of(own, LANES), LANES)]
     scale = lax.rsqrt(jnp.mean(x * x, axis=-1, keepdims=True) + 1e-05)
-    normed = (x * scale * gain_ref[...]).astype(jnp.bfloat16)
-    copies[1].wait()
+    normed = (x * scale * gain_ref[...].reshape(1, width)).astype(jnp.bfloat16)
+    copies[0].wait()
     pairs = jnp.dot(normed, wkv_ref[...], preferred_element_type=jnp.float32)
     query = None
     for n, (low, high) in enumerate(cuts):
-        copies[2 + n].wait()
+        copies[1 + n].wait()
         term = jnp.dot(normed[:, low:high], wq_ref[low:high, :], preferred_element_type=jnp.float32)
         query = term if query is None else query + term
 
@@ -339,19 +369,25 @@
         mine_ref[t] = chunk_ref[sec * tps + t]
 
 
-def attention_partial(flat, gain, w_query, key_value, sinks, w_output, cache, lengths, secs, tps):
+def attention_partial(flat, gain, w_query, key_value, sinks, w_output, cache, lengths, routes, weights, secs, tps):
     total_rows, width = flat.shape
     rows, slots, pair = cache.shape
     per_row = w_query.shape[1] // HEAD_SIZE * (total_rows // rows)
     shards = secs * tps
+    operands = (lengths, sinks, routes, weights, gain, flat, w_query, key_value, cache, w_output.swapaxes(0, 1))
     return pl.pallas_call(
         attention_kernel,
         name="attention",
         out_shape=[shape_of((tps, total_rows, LANES)), shape_of((tps, total_rows, LANES), jnp.float32),
                    shape_of((total_rows, LANES), jnp.float32)],
-        in_specs=[smem(), smem(), vmem(), outside(), outside(), outside(), outside(), outside()],
+        in_specs=[outside()] * len(operands),
         out_specs=[vmem()] * 3,
         scratch_shapes=[
+            pltpu.SMEM(lengths.shape, jnp.int32),
+            pltpu.SMEM(sinks.shape, jnp.float32),
+            pltpu.VMEM(routes.shape, jnp.int32),
+            pltpu.VMEM(weights.shape, jnp.float32),
+            pltpu.VMEM(gain.shape, jnp.float32),
             pltpu.VMEM((total_rows, width), jnp.bfloat16),
             pltpu.VMEM(w_query.shape, jnp.bfloat16),
             pltpu.VMEM(key_value.shape, jnp.bfloat16),
@@ -361,77 +397,102 @@
             pltpu.VMEM((rows * per_row, pair), jnp.float32),
             pltpu.VMEM((rows * per_row, pair), jnp.float32),
             pltpu.VMEM((shards, total_rows, LANES), jnp.float32),
-            pltpu.SemaphoreType.DMA((4 + len(split_width(width)),)),
+            pltpu.SemaphoreType.DMA((9 + len(split_width(width)),)),
         ],
-        compiler_params=pltpu.CompilerParams(vmem_limit_bytes=20 * MIB),
-    )(lengths, sinks, gain.reshape(1, -1), flat, w_query, key_value, cache, w_output.swapaxes(0, 1))
-
-
-def add_and_split_kernel(mine_ref, come_ref, *refs, with_extra):
-    extra_ref, refs = (refs[0], refs[1:]) if with_extra else (None, refs)
+        compiler_params=pltpu.CompilerParams(vmem_limit_bytes=24 * MIB),
+    )(*[pltpu.with_memory_space_constraint(operand, pltpu.HBM) for operand in operands])
+
+
+def call(kernel, name, outs, *operands, limit=4):
+    single = not isinstance(outs, list)
+    return pl.pallas_call(
+        kernel,
+        name=name,
+        out_shape=outs,
+        in_specs=[vmem()] * len(operands),
+        out_specs=vmem() if single else [vmem()] * len(outs),
+        compiler_params=pltpu.CompilerParams(vmem_limit_bytes=limit * MIB),
+    )(*operands)
+
+
+def after_core_kernel(mine_ref, come_ref, keep_ref, send_ref):
     tp = lax.axis_index("tp")
-    own = mine_ref[tp] + come_ref[tp].astype(jnp.float32)
-    refs[0][...] = own if extra_ref is None else own + extra_ref[...]
-    for m in range(1, mine_ref.shape[0]):
-        to = jnp.bitwise_xor(tp, m)
-        refs[m][...] = (mine_ref[to] + come_ref[to].astype(jnp.float32)).astype(jnp.bfloat16)
-
-
-def add_and_split(mine, come, extra=None):
-    tps = mine.shape[0]
-    shape = mine.shape[1:]
-    return pl.pallas_call(
-        functools.partial(add_and_split_kernel, with_extra=extra is not None),
-        name="add_and_split",
-        out_shape=[shape_of(shape, jnp.float32)] + [shape_of(shape)] * (tps - 1),
-        in_specs=[vmem()] * (2 if extra is None else 3),
-        out_specs=[vmem()] * tps,
-        compiler_params=pltpu.CompilerParams(vmem_limit_bytes=8 * MIB),
-    )(*((mine, come) if extra is None else (mine, come, extra)))
-
-
-def sum_kernel(own_ref, *refs):
-    come, out = refs[:-1], refs[-1]
-    total = own_ref[...]
-    for ref in come:
-        total = total + ref[...].astype(jnp.float32)
-    out[...] = total.astype(jnp.bfloat16).reshape(out.shape)
-
-
-def sum_pieces(own, come, shape):
-    return pl.pallas_call(
-        sum_kernel,
-        name="sum_pieces",
-        out_shape=shape_of(shape),
-        in_specs=[vmem()] * (1 + len(come)),
-        out_specs=vmem(),
-        compiler_params=pltpu.CompilerParams(vmem_limit_bytes=4 * MIB),
-    )(own, *come)
-
-
-def expert_kernel(gain_ref, gate_ref, up_ref, down_ref, *refs, secs, tps):
-    pieces, (other_ref, mine_ref, middle_ref, x_ref, chunk_ref, row_ref) = refs[:secs * tps], refs[secs * tps:]
-    groups, total_rows, _ = pieces[0].shape
-    width = gain_ref.shape[1]
-    part = mine_ref.shape[2]
-    sec, tp = lax.axis_index("sec"), lax.axis_index("tp")
-    for n, piece in enumerate(pieces):
-        at = jnp.bitwise_xor(sec, n // tps) * tps + jnp.bitwise_xor(tp, n % tps)
-        x_ref[:, pl.ds(pl.multiple_of(at * LANES, LANES), LANES)] = piece[...].reshape(groups * total_rows, LANES)
+    first, second = masks_by_core()
+    for n, at in enumerate((tp, jnp.bitwise_xor(tp, second))):
+        keep_ref[n] = mine_ref[at] + come_ref[at].astype(jnp.float32)
+        at = jnp.bitwise_xor(at, first)
+        send_ref[n] = (mine_ref[at] + come_ref[at].astype(jnp.float32)).astype(jnp.bfloat16)
+
+
+def after_swap_kernel(keep_ref, come_ref, stay_ref, send_ref):
+    stay_ref[...] = keep_ref[0] + come_ref[0].astype(jnp.float32)
+    send_ref[...] = (keep_ref[1] + come_ref[1].astype(jnp.float32)).astype(jnp.bfloat16)
+
+
+def sum_kernel(stay_ref, come_ref, extra_ref, out_ref):
+    total = stay_ref[...] + come_ref[...].astype(jnp.float32) + extra_ref[...]
+    out_ref[...] = total.astype(jnp.bfloat16).reshape(out_ref.shape)
+
+
+def divide_rows_kernel(stay_ref, come_ref, keep_ref, send_ref):
+    total = stay_ref[...] + come_ref[...].astype(jnp.float32)
+    lines = keep_ref.shape[1]
+    for n in range(2):
+        keep_ref[n] = total[n * lines:(n + 1) * lines]
+        send_ref[n] = total[(n + 2) * lines:(n + 3) * lines].astype(jnp.bfloat16)
+
+
+def scatter_shards(mine, come):
+    tps, lines, part = mine.shape
+    keep, send = call(after_core_kernel, "after_core", [shape_of((2, lines, part), jnp.float32), shape_of((2, lines, part))],
+                      mine, come)
+    stay, send = call(after_swap_kernel, "after_swap", [shape_of((lines, part), jnp.float32), shape_of((lines, part))],
+                      keep, swap_by_core(send, "tp", True))
+    return stay, swap_by_core(send, "tp", False)
+
+
+def expert_kernel(gain_ref, gate_ref, up_ref, down_ref, *refs):
+    pieces, (other_ref, mine_ref, middle_ref, x_ref, chunk_ref, row_ref) = refs[:6], refs[6:]
+    total_rows = middle_ref.shape[0]
+    tps, lines, part = mine_ref.shape
+    groups = lines // total_rows
+    secs = chunk_ref.shape[0] // tps
+    width = down_ref.shape[1]
+    sec, tp, grp = lax.axis_index("sec"), lax.axis_index("tp"), lax.axis_index("grp")
+    first, second = masks_by_core()
+
+    def place(piece, at, by_other_core):
+        at = pl.ds(pl.multiple_of(at * LANES, LANES), LANES)
+        for n, m in enumerate((0, 2, 1, 3) if by_other_core else range(groups)):
+            x_ref[n * total_rows:(n + 1) * total_rows, at] = piece[m]
+
+    for other in range(secs):
+        own, near, far = pieces[3 * other:3 * other + 3]
+        base = jnp.bitwise_xor(sec, other) * tps
+        one, two = (second, first) if other else (first, second)
+        place(own, base + tp, other)
+        place(near, base + jnp.bitwise_xor(tp, one), other)
+        place(far.at[0], base + jnp.bitwise_xor(tp, two), other)
+        place(far.at[1], base + jnp.bitwise_xor(tp, 3), other)
     x = x_ref[:, :width].astype(jnp.float32)
     for c in range(secs * tps):
         row_ref[c] = x[:total_rows, c * part:(c + 1) * part]
     middle_ref[...] = row_ref[sec * tps + tp]
+    spare = x_ref[:, width:].astype(jnp.float32)
+    spare_at = lax.broadcasted_iota(jnp.int32, spare.shape, 1)
+    weight = jnp.sum(jnp.where((spare_at == 2 * grp) | (spare_at == 2 * grp + 1), spare, 0.0), axis=1, keepdims=True)
     scale = lax.rsqrt(jnp.mean(x * x, axis=-1, keepdims=True) + 1e-05)
     expert_in = (x * scale * gain_ref[...]).astype(jnp.bfloat16)
     gate_h = dot_last(expert_in, gate_ref[...])
     up_h = dot_last(expert_in, up_ref[...])
     act = ((up_h + 1.0) * gate_h * jax.nn.sigmoid(1.702 * gate_h)).astype(jnp.bfloat16)
-    out = jnp.dot(act, down_ref[...], preferred_element_type=jnp.float32)
+    out = jnp.dot(act, down_ref[...], preferred_element_type=jnp.float32) * weight
     for c in range(secs * tps):
         chunk_ref[c] = out[:, c * part:(c + 1) * part]
     for t in range(tps):
-        other_ref[t] = chunk_ref[(1 - sec) * tps + t].astype(jnp.bfloat16)
+        for n, m in enumerate((0, 2, 1, 3)):
+            other_ref[t, n * total_rows:(n + 1) * total_rows] = chunk_ref[
+                (1 - sec) * tps + t, m * total_rows:(m + 1) * total_rows].astype(jnp.bfloat16)
         mine_ref[t] = chunk_ref[sec * tps + t]
 
 
@@ -442,11 +503,11 @@
     part = width // shards
     lines = groups * total_rows
     return pl.pallas_call(
-        functools.partial(expert_kernel, secs=secs, tps=tps),
+        expert_kernel,
         name="expert",
         out_shape=[shape_of((tps, lines, part)), shape_of((tps, lines, part), jnp.float32),
                    shape_of((total_rows, part), jnp.float32)],
-        in_specs=[vmem()] * (4 + shards),
+        in_specs=[vmem()] * (4 + len(pieces)),
         out_specs=[vmem()] * 3,
         scratch_shapes=[
             pltpu.VMEM((lines, shards * LANES), jnp.bfloat16),
@@ -457,81 +518,37 @@
     )(gain.reshape(1, -1), w_gate.swapaxes(0, 1), w_up.swapaxes(0, 1), w_down, *pieces)
 
 
-def combine_kernel(routes_ref, weights_ref, middle_ref, *refs):
-    come, out_ref = refs[:-1], refs[-1]
-    steps, rows, part = out_ref.shape
-    grp = lax.axis_index("grp")
-    corner = lax.broadcasted_iota(jnp.int32, (rows, rows), 0) == lax.broadcasted_iota(jnp.int32, (rows, rows), 1)
-    for s in range(steps):
-        at = pl.ds(s * rows, rows)
-        total = middle_ref[at, :]
-        for m, ref in enumerate(come):
-            named = routes_ref[s] == jnp.bitwise_xor(grp, m)
-            line = jnp.sum(jnp.where(named, weights_ref[s], 0.0), axis=0, keepdims=True)
-            column = jnp.sum(jnp.where(corner, line, 0.0), axis=1, keepdims=True)
-            total = total + column * ref[at, :].astype(jnp.float32)
-        out_ref[s] = total.astype(jnp.bfloat16)
-
-
-def combine(routes, weights, middle, come, steps):
-    total_rows, part = middle.shape
-    return pl.pallas_call(
-        combine_kernel,
-        name="combine",
-        out_shape=shape_of((steps, total_rows // steps, part)),
-        in_specs=[vmem()] * (3 + len(come)),
-        out_specs=vmem(),
-        compiler_params=pltpu.CompilerParams(vmem_limit_bytes=4 * MIB),
-    )(routes.swapaxes(1, 2), weights.swapaxes(1, 2), middle, *come)
-
-
-def unstack_kernel(own_ref, *refs, groups):
-    come, outs = refs[:-groups], refs[-groups:]
-    total = own_ref[...]
-    for ref in come:
-        total = total + ref[...].astype(jnp.float32)
-    lines = outs[0].shape[0]
-    for m, out in enumerate(outs):
-        out[...] = total[m * lines:(m + 1) * lines].astype(jnp.bfloat16)
-
-
-def sum_and_unstack(own, come, groups):
-    lines, part = own.shape
-    return pl.pallas_call(
-        functools.partial(unstack_kernel, groups=groups),
-        name="sum_and_unstack",
-        out_shape=[shape_of((lines // groups, part))] * groups,
-        in_specs=[vmem()] * (1 + len(come)),
-        out_specs=[vmem()] * groups,
-        compiler_params=pltpu.CompilerParams(vmem_limit_bytes=4 * MIB),
-    )(own, *come)
-
-
 def every_expert_body(inputs, attention_gain, w_query, key_value_weight, head_sink_logits, w_output, cache_pairs, lengths,
                       expert_gain, w_gate, w_up, w_down, routes, gate_weights):
     secs, tps, groups = lax.axis_size("sec"), lax.axis_size("tp"), lax.axis_size("grp")
     steps, rows, width = inputs.shape
     flat = inputs.reshape(steps * rows, width)
-    other, mine, own_x = attention_partial(flat, attention_gain, w_query, key_value_weight[:, 0], head_sink_logits, w_output,
-                                           cache_pairs[:, :, 0], lengths, secs, tps)
-    own, *parts = add_and_split(mine, swap(other, "sec", 1), own_x)
-    come = [swap(parts[m - 1], "tp", m) for m in reversed(range(1, tps))]
-    middle = sum_pieces(own, come, own.shape)
-    come = {m: swap(middle, "grp", m) for m in reversed(range(1, groups))}
-    stacked = jnp.stack([middle] + [come[m] for m in range(1, groups)])
-    come = {m: swap(stacked, "tp", m) for m in reversed(range(1, tps))}
-    pieces = [stacked] + [come[m] for m in range(1, tps)]
-    pieces = pieces + [swap(piece, "sec", 1) for piece in pieces]
+    other, mine, own_x = attention_partial(
+        flat, attention_gain, w_query, key_value_weight[:, 0], head_sink_logits, w_output, cache_pairs[:, :, 0], lengths,
+        routes.swapaxes(1, 2), gate_weights.swapaxes(1, 2), secs, tps)
+    stay, come = scatter_shards(mine, swap(other, "sec", 1))
+    middle = call(sum_kernel, "sum", shape_of((1, steps * rows, LANES)), stay, come, own_x)
+    middle = jnp.concatenate([middle, swap_by_core(middle, "grp", True)], axis=0)
+    own = jnp.concatenate([middle, swap_by_core(middle, "grp", False)], axis=0)
+    near = swap_by_core(own, "tp", True)
+    own_other = swap(own, "sec", 1)
+    far = swap_by_core(jnp.stack([own, near]), "tp", False)
+    near_other = swap(near, "sec", 1)
+    far_other = swap(far, "sec", 1)
+    pieces = [own, near, far, own_other, near_other, far_other]
     other, mine, own_middle = expert_partial(expert_gain, w_gate[0], w_up[0], w_down[0], pieces, secs, tps)
-    own, *parts = add_and_split(mine, swap(other, "sec", 1))
-    come = [swap(parts[m - 1], "tp", m) for m in reversed(range(1, tps))]
-    held = sum_and_unstack(own, come, groups)
-    come = {m: swap(held[m], "grp", m) for m in reversed(range(1, groups))}
-    return combine(routes, gate_weights, own_middle, [held[0]] + [come[m] for m in range(1, groups)], steps)
+    stay, come = scatter_shards(mine, swap(other, "sec", 1))
+    lines, part = steps * rows, stay.shape[1]
+    keep, send = call(divide_rows_kernel, "divide_rows", [shape_of((2, lines, part), jnp.float32), shape_of((2, lines, part))],
+                      stay, come)
+    stay, send = call(after_swap_kernel, "after_swap", [shape_of((lines, part), jnp.float32), shape_of((lines, part))],
+                      keep, swap_by_core(send, "grp", False))
+    return call(sum_kernel, "combine", shape_of((steps, rows, part)), stay, swap_by_core(send, "grp", True), own_middle)
 
 
 def body(*args):
-    if lax.axis_size("grp") * args[9].shape[0] == TOP and args[9].shape[0] == 1:
+    sizes = lax.axis_size("sec"), lax.axis_size("tp"), lax.axis_size("grp"), args[9].shape[0]
+    if sizes == (2, 4, TOP, 1):
         return every_expert_body(*args)
     return general_body(*args)
 

time: 61.4 us -> 62.9 us (1.024)
  waiting for transfers between devices: 22 us -> 35 us
  local copies, waits for them, and re-layouts: 8.98 us -> 0.03 us
  starting transfers between devices: 21.8 us -> 19.9 us
    ppermute x0 -> x10, waiting for transfers between devices: none -> 31.2 us  [swap_by_core(): return lax.ppermute(value, ('sec', axis), pairs)]
    ppermute x21 -> x5, starting transfers between devices: 21.8 us -> 1.25 us  [swap(): return lax.ppermute(value, axes, [(i, i ^ mask) for i in range(size)])]
    ppermute x0 -> x10, starting transfers between devices: none -> 18.6 us  [swap_by_core(): return lax.ppermute(value, ('sec', axis), pairs)]
    ppermute x21 -> x5, waiting for transfers between devices: 22 us -> 3.79 us  [swap(): return lax.ppermute(value, axes, [(i, i ^ mask) for i in range(size)])]
    unnamed x26 -> x8, local copies, waits for them, and re-layouts: 8.26 us -> 0.02 us
    reshape x1 -> x0, local copies, waits for them, and re-layouts: 0.71 us -> none  [attention_partial(): gain.reshape(1, -1)]
    pallas_call x6 -> x9, Pallas kernels: 2.93 us -> 2.89 us  [the longest x1 2.05 us: expert_partial(): pl.pallas_call(expert_kernel, name='expert', out_shape=[shape_of((tps, li...]
  transfers between devices with their start and end apart: 21 -> 15, of which waited for: 16 -> 14; matrix products, arithmetic and copies ran while one was open for 0% -> 0% of each run, Pallas kernels for 0% -> 0%
where the time goes in v3:
time: 62.9 us; the launch traced here: 62.8 us
  waiting for transfers between devices  35 us (56%)
  starting transfers between devices  19.9 us (32%)
  Pallas kernels  7.73 us (12%)
    ppermute x10, waiting for transfers between devices, swap_by_core(): return lax.ppermute(value, ('sec', axis), pairs)  31.2 us
    ppermute x10, starting transfers between devices, swap_by_core(): return lax.ppermute(value, ('sec', axis), pairs)  18.6 us
    pallas_call x1, Pallas kernels, attention_partial(): pl.pallas_call(attention_kernel, name='attention', out_shape=[shape_of((t...  4.85 us
    ppermute x5, waiting for transfers between devices, swap(): return lax.ppermute(value, axes, [(i, i ^ mask) for i in range(size)])  3.79 us
    pallas_call x1, Pallas kernels, expert_partial(): pl.pallas_call(expert_kernel, name='expert', out_shape=[shape_of((tps, li...  2.05 us
  transfers between devices with their start and end apart: 15, of which 14 were waited for; matrix products, arithmetic and copies ran while one was open for 0% of the time, Pallas kernels for 0%

profile of v3, /device:TPU:0, one launch (start us, length us, event | category | flops | bytes accessed | tf_op | source)
XLA Modules:
  0.0 62.8 jit_solution(15680773956555477086)
XLA Ops:
  0.0 4.8 %attention.1 = (bf16[4,32,384]{2,1,0:T(8,128)(2,1)S(1)}, f32[4,32,384]{2,1,0:T(8,128)S(1)}, f32[32,384]{1,0:T(8,128)S(1)}) custom-call(s32[16]{0:T(128)} %lengths_hbm.1, f32[8]{0:T(128)} %sinks_hbm.1, s32[2,4,16]{2,1,0:T(4,128)} %bitcast.24, f32[2,4,16]{2,1,0:T(4,128)} %bitcast.25, f32[2880]{0:T(1024)} %gain_hbm.1, bf16[32,2880]{1,0:T(8,128)(2,1)} %bitcast.23, ...), custom_call_target="tpu_custom_call" | custom-call | tf_op jit(solution)/shard_map/attention/pallas_call | solution.py:378
  5.4 0.9 %collective-permute-done.come_ref = bf16[4,32,384]{2,1,0:T(8,128)(2,1)S(1)} collective-permute-done((bf16[4,32,384]{2,1,0:T(8,128)(2,1)S(1)}, bf16[4,32,384]{2,1,0:T(8,128)(2,1)S(1)}, u32[]{:S(2)}, u32[]{:S(2)}) %collective-permute-start) | collective-permute-done | bytes 98336 | tf_op jit(solution)/shard_map/ppermute | solution.py:223
  6.4 2.9 %collective-permute-start.1 = (bf16[2,32,384]{2,1,0:T(8,128)(2,1)S(1)}, bf16[2,32,384]{2,1,0:T(8,128)(2,1)S(1)}, u32[]{:S(2)}, u32[]{:S(2)}) collective-permute-start(bf16[2,32,384]{2,1,0:T(8,128)(2,1)S(1)} %get-tuple-element.26), channel_id=1, source_target_pairs={{0,1},{1,0},{2,3},{3,2},{16,18},{17,19},{18,16},{19,17},{4,5},{5,4... | collective-permute-start | bytes 147464 | tf_op jit(solution)/shard_map/ppermute | solution.py:230
  9.3 2.1 %collective-permute-done.1.come_ref = bf16[2,32,384]{2,1,0:T(8,128)(2,1)S(1)} collective-permute-done((bf16[2,32,384]{2,1,0:T(8,128)(2,1)S(1)}, bf16[2,32,384]{2,1,0:T(8,128)(2,1)S(1)}, u32[]{:S(2)}, u32[]{:S(2)}) %collective-permute-start.1) | collective-permute-done | bytes 49184 | tf_op jit(solution)/shard_map/ppermute | solution.py:230
  11.4 2.1 %collective-permute-start.2 = (bf16[32,384]{1,0:T(8,128)(2,1)S(1)}, bf16[32,384]{1,0:T(8,128)(2,1)S(1)}, u32[]{:S(2)}, u32[]{:S(2)}) collective-permute-start(bf16[32,384]{1,0:T(8,128)(2,1)S(1)} %get-tuple-element.28), channel_id=1, source_target_pairs={{0,2},{1,3},{2,0},{3,1},{16,17},{17,16},{18,19},{19,18},{4,6},{5,7... | collective-permute-start | bytes 73736 | tf_op jit(solution)/shard_map/ppermute | solution.py:230
  13.5 1.8 %collective-permute-done.2.come_ref = bf16[32,384]{1,0:T(8,128)(2,1)S(1)} collective-permute-done((bf16[32,384]{1,0:T(8,128)(2,1)S(1)}, bf16[32,384]{1,0:T(8,128)(2,1)S(1)}, u32[]{:S(2)}, u32[]{:S(2)}) %collective-permute-start.2) | collective-permute-done | bytes 24608 | tf_op jit(solution)/shard_map/ppermute | solution.py:230
  15.3 2.1 %collective-permute-start.3 = (bf16[1,32,384]{2,1,0:T(8,128)(2,1)S(1)}, bf16[1,32,384]{2,1,0:T(8,128)(2,1)S(1)}, u32[]{:S(2)}, u32[]{:S(2)}) collective-permute-start(bf16[1,32,384]{2,1,0:T(8,128)(2,1)S(1)} %sum.1), channel_id=1, source_target_pairs={{0,4},{4,0},{8,12},{12,8},{16,24},{20,28},{24,16},{28,20},{1,5},{5... | collective-permute-start | bytes 73736 | tf_op jit(solution)/shard_map/ppermute | solution.py:230
  17.4 1.8 %collective-permute-done.3 = bf16[1,32,384]{2,1,0:T(8,128)(2,1)S(1)} collective-permute-done((bf16[1,32,384]{2,1,0:T(8,128)(2,1)S(1)}, bf16[1,32,384]{2,1,0:T(8,128)(2,1)S(1)}, u32[]{:S(2)}, u32[]{:S(2)}) %collective-permute-start.3) | collective-permute-done | bytes 24608 | tf_op jit(solution)/shard_map/ppermute | solution.py:230
  19.3 3.1 %collective-permute-start.4 = (bf16[2,32,384]{2,1,0:T(8,128)(2,1)S(1)}, bf16[2,32,384]{2,1,0:T(8,128)(2,1)S(1)}, u32[]{:S(2)}, u32[]{:S(2)}) collective-permute-start(bf16[2,32,384]{2,1,0:T(8,128)(2,1)S(1)} %pad_maximum_fusion.2), channel_id=1, source_target_pairs={{0,8},{4,12},{8,0},{12,4},{16,20},{20,16},{24,28},{28,24},{1,9},{5... | collective-permute-start | bytes 147464 | tf_op jit(solution)/shard_map/ppermute | solution.py:230
  22.4 2.1 %collective-permute-done.4 = bf16[2,32,384]{2,1,0:T(8,128)(2,1)S(1)} collective-permute-done((bf16[2,32,384]{2,1,0:T(8,128)(2,1)S(1)}, bf16[2,32,384]{2,1,0:T(8,128)(2,1)S(1)}, u32[]{:S(2)}, u32[]{:S(2)}) %collective-permute-start.4) | collective-permute-done | bytes 49184 | tf_op jit(solution)/shard_map/ppermute | solution.py:230
  24.5 1.9 %collective-permute-start.5 = (bf16[4,32,384]{2,1,0:T(8,128)(2,1)S(1)}, bf16[4,32,384]{2,1,0:T(8,128)(2,1)S(1)}, u32[]{:S(2)}, u32[]{:S(2)}) collective-permute-start(bf16[4,32,384]{2,1,0:T(8,128)(2,1)S(1)} %get-tuple-element.42.refs_0_), channel_id=1, source_target_pairs={{0,1},{1,0},{2,3},{3,2},{16,18},{17,19},{18,16},{19,17},{4,5},{5,4... | collective-permute-start | bytes 294920 | tf_op jit(solution)/shard_map/ppermute | solution.py:230
  26.3 3.7 %collective-permute-done.5.refs_1_ = bf16[4,32,384]{2,1,0:T(8,128)(2,1)S(1)} collective-permute-done((bf16[4,32,384]{2,1,0:T(8,128)(2,1)S(1)}, bf16[4,32,384]{2,1,0:T(8,128)(2,1)S(1)}, u32[]{:S(2)}, u32[]{:S(2)}) %collective-permute-start.5) | collective-permute-done | bytes 98336 | tf_op jit(solution)/shard_map/ppermute | solution.py:230
  30.1 1.2 %collective-permute-start.6 = (bf16[2,4,32,384]{3,2,1,0:T(8,128)(2,1)S(1)}, bf16[2,4,32,384]{3,2,1,0:T(8,128)(2,1)S(1)}, u32[]{:S(2)}, u32[]{:S(2)}) collective-permute-start(bf16[2,4,32,384]{3,2,1,0:T(8,128)(2,1)S(1)} %pad_maximum_fusion), channel_id=1, source_target_pairs={{0,2},{1,3},{2,0},{3,1},{16,17},{17,16},{18,19},{19,18},{4,6},{5,7... | collective-permute-start | bytes 589832 | tf_op jit(solution)/shard_map/ppermute | solution.py:230
  31.3 4.5 %collective-permute-done.6.refs_2_ = bf16[2,4,32,384]{3,2,1,0:T(8,128)(2,1)S(1)} collective-permute-done((bf16[2,4,32,384]{3,2,1,0:T(8,128)(2,1)S(1)}, bf16[2,4,32,384]{3,2,1,0:T(8,128)(2,1)S(1)}, u32[]{:S(2)}, u32[]{:S(2)}) %collective-permute-start.6) | collective-permute-done | bytes 196640 | tf_op jit(solution)/shard_map/ppermute | solution.py:230
  36.4 1.1 %collective-permute-done.7.refs_3_ = bf16[4,32,384]{2,1,0:T(8,128)(2,1)S(1)} collective-permute-done((bf16[4,32,384]{2,1,0:T(8,128)(2,1)S(1)}, bf16[4,32,384]{2,1,0:T(8,128)(2,1)S(1)}, u32[]{:S(2)}, u32[]{:S(2)}) %collective-permute-start.7) | collective-permute-done | bytes 98336 | tf_op jit(solution)/shard_map/ppermute | solution.py:223
  37.7 2.0 %expert.1 = (bf16[4,128,360]{2,1,0:T(8,128)(2,1)S(1)}, f32[4,128,360]{2,1,0:T(8,128)S(1)}, f32[32,360]{1,0:T(8,128)S(1)}) custom-call(f32[1,2880]{1,0:T(1,128)S(1)} %reshape.6.gain_ref, bf16[180,2880]{1,0:T(8,128)(2,1)S(1)} %bitcast.16, bf16[180,2880]{1,0:T(8,128)(2,1)S(1)} %bitcast.17, bf16[180,2880]{1,0:T(8,128)(2,1)S(1)} %bitcast.18, ...), custom_call_target="tpu_custom_call" | custom-call | tf_op jit(solution)/shard_map/expert/pallas_call | solution.py:505
  40.0 1.6 %collective-permute-done.10.come_ref = bf16[4,128,360]{2,1,0:T(8,128)(2,1)S(1)} collective-permute-done((bf16[4,128,360]{2,1,0:T(8,128)(2,1)S(1)}, bf16[4,128,360]{2,1,0:T(8,128)(2,1)S(1)}, u32[]{:S(2)}, u32[]{:S(2)}) %collective-permute-start.10) | collective-permute-done | bytes 368672 | tf_op jit(solution)/shard_map/ppermute | solution.py:223
  41.6 1.2 %collective-permute-start.11 = (bf16[2,128,360]{2,1,0:T(8,128)(2,1)S(1)}, bf16[2,128,360]{2,1,0:T(8,128)(2,1)S(1)}, u32[]{:S(2)}, u32[]{:S(2)}) collective-permute-start(bf16[2,128,360]{2,1,0:T(8,128)(2,1)S(1)} %get-tuple-element.33), channel_id=1, source_target_pairs={{0,1},{1,0},{2,3},{3,2},{16,18},{17,19},{18,16},{19,17},{4,5},{5,4... | collective-permute-start | bytes 552968 | tf_op jit(solution)/shard_map/ppermute | solution.py:230
  42.8 4.5 %collective-permute-done.11.come_ref = bf16[2,128,360]{2,1,0:T(8,128)(2,1)S(1)} collective-permute-done((bf16[2,128,360]{2,1,0:T(8,128)(2,1)S(1)}, bf16[2,128,360]{2,1,0:T(8,128)(2,1)S(1)}, u32[]{:S(2)}, u32[]{:S(2)}) %collective-permute-start.11) | collective-permute-done | bytes 184352 | tf_op jit(solution)/shard_map/ppermute | solution.py:230
  47.4 1.2 %collective-permute-start.12 = (bf16[128,360]{1,0:T(8,128)(2,1)S(1)}, bf16[128,360]{1,0:T(8,128)(2,1)S(1)}, u32[]{:S(2)}, u32[]{:S(2)}) collective-permute-start(bf16[128,360]{1,0:T(8,128)(2,1)S(1)} %get-tuple-element.35), channel_id=1, source_target_pairs={{0,2},{1,3},{2,0},{3,1},{16,17},{17,16},{18,19},{19,18},{4,6},{5,7... | collective-permute-start | bytes 276488 | tf_op jit(solution)/shard_map/ppermute | solution.py:230
  48.6 3.5 %collective-permute-done.12.come_ref = bf16[128,360]{1,0:T(8,128)(2,1)S(1)} collective-permute-done((bf16[128,360]{1,0:T(8,128)(2,1)S(1)}, bf16[128,360]{1,0:T(8,128)(2,1)S(1)}, u32[]{:S(2)}, u32[]{:S(2)}) %collective-permute-start.12) | collective-permute-done | bytes 92192 | tf_op jit(solution)/shard_map/ppermute | solution.py:230
  52.1 2.3 %collective-permute-start.13 = (bf16[2,32,360]{2,1,0:T(8,128)(2,1)S(1)}, bf16[2,32,360]{2,1,0:T(8,128)(2,1)S(1)}, u32[]{:S(2)}, u32[]{:S(2)}) collective-permute-start(bf16[2,32,360]{2,1,0:T(8,128)(2,1)S(1)} %get-tuple-element.37), channel_id=1, source_target_pairs={{0,8},{4,12},{8,0},{12,4},{16,20},{20,16},{24,28},{28,24},{1,9},{5... | collective-permute-start | bytes 138248 | tf_op jit(solution)/shard_map/ppermute | solution.py:230
  54.4 3.8 %collective-permute-done.13.come_ref = bf16[2,32,360]{2,1,0:T(8,128)(2,1)S(1)} collective-permute-done((bf16[2,32,360]{2,1,0:T(8,128)(2,1)S(1)}, bf16[2,32,360]{2,1,0:T(8,128)(2,1)S(1)}, u32[]{:S(2)}, u32[]{:S(2)}) %collective-permute-start.13) | collective-permute-done | bytes 46112 | tf_op jit(solution)/shard_map/ppermute | solution.py:230
  58.8 3.3 %collective-permute-done.14.come_ref = bf16[32,360]{1,0:T(8,128)(2,1)S(1)} collective-permute-done((bf16[32,360]{1,0:T(8,128)(2,1)S(1)}, bf16[32,360]{1,0:T(8,128)(2,1)S(1)}, u32[]{:S(2)}, u32[]{:S(2)}) %collective-permute-start.14) | collective-permute-done | bytes 23072 | tf_op jit(solution)/shard_map/ppermute | solution.py:230
  (28 shorter events, 3.0 us)
Async XLA Ops:
  0.0 37.7 %copy-start.1 = (bf16[1,2880,180]{1,2,0:T(8,128)(2,1)S(1)}, bf16[1,2880,180]{1,2,0:T(8,128)(2,1)}, u32[]{:S(2)}) copy-start(bf16[1,2880,180]{1,2,0:T(8,128)(2,1)} %param.24) | copy-start | bytes 3110404
  0.0 37.7 %copy-start.2 = (bf16[1,180,2880]{2,1,0:T(8,128)(2,1)S(1)}, bf16[1,180,2880]{2,1,0:T(8,128)(2,1)}, u32[]{:S(2)}) copy-start(bf16[1,180,2880]{2,1,0:T(8,128)(2,1)} %param.25) | copy-start | bytes 3110404
  4.9 31.5 %copy-start.3 = (f32[2880]{0:T(1024)S(1)}, f32[2880]{0:T(1024)}, u32[]{:S(2)}) copy-start(f32[2880]{0:T(1024)} %param.22) | copy-start | bytes 34564
  4.9 32.8 %copy-start = (bf16[1,2880,180]{1,2,0:T(8,128)(2,1)S(1)}, bf16[1,2880,180]{1,2,0:T(8,128)(2,1)}, u32[]{:S(2)}) copy-start(bf16[1,2880,180]{1,2,0:T(8,128)(2,1)} %param.23) | copy-start | bytes 3110404
  4.9 1.5 %collective-permute-start = (bf16[4,32,384]{2,1,0:T(8,128)(2,1)S(1)}, bf16[4,32,384]{2,1,0:T(8,128)(2,1)S(1)}, u32[]{:S(2)}, u32[]{:S(2)}) collective-permute-start(bf16[4,32,384]{2,1,0:T(8,128)(2,1)S(1)} %get-tuple-element.24), channel_id=1, source_target_pairs={{0,16},{16,0},{1,17},{17,1},{2,18},{18,2},{3,19},{19,3},{4,20},{20... | collective-permute-start | bytes 294920 | tf_op jit(solution)/shard_map/ppermute | solution.py:223
  6.4 5.0 %collective-permute-start.1 = (bf16[2,32,384]{2,1,0:T(8,128)(2,1)S(1)}, bf16[2,32,384]{2,1,0:T(8,128)(2,1)S(1)}, u32[]{:S(2)}, u32[]{:S(2)}) collective-permute-start(bf16[2,32,384]{2,1,0:T(8,128)(2,1)S(1)} %get-tuple-element.26), channel_id=1, source_target_pairs={{0,1},{1,0},{2,3},{3,2},{16,18},{17,19},{18,16},{19,17},{4,5},{5,4... | collective-permute-start | bytes 147464 | tf_op jit(solution)/shard_map/ppermute | solution.py:230
  11.4 3.9 %collective-permute-start.2 = (bf16[32,384]{1,0:T(8,128)(2,1)S(1)}, bf16[32,384]{1,0:T(8,128)(2,1)S(1)}, u32[]{:S(2)}, u32[]{:S(2)}) collective-permute-start(bf16[32,384]{1,0:T(8,128)(2,1)S(1)} %get-tuple-element.28), channel_id=1, source_target_pairs={{0,2},{1,3},{2,0},{3,1},{16,17},{17,16},{18,19},{19,18},{4,6},{5,7... | collective-permute-start | bytes 73736 | tf_op jit(solution)/shard_map/ppermute | solution.py:230
  15.3 4.0 %collective-permute-start.3 = (bf16[1,32,384]{2,1,0:T(8,128)(2,1)S(1)}, bf16[1,32,384]{2,1,0:T(8,128)(2,1)S(1)}, u32[]{:S(2)}, u32[]{:S(2)}) collective-permute-start(bf16[1,32,384]{2,1,0:T(8,128)(2,1)S(1)} %sum.1), channel_id=1, source_target_pairs={{0,4},{4,0},{8,12},{12,8},{16,24},{20,28},{24,16},{28,20},{1,5},{5... | collective-permute-start | bytes 73736 | tf_op jit(solution)/shard_map/ppermute | solution.py:230
  19.3 5.2 %collective-permute-start.4 = (bf16[2,32,384]{2,1,0:T(8,128)(2,1)S(1)}, bf16[2,32,384]{2,1,0:T(8,128)(2,1)S(1)}, u32[]{:S(2)}, u32[]{:S(2)}) collective-permute-start(bf16[2,32,384]{2,1,0:T(8,128)(2,1)S(1)} %pad_maximum_fusion.2), channel_id=1, source_target_pairs={{0,8},{4,12},{8,0},{12,4},{16,20},{20,16},{24,28},{28,24},{1,9},{5... | collective-permute-start | bytes 147464 | tf_op jit(solution)/shard_map/ppermute | solution.py:230
  24.5 5.6 %collective-permute-start.5 = (bf16[4,32,384]{2,1,0:T(8,128)(2,1)S(1)}, bf16[4,32,384]{2,1,0:T(8,128)(2,1)S(1)}, u32[]{:S(2)}, u32[]{:S(2)}) collective-permute-start(bf16[4,32,384]{2,1,0:T(8,128)(2,1)S(1)} %get-tuple-element.42.refs_0_), channel_id=1, source_target_pairs={{0,1},{1,0},{2,3},{3,2},{16,18},{17,19},{18,16},{19,17},{4,5},{5,4... | collective-permute-start | bytes 294920 | tf_op jit(solution)/shard_map/ppermute | solution.py:230
  30.1 5.7 %collective-permute-start.6 = (bf16[2,4,32,384]{3,2,1,0:T(8,128)(2,1)S(1)}, bf16[2,4,32,384]{3,2,1,0:T(8,128)(2,1)S(1)}, u32[]{:S(2)}, u32[]{:S(2)}) collective-permute-start(bf16[2,4,32,384]{3,2,1,0:T(8,128)(2,1)S(1)} %pad_maximum_fusion), channel_id=1, source_target_pairs={{0,2},{1,3},{2,0},{3,1},{16,17},{17,16},{18,19},{19,18},{4,6},{5,7... | collective-permute-start | bytes 589832 | tf_op jit(solution)/shard_map/ppermute | solution.py:230
  35.9 1.8 %collective-permute-start.9 = (bf16[2,4,32,384]{3,2,1,0:T(8,128)(2,1)S(1)}, bf16[2,4,32,384]{3,2,1,0:T(8,128)(2,1)S(1)}, u32[]{:S(2)}, u32[]{:S(2)}) collective-permute-start(bf16[2,4,32,384]{3,2,1,0:T(8,128)(2,1)S(1)} %collective-permute-done.6.refs_2_), channel_id=1, source_target_pairs={{0,16},{16,0},{1,17},{17,1},{2,18},{18,2},{3,19},{19,3},{4,20},{20... | collective-permute-start | bytes 589832 | tf_op jit(solution)/shard_map/ppermute | solution.py:223
  35.9 1.6 %collective-permute-start.7 = (bf16[4,32,384]{2,1,0:T(8,128)(2,1)S(1)}, bf16[4,32,384]{2,1,0:T(8,128)(2,1)S(1)}, u32[]{:S(2)}, u32[]{:S(2)}) collective-permute-start(bf16[4,32,384]{2,1,0:T(8,128)(2,1)S(1)} %get-tuple-element.42.refs_0_), channel_id=1, source_target_pairs={{0,16},{16,0},{1,17},{17,1},{2,18},{18,2},{3,19},{19,3},{4,20},{20... | collective-permute-start | bytes 294920 | tf_op jit(solution)/shard_map/ppermute | solution.py:223
  36.4 1.3 %collective-permute-start.8 = (bf16[4,32,384]{2,1,0:T(8,128)(2,1)S(1)}, bf16[4,32,384]{2,1,0:T(8,128)(2,1)S(1)}, u32[]{:S(2)}, u32[]{:S(2)}) collective-permute-start(bf16[4,32,384]{2,1,0:T(8,128)(2,1)S(1)} %collective-permute-done.5.refs_1_), channel_id=1, source_target_pairs={{0,16},{16,0},{1,17},{17,1},{2,18},{18,2},{3,19},{19,3},{4,20},{20... | collective-permute-start | bytes 294920 | tf_op jit(solution)/shard_map/ppermute | solution.py:223
  39.7 1.8 %collective-permute-start.10 = (bf16[4,128,360]{2,1,0:T(8,128)(2,1)S(1)}, bf16[4,128,360]{2,1,0:T(8,128)(2,1)S(1)}, u32[]{:S(2)}, u32[]{:S(2)}) collective-permute-start(bf16[4,128,360]{2,1,0:T(8,128)(2,1)S(1)} %get-tuple-element.31), channel_id=1, source_target_pairs={{0,16},{16,0},{1,17},{17,1},{2,18},{18,2},{3,19},{19,3},{4,20},{20... | collective-permute-start | bytes 1105928 | tf_op jit(solution)/shard_map/ppermute | solution.py:223
  41.6 5.7 %collective-permute-start.11 = (bf16[2,128,360]{2,1,0:T(8,128)(2,1)S(1)}, bf16[2,128,360]{2,1,0:T(8,128)(2,1)S(1)}, u32[]{:S(2)}, u32[]{:S(2)}) collective-permute-start(bf16[2,128,360]{2,1,0:T(8,128)(2,1)S(1)} %get-tuple-element.33), channel_id=1, source_target_pairs={{0,1},{1,0},{2,3},{3,2},{16,18},{17,19},{18,16},{19,17},{4,5},{5,4... | collective-permute-start | bytes 552968 | tf_op jit(solution)/shard_map/ppermute | solution.py:230
  47.4 4.7 %collective-permute-start.12 = (bf16[128,360]{1,0:T(8,128)(2,1)S(1)}, bf16[128,360]{1,0:T(8,128)(2,1)S(1)}, u32[]{:S(2)}, u32[]{:S(2)}) collective-permute-start(bf16[128,360]{1,0:T(8,128)(2,1)S(1)} %get-tuple-element.35), channel_id=1, source_target_pairs={{0,2},{1,3},{2,0},{3,1},{16,17},{17,16},{18,19},{19,18},{4,6},{5,7... | collective-permute-start | bytes 276488 | tf_op jit(solution)/shard_map/ppermute | solution.py:230
  52.1 6.1 %collective-permute-start.13 = (bf16[2,32,360]{2,1,0:T(8,128)(2,1)S(1)}, bf16[2,32,360]{2,1,0:T(8,128)(2,1)S(1)}, u32[]{:S(2)}, u32[]{:S(2)}) collective-permute-start(bf16[2,32,360]{2,1,0:T(8,128)(2,1)S(1)} %get-tuple-element.37), channel_id=1, source_target_pairs={{0,8},{4,12},{8,0},{12,4},{16,20},{20,16},{24,28},{28,24},{1,9},{5... | collective-permute-start | bytes 138248 | tf_op jit(solution)/shard_map/ppermute | solution.py:230
  58.2 3.9 %collective-permute-start.14 = (bf16[32,360]{1,0:T(8,128)(2,1)S(1)}, bf16[32,360]{1,0:T(8,128)(2,1)S(1)}, u32[]{:S(2)}, u32[]{:S(2)}) collective-permute-start(bf16[32,360]{1,0:T(8,128)(2,1)S(1)} %get-tuple-element.39), channel_id=1, source_target_pairs={{0,4},{4,0},{8,12},{12,8},{16,24},{20,28},{24,16},{28,20},{1,5},{5... | collective-permute-start | bytes 69128 | tf_op jit(solution)/shard_map/ppermute | solution.py:230

commit v4 on v3

--- a/solution.py
+++ b/solution.py
@@ -223,18 +223,6 @@
     return lax.ppermute(value, axes, [(i, i ^ mask) for i in range(size)])
 
 
-def swap_by_core(value, axis, first):
-    size = lax.axis_size(axis)
-    masks = (1, 2) if first else (2, 1)
-    pairs = [(s * size + i, s * size + (i ^ masks[s])) for s in range(2) for i in range(size)]
-    return lax.ppermute(value, ("sec", axis), pairs)
-
-
-def masks_by_core():
-    sec = lax.axis_index("sec")
-    return 1 + sec, 2 - sec
-
-
 def split_width(width):
     cuts = list(range(0, width, 768)) + [width]
     return list(zip(cuts[:-1], cuts[1:]))
@@ -415,65 +403,56 @@
     )(*operands)
 
 
-def after_core_kernel(mine_ref, come_ref, keep_ref, send_ref):
+def after_core_kernel(mine_ref, come_ref, own_ref, *send_refs):
     tp = lax.axis_index("tp")
-    first, second = masks_by_core()
-    for n, at in enumerate((tp, jnp.bitwise_xor(tp, second))):
-        keep_ref[n] = mine_ref[at] + come_ref[at].astype(jnp.float32)
-        at = jnp.bitwise_xor(at, first)
-        send_ref[n] = (mine_ref[at] + come_ref[at].astype(jnp.float32)).astype(jnp.bfloat16)
-
-
-def after_swap_kernel(keep_ref, come_ref, stay_ref, send_ref):
-    stay_ref[...] = keep_ref[0] + come_ref[0].astype(jnp.float32)
-    send_ref[...] = (keep_ref[1] + come_ref[1].astype(jnp.float32)).astype(jnp.bfloat16)
-
-
-def sum_kernel(stay_ref, come_ref, extra_ref, out_ref):
-    total = stay_ref[...] + come_ref[...].astype(jnp.float32) + extra_ref[...]
-    out_ref[...] = total.astype(jnp.bfloat16).reshape(out_ref.shape)
-
-
-def divide_rows_kernel(stay_ref, come_ref, keep_ref, send_ref):
-    total = stay_ref[...] + come_ref[...].astype(jnp.float32)
-    lines = keep_ref.shape[1]
-    for n in range(2):
-        keep_ref[n] = total[n * lines:(n + 1) * lines]
-        send_ref[n] = total[(n + 2) * lines:(n + 3) * lines].astype(jnp.bfloat16)
+    own_ref[...] = mine_ref[tp] + come_ref[tp].astype(jnp.float32)
+    for n, ref in enumerate(send_refs):
+        to = jnp.bitwise_xor(tp, n + 1)
+        ref[...] = (mine_ref[to] + come_ref[to].astype(jnp.float32)).astype(jnp.bfloat16)
+
+
+def add_all(*refs):
+    total = refs[0][...]
+    for ref in refs[1:]:
+        total = total + ref[...].astype(jnp.float32)
+    return total
+
+
+def sum_kernel(*refs):
+    refs[-1][...] = add_all(*refs[:-1]).astype(jnp.bfloat16).reshape(refs[-1].shape)
+
+
+def divide_rows_kernel(*refs, groups):
+    total = add_all(*refs[:-groups])
+    outs = refs[-groups:]
+    lines = outs[0].shape[0]
+    for n, out in enumerate(outs):
+        out[...] = total[n * lines:(n + 1) * lines].astype(out.dtype)
+
+
+def swap_all(parts, axis):
+    count = len(parts)
+    come = {m: swap(parts[m - 1], axis, m) for m in reversed(range(1, count + 1))}
+    return [come[m] for m in range(1, count + 1)]
 
 
 def scatter_shards(mine, come):
     tps, lines, part = mine.shape
-    keep, send = call(after_core_kernel, "after_core", [shape_of((2, lines, part), jnp.float32), shape_of((2, lines, part))],
-                      mine, come)
-    stay, send = call(after_swap_kernel, "after_swap", [shape_of((lines, part), jnp.float32), shape_of((lines, part))],
-                      keep, swap_by_core(send, "tp", True))
-    return stay, swap_by_core(send, "tp", False)
+    own, *parts = call(after_core_kernel, "after_core", [shape_of((lines, part), jnp.float32)] + [shape_of((lines, part))] * (tps - 1),
+                       mine, come)
+    return [own] + swap_all(parts, "tp")
 
 
 def expert_kernel(gain_ref, gate_ref, up_ref, down_ref, *refs):
-    pieces, (other_ref, mine_ref, middle_ref, x_ref, chunk_ref, row_ref) = refs[:6], refs[6:]
+    pieces, (other_ref, mine_ref, middle_ref, x_ref, chunk_ref, row_ref) = refs[:-6], refs[-6:]
     total_rows = middle_ref.shape[0]
     tps, lines, part = mine_ref.shape
-    groups = lines // total_rows
     secs = chunk_ref.shape[0] // tps
     width = down_ref.shape[1]
     sec, tp, grp = lax.axis_index("sec"), lax.axis_index("tp"), lax.axis_index("grp")
-    first, second = masks_by_core()
-
-    def place(piece, at, by_other_core):
-        at = pl.ds(pl.multiple_of(at * LANES, LANES), LANES)
-        for n, m in enumerate((0, 2, 1, 3) if by_other_core else range(groups)):
-            x_ref[n * total_rows:(n + 1) * total_rows, at] = piece[m]
-
-    for other in range(secs):
-        own, near, far = pieces[3 * other:3 * other + 3]
-        base = jnp.bitwise_xor(sec, other) * tps
-        one, two = (second, first) if other else (first, second)
-        place(own, base + tp, other)
-        place(near, base + jnp.bitwise_xor(tp, one), other)
-        place(far.at[0], base + jnp.bitwise_xor(tp, two), other)
-        place(far.at[1], base + jnp.bitwise_xor(tp, 3), other)
+    for n, piece in enumerate(pieces):
+        at = jnp.bitwise_xor(sec, n // tps) * tps + jnp.bitwise_xor(tp, n % tps)
+        x_ref[:, pl.ds(pl.multiple_of(at * LANES, LANES), LANES)] = piece[...].reshape(lines, LANES)
     x = x_ref[:, :width].astype(jnp.float32)
     for c in range(secs * tps):
         row_ref[c] = x[:total_rows, c * part:(c + 1) * part]
@@ -490,9 +469,7 @@
     for c in range(secs * tps):
         chunk_ref[c] = out[:, c * part:(c + 1) * part]
     for t in range(tps):
-        for n, m in enumerate((0, 2, 1, 3)):
-            other_ref[t, n * total_rows:(n + 1) * total_rows] = chunk_ref[
-                (1 - sec) * tps + t, m * total_rows:(m + 1) * total_rows].astype(jnp.bfloat16)
+        other_ref[t] = chunk_ref[(1 - sec) * tps + t].astype(jnp.bfloat16)
         mine_ref[t] = chunk_ref[sec * tps + t]
 
 
@@ -526,24 +503,17 @@
     other, mine, own_x = attention_partial(
         flat, attention_gain, w_query, key_value_weight[:, 0], head_sink_logits, w_output, cache_pairs[:, :, 0], lengths,
         routes.swapaxes(1, 2), gate_weights.swapaxes(1, 2), secs, tps)
-    stay, come = scatter_shards(mine, swap(other, "sec", 1))
-    middle = call(sum_kernel, "sum", shape_of((1, steps * rows, LANES)), stay, come, own_x)
-    middle = jnp.concatenate([middle, swap_by_core(middle, "grp", True)], axis=0)
-    own = jnp.concatenate([middle, swap_by_core(middle, "grp", False)], axis=0)
-    near = swap_by_core(own, "tp", True)
-    own_other = swap(own, "sec", 1)
-    far = swap_by_core(jnp.stack([own, near]), "tp", False)
-    near_other = swap(near, "sec", 1)
-    far_other = swap(far, "sec", 1)
-    pieces = [own, near, far, own_other, near_other, far_other]
+    terms = scatter_shards(mine, swap(other, "sec", 1))
+    middle = call(sum_kernel, "sum", shape_of((steps * rows, LANES)), *terms, own_x)
+    stacked = jnp.stack([middle] + swap_all([middle] * (groups - 1), "grp"))
+    pieces = [stacked] + swap_all([stacked] * (tps - 1), "tp")
+    pieces = pieces + [swap(piece, "sec", 1) for piece in pieces]
     other, mine, own_middle = expert_partial(expert_gain, w_gate[0], w_up[0], w_down[0], pieces, secs, tps)
-    stay, come = scatter_shards(mine, swap(other, "sec", 1))
-    lines, part = steps * rows, stay.shape[1]
-    keep, send = call(divide_rows_kernel, "divide_rows", [shape_of((2, lines, part), jnp.float32), shape_of((2, lines, part))],
-                      stay, come)
-    stay, send = call(after_swap_kernel, "after_swap", [shape_of((lines, part), jnp.float32), shape_of((lines, part))],
-                      keep, swap_by_core(send, "grp", False))
-    return call(sum_kernel, "combine", shape_of((steps, rows, part)), stay, swap_by_core(send, "grp", True), own_middle)
+    terms = scatter_shards(mine, swap(other, "sec", 1))
+    lines, part = steps * rows, terms[0].shape[1]
+    own, *parts = call(functools.partial(divide_rows_kernel, groups=groups), "divide_rows",
+                       [shape_of((lines, part), jnp.float32)] + [shape_of((lines, part))] * (groups - 1), *terms)
+    return call(sum_kernel, "combine", shape_of((steps, rows, part)), own, *swap_all(parts, "grp"), own_middle)
 
 
 def body(*args):

time: 62.9 us -> 52.8 us (0.84)
  waiting for transfers between devices: 35 us -> 23.6 us
  starting transfers between devices: 19.9 us -> 21.2 us
    ppermute x10 -> x0, waiting for transfers between devices: 31.2 us -> none  [swap_by_core(): return lax.ppermute(value, ('sec', axis), pairs)]
    ppermute x5 -> x21, starting transfers between devices: 1.25 us -> 21.2 us  [swap(): return lax.ppermute(value, axes, [(i, i ^ mask) for i in range(size)])]
    ppermute x5 -> x21, waiting for transfers between devices: 3.79 us -> 23.6 us  [swap(): return lax.ppermute(value, axes, [(i, i ^ mask) for i in range(size)])]
    ppermute x10 -> x0, starting transfers between devices: 18.6 us -> none  [swap_by_core(): return lax.ppermute(value, ('sec', axis), pairs)]
  transfers between devices with their start and end apart: 15 -> 21, of which waited for: 14 -> 17; matrix products, arithmetic and copies ran while one was open for 0% -> 0% of each run, Pallas kernels for 0% -> 0%
where the time goes in v4:
time: 52.8 us; the launch traced here: 52.6 us
  waiting for transfers between devices  23.6 us (45%)
  starting transfers between devices  21.2 us (40%)
  Pallas kernels  7.69 us (15%)
    ppermute x21, waiting for transfers between devices, swap(): return lax.ppermute(value, axes, [(i, i ^ mask) for i in range(size)])  23.6 us
    ppermute x21, starting transfers between devices, swap(): return lax.ppermute(value, axes, [(i, i ^ mask) for i in range(size)])  21.2 us
    pallas_call x1, Pallas kernels, attention_partial(): pl.pallas_call(attention_kernel, name='attention', out_shape=[shape_of((t...  4.84 us
    pallas_call x1, Pallas kernels, expert_partial(): pl.pallas_call(expert_kernel, name='expert', out_shape=[shape_of((tps, li...  2.03 us
  transfers between devices with their start and end apart: 21, of which 17 were waited for; matrix products, arithmetic and copies ran while one was open for 0% of the time, Pallas kernels for 0%

profile of v4, /device:TPU:0, one launch (start us, length us, event | category | flops | bytes accessed | tf_op | source)
XLA Modules:
  0.0 52.6 jit_solution(12163381245762873248)
XLA Ops:
  0.0 4.8 %attention.1 = (bf16[4,32,384]{2,1,0:T(8,128)(2,1)S(1)}, f32[4,32,384]{2,1,0:T(8,128)S(1)}, f32[32,384]{1,0:T(8,128)S(1)}) custom-call(s32[16]{0:T(128)} %lengths_hbm.1, f32[8]{0:T(128)} %sinks_hbm.1, s32[2,4,16]{2,1,0:T(4,128)} %bitcast.28, f32[2,4,16]{2,1,0:T(4,128)} %bitcast.29, f32[2880]{0:T(1024)} %gain_hbm.1, bf16[32,2880]{1,0:T(8,128)(2,1)} %bitcast.24, ...), custom_call_target="tpu_custom_call" | custom-call | tf_op jit(solution)/shard_map/attention/pallas_call | solution.py:366
  5.4 0.9 %collective-permute-done.come_ref = bf16[4,32,384]{2,1,0:T(8,128)(2,1)S(1)} collective-permute-done((bf16[4,32,384]{2,1,0:T(8,128)(2,1)S(1)}, bf16[4,32,384]{2,1,0:T(8,128)(2,1)S(1)}, u32[]{:S(2)}, u32[]{:S(2)}) %collective-permute-start) | collective-permute-done | bytes 98336 | tf_op jit(solution)/shard_map/ppermute | solution.py:223
  6.4 2.9 %collective-permute-start.1 = (bf16[32,384]{1,0:T(8,128)(2,1)S(1)}, bf16[32,384]{1,0:T(8,128)(2,1)S(1)}, u32[]{:S(2)}, u32[]{:S(2)}) collective-permute-start(bf16[32,384]{1,0:T(8,128)(2,1)S(1)} %get-tuple-element.26), channel_id=1, source_target_pairs={{0,1},{1,0},{2,3},{3,2},{4,5},{5,4},{6,7},{7,6},{8,9},{9,8},{10,11... | collective-permute-start | bytes 73736 | tf_op jit(solution)/shard_map/ppermute | solution.py:223
  9.3 1.5 %collective-permute-start.2 = (bf16[32,384]{1,0:T(8,128)(2,1)S(1)}, bf16[32,384]{1,0:T(8,128)(2,1)S(1)}, u32[]{:S(2)}, u32[]{:S(2)}) collective-permute-start(bf16[32,384]{1,0:T(8,128)(2,1)S(1)} %get-tuple-element.27), channel_id=1, source_target_pairs={{0,2},{1,3},{2,0},{3,1},{4,6},{5,7},{6,4},{7,5},{8,10},{9,11},{10,... | collective-permute-start | bytes 73736 | tf_op jit(solution)/shard_map/ppermute | solution.py:223
  11.1 2.0 %collective-permute-done.2.refs_2_ = bf16[32,384]{1,0:T(8,128)(2,1)S(1)} collective-permute-done((bf16[32,384]{1,0:T(8,128)(2,1)S(1)}, bf16[32,384]{1,0:T(8,128)(2,1)S(1)}, u32[]{:S(2)}, u32[]{:S(2)}) %collective-permute-start.2) | collective-permute-done | bytes 24608 | tf_op jit(solution)/shard_map/ppermute | solution.py:223
  13.1 2.4 %collective-permute-done.3.refs_3_ = bf16[32,384]{1,0:T(8,128)(2,1)S(1)} collective-permute-done((bf16[32,384]{1,0:T(8,128)(2,1)S(1)}, bf16[32,384]{1,0:T(8,128)(2,1)S(1)}, u32[]{:S(2)}, u32[]{:S(2)}) %collective-permute-start.3) | collective-permute-done | bytes 24608 | tf_op jit(solution)/shard_map/ppermute | solution.py:223
  15.5 3.7 %collective-permute-start.6 = (bf16[32,384]{1,0:T(8,128)(2,1)S(1)}, bf16[32,384]{1,0:T(8,128)(2,1)S(1)}, u32[]{:S(2)}, u32[]{:S(2)}) collective-permute-start(bf16[32,384]{1,0:T(8,128)(2,1)S(1)} %sum.1), channel_id=1, source_target_pairs={{0,12},{4,8},{8,4},{12,0},{1,13},{5,9},{9,5},{13,1},{2,14},{6,10},... | collective-permute-start | bytes 73736 | tf_op jit(solution)/shard_map/ppermute | solution.py:223
  19.2 0.8 %collective-permute-start.4 = (bf16[32,384]{1,0:T(8,128)(2,1)S(1)}, bf16[32,384]{1,0:T(8,128)(2,1)S(1)}, u32[]{:S(2)}, u32[]{:S(2)}) collective-permute-start(bf16[32,384]{1,0:T(8,128)(2,1)S(1)} %sum.1), channel_id=1, source_target_pairs={{0,4},{4,0},{8,12},{12,8},{1,5},{5,1},{9,13},{13,9},{2,6},{6,2},{1... | collective-permute-start | bytes 73736 | tf_op jit(solution)/shard_map/ppermute | solution.py:223
  20.0 1.3 %collective-permute-done.6 = bf16[32,384]{1,0:T(8,128)(2,1)S(1)} collective-permute-done((bf16[32,384]{1,0:T(8,128)(2,1)S(1)}, bf16[32,384]{1,0:T(8,128)(2,1)S(1)}, u32[]{:S(2)}, u32[]{:S(2)}) %collective-permute-start.6) | collective-permute-done | bytes 24608 | tf_op jit(solution)/shard_map/ppermute | solution.py:223
  21.3 2.6 %collective-permute-done.5 = bf16[32,384]{1,0:T(8,128)(2,1)S(1)} collective-permute-done((bf16[32,384]{1,0:T(8,128)(2,1)S(1)}, bf16[32,384]{1,0:T(8,128)(2,1)S(1)}, u32[]{:S(2)}, u32[]{:S(2)}) %collective-permute-start.5) | collective-permute-done | bytes 24608 | tf_op jit(solution)/shard_map/ppermute | solution.py:223
  24.0 0.5 %collective-permute-start.9 = (bf16[4,32,384]{2,1,0:T(8,128)(2,1)S(1)}, bf16[4,32,384]{2,1,0:T(8,128)(2,1)S(1)}, u32[]{:S(2)}, u32[]{:S(2)}) collective-permute-start(bf16[4,32,384]{2,1,0:T(8,128)(2,1)S(1)} %pad_maximum_fusion.refs_0_), channel_id=1, source_target_pairs={{0,3},{1,2},{2,1},{3,0},{4,7},{5,6},{6,5},{7,4},{8,11},{9,10},{10,... | collective-permute-start | bytes 294920 | tf_op jit(solution)/shard_map/ppermute | solution.py:223
  24.5 1.5 %collective-permute-start.8 = (bf16[4,32,384]{2,1,0:T(8,128)(2,1)S(1)}, bf16[4,32,384]{2,1,0:T(8,128)(2,1)S(1)}, u32[]{:S(2)}, u32[]{:S(2)}) collective-permute-start(bf16[4,32,384]{2,1,0:T(8,128)(2,1)S(1)} %pad_maximum_fusion.refs_0_), channel_id=1, source_target_pairs={{0,2},{1,3},{2,0},{3,1},{4,6},{5,7},{6,4},{7,5},{8,10},{9,11},{10,... | collective-permute-start | bytes 294920 | tf_op jit(solution)/shard_map/ppermute | solution.py:223
  26.0 1.5 %collective-permute-start.7 = (bf16[4,32,384]{2,1,0:T(8,128)(2,1)S(1)}, bf16[4,32,384]{2,1,0:T(8,128)(2,1)S(1)}, u32[]{:S(2)}, u32[]{:S(2)}) collective-permute-start(bf16[4,32,384]{2,1,0:T(8,128)(2,1)S(1)} %pad_maximum_fusion.refs_0_), channel_id=1, source_target_pairs={{0,1},{1,0},{2,3},{3,2},{4,5},{5,4},{6,7},{7,6},{8,9},{9,8},{10,11... | collective-permute-start | bytes 294920 | tf_op jit(solution)/shard_map/ppermute | solution.py:223
  27.5 2.1 %collective-permute-done.9.refs_3_ = bf16[4,32,384]{2,1,0:T(8,128)(2,1)S(1)} collective-permute-done((bf16[4,32,384]{2,1,0:T(8,128)(2,1)S(1)}, bf16[4,32,384]{2,1,0:T(8,128)(2,1)S(1)}, u32[]{:S(2)}, u32[]{:S(2)}) %collective-permute-start.9) | collective-permute-done | bytes 98336 | tf_op jit(solution)/shard_map/ppermute | solution.py:223
  32.0 2.0 %expert.1 = (bf16[4,128,360]{2,1,0:T(8,128)(2,1)S(1)}, f32[4,128,360]{2,1,0:T(8,128)S(1)}, f32[32,360]{1,0:T(8,128)S(1)}) custom-call(f32[1,2880]{1,0:T(1,128)S(1)} %reshape.6.gain_ref, bf16[180,2880]{1,0:T(8,128)(2,1)S(1)} %bitcast.17, bf16[180,2880]{1,0:T(8,128)(2,1)S(1)} %bitcast.18, bf16[180,2880]{1,0:T(8,128)(2,1)S(1)} %bitcast.19, ...), custom_call_target="tpu_custom_call" | custom-call | tf_op jit(solution)/shard_map/expert/pallas_call | solution.py:482
  34.2 1.6 %collective-permute-done.14.come_ref = bf16[4,128,360]{2,1,0:T(8,128)(2,1)S(1)} collective-permute-done((bf16[4,128,360]{2,1,0:T(8,128)(2,1)S(1)}, bf16[4,128,360]{2,1,0:T(8,128)(2,1)S(1)}, u32[]{:S(2)}, u32[]{:S(2)}) %collective-permute-start.14) | collective-permute-done | bytes 368672 | tf_op jit(solution)/shard_map/ppermute | solution.py:223
  35.9 1.6 %collective-permute-start.15 = (bf16[128,360]{1,0:T(8,128)(2,1)S(1)}, bf16[128,360]{1,0:T(8,128)(2,1)S(1)}, u32[]{:S(2)}, u32[]{:S(2)}) collective-permute-start(bf16[128,360]{1,0:T(8,128)(2,1)S(1)} %get-tuple-element.33), channel_id=1, source_target_pairs={{0,1},{1,0},{2,3},{3,2},{4,5},{5,4},{6,7},{7,6},{8,9},{9,8},{10,11... | collective-permute-start | bytes 276488 | tf_op jit(solution)/shard_map/ppermute | solution.py:223
  37.9 1.5 %collective-permute-start.17 = (bf16[128,360]{1,0:T(8,128)(2,1)S(1)}, bf16[128,360]{1,0:T(8,128)(2,1)S(1)}, u32[]{:S(2)}, u32[]{:S(2)}) collective-permute-start(bf16[128,360]{1,0:T(8,128)(2,1)S(1)} %get-tuple-element.35), channel_id=1, source_target_pairs={{0,3},{1,2},{2,1},{3,0},{4,7},{5,6},{6,5},{7,4},{8,11},{9,10},{10,... | collective-permute-start | bytes 276488 | tf_op jit(solution)/shard_map/ppermute | solution.py:223
  39.4 1.4 %collective-permute-done.15.refs_1_ = bf16[128,360]{1,0:T(8,128)(2,1)S(1)} collective-permute-done((bf16[128,360]{1,0:T(8,128)(2,1)S(1)}, bf16[128,360]{1,0:T(8,128)(2,1)S(1)}, u32[]{:S(2)}, u32[]{:S(2)}) %collective-permute-start.15) | collective-permute-done | bytes 92192 | tf_op jit(solution)/shard_map/ppermute | solution.py:223
  40.8 3.4 %collective-permute-done.16.refs_2_ = bf16[128,360]{1,0:T(8,128)(2,1)S(1)} collective-permute-done((bf16[128,360]{1,0:T(8,128)(2,1)S(1)}, bf16[128,360]{1,0:T(8,128)(2,1)S(1)}, u32[]{:S(2)}, u32[]{:S(2)}) %collective-permute-start.16) | collective-permute-done | bytes 92192 | tf_op jit(solution)/shard_map/ppermute | solution.py:223
  44.3 2.1 %collective-permute-start.19 = (bf16[32,360]{1,0:T(8,128)(2,1)S(1)}, bf16[32,360]{1,0:T(8,128)(2,1)S(1)}, u32[]{:S(2)}, u32[]{:S(2)}) collective-permute-start(bf16[32,360]{1,0:T(8,128)(2,1)S(1)} %get-tuple-element.38), channel_id=1, source_target_pairs={{0,8},{4,12},{8,0},{12,4},{1,9},{5,13},{9,1},{13,5},{2,10},{6,14},... | collective-permute-start | bytes 69128 | tf_op jit(solution)/shard_map/ppermute | solution.py:223
  46.4 2.3 %collective-permute-start.20 = (bf16[32,360]{1,0:T(8,128)(2,1)S(1)}, bf16[32,360]{1,0:T(8,128)(2,1)S(1)}, u32[]{:S(2)}, u32[]{:S(2)}) collective-permute-start(bf16[32,360]{1,0:T(8,128)(2,1)S(1)} %get-tuple-element.39), channel_id=1, source_target_pairs={{0,12},{4,8},{8,4},{12,0},{1,13},{5,9},{9,5},{13,1},{2,14},{6,10},... | collective-permute-start | bytes 69128 | tf_op jit(solution)/shard_map/ppermute | solution.py:223
  49.1 2.9 %collective-permute-done.20.refs_3_ = bf16[32,360]{1,0:T(8,128)(2,1)S(1)} collective-permute-done((bf16[32,360]{1,0:T(8,128)(2,1)S(1)}, bf16[32,360]{1,0:T(8,128)(2,1)S(1)}, u32[]{:S(2)}, u32[]{:S(2)}) %collective-permute-start.20) | collective-permute-done | bytes 23072 | tf_op jit(solution)/shard_map/ppermute | solution.py:223
  52.0 0.6 %combine.1 = bf16[2,16,360]{2,1,0:T(8,128)(2,1)} custom-call(f32[32,360]{1,0:T(8,128)S(1)} %get-tuple-element.36.refs_0_, bf16[32,360]{1,0:T(8,128)(2,1)S(1)} %collective-permute-done.18.refs_1_, bf16[32,360]{1,0:T(8,128)(2,1)S(1)} %collective-permute-done.19.refs_2_, bf16[32,360]{1,0:T(8,128)(2,1)S(1)} %collective-permute-done.20.refs_3_, ...), custom_call_target="tpu_custom_call" | custom-call | tf_op jit(solution)/shard_map/combine/pallas_call | solution.py:396
  (35 shorter events, 4.5 us)
Async XLA Ops:
  0.0 32.0 %copy-start = (bf16[1,2880,180]{1,2,0:T(8,128)(2,1)S(1)}, bf16[1,2880,180]{1,2,0:T(8,128)(2,1)}, u32[]{:S(2)}) copy-start(bf16[1,2880,180]{1,2,0:T(8,128)(2,1)} %param.23) | copy-start | bytes 3110404
  0.0 32.0 %copy-start.1 = (bf16[1,2880,180]{1,2,0:T(8,128)(2,1)S(1)}, bf16[1,2880,180]{1,2,0:T(8,128)(2,1)}, u32[]{:S(2)}) copy-start(bf16[1,2880,180]{1,2,0:T(8,128)(2,1)} %param.24) | copy-start | bytes 3110404
  0.0 32.0 %copy-start.2 = (bf16[1,180,2880]{2,1,0:T(8,128)(2,1)S(1)}, bf16[1,180,2880]{2,1,0:T(8,128)(2,1)}, u32[]{:S(2)}) copy-start(bf16[1,180,2880]{2,1,0:T(8,128)(2,1)} %param.25) | copy-start | bytes 3110404
  4.9 1.5 %collective-permute-start = (bf16[4,32,384]{2,1,0:T(8,128)(2,1)S(1)}, bf16[4,32,384]{2,1,0:T(8,128)(2,1)S(1)}, u32[]{:S(2)}, u32[]{:S(2)}) collective-permute-start(bf16[4,32,384]{2,1,0:T(8,128)(2,1)S(1)} %get-tuple-element.24), channel_id=1, source_target_pairs={{0,16},{16,0},{1,17},{17,1},{2,18},{18,2},{3,19},{19,3},{4,20},{20... | collective-permute-start | bytes 294920 | tf_op jit(solution)/shard_map/ppermute | solution.py:223
  6.4 4.7 %collective-permute-start.1 = (bf16[32,384]{1,0:T(8,128)(2,1)S(1)}, bf16[32,384]{1,0:T(8,128)(2,1)S(1)}, u32[]{:S(2)}, u32[]{:S(2)}) collective-permute-start(bf16[32,384]{1,0:T(8,128)(2,1)S(1)} %get-tuple-element.26), channel_id=1, source_target_pairs={{0,1},{1,0},{2,3},{3,2},{4,5},{5,4},{6,7},{7,6},{8,9},{9,8},{10,11... | collective-permute-start | bytes 73736 | tf_op jit(solution)/shard_map/ppermute | solution.py:223
  9.3 3.8 %collective-permute-start.2 = (bf16[32,384]{1,0:T(8,128)(2,1)S(1)}, bf16[32,384]{1,0:T(8,128)(2,1)S(1)}, u32[]{:S(2)}, u32[]{:S(2)}) collective-permute-start(bf16[32,384]{1,0:T(8,128)(2,1)S(1)} %get-tuple-element.27), channel_id=1, source_target_pairs={{0,2},{1,3},{2,0},{3,1},{4,6},{5,7},{6,4},{7,5},{8,10},{9,11},{10,... | collective-permute-start | bytes 73736 | tf_op jit(solution)/shard_map/ppermute | solution.py:223
  10.8 4.7 %collective-permute-start.3 = (bf16[32,384]{1,0:T(8,128)(2,1)S(1)}, bf16[32,384]{1,0:T(8,128)(2,1)S(1)}, u32[]{:S(2)}, u32[]{:S(2)}) collective-permute-start(bf16[32,384]{1,0:T(8,128)(2,1)S(1)} %get-tuple-element.28), channel_id=1, source_target_pairs={{0,3},{1,2},{2,1},{3,0},{4,7},{5,6},{6,5},{7,4},{8,11},{9,10},{10,... | collective-permute-start | bytes 73736 | tf_op jit(solution)/shard_map/ppermute | solution.py:223
  15.5 5.8 %collective-permute-start.6 = (bf16[32,384]{1,0:T(8,128)(2,1)S(1)}, bf16[32,384]{1,0:T(8,128)(2,1)S(1)}, u32[]{:S(2)}, u32[]{:S(2)}) collective-permute-start(bf16[32,384]{1,0:T(8,128)(2,1)S(1)} %sum.1), channel_id=1, source_target_pairs={{0,12},{4,8},{8,4},{12,0},{1,13},{5,9},{9,5},{13,1},{2,14},{6,10},... | collective-permute-start | bytes 73736 | tf_op jit(solution)/shard_map/ppermute | solution.py:223
  19.2 4.7 %collective-permute-start.5 = (bf16[32,384]{1,0:T(8,128)(2,1)S(1)}, bf16[32,384]{1,0:T(8,128)(2,1)S(1)}, u32[]{:S(2)}, u32[]{:S(2)}) collective-permute-start(bf16[32,384]{1,0:T(8,128)(2,1)S(1)} %sum.1), channel_id=1, source_target_pairs={{0,8},{4,12},{8,0},{12,4},{1,9},{5,13},{9,1},{13,5},{2,10},{6,14},... | collective-permute-start | bytes 73736 | tf_op jit(solution)/shard_map/ppermute | solution.py:223
  19.2 4.7 %collective-permute-start.4 = (bf16[32,384]{1,0:T(8,128)(2,1)S(1)}, bf16[32,384]{1,0:T(8,128)(2,1)S(1)}, u32[]{:S(2)}, u32[]{:S(2)}) collective-permute-start(bf16[32,384]{1,0:T(8,128)(2,1)S(1)} %sum.1), channel_id=1, source_target_pairs={{0,4},{4,0},{8,12},{12,8},{1,5},{5,1},{9,13},{13,9},{2,6},{6,2},{1... | collective-permute-start | bytes 73736 | tf_op jit(solution)/shard_map/ppermute | solution.py:223
  24.0 5.7 %collective-permute-start.9 = (bf16[4,32,384]{2,1,0:T(8,128)(2,1)S(1)}, bf16[4,32,384]{2,1,0:T(8,128)(2,1)S(1)}, u32[]{:S(2)}, u32[]{:S(2)}) collective-permute-start(bf16[4,32,384]{2,1,0:T(8,128)(2,1)S(1)} %pad_maximum_fusion.refs_0_), channel_id=1, source_target_pairs={{0,3},{1,2},{2,1},{3,0},{4,7},{5,6},{6,5},{7,4},{8,11},{9,10},{10,... | collective-permute-start | bytes 294920 | tf_op jit(solution)/shard_map/ppermute | solution.py:223
  24.5 5.7 %collective-permute-start.8 = (bf16[4,32,384]{2,1,0:T(8,128)(2,1)S(1)}, bf16[4,32,384]{2,1,0:T(8,128)(2,1)S(1)}, u32[]{:S(2)}, u32[]{:S(2)}) collective-permute-start(bf16[4,32,384]{2,1,0:T(8,128)(2,1)S(1)} %pad_maximum_fusion.refs_0_), channel_id=1, source_target_pairs={{0,2},{1,3},{2,0},{3,1},{4,6},{5,7},{6,4},{7,5},{8,10},{9,11},{10,... | collective-permute-start | bytes 294920 | tf_op jit(solution)/shard_map/ppermute | solution.py:223
  26.0 4.6 %collective-permute-start.7 = (bf16[4,32,384]{2,1,0:T(8,128)(2,1)S(1)}, bf16[4,32,384]{2,1,0:T(8,128)(2,1)S(1)}, u32[]{:S(2)}, u32[]{:S(2)}) collective-permute-start(bf16[4,32,384]{2,1,0:T(8,128)(2,1)S(1)} %pad_maximum_fusion.refs_0_), channel_id=1, source_target_pairs={{0,1},{1,0},{2,3},{3,2},{4,5},{5,4},{6,7},{7,6},{8,9},{9,8},{10,11... | collective-permute-start | bytes 294920 | tf_op jit(solution)/shard_map/ppermute | solution.py:223
  27.5 3.2 %collective-permute-start.10 = (bf16[4,32,384]{2,1,0:T(8,128)(2,1)S(1)}, bf16[4,32,384]{2,1,0:T(8,128)(2,1)S(1)}, u32[]{:S(2)}, u32[]{:S(2)}) collective-permute-start(bf16[4,32,384]{2,1,0:T(8,128)(2,1)S(1)} %pad_maximum_fusion.refs_0_), channel_id=1, source_target_pairs={{0,16},{16,0},{1,17},{17,1},{2,18},{18,2},{3,19},{19,3},{4,20},{20... | collective-permute-start | bytes 294920 | tf_op jit(solution)/shard_map/ppermute | solution.py:223
  29.7 1.3 %collective-permute-start.13 = (bf16[4,32,384]{2,1,0:T(8,128)(2,1)S(1)}, bf16[4,32,384]{2,1,0:T(8,128)(2,1)S(1)}, u32[]{:S(2)}, u32[]{:S(2)}) collective-permute-start(bf16[4,32,384]{2,1,0:T(8,128)(2,1)S(1)} %collective-permute-done.9.refs_3_), channel_id=1, source_target_pairs={{0,16},{16,0},{1,17},{17,1},{2,18},{18,2},{3,19},{19,3},{4,20},{20... | collective-permute-start | bytes 294920 | tf_op jit(solution)/shard_map/ppermute | solution.py:223
  30.2 1.3 %collective-permute-start.12 = (bf16[4,32,384]{2,1,0:T(8,128)(2,1)S(1)}, bf16[4,32,384]{2,1,0:T(8,128)(2,1)S(1)}, u32[]{:S(2)}, u32[]{:S(2)}) collective-permute-start(bf16[4,32,384]{2,1,0:T(8,128)(2,1)S(1)} %collective-permute-done.8.refs_2_), channel_id=1, source_target_pairs={{0,16},{16,0},{1,17},{17,1},{2,18},{18,2},{3,19},{19,3},{4,20},{20... | collective-permute-start | bytes 294920 | tf_op jit(solution)/shard_map/ppermute | solution.py:223
  30.6 1.3 %collective-permute-start.11 = (bf16[4,32,384]{2,1,0:T(8,128)(2,1)S(1)}, bf16[4,32,384]{2,1,0:T(8,128)(2,1)S(1)}, u32[]{:S(2)}, u32[]{:S(2)}) collective-permute-start(bf16[4,32,384]{2,1,0:T(8,128)(2,1)S(1)} %collective-permute-done.7.refs_1_), channel_id=1, source_target_pairs={{0,16},{16,0},{1,17},{17,1},{2,18},{18,2},{3,19},{19,3},{4,20},{20... | collective-permute-start | bytes 294920 | tf_op jit(solution)/shard_map/ppermute | solution.py:223
  34.0 1.8 %collective-permute-start.14 = (bf16[4,128,360]{2,1,0:T(8,128)(2,1)S(1)}, bf16[4,128,360]{2,1,0:T(8,128)(2,1)S(1)}, u32[]{:S(2)}, u32[]{:S(2)}) collective-permute-start(bf16[4,128,360]{2,1,0:T(8,128)(2,1)S(1)} %get-tuple-element.31), channel_id=1, source_target_pairs={{0,16},{16,0},{1,17},{17,1},{2,18},{18,2},{3,19},{19,3},{4,20},{20... | collective-permute-start | bytes 1105928 | tf_op jit(solution)/shard_map/ppermute | solution.py:223
  35.9 4.9 %collective-permute-start.15 = (bf16[128,360]{1,0:T(8,128)(2,1)S(1)}, bf16[128,360]{1,0:T(8,128)(2,1)S(1)}, u32[]{:S(2)}, u32[]{:S(2)}) collective-permute-start(bf16[128,360]{1,0:T(8,128)(2,1)S(1)} %get-tuple-element.33), channel_id=1, source_target_pairs={{0,1},{1,0},{2,3},{3,2},{4,5},{5,4},{6,7},{7,6},{8,9},{9,8},{10,11... | collective-permute-start | bytes 276488 | tf_op jit(solution)/shard_map/ppermute | solution.py:223
  37.4 6.7 %collective-permute-start.16 = (bf16[128,360]{1,0:T(8,128)(2,1)S(1)}, bf16[128,360]{1,0:T(8,128)(2,1)S(1)}, u32[]{:S(2)}, u32[]{:S(2)}) collective-permute-start(bf16[128,360]{1,0:T(8,128)(2,1)S(1)} %get-tuple-element.34), channel_id=1, source_target_pairs={{0,2},{1,3},{2,0},{3,1},{4,6},{5,7},{6,4},{7,5},{8,10},{9,11},{10,... | collective-permute-start | bytes 276488 | tf_op jit(solution)/shard_map/ppermute | solution.py:223
  37.9 6.2 %collective-permute-start.17 = (bf16[128,360]{1,0:T(8,128)(2,1)S(1)}, bf16[128,360]{1,0:T(8,128)(2,1)S(1)}, u32[]{:S(2)}, u32[]{:S(2)}) collective-permute-start(bf16[128,360]{1,0:T(8,128)(2,1)S(1)} %get-tuple-element.35), channel_id=1, source_target_pairs={{0,3},{1,2},{2,1},{3,0},{4,7},{5,6},{6,5},{7,4},{8,11},{9,10},{10,... | collective-permute-start | bytes 276488 | tf_op jit(solution)/shard_map/ppermute | solution.py:223
  44.2 4.5 %collective-permute-start.18 = (bf16[32,360]{1,0:T(8,128)(2,1)S(1)}, bf16[32,360]{1,0:T(8,128)(2,1)S(1)}, u32[]{:S(2)}, u32[]{:S(2)}) collective-permute-start(bf16[32,360]{1,0:T(8,128)(2,1)S(1)} %get-tuple-element.37), channel_id=1, source_target_pairs={{0,4},{4,0},{8,12},{12,8},{1,5},{5,1},{9,13},{13,9},{2,6},{6,2},{1... | collective-permute-start | bytes 69128 | tf_op jit(solution)/shard_map/ppermute | solution.py:223
  44.3 4.8 %collective-permute-start.19 = (bf16[32,360]{1,0:T(8,128)(2,1)S(1)}, bf16[32,360]{1,0:T(8,128)(2,1)S(1)}, u32[]{:S(2)}, u32[]{:S(2)}) collective-permute-start(bf16[32,360]{1,0:T(8,128)(2,1)S(1)} %get-tuple-element.38), channel_id=1, source_target_pairs={{0,8},{4,12},{8,0},{12,4},{1,9},{5,13},{9,1},{13,5},{2,10},{6,14},... | collective-permute-start | bytes 69128 | tf_op jit(solution)/shard_map/ppermute | solution.py:223
  46.4 5.6 %collective-permute-start.20 = (bf16[32,360]{1,0:T(8,128)(2,1)S(1)}, bf16[32,360]{1,0:T(8,128)(2,1)S(1)}, u32[]{:S(2)}, u32[]{:S(2)}) collective-permute-start(bf16[32,360]{1,0:T(8,128)(2,1)S(1)} %get-tuple-element.39), channel_id=1, source_target_pairs={{0,12},{4,8},{8,4},{12,0},{1,13},{5,9},{9,5},{13,1},{2,14},{6,10},... | collective-permute-start | bytes 69128 | tf_op jit(solution)/shard_map/ppermute | solution.py:223
  (1 other events, 30.7 us)

commit v5 on v4

--- a/solution.py
+++ b/solution.py
@@ -229,16 +229,16 @@
 
 
 def attention_kernel(lengths_hbm, sinks_hbm, routes_hbm, weights_hbm, gain_hbm, x_hbm, wq_hbm, wkv_hbm, cache_hbm, wo_hbm,
-                     other_ref, mine_ref, own_x_ref,
+                     parts_ref, own_x_ref,
                      lengths_ref, sinks_ref, routes_ref, weights_ref, gain_ref, x_ref, wq_ref, wkv_ref, cache_ref, wo_ref,
-                     xs_ref, turned_ref, mixed_ref, chunk_ref, sems):
+                     xs_ref, turned_ref, mixed_ref, sems):
     total_rows, width = x_ref.shape
     rows, slots, pair = cache_ref.shape
     steps = total_rows // rows
     heads = wq_ref.shape[1] // HEAD_SIZE
     per_row = heads * steps
-    tps = mine_ref.shape[0]
-    secs = chunk_ref.shape[0] // tps
+    shards = parts_ref.shape[0]
+    tps = lax.axis_size("tp")
     cuts = split_width(width)
     small = [(lengths_hbm, lengths_ref), (x_hbm, x_ref), (gain_hbm, gain_ref), (routes_hbm, routes_ref), (weights_hbm, weights_ref),
              (sinks_hbm, sinks_ref)]
@@ -345,16 +345,12 @@
     ).astype(jnp.bfloat16)
     copies[-1].wait()
     partial = dot_last(mix, wo_ref[...])
-    for c in range(secs * tps):
+    for c in range(shards):
         low, high = c * LANES, min((c + 1) * LANES, width)
         piece = partial[:, low:high]
         if high - low < LANES:
             piece = jnp.concatenate([piece, jnp.zeros((total_rows, LANES - (high - low)), jnp.float32)], axis=1)
-        chunk_ref[c] = piece
-    sec = lax.axis_index("sec")
-    for t in range(tps):
-        other_ref[t] = chunk_ref[(1 - sec) * tps + t].astype(jnp.bfloat16)
-        mine_ref[t] = chunk_ref[sec * tps + t]
+        parts_ref[c] = piece.astype(jnp.bfloat16)
 
 
 def attention_partial(flat, gain, w_query, key_value, sinks, w_output, cache, lengths, routes, weights, secs, tps):
@@ -366,10 +362,9 @@
     return pl.pallas_call(
         attention_kernel,
         name="attention",
-        out_shape=[shape_of((tps, total_rows, LANES)), shape_of((tps, total_rows, LANES), jnp.float32),
-                   shape_of((total_rows, LANES), jnp.float32)],
+        out_shape=[shape_of((shards, total_rows, LANES)), shape_of((total_rows, LANES), jnp.float32)],
         in_specs=[outside()] * len(operands),
-        out_specs=[vmem()] * 3,
+        out_specs=[vmem()] * 2,
         scratch_shapes=[
             pltpu.SMEM(lengths.shape, jnp.int32),
             pltpu.SMEM(sinks.shape, jnp.float32),
@@ -384,7 +379,6 @@
             pltpu.VMEM((total_rows, shards * LANES), jnp.float32),
             pltpu.VMEM((rows * per_row, pair), jnp.float32),
             pltpu.VMEM((rows * per_row, pair), jnp.float32),
-            pltpu.VMEM((shards, total_rows, LANES), jnp.float32),
             pltpu.SemaphoreType.DMA((9 + len(split_width(width)),)),
         ],
         compiler_params=pltpu.CompilerParams(vmem_limit_bytes=24 * MIB),
@@ -416,6 +410,13 @@
     for ref in refs[1:]:
         total = total + ref[...].astype(jnp.float32)
     return total
+
+
+def sum_parts_kernel(parts_ref, own_ref, out_ref):
+    total = own_ref[...]
+    for n in range(parts_ref.shape[0]):
+        total = total + parts_ref[n].astype(jnp.float32)
+    out_ref[...] = total.astype(jnp.bfloat16)
 
 
 def sum_kernel(*refs):
@@ -500,11 +501,11 @@
     secs, tps, groups = lax.axis_size("sec"), lax.axis_size("tp"), lax.axis_size("grp")
     steps, rows, width = inputs.shape
     flat = inputs.reshape(steps * rows, width)
-    other, mine, own_x = attention_partial(
+    parts, own_x = attention_partial(
         flat, attention_gain, w_query, key_value_weight[:, 0], head_sink_logits, w_output, cache_pairs[:, :, 0], lengths,
         routes.swapaxes(1, 2), gate_weights.swapaxes(1, 2), secs, tps)
-    terms = scatter_shards(mine, swap(other, "sec", 1))
-    middle = call(sum_kernel, "sum", shape_of((steps * rows, LANES)), *terms, own_x)
+    parts = lax.all_to_all(parts, ("sec", "tp"), 0, 0, tiled=True)
+    middle = call(sum_parts_kernel, "sum_parts", shape_of((steps * rows, LANES)), parts, own_x)
     stacked = jnp.stack([middle] + swap_all([middle] * (groups - 1), "grp"))
     pieces = [stacked] + swap_all([stacked] * (tps - 1), "tp")
     pieces = pieces + [swap(piece, "sec", 1) for piece in pieces]

time: 52.8 us -> 53.1 us (level)
  blocking collectives: 0 us -> 11 us
  waiting for transfers between devices: 23.6 us -> 17.8 us
  starting transfers between devices: 21.2 us -> 16.4 us
    all_to_all x0 -> x1, blocking collectives: none -> 11 us  [every_expert_body(): parts = lax.all_to_all(parts, ('sec', 'tp'), 0, 0, tiled=True)]
    ppermute x21 -> x17, waiting for transfers between devices: 23.6 us -> 17.8 us  [swap(): return lax.ppermute(value, axes, [(i, i ^ mask) for i in range(size)])]
    ppermute x21 -> x17, starting transfers between devices: 21.2 us -> 16.4 us  [swap(): return lax.ppermute(value, axes, [(i, i ^ mask) for i in range(size)])]
  transfers between devices with their start and end apart: 21 -> 17, of which waited for: 17 -> 12; matrix products, arithmetic and copies ran while one was open for 0% -> 0% of each run, Pallas kernels for 0% -> 0%
where the time goes in v5:
time: 53.1 us; the launch traced here: 52.9 us
  waiting for transfers between devices  17.8 us (34%)
  starting transfers between devices  16.4 us (31%)
  blocking collectives  11 us (21%)
  Pallas kernels  7.65 us (14%)
    ppermute x17, waiting for transfers between devices, swap(): return lax.ppermute(value, axes, [(i, i ^ mask) for i in range(size)])  17.8 us
    ppermute x17, starting transfers between devices, swap(): return lax.ppermute(value, axes, [(i, i ^ mask) for i in range(size)])  16.4 us
    all_to_all x1, blocking collectives, every_expert_body(): parts = lax.all_to_all(parts, ('sec', 'tp'), 0, 0, tiled=True)  11 us
    pallas_call x1, Pallas kernels, attention_partial(): pl.pallas_call(attention_kernel, name='attention', out_shape=[shape_of((s...  4.82 us
    pallas_call x1, Pallas kernels, expert_partial(): pl.pallas_call(expert_kernel, name='expert', out_shape=[shape_of((tps, li...  2.02 us
  transfers between devices with their start and end apart: 17, of which 12 were waited for; matrix products, arithmetic and copies ran while one was open for 0% of the time, Pallas kernels for 0%

profile of v5, /device:TPU:0, one launch (start us, length us, event | category | flops | bytes accessed | tf_op | source)
XLA Modules:
  0.0 52.9 jit_solution(7737209957784929478)
XLA Ops:
  0.0 4.8 %attention.1 = (bf16[8,32,384]{2,1,0:T(8,128)(2,1)S(1)}, f32[32,384]{1,0:T(8,128)S(1)}) custom-call(s32[16]{0:T(128)} %lengths_hbm.1, f32[8]{0:T(128)} %sinks_hbm.1, s32[2,4,16]{2,1,0:T(4,128)} %bitcast.28, f32[2,4,16]{2,1,0:T(4,128)} %bitcast.29, f32[2880]{0:T(1024)} %gain_hbm.1, bf16[32,2880]{1,0:T(8,128)(2,1)} %bitcast.24, bf16[2880,512]{1,0:T(8,128)(2,1)} %wq_hbm.1, ...), custom_call_target="tpu_custom_call" | custom-call | tf_op jit(solution)/shard_map/attention/pallas_call | solution.py:362
  4.8 11.0 %all_to_all.5.parts_ref = bf16[8,32,384]{2,1,0:T(8,128)(2,1)S(1)} all-to-all(bf16[8,32,384]{2,1,0:T(8,128)(2,1)S(1)} %get-tuple-element.18), channel_id=1, replica_groups=mesh['sec'=2,'grp'=4,'tp'=4] {'sec','tp'}, dimensions={0} | all-to-all | bytes 393216 | tf_op jit(solution)/shard_map/all_to_all | solution.py:507
  15.8 3.7 %collective-permute-start.2 = (bf16[32,384]{1,0:T(8,128)(2,1)S(1)}, bf16[32,384]{1,0:T(8,128)(2,1)S(1)}, u32[]{:S(2)}, u32[]{:S(2)}) collective-permute-start(bf16[32,384]{1,0:T(8,128)(2,1)S(1)} %sum_parts.1), channel_id=1, source_target_pairs={{0,12},{4,8},{8,4},{12,0},{1,13},{5,9},{9,5},{13,1},{2,14},{6,10},... | collective-permute-start | bytes 73736 | tf_op jit(solution)/shard_map/ppermute | solution.py:223
  19.5 0.8 %collective-permute-start = (bf16[32,384]{1,0:T(8,128)(2,1)S(1)}, bf16[32,384]{1,0:T(8,128)(2,1)S(1)}, u32[]{:S(2)}, u32[]{:S(2)}) collective-permute-start(bf16[32,384]{1,0:T(8,128)(2,1)S(1)} %sum_parts.1), channel_id=1, source_target_pairs={{0,4},{4,0},{8,12},{12,8},{1,5},{5,1},{9,13},{13,9},{2,6},{6,2},{1... | collective-permute-start | bytes 73736 | tf_op jit(solution)/shard_map/ppermute | solution.py:223
  20.3 1.2 %collective-permute-done.2 = bf16[32,384]{1,0:T(8,128)(2,1)S(1)} collective-permute-done((bf16[32,384]{1,0:T(8,128)(2,1)S(1)}, bf16[32,384]{1,0:T(8,128)(2,1)S(1)}, u32[]{:S(2)}, u32[]{:S(2)}) %collective-permute-start.2) | collective-permute-done | bytes 24608 | tf_op jit(solution)/shard_map/ppermute | solution.py:223
  21.5 2.7 %collective-permute-done.1 = bf16[32,384]{1,0:T(8,128)(2,1)S(1)} collective-permute-done((bf16[32,384]{1,0:T(8,128)(2,1)S(1)}, bf16[32,384]{1,0:T(8,128)(2,1)S(1)}, u32[]{:S(2)}, u32[]{:S(2)}) %collective-permute-start.1) | collective-permute-done | bytes 24608 | tf_op jit(solution)/shard_map/ppermute | solution.py:223
  24.2 0.9 %collective-permute-start.5 = (bf16[4,32,384]{2,1,0:T(8,128)(2,1)S(1)}, bf16[4,32,384]{2,1,0:T(8,128)(2,1)S(1)}, u32[]{:S(2)}, u32[]{:S(2)}) collective-permute-start(bf16[4,32,384]{2,1,0:T(8,128)(2,1)S(1)} %pad_maximum_fusion.refs_0_), channel_id=1, source_target_pairs={{0,3},{1,2},{2,1},{3,0},{4,7},{5,6},{6,5},{7,4},{8,11},{9,10},{10,... | collective-permute-start | bytes 294920 | tf_op jit(solution)/shard_map/ppermute | solution.py:223
  25.1 1.4 %collective-permute-start.4 = (bf16[4,32,384]{2,1,0:T(8,128)(2,1)S(1)}, bf16[4,32,384]{2,1,0:T(8,128)(2,1)S(1)}, u32[]{:S(2)}, u32[]{:S(2)}) collective-permute-start(bf16[4,32,384]{2,1,0:T(8,128)(2,1)S(1)} %pad_maximum_fusion.refs_0_), channel_id=1, source_target_pairs={{0,2},{1,3},{2,0},{3,1},{4,6},{5,7},{6,4},{7,5},{8,10},{9,11},{10,... | collective-permute-start | bytes 294920 | tf_op jit(solution)/shard_map/ppermute | solution.py:223
  26.6 1.2 %collective-permute-start.3 = (bf16[4,32,384]{2,1,0:T(8,128)(2,1)S(1)}, bf16[4,32,384]{2,1,0:T(8,128)(2,1)S(1)}, u32[]{:S(2)}, u32[]{:S(2)}) collective-permute-start(bf16[4,32,384]{2,1,0:T(8,128)(2,1)S(1)} %pad_maximum_fusion.refs_0_), channel_id=1, source_target_pairs={{0,1},{1,0},{2,3},{3,2},{4,5},{5,4},{6,7},{7,6},{8,9},{9,8},{10,11... | collective-permute-start | bytes 294920 | tf_op jit(solution)/shard_map/ppermute | solution.py:223
  27.8 2.3 %collective-permute-done.5.refs_3_ = bf16[4,32,384]{2,1,0:T(8,128)(2,1)S(1)} collective-permute-done((bf16[4,32,384]{2,1,0:T(8,128)(2,1)S(1)}, bf16[4,32,384]{2,1,0:T(8,128)(2,1)S(1)}, u32[]{:S(2)}, u32[]{:S(2)}) %collective-permute-start.5) | collective-permute-done | bytes 98336 | tf_op jit(solution)/shard_map/ppermute | solution.py:223
  30.1 0.7 %collective-permute-done.4.refs_2_ = bf16[4,32,384]{2,1,0:T(8,128)(2,1)S(1)} collective-permute-done((bf16[4,32,384]{2,1,0:T(8,128)(2,1)S(1)}, bf16[4,32,384]{2,1,0:T(8,128)(2,1)S(1)}, u32[]{:S(2)}, u32[]{:S(2)}) %collective-permute-start.4) | collective-permute-done | bytes 98336 | tf_op jit(solution)/shard_map/ppermute | solution.py:223
  31.4 0.7 %collective-permute-done.8.refs_6_ = bf16[4,32,384]{2,1,0:T(8,128)(2,1)S(1)} collective-permute-done((bf16[4,32,384]{2,1,0:T(8,128)(2,1)S(1)}, bf16[4,32,384]{2,1,0:T(8,128)(2,1)S(1)}, u32[]{:S(2)}, u32[]{:S(2)}) %collective-permute-start.8) | collective-permute-done | bytes 98336 | tf_op jit(solution)/shard_map/ppermute | solution.py:223
  32.5 2.0 %expert.1 = (bf16[4,128,360]{2,1,0:T(8,128)(2,1)S(1)}, f32[4,128,360]{2,1,0:T(8,128)S(1)}, f32[32,360]{1,0:T(8,128)S(1)}) custom-call(f32[1,2880]{1,0:T(1,128)S(1)} %reshape.6.gain_ref, bf16[180,2880]{1,0:T(8,128)(2,1)S(1)} %bitcast.17, bf16[180,2880]{1,0:T(8,128)(2,1)S(1)} %bitcast.18, bf16[180,2880]{1,0:T(8,128)(2,1)S(1)} %bitcast.19, ...), custom_call_target="tpu_custom_call" | custom-call | tf_op jit(solution)/shard_map/expert/pallas_call | solution.py:483
  34.7 1.5 %collective-permute-done.10.come_ref = bf16[4,128,360]{2,1,0:T(8,128)(2,1)S(1)} collective-permute-done((bf16[4,128,360]{2,1,0:T(8,128)(2,1)S(1)}, bf16[4,128,360]{2,1,0:T(8,128)(2,1)S(1)}, u32[]{:S(2)}, u32[]{:S(2)}) %collective-permute-start.10) | collective-permute-done | bytes 368672 | tf_op jit(solution)/shard_map/ppermute | solution.py:223
  36.4 1.3 %collective-permute-start.11 = (bf16[128,360]{1,0:T(8,128)(2,1)S(1)}, bf16[128,360]{1,0:T(8,128)(2,1)S(1)}, u32[]{:S(2)}, u32[]{:S(2)}) collective-permute-start(bf16[128,360]{1,0:T(8,128)(2,1)S(1)} %get-tuple-element.23), channel_id=1, source_target_pairs={{0,1},{1,0},{2,3},{3,2},{4,5},{5,4},{6,7},{7,6},{8,9},{9,8},{10,11... | collective-permute-start | bytes 276488 | tf_op jit(solution)/shard_map/ppermute | solution.py:223
  37.7 0.8 %collective-permute-start.12 = (bf16[128,360]{1,0:T(8,128)(2,1)S(1)}, bf16[128,360]{1,0:T(8,128)(2,1)S(1)}, u32[]{:S(2)}, u32[]{:S(2)}) collective-permute-start(bf16[128,360]{1,0:T(8,128)(2,1)S(1)} %get-tuple-element.24), channel_id=1, source_target_pairs={{0,2},{1,3},{2,0},{3,1},{4,6},{5,7},{6,4},{7,5},{8,10},{9,11},{10,... | collective-permute-start | bytes 276488 | tf_op jit(solution)/shard_map/ppermute | solution.py:223
  38.5 1.4 %collective-permute-start.13 = (bf16[128,360]{1,0:T(8,128)(2,1)S(1)}, bf16[128,360]{1,0:T(8,128)(2,1)S(1)}, u32[]{:S(2)}, u32[]{:S(2)}) collective-permute-start(bf16[128,360]{1,0:T(8,128)(2,1)S(1)} %get-tuple-element.25), channel_id=1, source_target_pairs={{0,3},{1,2},{2,1},{3,0},{4,7},{5,6},{6,5},{7,4},{8,11},{9,10},{10,... | collective-permute-start | bytes 276488 | tf_op jit(solution)/shard_map/ppermute | solution.py:223
  39.9 1.4 %collective-permute-done.11.refs_1_ = bf16[128,360]{1,0:T(8,128)(2,1)S(1)} collective-permute-done((bf16[128,360]{1,0:T(8,128)(2,1)S(1)}, bf16[128,360]{1,0:T(8,128)(2,1)S(1)}, u32[]{:S(2)}, u32[]{:S(2)}) %collective-permute-start.11) | collective-permute-done | bytes 92192 | tf_op jit(solution)/shard_map/ppermute | solution.py:223
  41.3 3.1 %collective-permute-done.12.refs_2_ = bf16[128,360]{1,0:T(8,128)(2,1)S(1)} collective-permute-done((bf16[128,360]{1,0:T(8,128)(2,1)S(1)}, bf16[128,360]{1,0:T(8,128)(2,1)S(1)}, u32[]{:S(2)}, u32[]{:S(2)}) %collective-permute-start.12) | collective-permute-done | bytes 92192 | tf_op jit(solution)/shard_map/ppermute | solution.py:223
  44.6 2.1 %collective-permute-start.15 = (bf16[32,360]{1,0:T(8,128)(2,1)S(1)}, bf16[32,360]{1,0:T(8,128)(2,1)S(1)}, u32[]{:S(2)}, u32[]{:S(2)}) collective-permute-start(bf16[32,360]{1,0:T(8,128)(2,1)S(1)} %get-tuple-element.28), channel_id=1, source_target_pairs={{0,8},{4,12},{8,0},{12,4},{1,9},{5,13},{9,1},{13,5},{2,10},{6,14},... | collective-permute-start | bytes 69128 | tf_op jit(solution)/shard_map/ppermute | solution.py:223
  46.7 2.3 %collective-permute-start.16 = (bf16[32,360]{1,0:T(8,128)(2,1)S(1)}, bf16[32,360]{1,0:T(8,128)(2,1)S(1)}, u32[]{:S(2)}, u32[]{:S(2)}) collective-permute-start(bf16[32,360]{1,0:T(8,128)(2,1)S(1)} %get-tuple-element.29), channel_id=1, source_target_pairs={{0,12},{4,8},{8,4},{12,0},{1,13},{5,9},{9,5},{13,1},{2,14},{6,10},... | collective-permute-start | bytes 69128 | tf_op jit(solution)/shard_map/ppermute | solution.py:223
  49.0 0.5 %collective-permute-done.15.refs_2_ = bf16[32,360]{1,0:T(8,128)(2,1)S(1)} collective-permute-done((bf16[32,360]{1,0:T(8,128)(2,1)S(1)}, bf16[32,360]{1,0:T(8,128)(2,1)S(1)}, u32[]{:S(2)}, u32[]{:S(2)}) %collective-permute-start.15) | collective-permute-done | bytes 23072 | tf_op jit(solution)/shard_map/ppermute | solution.py:223
  49.5 2.8 %collective-permute-done.16.refs_3_ = bf16[32,360]{1,0:T(8,128)(2,1)S(1)} collective-permute-done((bf16[32,360]{1,0:T(8,128)(2,1)S(1)}, bf16[32,360]{1,0:T(8,128)(2,1)S(1)}, u32[]{:S(2)}, u32[]{:S(2)}) %collective-permute-start.16) | collective-permute-done | bytes 23072 | tf_op jit(solution)/shard_map/ppermute | solution.py:223
  52.3 0.6 %combine.1 = bf16[2,16,360]{2,1,0:T(8,128)(2,1)} custom-call(f32[32,360]{1,0:T(8,128)S(1)} %get-tuple-element.26.refs_0_, bf16[32,360]{1,0:T(8,128)(2,1)S(1)} %collective-permute-done.14.refs_1_, bf16[32,360]{1,0:T(8,128)(2,1)S(1)} %collective-permute-done.15.refs_2_, bf16[32,360]{1,0:T(8,128)(2,1)S(1)} %collective-permute-done.16.refs_3_, ...), custom_call_target="tpu_custom_call" | custom-call | tf_op jit(solution)/shard_map/combine/pallas_call | solution.py:390
  (27 shorter events, 1.5 us)
Async XLA Ops:
  0.0 31.3 %copy-start.3 = (f32[2880]{0:T(1024)S(1)}, f32[2880]{0:T(1024)}, u32[]{:S(2)}) copy-start(f32[2880]{0:T(1024)} %param.22) | copy-start | bytes 34564
  0.0 32.5 %copy-start = (bf16[1,2880,180]{1,2,0:T(8,128)(2,1)S(1)}, bf16[1,2880,180]{1,2,0:T(8,128)(2,1)}, u32[]{:S(2)}) copy-start(bf16[1,2880,180]{1,2,0:T(8,128)(2,1)} %param.23) | copy-start | bytes 3110404
  0.0 32.5 %copy-start.1 = (bf16[1,2880,180]{1,2,0:T(8,128)(2,1)S(1)}, bf16[1,2880,180]{1,2,0:T(8,128)(2,1)}, u32[]{:S(2)}) copy-start(bf16[1,2880,180]{1,2,0:T(8,128)(2,1)} %param.24) | copy-start | bytes 3110404
  0.0 32.5 %copy-start.2 = (bf16[1,180,2880]{2,1,0:T(8,128)(2,1)S(1)}, bf16[1,180,2880]{2,1,0:T(8,128)(2,1)}, u32[]{:S(2)}) copy-start(bf16[1,180,2880]{2,1,0:T(8,128)(2,1)} %param.25) | copy-start | bytes 3110404
  15.8 5.7 %collective-permute-start.2 = (bf16[32,384]{1,0:T(8,128)(2,1)S(1)}, bf16[32,384]{1,0:T(8,128)(2,1)S(1)}, u32[]{:S(2)}, u32[]{:S(2)}) collective-permute-start(bf16[32,384]{1,0:T(8,128)(2,1)S(1)} %sum_parts.1), channel_id=1, source_target_pairs={{0,12},{4,8},{8,4},{12,0},{1,13},{5,9},{9,5},{13,1},{2,14},{6,10},... | collective-permute-start | bytes 73736 | tf_op jit(solution)/shard_map/ppermute | solution.py:223
  19.5 4.7 %collective-permute-start.1 = (bf16[32,384]{1,0:T(8,128)(2,1)S(1)}, bf16[32,384]{1,0:T(8,128)(2,1)S(1)}, u32[]{:S(2)}, u32[]{:S(2)}) collective-permute-start(bf16[32,384]{1,0:T(8,128)(2,1)S(1)} %sum_parts.1), channel_id=1, source_target_pairs={{0,8},{4,12},{8,0},{12,4},{1,9},{5,13},{9,1},{13,5},{2,10},{6,14},... | collective-permute-start | bytes 73736 | tf_op jit(solution)/shard_map/ppermute | solution.py:223
  19.5 4.7 %collective-permute-start = (bf16[32,384]{1,0:T(8,128)(2,1)S(1)}, bf16[32,384]{1,0:T(8,128)(2,1)S(1)}, u32[]{:S(2)}, u32[]{:S(2)}) collective-permute-start(bf16[32,384]{1,0:T(8,128)(2,1)S(1)} %sum_parts.1), channel_id=1, source_target_pairs={{0,4},{4,0},{8,12},{12,8},{1,5},{5,1},{9,13},{13,9},{2,6},{6,2},{1... | collective-permute-start | bytes 73736 | tf_op jit(solution)/shard_map/ppermute | solution.py:223
  24.2 5.8 %collective-permute-start.5 = (bf16[4,32,384]{2,1,0:T(8,128)(2,1)S(1)}, bf16[4,32,384]{2,1,0:T(8,128)(2,1)S(1)}, u32[]{:S(2)}, u32[]{:S(2)}) collective-permute-start(bf16[4,32,384]{2,1,0:T(8,128)(2,1)S(1)} %pad_maximum_fusion.refs_0_), channel_id=1, source_target_pairs={{0,3},{1,2},{2,1},{3,0},{4,7},{5,6},{6,5},{7,4},{8,11},{9,10},{10,... | collective-permute-start | bytes 294920 | tf_op jit(solution)/shard_map/ppermute | solution.py:223
  25.1 5.7 %collective-permute-start.4 = (bf16[4,32,384]{2,1,0:T(8,128)(2,1)S(1)}, bf16[4,32,384]{2,1,0:T(8,128)(2,1)S(1)}, u32[]{:S(2)}, u32[]{:S(2)}) collective-permute-start(bf16[4,32,384]{2,1,0:T(8,128)(2,1)S(1)} %pad_maximum_fusion.refs_0_), channel_id=1, source_target_pairs={{0,2},{1,3},{2,0},{3,1},{4,6},{5,7},{6,4},{7,5},{8,10},{9,11},{10,... | collective-permute-start | bytes 294920 | tf_op jit(solution)/shard_map/ppermute | solution.py:223
  26.6 4.6 %collective-permute-start.3 = (bf16[4,32,384]{2,1,0:T(8,128)(2,1)S(1)}, bf16[4,32,384]{2,1,0:T(8,128)(2,1)S(1)}, u32[]{:S(2)}, u32[]{:S(2)}) collective-permute-start(bf16[4,32,384]{2,1,0:T(8,128)(2,1)S(1)} %pad_maximum_fusion.refs_0_), channel_id=1, source_target_pairs={{0,1},{1,0},{2,3},{3,2},{4,5},{5,4},{6,7},{7,6},{8,9},{9,8},{10,11... | collective-permute-start | bytes 294920 | tf_op jit(solution)/shard_map/ppermute | solution.py:223
  27.8 3.5 %collective-permute-start.6 = (bf16[4,32,384]{2,1,0:T(8,128)(2,1)S(1)}, bf16[4,32,384]{2,1,0:T(8,128)(2,1)S(1)}, u32[]{:S(2)}, u32[]{:S(2)}) collective-permute-start(bf16[4,32,384]{2,1,0:T(8,128)(2,1)S(1)} %pad_maximum_fusion.refs_0_), channel_id=1, source_target_pairs={{0,16},{16,0},{1,17},{17,1},{2,18},{18,2},{3,19},{19,3},{4,20},{20... | collective-permute-start | bytes 294920 | tf_op jit(solution)/shard_map/ppermute | solution.py:223
  30.1 1.3 %collective-permute-start.9 = (bf16[4,32,384]{2,1,0:T(8,128)(2,1)S(1)}, bf16[4,32,384]{2,1,0:T(8,128)(2,1)S(1)}, u32[]{:S(2)}, u32[]{:S(2)}) collective-permute-start(bf16[4,32,384]{2,1,0:T(8,128)(2,1)S(1)} %collective-permute-done.5.refs_3_), channel_id=1, source_target_pairs={{0,16},{16,0},{1,17},{17,1},{2,18},{18,2},{3,19},{19,3},{4,20},{20... | collective-permute-start | bytes 294920 | tf_op jit(solution)/shard_map/ppermute | solution.py:223
  30.8 1.3 %collective-permute-start.8 = (bf16[4,32,384]{2,1,0:T(8,128)(2,1)S(1)}, bf16[4,32,384]{2,1,0:T(8,128)(2,1)S(1)}, u32[]{:S(2)}, u32[]{:S(2)}) collective-permute-start(bf16[4,32,384]{2,1,0:T(8,128)(2,1)S(1)} %collective-permute-done.4.refs_2_), channel_id=1, source_target_pairs={{0,16},{16,0},{1,17},{17,1},{2,18},{18,2},{3,19},{19,3},{4,20},{20... | collective-permute-start | bytes 294920 | tf_op jit(solution)/shard_map/ppermute | solution.py:223
  31.2 1.3 %collective-permute-start.7 = (bf16[4,32,384]{2,1,0:T(8,128)(2,1)S(1)}, bf16[4,32,384]{2,1,0:T(8,128)(2,1)S(1)}, u32[]{:S(2)}, u32[]{:S(2)}) collective-permute-start(bf16[4,32,384]{2,1,0:T(8,128)(2,1)S(1)} %collective-permute-done.3.refs_1_), channel_id=1, source_target_pairs={{0,16},{16,0},{1,17},{17,1},{2,18},{18,2},{3,19},{19,3},{4,20},{20... | collective-permute-start | bytes 294920 | tf_op jit(solution)/shard_map/ppermute | solution.py:223
  34.5 1.8 %collective-permute-start.10 = (bf16[4,128,360]{2,1,0:T(8,128)(2,1)S(1)}, bf16[4,128,360]{2,1,0:T(8,128)(2,1)S(1)}, u32[]{:S(2)}, u32[]{:S(2)}) collective-permute-start(bf16[4,128,360]{2,1,0:T(8,128)(2,1)S(1)} %get-tuple-element.21), channel_id=1, source_target_pairs={{0,16},{16,0},{1,17},{17,1},{2,18},{18,2},{3,19},{19,3},{4,20},{20... | collective-permute-start | bytes 1105928 | tf_op jit(solution)/shard_map/ppermute | solution.py:223
  36.4 4.9 %collective-permute-start.11 = (bf16[128,360]{1,0:T(8,128)(2,1)S(1)}, bf16[128,360]{1,0:T(8,128)(2,1)S(1)}, u32[]{:S(2)}, u32[]{:S(2)}) collective-permute-start(bf16[128,360]{1,0:T(8,128)(2,1)S(1)} %get-tuple-element.23), channel_id=1, source_target_pairs={{0,1},{1,0},{2,3},{3,2},{4,5},{5,4},{6,7},{7,6},{8,9},{9,8},{10,11... | collective-permute-start | bytes 276488 | tf_op jit(solution)/shard_map/ppermute | solution.py:223
  37.7 6.7 %collective-permute-start.12 = (bf16[128,360]{1,0:T(8,128)(2,1)S(1)}, bf16[128,360]{1,0:T(8,128)(2,1)S(1)}, u32[]{:S(2)}, u32[]{:S(2)}) collective-permute-start(bf16[128,360]{1,0:T(8,128)(2,1)S(1)} %get-tuple-element.24), channel_id=1, source_target_pairs={{0,2},{1,3},{2,0},{3,1},{4,6},{5,7},{6,4},{7,5},{8,10},{9,11},{10,... | collective-permute-start | bytes 276488 | tf_op jit(solution)/shard_map/ppermute | solution.py:223
  38.5 5.9 %collective-permute-start.13 = (bf16[128,360]{1,0:T(8,128)(2,1)S(1)}, bf16[128,360]{1,0:T(8,128)(2,1)S(1)}, u32[]{:S(2)}, u32[]{:S(2)}) collective-permute-start(bf16[128,360]{1,0:T(8,128)(2,1)S(1)} %get-tuple-element.25), channel_id=1, source_target_pairs={{0,3},{1,2},{2,1},{3,0},{4,7},{5,6},{6,5},{7,4},{8,11},{9,10},{10,... | collective-permute-start | bytes 276488 | tf_op jit(solution)/shard_map/ppermute | solution.py:223
  44.5 4.5 %collective-permute-start.14 = (bf16[32,360]{1,0:T(8,128)(2,1)S(1)}, bf16[32,360]{1,0:T(8,128)(2,1)S(1)}, u32[]{:S(2)}, u32[]{:S(2)}) collective-permute-start(bf16[32,360]{1,0:T(8,128)(2,1)S(1)} %get-tuple-element.27), channel_id=1, source_target_pairs={{0,4},{4,0},{8,12},{12,8},{1,5},{5,1},{9,13},{13,9},{2,6},{6,2},{1... | collective-permute-start | bytes 69128 | tf_op jit(solution)/shard_map/ppermute | solution.py:223
  44.6 4.9 %collective-permute-start.15 = (bf16[32,360]{1,0:T(8,128)(2,1)S(1)}, bf16[32,360]{1,0:T(8,128)(2,1)S(1)}, u32[]{:S(2)}, u32[]{:S(2)}) collective-permute-start(bf16[32,360]{1,0:T(8,128)(2,1)S(1)} %get-tuple-element.28), channel_id=1, source_target_pairs={{0,8},{4,12},{8,0},{12,4},{1,9},{5,13},{9,1},{13,5},{2,10},{6,14},... | collective-permute-start | bytes 69128 | tf_op jit(solution)/shard_map/ppermute | solution.py:223
  46.7 5.6 %collective-permute-start.16 = (bf16[32,360]{1,0:T(8,128)(2,1)S(1)}, bf16[32,360]{1,0:T(8,128)(2,1)S(1)}, u32[]{:S(2)}, u32[]{:S(2)}) collective-permute-start(bf16[32,360]{1,0:T(8,128)(2,1)S(1)} %get-tuple-element.29), channel_id=1, source_target_pairs={{0,12},{4,8},{8,4},{12,0},{1,13},{5,9},{9,5},{13,1},{2,14},{6,10},... | collective-permute-start | bytes 69128 | tf_op jit(solution)/shard_map/ppermute | solution.py:223

commit v6 on v5

--- a/solution.py
+++ b/solution.py
@@ -1,4 +1,5 @@
 import functools
+import math
 
 import jax
 import jax.numpy as jnp
@@ -223,22 +224,36 @@
     return lax.ppermute(value, axes, [(i, i ^ mask) for i in range(size)])
 
 
+def swap_by_core(value, axis, masks):
+    size = lax.axis_size(axis)
+    pairs = [(s * size + i, s * size + (i ^ masks[s])) for s in range(2) for i in range(size)]
+    return lax.ppermute(value, ("sec", axis), pairs)
+
+
+def shard_swaps(parts):
+    return [swap_by_core(part, "tp", masks) for part, masks in zip(parts, ((3, 3), (1, 2), (2, 1)))]
+
+
+def shard_masks():
+    sec = lax.axis_index("sec")
+    return 3, 1 + sec, 2 - sec
+
+
 def split_width(width):
     cuts = list(range(0, width, 768)) + [width]
     return list(zip(cuts[:-1], cuts[1:]))
 
 
 def attention_kernel(lengths_hbm, sinks_hbm, routes_hbm, weights_hbm, gain_hbm, x_hbm, wq_hbm, wkv_hbm, cache_hbm, wo_hbm,
-                     parts_ref, own_x_ref,
-                     lengths_ref, sinks_ref, routes_ref, weights_ref, gain_ref, x_ref, wq_ref, wkv_ref, cache_ref, wo_ref,
+                     other_ref, own_x_ref, mix_ref, wo_ref,
+                     lengths_ref, sinks_ref, routes_ref, weights_ref, gain_ref, x_ref, wq_ref, wkv_ref, cache_ref,
                      xs_ref, turned_ref, mixed_ref, sems):
     total_rows, width = x_ref.shape
     rows, slots, pair = cache_ref.shape
     steps = total_rows // rows
     heads = wq_ref.shape[1] // HEAD_SIZE
     per_row = heads * steps
-    shards = parts_ref.shape[0]
-    tps = lax.axis_size("tp")
+    tps = other_ref.shape[0]
     cuts = split_width(width)
     small = [(lengths_hbm, lengths_ref), (x_hbm, x_ref), (gain_hbm, gain_ref), (routes_hbm, routes_ref), (weights_hbm, weights_ref),
              (sinks_hbm, sinks_ref)]
@@ -340,17 +355,31 @@
     def head(h):
         return jnp.concatenate([mixed_ref[pl.ds(h * steps + s, rows, stride=per_row), :] for s in range(steps)], axis=0)
 
-    mix = jnp.concatenate(
+    mix_ref[...] = jnp.concatenate(
         [jnp.where(is_key, pltpu.roll(head(2 * m), HEAD_SIZE, 1), head(2 * m + 1)) for m in range(heads // 2)], axis=1
     ).astype(jnp.bfloat16)
     copies[-1].wait()
-    partial = dot_last(mix, wo_ref[...])
-    for c in range(shards):
-        low, high = c * LANES, min((c + 1) * LANES, width)
-        piece = partial[:, low:high]
-        if high - low < LANES:
-            piece = jnp.concatenate([piece, jnp.zeros((total_rows, LANES - (high - low)), jnp.float32)], axis=1)
-        parts_ref[c] = piece.astype(jnp.bfloat16)
+    project(mix_ref, wo_ref, other_ref, 1 - lax.axis_index("sec"))
+
+
+def project(mix_ref, wo_ref, out_ref, side):
+    width, (tps, total_rows, _) = wo_ref.shape[0], out_ref.shape
+    for at in range(2):
+        start, stop = at * tps * LANES, min((at + 1) * tps * LANES, width)
+
+        @pl.when(side == at)
+        def _(start=start, stop=stop):
+            partial = dot_last(mix_ref[...], wo_ref[start:stop, :])
+            for t in range(tps):
+                low, high = t * LANES, min((t + 1) * LANES, stop - start)
+                piece = partial[:, low:high]
+                if high - low < LANES:
+                    piece = jnp.concatenate([piece, jnp.zeros((total_rows, LANES - (high - low)), jnp.float32)], axis=1)
+                out_ref[t] = piece.astype(out_ref.dtype)
+
+
+def own_projection_kernel(mix_ref, wo_ref, mine_ref):
+    project(mix_ref, wo_ref, mine_ref, lax.axis_index("sec"))
 
 
 def attention_partial(flat, gain, w_query, key_value, sinks, w_output, cache, lengths, routes, weights, secs, tps):
@@ -362,9 +391,10 @@
     return pl.pallas_call(
         attention_kernel,
         name="attention",
-        out_shape=[shape_of((shards, total_rows, LANES)), shape_of((total_rows, LANES), jnp.float32)],
+        out_shape=[shape_of((tps, total_rows, LANES)), shape_of((total_rows, LANES), jnp.float32),
+                   shape_of((total_rows, w_output.shape[0])), shape_of((width, w_output.shape[0]))],
         in_specs=[outside()] * len(operands),
-        out_specs=[vmem()] * 2,
+        out_specs=[vmem()] * 4,
         scratch_shapes=[
             pltpu.SMEM(lengths.shape, jnp.int32),
             pltpu.SMEM(sinks.shape, jnp.float32),
@@ -375,7 +405,6 @@
             pltpu.VMEM(w_query.shape, jnp.bfloat16),
             pltpu.VMEM(key_value.shape, jnp.bfloat16),
             pltpu.VMEM(cache.shape, jnp.bfloat16),
-            pltpu.VMEM((width, w_output.shape[0]), jnp.bfloat16),
             pltpu.VMEM((total_rows, shards * LANES), jnp.float32),
             pltpu.VMEM((rows * per_row, pair), jnp.float32),
             pltpu.VMEM((rows * per_row, pair), jnp.float32),
@@ -385,8 +414,9 @@
     )(*[pltpu.with_memory_space_constraint(operand, pltpu.HBM) for operand in operands])
 
 
-def call(kernel, name, outs, *operands, limit=4):
+def call(kernel, name, outs, *operands, limit=4, flops=0):
     single = not isinstance(outs, list)
+    held = [*operands, *([outs] if single else outs)]
     return pl.pallas_call(
         kernel,
         name=name,
@@ -394,14 +424,16 @@
         in_specs=[vmem()] * len(operands),
         out_specs=vmem() if single else [vmem()] * len(outs),
         compiler_params=pltpu.CompilerParams(vmem_limit_bytes=limit * MIB),
+        cost_estimate=pl.CostEstimate(flops=flops, transcendentals=0,
+                                      bytes_accessed=sum(math.prod(a.shape) * a.dtype.itemsize for a in held)),
     )(*operands)
 
 
 def after_core_kernel(mine_ref, come_ref, own_ref, *send_refs):
     tp = lax.axis_index("tp")
     own_ref[...] = mine_ref[tp] + come_ref[tp].astype(jnp.float32)
-    for n, ref in enumerate(send_refs):
-        to = jnp.bitwise_xor(tp, n + 1)
+    for mask, ref in zip(shard_masks(), send_refs):
+        to = jnp.bitwise_xor(tp, mask)
         ref[...] = (mine_ref[to] + come_ref[to].astype(jnp.float32)).astype(jnp.bfloat16)
 
 
@@ -410,13 +442,6 @@
     for ref in refs[1:]:
         total = total + ref[...].astype(jnp.float32)
     return total
-
-
-def sum_parts_kernel(parts_ref, own_ref, out_ref):
-    total = own_ref[...]
-    for n in range(parts_ref.shape[0]):
-        total = total + parts_ref[n].astype(jnp.float32)
-    out_ref[...] = total.astype(jnp.bfloat16)
 
 
 def sum_kernel(*refs):
@@ -441,59 +466,104 @@
     tps, lines, part = mine.shape
     own, *parts = call(after_core_kernel, "after_core", [shape_of((lines, part), jnp.float32)] + [shape_of((lines, part))] * (tps - 1),
                        mine, come)
-    return [own] + swap_all(parts, "tp")
-
-
-def expert_kernel(gain_ref, gate_ref, up_ref, down_ref, *refs):
-    pieces, (other_ref, mine_ref, middle_ref, x_ref, chunk_ref, row_ref) = refs[:-6], refs[-6:]
-    total_rows = middle_ref.shape[0]
-    tps, lines, part = mine_ref.shape
-    secs = chunk_ref.shape[0] // tps
-    width = down_ref.shape[1]
-    sec, tp, grp = lax.axis_index("sec"), lax.axis_index("tp"), lax.axis_index("grp")
-    for n, piece in enumerate(pieces):
-        at = jnp.bitwise_xor(sec, n // tps) * tps + jnp.bitwise_xor(tp, n % tps)
-        x_ref[:, pl.ds(pl.multiple_of(at * LANES, LANES), LANES)] = piece[...].reshape(lines, LANES)
-    x = x_ref[:, :width].astype(jnp.float32)
-    for c in range(secs * tps):
-        row_ref[c] = x[:total_rows, c * part:(c + 1) * part]
-    middle_ref[...] = row_ref[sec * tps + tp]
-    spare = x_ref[:, width:].astype(jnp.float32)
+    return [own] + shard_swaps(parts)
+
+
+def first_products(pieces, masks, side, x_ref, gain_ref, gate_ref, up_ref, gate_out, up_out, square_out):
+    width, lines = gate_ref.shape[1], x_ref.shape[0]
+    tp = lax.axis_index("tp")
+    for mask, piece in zip(masks, pieces):
+        at = pl.multiple_of(jnp.bitwise_xor(tp, mask) * LANES, LANES)
+        x_ref[:, pl.ds(at, LANES)] = piece[...].reshape(lines, LANES)
+    for at in range(2):
+        start, stop = at * x_ref.shape[1], min((at + 1) * x_ref.shape[1], width)
+
+        @pl.when(side == at)
+        def _(start=start, stop=stop):
+            x = x_ref[:, :stop - start].astype(jnp.float32)
+            square_out[...] = jnp.broadcast_to(jnp.sum(x * x, axis=-1, keepdims=True), square_out.shape)
+            scaled = (x * gain_ref[:, start:stop]).astype(jnp.bfloat16)
+            gate_out[...] = dot_last(scaled, gate_ref[:, start:stop])
+            up_out[...] = dot_last(scaled, up_ref[:, start:stop])
+
+
+def near_kernel(gain_ref, gate_ref, up_ref, *refs):
+    pieces, (x_ref, gate_out, up_out, square_out) = refs[:-4], refs[-4:]
+    first_products(pieces, (0, *shard_masks()), lax.axis_index("sec"), x_ref, gain_ref, gate_ref, up_ref, gate_out, up_out,
+                   square_out)
+
+
+def second_product(act_ref, down_ref, out_ref, side):
+    width, (tps, lines, part) = down_ref.shape[1], out_ref.shape
+    for at in range(2):
+        start, stop = at * tps * part, (at + 1) * tps * part
+        shift = start % 128
+
+        @pl.when(side == at)
+        def _(start=start, stop=stop, shift=shift):
+            out = jnp.dot(act_ref[...], down_ref[:, start - shift:stop], preferred_element_type=jnp.float32)
+            for t in range(tps):
+                out_ref[t] = out[:, shift + t * part:shift + (t + 1) * part].astype(out_ref.dtype)
+
+
+def far_kernel(gain_ref, gate_ref, up_ref, down_ref, near_x_ref, near_gate_ref, near_up_ref, near_square_ref, *refs):
+    pieces, (other_ref, act_ref, far_x_ref, gate_out, up_out, square_out) = refs[:-6], refs[-6:]
+    sec, grp = lax.axis_index("sec"), lax.axis_index("grp")
+    masks = shard_masks()
+    first_products(pieces, (0, masks[0], masks[2], masks[1]), 1 - sec, far_x_ref, gain_ref, gate_ref, up_ref, gate_out, up_out,
+                   square_out)
+    width, half = gate_ref.shape[1], near_x_ref.shape[1]
+    spare = jnp.where(sec == 1, near_x_ref[:, width - half:], far_x_ref[:, width - half:]).astype(jnp.float32)
     spare_at = lax.broadcasted_iota(jnp.int32, spare.shape, 1)
     weight = jnp.sum(jnp.where((spare_at == 2 * grp) | (spare_at == 2 * grp + 1), spare, 0.0), axis=1, keepdims=True)
-    scale = lax.rsqrt(jnp.mean(x * x, axis=-1, keepdims=True) + 1e-05)
-    expert_in = (x * scale * gain_ref[...]).astype(jnp.bfloat16)
-    gate_h = dot_last(expert_in, gate_ref[...])
-    up_h = dot_last(expert_in, up_ref[...])
-    act = ((up_h + 1.0) * gate_h * jax.nn.sigmoid(1.702 * gate_h)).astype(jnp.bfloat16)
-    out = jnp.dot(act, down_ref[...], preferred_element_type=jnp.float32) * weight
-    for c in range(secs * tps):
-        chunk_ref[c] = out[:, c * part:(c + 1) * part]
-    for t in range(tps):
-        other_ref[t] = chunk_ref[(1 - sec) * tps + t].astype(jnp.bfloat16)
-        mine_ref[t] = chunk_ref[sec * tps + t]
-
-
-def expert_partial(gain, w_gate, w_up, w_down, pieces, secs, tps):
+    square = (near_square_ref[...] + square_out[...])[:, :1]
+    scale = lax.rsqrt(square / width + 1e-05)
+    gate_h = (near_gate_ref[...] + gate_out[...]) * scale
+    up_h = (near_up_ref[...] + up_out[...]) * scale
+    act_ref[...] = ((up_h + 1.0) * gate_h * jax.nn.sigmoid(1.702 * gate_h) * weight).astype(jnp.bfloat16)
+    second_product(act_ref, down_ref, other_ref, 1 - sec)
+
+
+def last_kernel(act_ref, down_ref, near_x_ref, far_x_ref, mine_ref, middle_ref, row_ref):
+    sec, tp = lax.axis_index("sec"), lax.axis_index("tp")
+    second_product(act_ref, down_ref, mine_ref, sec)
+    total_rows, part = middle_ref.shape
+    near, far = near_x_ref[:total_rows].astype(jnp.float32), far_x_ref[:total_rows].astype(jnp.float32)
+    first = sec == 0
+    x = jnp.concatenate([jnp.where(first, near, far), jnp.where(first, far, near)], axis=1)
+    for c in range(row_ref.shape[0]):
+        row_ref[c] = x[:, c * part:(c + 1) * part]
+    middle_ref[...] = row_ref[sec * mine_ref.shape[0] + tp]
+
+
+def experts(gain, w_gate, w_up, w_down, pieces, far_pieces, part):
     groups, total_rows, _ = pieces[0].shape
-    width = gain.shape[0]
-    shards = secs * tps
-    part = width // shards
-    lines = groups * total_rows
-    return pl.pallas_call(
-        expert_kernel,
-        name="expert",
-        out_shape=[shape_of((tps, lines, part)), shape_of((tps, lines, part), jnp.float32),
-                   shape_of((total_rows, part), jnp.float32)],
-        in_specs=[vmem()] * (4 + len(pieces)),
+    tps, lines, (width, hidden) = len(pieces), groups * total_rows, w_gate.shape
+    gain, w_gate, w_up = gain.reshape(1, -1), w_gate.swapaxes(0, 1), w_up.swapaxes(0, 1)
+    halves = [shape_of((lines, tps * LANES)), shape_of((lines, hidden), jnp.float32), shape_of((lines, hidden), jnp.float32),
+              shape_of((lines, 128), jnp.float32)]
+    near = call(near_kernel, "near_columns", halves, gain, w_gate, w_up, *pieces, limit=12, flops=2 * lines * width * hidden)
+    other, act, far_x = pl.pallas_call(
+        far_kernel,
+        name="far_columns",
+        out_shape=[shape_of((tps, lines, part)), shape_of((lines, hidden)), halves[0]],
+        in_specs=[vmem()] * (8 + tps),
         out_specs=[vmem()] * 3,
-        scratch_shapes=[
-            pltpu.VMEM((lines, shards * LANES), jnp.bfloat16),
-            pltpu.VMEM((shards, lines, part), jnp.float32),
-            pltpu.VMEM((shards, total_rows, part), jnp.float32),
-        ],
-        compiler_params=pltpu.CompilerParams(vmem_limit_bytes=20 * MIB),
-    )(gain.reshape(1, -1), w_gate.swapaxes(0, 1), w_up.swapaxes(0, 1), w_down, *pieces)
+        scratch_shapes=[pltpu.VMEM(half.shape, half.dtype) for half in halves[1:]],
+        compiler_params=pltpu.CompilerParams(vmem_limit_bytes=16 * MIB),
+    )(gain, w_gate, w_up, w_down, *near, *far_pieces)
+    come = swap(other, "sec", 1)
+    mine, middle = pl.pallas_call(
+        last_kernel,
+        name="own_columns",
+        out_shape=[shape_of((tps, lines, part), jnp.float32), shape_of((total_rows, part), jnp.float32)],
+        in_specs=[vmem()] * 4,
+        out_specs=[vmem()] * 2,
+        scratch_shapes=[pltpu.VMEM((2 * tps, total_rows, part), jnp.float32)],
+        compiler_params=pltpu.CompilerParams(vmem_limit_bytes=12 * MIB),
+        cost_estimate=pl.CostEstimate(flops=lines * width * hidden, transcendentals=0, bytes_accessed=2 * lines * width),
+    )(act, w_down, near[0], far_x)
+    return mine, come, middle
 
 
 def every_expert_body(inputs, attention_gain, w_query, key_value_weight, head_sink_logits, w_output, cache_pairs, lengths,
@@ -501,16 +571,18 @@
     secs, tps, groups = lax.axis_size("sec"), lax.axis_size("tp"), lax.axis_size("grp")
     steps, rows, width = inputs.shape
     flat = inputs.reshape(steps * rows, width)
-    parts, own_x = attention_partial(
+    other, own_x, mix, held = attention_partial(
         flat, attention_gain, w_query, key_value_weight[:, 0], head_sink_logits, w_output, cache_pairs[:, :, 0], lengths,
         routes.swapaxes(1, 2), gate_weights.swapaxes(1, 2), secs, tps)
-    parts = lax.all_to_all(parts, ("sec", "tp"), 0, 0, tiled=True)
-    middle = call(sum_parts_kernel, "sum_parts", shape_of((steps * rows, LANES)), parts, own_x)
+    come = swap(other, "sec", 1)
+    mine = call(own_projection_kernel, "own_projection", shape_of(other.shape, jnp.float32), mix, held, limit=12,
+                flops=mix.size * width)
+    middle = call(sum_kernel, "sum", shape_of((steps * rows, LANES)), *scatter_shards(mine, come), own_x)
     stacked = jnp.stack([middle] + swap_all([middle] * (groups - 1), "grp"))
-    pieces = [stacked] + swap_all([stacked] * (tps - 1), "tp")
-    pieces = pieces + [swap(piece, "sec", 1) for piece in pieces]
-    other, mine, own_middle = expert_partial(expert_gain, w_gate[0], w_up[0], w_down[0], pieces, secs, tps)
-    terms = scatter_shards(mine, swap(other, "sec", 1))
+    pieces = [stacked] + shard_swaps([stacked] * (tps - 1))
+    far_pieces = [swap(piece, "sec", 1) for piece in pieces]
+    mine, come, own_middle = experts(expert_gain, w_gate[0], w_up[0], w_down[0], pieces, far_pieces, width // (secs * tps))
+    terms = scatter_shards(mine, come)
     lines, part = steps * rows, terms[0].shape[1]
     own, *parts = call(functools.partial(divide_rows_kernel, groups=groups), "divide_rows",
                        [shape_of((lines, part), jnp.float32)] + [shape_of((lines, part))] * (groups - 1), *terms)

time: 53.1 us -> 50.2 us (0.945)
  blocking collectives: 11 us -> 0 us
  starting transfers between devices: 16.4 us -> 21.2 us
  waiting for transfers between devices: 17.8 us -> 20.7 us
    ppermute x0 -> x9, starting transfers between devices: none -> 11.6 us  [swap_by_core(): return lax.ppermute(value, ('sec', axis), pairs)]
    ppermute x0 -> x9, waiting for transfers between devices: none -> 11.2 us  [swap_by_core(): return lax.ppermute(value, ('sec', axis), pairs)]
    all_to_all x1 -> x0, blocking collectives: 11 us -> none  [every_expert_body(): parts = lax.all_to_all(parts, ('sec', 'tp'), 0, 0, tiled=True)]
    ppermute x17 -> x12, waiting for transfers between devices: 17.8 us -> 9.52 us  [swap(): return lax.ppermute(value, axes, [(i, i ^ mask) for i in range(size)])]
    ppermute x17 -> x12, starting transfers between devices: 16.4 us -> 9.68 us  [swap(): return lax.ppermute(value, axes, [(i, i ^ mask) for i in range(size)])]
    pallas_call x4 -> x7, Pallas kernels: 0.81 us -> 1.94 us  [call(): pl.pallas_call(kernel, name=name, out_shape=outs, in_specs=[vmem()] * len...]
    pallas_call x2 -> x3, Pallas kernels: 6.84 us -> 5.92 us  [the longest x1 4.19 us: attention_partial(): pl.pallas_call(attention_kernel, name='attention', out_shape=[shape_of((t...]
  transfers between devices with their start and end apart: 17 -> 21, of which waited for: 12 -> 16; matrix products, arithmetic and copies ran while one was open for 0% -> 0% of each run, Pallas kernels for 0% -> 3%
where the time goes in v6:
time: 50.2 us; the launch traced here: 50 us
  starting transfers between devices  21.2 us (42%)
  waiting for transfers between devices  20.7 us (41%)
  Pallas kernels  7.86 us (16%)
    ppermute x9, starting transfers between devices, swap_by_core(): return lax.ppermute(value, ('sec', axis), pairs)  11.6 us
    ppermute x9, waiting for transfers between devices, swap_by_core(): return lax.ppermute(value, ('sec', axis), pairs)  11.2 us
    ppermute x12, starting transfers between devices, swap(): return lax.ppermute(value, axes, [(i, i ^ mask) for i in range(size)])  9.68 us
    ppermute x12, waiting for transfers between devices, swap(): return lax.ppermute(value, axes, [(i, i ^ mask) for i in range(size)])  9.52 us
    pallas_call x1, Pallas kernels, attention_partial(): pl.pallas_call(attention_kernel, name='attention', out_shape=[shape_of((t...  4.19 us
    pallas_call x7, Pallas kernels, call(): pl.pallas_call(kernel, name=name, out_shape=outs, in_specs=[vmem()] * len...  1.94 us
    pallas_call x1, Pallas kernels, experts(): pl.pallas_call(far_kernel, name='far_columns', out_shape=[shape_of((tps,...  1.16 us
  transfers between devices with their start and end apart: 21, of which 16 were waited for; matrix products, arithmetic and copies ran while one was open for 0% of the time, Pallas kernels for 3%

profile of v6, /device:TPU:0, one launch (start us, length us, event | category | flops | bytes accessed | tf_op | source)
XLA Modules:
  0.0 50.0 jit_solution(3564278355007653137)
XLA Ops:
  0.0 4.2 %attention.1 = (bf16[4,32,384]{2,1,0:T(8,128)(2,1)S(1)}, f32[32,384]{1,0:T(8,128)S(1)}, bf16[32,512]{1,0:T(8,128)(2,1)S(1)}, bf16[2880,512]{1,0:T(8,128)(2,1)S(1)}) custom-call(s32[16]{0:T(128)} %lengths_hbm.1, f32[8]{0:T(128)} %sinks_hbm.1, s32[2,4,16]{2,1,0:T(4,128)} %bitcast.31, f32[2,4,16]{2,1,0:T(4,128)} %bitcast.32, f32[2880]{0:T(1024)} %gain_hbm.1, ...), custom_call_target="tpu_custom_call" | custom-call | tf_op jit(solution)/shard_map/attention/pallas_call | solution.py:391
  4.2 0.6 %collective-permute-start = (bf16[4,32,384]{2,1,0:T(8,128)(2,1)S(1)}, bf16[4,32,384]{2,1,0:T(8,128)(2,1)S(1)}, u32[]{:S(2)}, u32[]{:S(2)}) collective-permute-start(bf16[4,32,384]{2,1,0:T(8,128)(2,1)S(1)} %get-tuple-element.32), channel_id=1, source_target_pairs={{0,16},{16,0},{1,17},{17,1},{2,18},{18,2},{3,19},{19,3},{4,20},{20... | collective-permute-start | bytes 294920 | tf_op jit(solution)/shard_map/ppermute | solution.py:224
  4.8 0.5 %own_projection.1.mine_ref = f32[4,32,384]{2,1,0:T(8,128)S(1)} custom-call(bf16[32,512]{1,0:T(8,128)(2,1)S(1)} %get-tuple-element.30.mix_ref, bf16[2880,512]{1,0:T(8,128)(2,1)S(1)} %get-tuple-element.31.wo_ref), custom_call_target="tpu_custom_call" | custom-call | flops 47185920 | bytes 3178496 | tf_op jit(solution)/shard_map/own_projection/pallas_call | solution.py:420
  5.8 3.8 %collective-permute-start.1 = (bf16[32,384]{1,0:T(8,128)(2,1)S(1)}, bf16[32,384]{1,0:T(8,128)(2,1)S(1)}, u32[]{:S(2)}, u32[]{:S(2)}) collective-permute-start(bf16[32,384]{1,0:T(8,128)(2,1)S(1)} %get-tuple-element.34), channel_id=1, source_target_pairs={{0,3},{1,2},{2,1},{3,0},{16,19},{17,18},{18,17},{19,16},{4,7},{5,6... | collective-permute-start | bytes 73736 | tf_op jit(solution)/shard_map/ppermute | solution.py:230
  10.2 1.2 %collective-permute-done.1.refs_1_ = bf16[32,384]{1,0:T(8,128)(2,1)S(1)} collective-permute-done((bf16[32,384]{1,0:T(8,128)(2,1)S(1)}, bf16[32,384]{1,0:T(8,128)(2,1)S(1)}, u32[]{:S(2)}, u32[]{:S(2)}) %collective-permute-start.1) | collective-permute-done | bytes 24608 | tf_op jit(solution)/shard_map/ppermute | solution.py:230
  11.4 2.0 %collective-permute-done.2.refs_2_ = bf16[32,384]{1,0:T(8,128)(2,1)S(1)} collective-permute-done((bf16[32,384]{1,0:T(8,128)(2,1)S(1)}, bf16[32,384]{1,0:T(8,128)(2,1)S(1)}, u32[]{:S(2)}, u32[]{:S(2)}) %collective-permute-start.2) | collective-permute-done | bytes 24608 | tf_op jit(solution)/shard_map/ppermute | solution.py:230
  14.0 1.6 %collective-permute-start.4 = (bf16[32,384]{1,0:T(8,128)(2,1)S(1)}, bf16[32,384]{1,0:T(8,128)(2,1)S(1)}, u32[]{:S(2)}, u32[]{:S(2)}) collective-permute-start(bf16[32,384]{1,0:T(8,128)(2,1)S(1)} %sum.1), channel_id=1, source_target_pairs={{0,4},{4,0},{8,12},{12,8},{1,5},{5,1},{9,13},{13,9},{2,6},{6,2},{1... | collective-permute-start | bytes 73736 | tf_op jit(solution)/shard_map/ppermute | solution.py:224
  15.6 2.6 %collective-permute-start.5 = (bf16[32,384]{1,0:T(8,128)(2,1)S(1)}, bf16[32,384]{1,0:T(8,128)(2,1)S(1)}, u32[]{:S(2)}, u32[]{:S(2)}) collective-permute-start(bf16[32,384]{1,0:T(8,128)(2,1)S(1)} %sum.1), channel_id=1, source_target_pairs={{0,8},{4,12},{8,0},{12,4},{1,9},{5,13},{9,1},{13,5},{2,10},{6,14},... | collective-permute-start | bytes 73736 | tf_op jit(solution)/shard_map/ppermute | solution.py:224
  18.4 2.3 %collective-permute-done.5 = bf16[32,384]{1,0:T(8,128)(2,1)S(1)} collective-permute-done((bf16[32,384]{1,0:T(8,128)(2,1)S(1)}, bf16[32,384]{1,0:T(8,128)(2,1)S(1)}, u32[]{:S(2)}, u32[]{:S(2)}) %collective-permute-start.5) | collective-permute-done | bytes 24608 | tf_op jit(solution)/shard_map/ppermute | solution.py:224
  20.8 3.1 %collective-permute-done.6 = bf16[32,384]{1,0:T(8,128)(2,1)S(1)} collective-permute-done((bf16[32,384]{1,0:T(8,128)(2,1)S(1)}, bf16[32,384]{1,0:T(8,128)(2,1)S(1)}, u32[]{:S(2)}, u32[]{:S(2)}) %collective-permute-start.6) | collective-permute-done | bytes 24608 | tf_op jit(solution)/shard_map/ppermute | solution.py:224
  23.9 1.5 %collective-permute-start.7 = (bf16[4,32,384]{2,1,0:T(8,128)(2,1)S(1)}, bf16[4,32,384]{2,1,0:T(8,128)(2,1)S(1)}, u32[]{:S(2)}, u32[]{:S(2)}) collective-permute-start(bf16[4,32,384]{2,1,0:T(8,128)(2,1)S(1)} %pad_maximum_fusion.refs_0_), channel_id=1, source_target_pairs={{0,3},{1,2},{2,1},{3,0},{16,19},{17,18},{18,17},{19,16},{4,7},{5,6... | collective-permute-start | bytes 294920 | tf_op jit(solution)/shard_map/ppermute | solution.py:230
  25.9 1.5 %collective-permute-start.9 = (bf16[4,32,384]{2,1,0:T(8,128)(2,1)S(1)}, bf16[4,32,384]{2,1,0:T(8,128)(2,1)S(1)}, u32[]{:S(2)}, u32[]{:S(2)}) collective-permute-start(bf16[4,32,384]{2,1,0:T(8,128)(2,1)S(1)} %pad_maximum_fusion.refs_0_), channel_id=1, source_target_pairs={{0,2},{1,3},{2,0},{3,1},{16,17},{17,16},{18,19},{19,18},{4,6},{5,7... | collective-permute-start | bytes 294920 | tf_op jit(solution)/shard_map/ppermute | solution.py:230
  27.4 2.0 %collective-permute-done.7.refs_1_ = bf16[4,32,384]{2,1,0:T(8,128)(2,1)S(1)} collective-permute-done((bf16[4,32,384]{2,1,0:T(8,128)(2,1)S(1)}, bf16[4,32,384]{2,1,0:T(8,128)(2,1)S(1)}, u32[]{:S(2)}, u32[]{:S(2)}) %collective-permute-start.7) | collective-permute-done | bytes 98336 | tf_op jit(solution)/shard_map/ppermute | solution.py:230
  30.5 0.6 %near_columns.1 = (bf16[128,1536]{1,0:T(8,128)(2,1)S(1)}, f32[128,180]{1,0:T(8,128)S(1)}, f32[128,180]{1,0:T(8,128)S(1)}, f32[128,128]{1,0:T(8,128)S(1)}) custom-call(f32[1,2880]{1,0:T(1,128)S(1)} %reshape.6.gain_ref, bf16[180,2880]{1,0:T(8,128)(2,1)S(1)} %bitcast.17, bf16[180,2880]{1,0:T(8,128)(2,1)S(1)} %bitcast.19, ...), custom_call_target="tpu_custom_call" | custom-call | flops 132710400 | bytes 3121408 | tf_op jit(solution)/shard_map/near_columns/pallas_call | solution.py:420
  31.8 1.2 %far_columns.1 = (bf16[4,128,360]{2,1,0:T(8,128)(2,1)S(1)}, bf16[128,180]{1,0:T(8,128)(2,1)S(1)}, bf16[128,1536]{1,0:T(8,128)(2,1)S(1)}) custom-call(f32[1,2880]{1,0:T(1,128)S(1)} %reshape.6.gain_ref, bf16[180,2880]{1,0:T(8,128)(2,1)S(1)} %bitcast.18, bf16[180,2880]{1,0:T(8,128)(2,1)S(1)} %bitcast.20, bf16[180,2880]{1,0:T(8,128)(2,1)S(1)} %bitcast.21, ...), custom_call_target="tpu_custom_call" | custom-call | tf_op jit(solution)/shard_map/far_columns/pallas_call | solution.py:546
  33.2 0.6 %own_columns.1 = (f32[4,128,360]{2,1,0:T(8,128)S(1)}, f32[32,360]{1,0:T(8,128)S(1)}) custom-call(bf16[128,180]{1,0:T(8,128)(2,1)S(1)} %get-tuple-element.42.act_ref, bf16[180,2880]{1,0:T(8,128)(2,1)S(1)} %bitcast.22, bf16[128,1536]{1,0:T(8,128)(2,1)S(1)} %get-tuple-element.38.near_x_ref, bf16[128,1536]{1,0:T(8,128)(2,1)S(1)} %get-tuple-element.43.far_x_ref), custom_call_target="tpu_custom_call" | custom-call | flops 66355200 | bytes 737280 | tf_op jit(solution)/shard_map/own_columns/pallas_call | solution.py:556
  33.8 1.0 %collective-permute-done.14.come_ref = bf16[4,128,360]{2,1,0:T(8,128)(2,1)S(1)} collective-permute-done((bf16[4,128,360]{2,1,0:T(8,128)(2,1)S(1)}, bf16[4,128,360]{2,1,0:T(8,128)(2,1)S(1)}, u32[]{:S(2)}, u32[]{:S(2)}) %collective-permute-start.14) | collective-permute-done | bytes 368672 | tf_op jit(solution)/shard_map/ppermute | solution.py:224
  34.8 2.5 %collective-permute-start.15 = (bf16[128,360]{1,0:T(8,128)(2,1)S(1)}, bf16[128,360]{1,0:T(8,128)(2,1)S(1)}, u32[]{:S(2)}, u32[]{:S(2)}) collective-permute-start(bf16[128,360]{1,0:T(8,128)(2,1)S(1)} %get-tuple-element.47), channel_id=1, source_target_pairs={{0,3},{1,2},{2,1},{3,0},{16,19},{17,18},{18,17},{19,16},{4,7},{5,6... | collective-permute-start | bytes 276488 | tf_op jit(solution)/shard_map/ppermute | solution.py:230
  38.4 2.3 %collective-permute-done.15.refs_1_ = bf16[128,360]{1,0:T(8,128)(2,1)S(1)} collective-permute-done((bf16[128,360]{1,0:T(8,128)(2,1)S(1)}, bf16[128,360]{1,0:T(8,128)(2,1)S(1)}, u32[]{:S(2)}, u32[]{:S(2)}) %collective-permute-start.15) | collective-permute-done | bytes 92192 | tf_op jit(solution)/shard_map/ppermute | solution.py:230
  40.7 2.1 %collective-permute-done.16.refs_2_ = bf16[128,360]{1,0:T(8,128)(2,1)S(1)} collective-permute-done((bf16[128,360]{1,0:T(8,128)(2,1)S(1)}, bf16[128,360]{1,0:T(8,128)(2,1)S(1)}, u32[]{:S(2)}, u32[]{:S(2)}) %collective-permute-start.16) | collective-permute-done | bytes 92192 | tf_op jit(solution)/shard_map/ppermute | solution.py:230
  42.9 0.8 %collective-permute-start.19 = (bf16[32,360]{1,0:T(8,128)(2,1)S(1)}, bf16[32,360]{1,0:T(8,128)(2,1)S(1)}, u32[]{:S(2)}, u32[]{:S(2)}) collective-permute-start(bf16[32,360]{1,0:T(8,128)(2,1)S(1)} %get-tuple-element.52), channel_id=1, source_target_pairs={{0,8},{4,12},{8,0},{12,4},{1,9},{5,13},{9,1},{13,5},{2,10},{6,14},... | collective-permute-start | bytes 69128 | tf_op jit(solution)/shard_map/ppermute | solution.py:224
  43.8 3.6 %collective-permute-start.20 = (bf16[32,360]{1,0:T(8,128)(2,1)S(1)}, bf16[32,360]{1,0:T(8,128)(2,1)S(1)}, u32[]{:S(2)}, u32[]{:S(2)}) collective-permute-start(bf16[32,360]{1,0:T(8,128)(2,1)S(1)} %get-tuple-element.53), channel_id=1, source_target_pairs={{0,12},{4,8},{8,4},{12,0},{1,13},{5,9},{9,5},{13,1},{2,14},{6,10},... | collective-permute-start | bytes 69128 | tf_op jit(solution)/shard_map/ppermute | solution.py:224
  47.8 1.6 %collective-permute-done.20.refs_3_ = bf16[32,360]{1,0:T(8,128)(2,1)S(1)} collective-permute-done((bf16[32,360]{1,0:T(8,128)(2,1)S(1)}, bf16[32,360]{1,0:T(8,128)(2,1)S(1)}, u32[]{:S(2)}, u32[]{:S(2)}) %collective-permute-start.20) | collective-permute-done | bytes 23072 | tf_op jit(solution)/shard_map/ppermute | solution.py:224
  49.4 0.6 %combine.1 = bf16[2,16,360]{2,1,0:T(8,128)(2,1)} custom-call(f32[32,360]{1,0:T(8,128)S(1)} %get-tuple-element.50.refs_0_, bf16[32,360]{1,0:T(8,128)(2,1)S(1)} %collective-permute-done.18.refs_1_, bf16[32,360]{1,0:T(8,128)(2,1)S(1)} %collective-permute-done.19.refs_2_, bf16[32,360]{1,0:T(8,128)(2,1)S(1)} %collective-permute-done.20.refs_3_, ...), custom_call_target="tpu_custom_call" | custom-call | bytes 184320 | tf_op jit(solution)/shard_map/combine/pallas_call | solution.py:420
  (38 shorter events, 6.1 us)
Async XLA Ops:
  4.2 26.3 %copy-start = (bf16[1,2880,180]{1,2,0:T(8,128)(2,1)S(1)}, bf16[1,2880,180]{1,2,0:T(8,128)(2,1)}, u32[]{:S(2)}) copy-start(bf16[1,2880,180]{1,2,0:T(8,128)(2,1)} %param.23) | copy-start | bytes 3110404
  4.2 26.3 %copy-start.1 = (bf16[1,2880,180]{1,2,0:T(8,128)(2,1)S(1)}, bf16[1,2880,180]{1,2,0:T(8,128)(2,1)}, u32[]{:S(2)}) copy-start(bf16[1,2880,180]{1,2,0:T(8,128)(2,1)} %param.24) | copy-start | bytes 3110404
  4.2 1.5 %collective-permute-start = (bf16[4,32,384]{2,1,0:T(8,128)(2,1)S(1)}, bf16[4,32,384]{2,1,0:T(8,128)(2,1)S(1)}, u32[]{:S(2)}, u32[]{:S(2)}) collective-permute-start(bf16[4,32,384]{2,1,0:T(8,128)(2,1)S(1)} %get-tuple-element.32), channel_id=1, source_target_pairs={{0,16},{16,0},{1,17},{17,1},{2,18},{18,2},{3,19},{19,3},{4,20},{20... | collective-permute-start | bytes 294920 | tf_op jit(solution)/shard_map/ppermute | solution.py:224
  4.8 27.0 %copy-start.2 = (bf16[1,180,2880]{2,1,0:T(8,128)(2,1)S(1)}, bf16[1,180,2880]{2,1,0:T(8,128)(2,1)}, u32[]{:S(2)}) copy-start(bf16[1,180,2880]{2,1,0:T(8,128)(2,1)} %param.25) | copy-start | bytes 3110404
  5.8 5.6 %collective-permute-start.1 = (bf16[32,384]{1,0:T(8,128)(2,1)S(1)}, bf16[32,384]{1,0:T(8,128)(2,1)S(1)}, u32[]{:S(2)}, u32[]{:S(2)}) collective-permute-start(bf16[32,384]{1,0:T(8,128)(2,1)S(1)} %get-tuple-element.34), channel_id=1, source_target_pairs={{0,3},{1,2},{2,1},{3,0},{16,19},{17,18},{18,17},{19,16},{4,7},{5,6... | collective-permute-start | bytes 73736 | tf_op jit(solution)/shard_map/ppermute | solution.py:230
  9.6 3.8 %collective-permute-start.2 = (bf16[32,384]{1,0:T(8,128)(2,1)S(1)}, bf16[32,384]{1,0:T(8,128)(2,1)S(1)}, u32[]{:S(2)}, u32[]{:S(2)}) collective-permute-start(bf16[32,384]{1,0:T(8,128)(2,1)S(1)} %get-tuple-element.35), channel_id=1, source_target_pairs={{0,1},{1,0},{2,3},{3,2},{16,18},{17,19},{18,16},{19,17},{4,5},{5,4... | collective-permute-start | bytes 73736 | tf_op jit(solution)/shard_map/ppermute | solution.py:230
  10.1 3.8 %collective-permute-start.3 = (bf16[32,384]{1,0:T(8,128)(2,1)S(1)}, bf16[32,384]{1,0:T(8,128)(2,1)S(1)}, u32[]{:S(2)}, u32[]{:S(2)}) collective-permute-start(bf16[32,384]{1,0:T(8,128)(2,1)S(1)} %get-tuple-element.36), channel_id=1, source_target_pairs={{0,2},{1,3},{2,0},{3,1},{16,17},{17,16},{18,19},{19,18},{4,6},{5,7... | collective-permute-start | bytes 73736 | tf_op jit(solution)/shard_map/ppermute | solution.py:230
  14.0 4.5 %collective-permute-start.4 = (bf16[32,384]{1,0:T(8,128)(2,1)S(1)}, bf16[32,384]{1,0:T(8,128)(2,1)S(1)}, u32[]{:S(2)}, u32[]{:S(2)}) collective-permute-start(bf16[32,384]{1,0:T(8,128)(2,1)S(1)} %sum.1), channel_id=1, source_target_pairs={{0,4},{4,0},{8,12},{12,8},{1,5},{5,1},{9,13},{13,9},{2,6},{6,2},{1... | collective-permute-start | bytes 73736 | tf_op jit(solution)/shard_map/ppermute | solution.py:224
  15.6 5.1 %collective-permute-start.5 = (bf16[32,384]{1,0:T(8,128)(2,1)S(1)}, bf16[32,384]{1,0:T(8,128)(2,1)S(1)}, u32[]{:S(2)}, u32[]{:S(2)}) collective-permute-start(bf16[32,384]{1,0:T(8,128)(2,1)S(1)} %sum.1), channel_id=1, source_target_pairs={{0,8},{4,12},{8,0},{12,4},{1,9},{5,13},{9,1},{13,5},{2,10},{6,14},... | collective-permute-start | bytes 73736 | tf_op jit(solution)/shard_map/ppermute | solution.py:224
  18.2 5.6 %collective-permute-start.6 = (bf16[32,384]{1,0:T(8,128)(2,1)S(1)}, bf16[32,384]{1,0:T(8,128)(2,1)S(1)}, u32[]{:S(2)}, u32[]{:S(2)}) collective-permute-start(bf16[32,384]{1,0:T(8,128)(2,1)S(1)} %sum.1), channel_id=1, source_target_pairs={{0,12},{4,8},{8,4},{12,0},{1,13},{5,9},{9,5},{13,1},{2,14},{6,10},... | collective-permute-start | bytes 73736 | tf_op jit(solution)/shard_map/ppermute | solution.py:224
  23.9 5.6 %collective-permute-start.7 = (bf16[4,32,384]{2,1,0:T(8,128)(2,1)S(1)}, bf16[4,32,384]{2,1,0:T(8,128)(2,1)S(1)}, u32[]{:S(2)}, u32[]{:S(2)}) collective-permute-start(bf16[4,32,384]{2,1,0:T(8,128)(2,1)S(1)} %pad_maximum_fusion.refs_0_), channel_id=1, source_target_pairs={{0,3},{1,2},{2,1},{3,0},{16,19},{17,18},{18,17},{19,16},{4,7},{5,6... | collective-permute-start | bytes 294920 | tf_op jit(solution)/shard_map/ppermute | solution.py:230
  25.4 4.6 %collective-permute-start.8 = (bf16[4,32,384]{2,1,0:T(8,128)(2,1)S(1)}, bf16[4,32,384]{2,1,0:T(8,128)(2,1)S(1)}, u32[]{:S(2)}, u32[]{:S(2)}) collective-permute-start(bf16[4,32,384]{2,1,0:T(8,128)(2,1)S(1)} %pad_maximum_fusion.refs_0_), channel_id=1, source_target_pairs={{0,1},{1,0},{2,3},{3,2},{16,18},{17,19},{18,16},{19,17},{4,5},{5,4... | collective-permute-start | bytes 294920 | tf_op jit(solution)/shard_map/ppermute | solution.py:230
  25.9 4.6 %collective-permute-start.9 = (bf16[4,32,384]{2,1,0:T(8,128)(2,1)S(1)}, bf16[4,32,384]{2,1,0:T(8,128)(2,1)S(1)}, u32[]{:S(2)}, u32[]{:S(2)}) collective-permute-start(bf16[4,32,384]{2,1,0:T(8,128)(2,1)S(1)} %pad_maximum_fusion.refs_0_), channel_id=1, source_target_pairs={{0,2},{1,3},{2,0},{3,1},{16,17},{17,16},{18,19},{19,18},{4,6},{5,7... | collective-permute-start | bytes 294920 | tf_op jit(solution)/shard_map/ppermute | solution.py:230
  27.4 3.7 %collective-permute-start.10 = (bf16[4,32,384]{2,1,0:T(8,128)(2,1)S(1)}, bf16[4,32,384]{2,1,0:T(8,128)(2,1)S(1)}, u32[]{:S(2)}, u32[]{:S(2)}) collective-permute-start(bf16[4,32,384]{2,1,0:T(8,128)(2,1)S(1)} %pad_maximum_fusion.refs_0_), channel_id=1, source_target_pairs={{0,16},{16,0},{1,17},{17,1},{2,18},{18,2},{3,19},{19,3},{4,20},{20... | collective-permute-start | bytes 294920 | tf_op jit(solution)/shard_map/ppermute | solution.py:224
  29.4 1.7 %collective-permute-start.11 = (bf16[4,32,384]{2,1,0:T(8,128)(2,1)S(1)}, bf16[4,32,384]{2,1,0:T(8,128)(2,1)S(1)}, u32[]{:S(2)}, u32[]{:S(2)}) collective-permute-start(bf16[4,32,384]{2,1,0:T(8,128)(2,1)S(1)} %collective-permute-done.7.refs_1_), channel_id=1, source_target_pairs={{0,16},{16,0},{1,17},{17,1},{2,18},{18,2},{3,19},{19,3},{4,20},{20... | collective-permute-start | bytes 294920 | tf_op jit(solution)/shard_map/ppermute | solution.py:224
  30.0 1.3 %collective-permute-start.12 = (bf16[4,32,384]{2,1,0:T(8,128)(2,1)S(1)}, bf16[4,32,384]{2,1,0:T(8,128)(2,1)S(1)}, u32[]{:S(2)}, u32[]{:S(2)}) collective-permute-start(bf16[4,32,384]{2,1,0:T(8,128)(2,1)S(1)} %collective-permute-done.8.refs_2_), channel_id=1, source_target_pairs={{0,16},{16,0},{1,17},{17,1},{2,18},{18,2},{3,19},{19,3},{4,20},{20... | collective-permute-start | bytes 294920 | tf_op jit(solution)/shard_map/ppermute | solution.py:224
  30.5 1.3 %collective-permute-start.13 = (bf16[4,32,384]{2,1,0:T(8,128)(2,1)S(1)}, bf16[4,32,384]{2,1,0:T(8,128)(2,1)S(1)}, u32[]{:S(2)}, u32[]{:S(2)}) collective-permute-start(bf16[4,32,384]{2,1,0:T(8,128)(2,1)S(1)} %collective-permute-done.9.refs_3_), channel_id=1, source_target_pairs={{0,16},{16,0},{1,17},{17,1},{2,18},{18,2},{3,19},{19,3},{4,20},{20... | collective-permute-start | bytes 294920 | tf_op jit(solution)/shard_map/ppermute | solution.py:224
  33.0 1.8 %collective-permute-start.14 = (bf16[4,128,360]{2,1,0:T(8,128)(2,1)S(1)}, bf16[4,128,360]{2,1,0:T(8,128)(2,1)S(1)}, u32[]{:S(2)}, u32[]{:S(2)}) collective-permute-start(bf16[4,128,360]{2,1,0:T(8,128)(2,1)S(1)} %get-tuple-element.45), channel_id=1, source_target_pairs={{0,16},{16,0},{1,17},{17,1},{2,18},{18,2},{3,19},{19,3},{4,20},{20... | collective-permute-start | bytes 1105928 | tf_op jit(solution)/shard_map/ppermute | solution.py:224
  34.8 5.9 %collective-permute-start.15 = (bf16[128,360]{1,0:T(8,128)(2,1)S(1)}, bf16[128,360]{1,0:T(8,128)(2,1)S(1)}, u32[]{:S(2)}, u32[]{:S(2)}) collective-permute-start(bf16[128,360]{1,0:T(8,128)(2,1)S(1)} %get-tuple-element.47), channel_id=1, source_target_pairs={{0,3},{1,2},{2,1},{3,0},{16,19},{17,18},{18,17},{19,16},{4,7},{5,6... | collective-permute-start | bytes 276488 | tf_op jit(solution)/shard_map/ppermute | solution.py:230
  37.4 5.4 %collective-permute-start.16 = (bf16[128,360]{1,0:T(8,128)(2,1)S(1)}, bf16[128,360]{1,0:T(8,128)(2,1)S(1)}, u32[]{:S(2)}, u32[]{:S(2)}) collective-permute-start(bf16[128,360]{1,0:T(8,128)(2,1)S(1)} %get-tuple-element.48), channel_id=1, source_target_pairs={{0,1},{1,0},{2,3},{3,2},{16,18},{17,19},{18,16},{19,17},{4,5},{5,4... | collective-permute-start | bytes 276488 | tf_op jit(solution)/shard_map/ppermute | solution.py:230
  37.9 4.9 %collective-permute-start.17 = (bf16[128,360]{1,0:T(8,128)(2,1)S(1)}, bf16[128,360]{1,0:T(8,128)(2,1)S(1)}, u32[]{:S(2)}, u32[]{:S(2)}) collective-permute-start(bf16[128,360]{1,0:T(8,128)(2,1)S(1)} %get-tuple-element.49), channel_id=1, source_target_pairs={{0,2},{1,3},{2,0},{3,1},{16,17},{17,16},{18,19},{19,18},{4,6},{5,7... | collective-permute-start | bytes 276488 | tf_op jit(solution)/shard_map/ppermute | solution.py:230
  42.9 4.5 %collective-permute-start.18 = (bf16[32,360]{1,0:T(8,128)(2,1)S(1)}, bf16[32,360]{1,0:T(8,128)(2,1)S(1)}, u32[]{:S(2)}, u32[]{:S(2)}) collective-permute-start(bf16[32,360]{1,0:T(8,128)(2,1)S(1)} %get-tuple-element.51), channel_id=1, source_target_pairs={{0,4},{4,0},{8,12},{12,8},{1,5},{5,1},{9,13},{13,9},{2,6},{6,2},{1... | collective-permute-start | bytes 69128 | tf_op jit(solution)/shard_map/ppermute | solution.py:224
  42.9 4.9 %collective-permute-start.19 = (bf16[32,360]{1,0:T(8,128)(2,1)S(1)}, bf16[32,360]{1,0:T(8,128)(2,1)S(1)}, u32[]{:S(2)}, u32[]{:S(2)}) collective-permute-start(bf16[32,360]{1,0:T(8,128)(2,1)S(1)} %get-tuple-element.52), channel_id=1, source_target_pairs={{0,8},{4,12},{8,0},{12,4},{1,9},{5,13},{9,1},{13,5},{2,10},{6,14},... | collective-permute-start | bytes 69128 | tf_op jit(solution)/shard_map/ppermute | solution.py:224
  43.8 5.6 %collective-permute-start.20 = (bf16[32,360]{1,0:T(8,128)(2,1)S(1)}, bf16[32,360]{1,0:T(8,128)(2,1)S(1)}, u32[]{:S(2)}, u32[]{:S(2)}) collective-permute-start(bf16[32,360]{1,0:T(8,128)(2,1)S(1)} %get-tuple-element.53), channel_id=1, source_target_pairs={{0,12},{4,8},{8,4},{12,0},{1,13},{5,9},{9,5},{13,1},{2,14},{6,10},... | collective-permute-start | bytes 69128 | tf_op jit(solution)/shard_map/ppermute | solution.py:224
  (1 other events, 26.3 us)

commit v7 on v6

--- a/solution.py
+++ b/solution.py
@@ -437,6 +437,16 @@
         ref[...] = (mine_ref[to] + come_ref[to].astype(jnp.float32)).astype(jnp.bfloat16)
 
 
+def after_core_halves_kernel(mine_ref, come_ref, own_ref, *send_refs):
+    tp, half = lax.axis_index("tp"), mine_ref.shape[1] // 2
+    own_ref[...] = mine_ref[tp] + come_ref[tp].astype(jnp.float32)
+    for mask, second, first in zip(shard_masks(), send_refs[:3], send_refs[3:]):
+        to = jnp.bitwise_xor(tp, mask)
+        part = (mine_ref[to] + come_ref[to].astype(jnp.float32)).astype(jnp.bfloat16)
+        second[...] = part[half:]
+        first[...] = part[:half]
+
+
 def add_all(*refs):
     total = refs[0][...]
     for ref in refs[1:]:
@@ -448,18 +458,14 @@
     refs[-1][...] = add_all(*refs[:-1]).astype(jnp.bfloat16).reshape(refs[-1].shape)
 
 
-def divide_rows_kernel(*refs, groups):
-    total = add_all(*refs[:-groups])
-    outs = refs[-groups:]
+def sum_rows_kernel(own_ref, *refs, line):
+    come, outs = refs[:3], refs[3:]
     lines = outs[0].shape[0]
+    total = own_ref[line:line + len(outs) * lines]
+    for ref in come:
+        total = total + ref[...].astype(jnp.float32)
     for n, out in enumerate(outs):
         out[...] = total[n * lines:(n + 1) * lines].astype(out.dtype)
-
-
-def swap_all(parts, axis):
-    count = len(parts)
-    come = {m: swap(parts[m - 1], axis, m) for m in reversed(range(1, count + 1))}
-    return [come[m] for m in range(1, count + 1)]
 
 
 def scatter_shards(mine, come):
@@ -470,11 +476,12 @@
 
 
 def first_products(pieces, masks, side, x_ref, gain_ref, gate_ref, up_ref, gate_out, up_out, square_out):
-    width, lines = gate_ref.shape[1], x_ref.shape[0]
+    width, lines = gate_ref.shape[1], x_ref.shape[0] // 2
     tp = lax.axis_index("tp")
-    for mask, piece in zip(masks, pieces):
+    for n, piece in enumerate(pieces):
+        half, mask = 1 - n // len(masks), masks[n % len(masks)]
         at = pl.multiple_of(jnp.bitwise_xor(tp, mask) * LANES, LANES)
-        x_ref[:, pl.ds(at, LANES)] = piece[...].reshape(lines, LANES)
+        x_ref[half * lines:(half + 1) * lines, pl.ds(at, LANES)] = piece[...].reshape(lines, LANES)
     for at in range(2):
         start, stop = at * x_ref.shape[1], min((at + 1) * x_ref.shape[1], width)
 
@@ -536,10 +543,11 @@
     middle_ref[...] = row_ref[sec * mine_ref.shape[0] + tp]
 
 
-def experts(gain, w_gate, w_up, w_down, pieces, far_pieces, part):
-    groups, total_rows, _ = pieces[0].shape
-    tps, lines, (width, hidden) = len(pieces), groups * total_rows, w_gate.shape
+def experts(gain, w_gate, w_up, w_down, pieces, part):
     gain, w_gate, w_up = gain.reshape(1, -1), w_gate.swapaxes(0, 1), w_up.swapaxes(0, 1)
+    (hidden, width), tps, (groups, total_rows, _) = w_gate.shape, len(pieces) // 2, pieces[0].shape
+    lines = 2 * groups * total_rows
+    far_pieces = [swap(piece, "sec", 1) for piece in pieces]
     halves = [shape_of((lines, tps * LANES)), shape_of((lines, hidden), jnp.float32), shape_of((lines, hidden), jnp.float32),
               shape_of((lines, 128), jnp.float32)]
     near = call(near_kernel, "near_columns", halves, gain, w_gate, w_up, *pieces, limit=12, flops=2 * lines * width * hidden)
@@ -547,7 +555,7 @@
         far_kernel,
         name="far_columns",
         out_shape=[shape_of((tps, lines, part)), shape_of((lines, hidden)), halves[0]],
-        in_specs=[vmem()] * (8 + tps),
+        in_specs=[vmem()] * (8 + len(far_pieces)),
         out_specs=[vmem()] * 3,
         scratch_shapes=[pltpu.VMEM(half.shape, half.dtype) for half in halves[1:]],
         compiler_params=pltpu.CompilerParams(vmem_limit_bytes=16 * MIB),
@@ -578,15 +586,23 @@
     mine = call(own_projection_kernel, "own_projection", shape_of(other.shape, jnp.float32), mix, held, limit=12,
                 flops=mix.size * width)
     middle = call(sum_kernel, "sum", shape_of((steps * rows, LANES)), *scatter_shards(mine, come), own_x)
-    stacked = jnp.stack([middle] + swap_all([middle] * (groups - 1), "grp"))
-    pieces = [stacked] + shard_swaps([stacked] * (tps - 1))
-    far_pieces = [swap(piece, "sec", 1) for piece in pieces]
-    mine, come, own_middle = experts(expert_gain, w_gate[0], w_up[0], w_down[0], pieces, far_pieces, width // (secs * tps))
-    terms = scatter_shards(mine, come)
-    lines, part = steps * rows, terms[0].shape[1]
-    own, *parts = call(functools.partial(divide_rows_kernel, groups=groups), "divide_rows",
-                       [shape_of((lines, part), jnp.float32)] + [shape_of((lines, part))] * (groups - 1), *terms)
-    return call(sum_kernel, "combine", shape_of((steps, rows, part)), own, *swap_all(parts, "grp"), own_middle)
+    nearest, second, third = [swap(middle, "grp", m) for m in (1, 2, 3)]
+    near_rows = jnp.stack([middle, nearest])
+    first_pieces = [near_rows] + shard_swaps([near_rows] * (tps - 1))
+    far_rows = jnp.stack([second, third])
+    second_pieces = [far_rows] + shard_swaps([far_rows] * (tps - 1))
+    part = width // (secs * tps)
+    mine, come, own_middle = experts(expert_gain, w_gate[0], w_up[0], w_down[0], second_pieces + first_pieces, part)
+    lines = steps * rows
+    own, *parts = call(after_core_halves_kernel, "after_core_halves",
+                       [shape_of((groups * lines, part), jnp.float32)] + [shape_of((groups // 2 * lines, part))] * 6, mine, come)
+    second_come, first_come = shard_swaps(parts[:3]), shard_swaps(parts[3:])
+    second, third = call(functools.partial(sum_rows_kernel, line=2 * lines), "sum_far_rows", [shape_of((lines, part))] * 2,
+                         own, *second_come)
+    third, second = swap(third, "grp", 3), swap(second, "grp", 2)
+    own, nearest = call(functools.partial(sum_rows_kernel, line=0), "sum_near_rows",
+                        [shape_of((lines, part), jnp.float32), shape_of((lines, part))], own, *first_come)
+    return call(sum_kernel, "combine", shape_of((steps, rows, part)), own, third, second, swap(nearest, "grp", 1), own_middle)
 
 
 def body(*args):

time: 50.2 us -> 50.3 us (level)
  starting transfers between devices: 21.2 us -> 28.8 us
  waiting for transfers between devices: 20.7 us -> 13.2 us
    ppermute x9 -> x15, starting transfers between devices: 11.6 us -> 18.6 us  [swap_by_core(): return lax.ppermute(value, ('sec', axis), pairs)]
    ppermute x9 -> x15, waiting for transfers between devices: 11.2 us -> 7.14 us  [swap_by_core(): return lax.ppermute(value, ('sec', axis), pairs)]
    ppermute x12 -> x16, waiting for transfers between devices: 9.52 us -> 6.08 us  [swap(): return lax.ppermute(value, axes, [(i, i ^ mask) for i in range(size)])]
    ppermute x12 -> x16, starting transfers between devices: 9.68 us -> 10.2 us  [swap(): return lax.ppermute(value, axes, [(i, i ^ mask) for i in range(size)])]
    pallas_call x7 -> x8, Pallas kernels: 1.94 us -> 1.94 us  [call(): pl.pallas_call(kernel, name=name, out_shape=outs, in_specs=[vmem()] * len...]
  transfers between devices with their start and end apart: 21 -> 31, of which waited for: 16 -> 16; matrix products, arithmetic and copies ran while one was open for 0% -> 0% of each run, Pallas kernels for 3% -> 4%
where the time goes in v7:
time: 50.3 us; the launch traced here: 50.1 us
  starting transfers between devices  28.8 us (57%)
  waiting for transfers between devices  13.2 us (26%)
  Pallas kernels  7.87 us (16%)
    ppermute x15, starting transfers between devices, swap_by_core(): return lax.ppermute(value, ('sec', axis), pairs)  18.6 us
    ppermute x16, starting transfers between devices, swap(): return lax.ppermute(value, axes, [(i, i ^ mask) for i in range(size)])  10.2 us
    ppermute x15, waiting for transfers between devices, swap_by_core(): return lax.ppermute(value, ('sec', axis), pairs)  7.14 us
    ppermute x16, waiting for transfers between devices, swap(): return lax.ppermute(value, axes, [(i, i ^ mask) for i in range(size)])  6.08 us
    pallas_call x1, Pallas kernels, attention_partial(): pl.pallas_call(attention_kernel, name='attention', out_shape=[shape_of((t...  4.19 us
    pallas_call x8, Pallas kernels, call(): pl.pallas_call(kernel, name=name, out_shape=outs, in_specs=[vmem()] * len...  1.94 us
    pallas_call x1, Pallas kernels, experts(): pl.pallas_call(far_kernel, name='far_columns', out_shape=[shape_of((tps,...  1.17 us
  transfers between devices with their start and end apart: 31, of which 16 were waited for; matrix products, arithmetic and copies ran while one was open for 0% of the time, Pallas kernels for 4%

profile of v7, /device:TPU:0, one launch (start us, length us, event | category | flops | bytes accessed | tf_op | source)
XLA Modules:
  0.0 50.1 jit_solution(1015608394099018788)
XLA Ops:
  0.0 4.2 %attention.1 = (bf16[4,32,384]{2,1,0:T(8,128)(2,1)S(1)}, f32[32,384]{1,0:T(8,128)S(1)}, bf16[32,512]{1,0:T(8,128)(2,1)S(1)}, bf16[2880,512]{1,0:T(8,128)(2,1)S(1)}) custom-call(s32[16]{0:T(128)} %lengths_hbm.1, f32[8]{0:T(128)} %sinks_hbm.1, s32[2,4,16]{2,1,0:T(4,128)} %bitcast.31, f32[2,4,16]{2,1,0:T(4,128)} %bitcast.32, f32[2880]{0:T(1024)} %gain_hbm.1, ...), custom_call_target="tpu_custom_call" | custom-call | tf_op jit(solution)/shard_map/attention/pallas_call | solution.py:391
  5.8 3.8 %collective-permute-start.1 = (bf16[32,384]{1,0:T(8,128)(2,1)S(1)}, bf16[32,384]{1,0:T(8,128)(2,1)S(1)}, u32[]{:S(2)}, u32[]{:S(2)}) collective-permute-start(bf16[32,384]{1,0:T(8,128)(2,1)S(1)} %get-tuple-element.37), channel_id=1, source_target_pairs={{0,3},{1,2},{2,1},{3,0},{16,19},{17,18},{18,17},{19,16},{4,7},{5,6... | collective-permute-start | bytes 73736 | tf_op jit(solution)/shard_map/ppermute | solution.py:230
  10.2 1.2 %collective-permute-done.1.refs_1_ = bf16[32,384]{1,0:T(8,128)(2,1)S(1)} collective-permute-done((bf16[32,384]{1,0:T(8,128)(2,1)S(1)}, bf16[32,384]{1,0:T(8,128)(2,1)S(1)}, u32[]{:S(2)}, u32[]{:S(2)}) %collective-permute-start.1) | collective-permute-done | bytes 24608 | tf_op jit(solution)/shard_map/ppermute | solution.py:230
  11.4 2.0 %collective-permute-done.2.refs_2_ = bf16[32,384]{1,0:T(8,128)(2,1)S(1)} collective-permute-done((bf16[32,384]{1,0:T(8,128)(2,1)S(1)}, bf16[32,384]{1,0:T(8,128)(2,1)S(1)}, u32[]{:S(2)}, u32[]{:S(2)}) %collective-permute-start.2) | collective-permute-done | bytes 24608 | tf_op jit(solution)/shard_map/ppermute | solution.py:230
  14.0 1.6 %collective-permute-start.9 = (bf16[32,384]{1,0:T(8,128)(2,1)S(1)}, bf16[32,384]{1,0:T(8,128)(2,1)S(1)}, u32[]{:S(2)}, u32[]{:S(2)}) collective-permute-start(bf16[32,384]{1,0:T(8,128)(2,1)S(1)} %sum.1), channel_id=1, source_target_pairs={{0,4},{4,0},{8,12},{12,8},{1,5},{5,1},{9,13},{13,9},{2,6},{6,2},{1... | collective-permute-start | bytes 73736 | tf_op jit(solution)/shard_map/ppermute | solution.py:224
  15.6 2.6 %collective-permute-start.4 = (bf16[32,384]{1,0:T(8,128)(2,1)S(1)}, bf16[32,384]{1,0:T(8,128)(2,1)S(1)}, u32[]{:S(2)}, u32[]{:S(2)}) collective-permute-start(bf16[32,384]{1,0:T(8,128)(2,1)S(1)} %sum.1), channel_id=1, source_target_pairs={{0,8},{4,12},{8,0},{12,4},{1,9},{5,13},{9,1},{13,5},{2,10},{6,14},... | collective-permute-start | bytes 73736 | tf_op jit(solution)/shard_map/ppermute | solution.py:224
  18.4 1.5 %collective-permute-start.10 = (bf16[2,32,384]{2,1,0:T(8,128)(2,1)S(1)}, bf16[2,32,384]{2,1,0:T(8,128)(2,1)S(1)}, u32[]{:S(2)}, u32[]{:S(2)}) collective-permute-start(bf16[2,32,384]{2,1,0:T(8,128)(2,1)S(1)} %pad_maximum_fusion.1.refs_4_), channel_id=1, source_target_pairs={{0,3},{1,2},{2,1},{3,0},{16,19},{17,18},{18,17},{19,16},{4,7},{5,6... | collective-permute-start | bytes 147464 | tf_op jit(solution)/shard_map/ppermute | solution.py:230
  20.3 1.7 %collective-permute-start.12 = (bf16[2,32,384]{2,1,0:T(8,128)(2,1)S(1)}, bf16[2,32,384]{2,1,0:T(8,128)(2,1)S(1)}, u32[]{:S(2)}, u32[]{:S(2)}) collective-permute-start(bf16[2,32,384]{2,1,0:T(8,128)(2,1)S(1)} %pad_maximum_fusion.1.refs_4_), channel_id=1, source_target_pairs={{0,2},{1,3},{2,0},{3,1},{16,17},{17,16},{18,19},{19,18},{4,6},{5,7... | collective-permute-start | bytes 147464 | tf_op jit(solution)/shard_map/ppermute | solution.py:230
  22.0 1.8 %collective-permute-done.5 = bf16[32,384]{1,0:T(8,128)(2,1)S(1)} collective-permute-done((bf16[32,384]{1,0:T(8,128)(2,1)S(1)}, bf16[32,384]{1,0:T(8,128)(2,1)S(1)}, u32[]{:S(2)}, u32[]{:S(2)}) %collective-permute-start.5) | collective-permute-done | bytes 24608 | tf_op jit(solution)/shard_map/ppermute | solution.py:224
  23.8 1.5 %collective-permute-start.6 = (bf16[2,32,384]{2,1,0:T(8,128)(2,1)S(1)}, bf16[2,32,384]{2,1,0:T(8,128)(2,1)S(1)}, u32[]{:S(2)}, u32[]{:S(2)}) collective-permute-start(bf16[2,32,384]{2,1,0:T(8,128)(2,1)S(1)} %pad_maximum_fusion.refs_0_), channel_id=1, source_target_pairs={{0,3},{1,2},{2,1},{3,0},{16,19},{17,18},{18,17},{19,16},{4,7},{5,6... | collective-permute-start | bytes 147464 | tf_op jit(solution)/shard_map/ppermute | solution.py:230
  25.9 1.5 %collective-permute-start.8 = (bf16[2,32,384]{2,1,0:T(8,128)(2,1)S(1)}, bf16[2,32,384]{2,1,0:T(8,128)(2,1)S(1)}, u32[]{:S(2)}, u32[]{:S(2)}) collective-permute-start(bf16[2,32,384]{2,1,0:T(8,128)(2,1)S(1)} %pad_maximum_fusion.refs_0_), channel_id=1, source_target_pairs={{0,2},{1,3},{2,0},{3,1},{16,17},{17,16},{18,19},{19,18},{4,6},{5,7... | collective-permute-start | bytes 147464 | tf_op jit(solution)/shard_map/ppermute | solution.py:230
  27.9 1.0 %collective-permute-done.6.refs_1_ = bf16[2,32,384]{2,1,0:T(8,128)(2,1)S(1)} collective-permute-done((bf16[2,32,384]{2,1,0:T(8,128)(2,1)S(1)}, bf16[2,32,384]{2,1,0:T(8,128)(2,1)S(1)}, u32[]{:S(2)}, u32[]{:S(2)}) %collective-permute-start.6) | collective-permute-done | bytes 49184 | tf_op jit(solution)/shard_map/ppermute | solution.py:230
  31.0 0.6 %near_columns.1 = (bf16[128,1536]{1,0:T(8,128)(2,1)S(1)}, f32[128,180]{1,0:T(8,128)S(1)}, f32[128,180]{1,0:T(8,128)S(1)}, f32[128,128]{1,0:T(8,128)S(1)}) custom-call(f32[1,2880]{1,0:T(1,128)S(1)} %reshape.6.gain_ref, bf16[180,2880]{1,0:T(8,128)(2,1)S(1)} %bitcast.17, bf16[180,2880]{1,0:T(8,128)(2,1)S(1)} %bitcast.19, ...), custom_call_target="tpu_custom_call" | custom-call | flops 132710400 | bytes 3121408 | tf_op jit(solution)/shard_map/near_columns/pallas_call | solution.py:420
  31.9 1.2 %far_columns.1 = (bf16[4,128,360]{2,1,0:T(8,128)(2,1)S(1)}, bf16[128,180]{1,0:T(8,128)(2,1)S(1)}, bf16[128,1536]{1,0:T(8,128)(2,1)S(1)}) custom-call(f32[1,2880]{1,0:T(1,128)S(1)} %reshape.6.gain_ref, bf16[180,2880]{1,0:T(8,128)(2,1)S(1)} %bitcast.18, bf16[180,2880]{1,0:T(8,128)(2,1)S(1)} %bitcast.20, bf16[180,2880]{1,0:T(8,128)(2,1)S(1)} %bitcast.21, ...), custom_call_target="tpu_custom_call" | custom-call | tf_op jit(solution)/shard_map/far_columns/pallas_call | solution.py:554
  34.0 0.8 %collective-permute-done.21.come_ref = bf16[4,128,360]{2,1,0:T(8,128)(2,1)S(1)} collective-permute-done((bf16[4,128,360]{2,1,0:T(8,128)(2,1)S(1)}, bf16[4,128,360]{2,1,0:T(8,128)(2,1)S(1)}, u32[]{:S(2)}, u32[]{:S(2)}) %collective-permute-start.21) | collective-permute-done | bytes 368672 | tf_op jit(solution)/shard_map/ppermute | solution.py:224
  34.9 2.5 %collective-permute-start.25 = (bf16[64,360]{1,0:T(8,128)(2,1)S(1)}, bf16[64,360]{1,0:T(8,128)(2,1)S(1)}, u32[]{:S(2)}, u32[]{:S(2)}) collective-permute-start(bf16[64,360]{1,0:T(8,128)(2,1)S(1)} %get-tuple-element.54), channel_id=1, source_target_pairs={{0,3},{1,2},{2,1},{3,0},{16,19},{17,18},{18,17},{19,16},{4,7},{5,6... | collective-permute-start | bytes 138248 | tf_op jit(solution)/shard_map/ppermute | solution.py:230
  38.5 2.5 %collective-permute-start.22 = (bf16[64,360]{1,0:T(8,128)(2,1)S(1)}, bf16[64,360]{1,0:T(8,128)(2,1)S(1)}, u32[]{:S(2)}, u32[]{:S(2)}) collective-permute-start(bf16[64,360]{1,0:T(8,128)(2,1)S(1)} %get-tuple-element.50), channel_id=1, source_target_pairs={{0,3},{1,2},{2,1},{3,0},{16,19},{17,18},{18,17},{19,16},{4,7},{5,6... | collective-permute-start | bytes 138248 | tf_op jit(solution)/shard_map/ppermute | solution.py:230
  42.1 1.9 %collective-permute-start.28 = (bf16[32,360]{1,0:T(8,128)(2,1)S(1)}, bf16[32,360]{1,0:T(8,128)(2,1)S(1)}, u32[]{:S(2)}, u32[]{:S(2)}) collective-permute-start(bf16[32,360]{1,0:T(8,128)(2,1)S(1)} %get-tuple-element.57), channel_id=1, source_target_pairs={{0,12},{4,8},{8,4},{12,0},{1,13},{5,9},{9,5},{13,1},{2,14},{6,10},... | collective-permute-start | bytes 69128 | tf_op jit(solution)/shard_map/ppermute | solution.py:224
  44.3 0.7 %collective-permute-done.23.refs_1_ = bf16[64,360]{1,0:T(8,128)(2,1)S(1)} collective-permute-done((bf16[64,360]{1,0:T(8,128)(2,1)S(1)}, bf16[64,360]{1,0:T(8,128)(2,1)S(1)}, u32[]{:S(2)}, u32[]{:S(2)}) %collective-permute-start.23) | collective-permute-done | bytes 46112 | tf_op jit(solution)/shard_map/ppermute | solution.py:230
  45.6 1.1 %collective-permute-start.30 = (bf16[32,360]{1,0:T(8,128)(2,1)S(1)}, bf16[32,360]{1,0:T(8,128)(2,1)S(1)}, u32[]{:S(2)}, u32[]{:S(2)}) collective-permute-start(bf16[32,360]{1,0:T(8,128)(2,1)S(1)} %get-tuple-element.59), channel_id=1, source_target_pairs={{0,4},{4,0},{8,12},{12,8},{1,5},{5,1},{9,13},{13,9},{2,6},{6,2},{1... | collective-permute-start | bytes 69128 | tf_op jit(solution)/shard_map/ppermute | solution.py:224
  46.7 1.1 %collective-permute-done.28.refs_1_ = bf16[32,360]{1,0:T(8,128)(2,1)S(1)} collective-permute-done((bf16[32,360]{1,0:T(8,128)(2,1)S(1)}, bf16[32,360]{1,0:T(8,128)(2,1)S(1)}, u32[]{:S(2)}, u32[]{:S(2)}) %collective-permute-start.28) | collective-permute-done | bytes 23072 | tf_op jit(solution)/shard_map/ppermute | solution.py:224
  47.8 0.9 %collective-permute-done.29.refs_2_ = bf16[32,360]{1,0:T(8,128)(2,1)S(1)} collective-permute-done((bf16[32,360]{1,0:T(8,128)(2,1)S(1)}, bf16[32,360]{1,0:T(8,128)(2,1)S(1)}, u32[]{:S(2)}, u32[]{:S(2)}) %collective-permute-start.29) | collective-permute-done | bytes 23072 | tf_op jit(solution)/shard_map/ppermute | solution.py:224
  48.7 0.8 %collective-permute-done.30.refs_3_ = bf16[32,360]{1,0:T(8,128)(2,1)S(1)} collective-permute-done((bf16[32,360]{1,0:T(8,128)(2,1)S(1)}, bf16[32,360]{1,0:T(8,128)(2,1)S(1)}, u32[]{:S(2)}, u32[]{:S(2)}) %collective-permute-start.30) | collective-permute-done | bytes 23072 | tf_op jit(solution)/shard_map/ppermute | solution.py:224
  49.5 0.6 %combine.1 = bf16[2,16,360]{2,1,0:T(8,128)(2,1)} custom-call(f32[32,360]{1,0:T(8,128)S(1)} %get-tuple-element.53.refs_0_, bf16[32,360]{1,0:T(8,128)(2,1)S(1)} %collective-permute-done.28.refs_1_, bf16[32,360]{1,0:T(8,128)(2,1)S(1)} %collective-permute-done.29.refs_2_, bf16[32,360]{1,0:T(8,128)(2,1)S(1)} %collective-permute-done.30.refs_3_, ...), custom_call_target="tpu_custom_call" | custom-call | bytes 184320 | tf_op jit(solution)/shard_map/combine/pallas_call | solution.py:420
  (60 shorter events, 10.8 us)
Async XLA Ops:
  5.8 5.6 %collective-permute-start.1 = (bf16[32,384]{1,0:T(8,128)(2,1)S(1)}, bf16[32,384]{1,0:T(8,128)(2,1)S(1)}, u32[]{:S(2)}, u32[]{:S(2)}) collective-permute-start(bf16[32,384]{1,0:T(8,128)(2,1)S(1)} %get-tuple-element.37), channel_id=1, source_target_pairs={{0,3},{1,2},{2,1},{3,0},{16,19},{17,18},{18,17},{19,16},{4,7},{5,6... | collective-permute-start | bytes 73736 | tf_op jit(solution)/shard_map/ppermute | solution.py:230
  9.6 3.8 %collective-permute-start.2 = (bf16[32,384]{1,0:T(8,128)(2,1)S(1)}, bf16[32,384]{1,0:T(8,128)(2,1)S(1)}, u32[]{:S(2)}, u32[]{:S(2)}) collective-permute-start(bf16[32,384]{1,0:T(8,128)(2,1)S(1)} %get-tuple-element.38), channel_id=1, source_target_pairs={{0,1},{1,0},{2,3},{3,2},{16,18},{17,19},{18,16},{19,17},{4,5},{5,4... | collective-permute-start | bytes 73736 | tf_op jit(solution)/shard_map/ppermute | solution.py:230
  10.1 3.8 %collective-permute-start.3 = (bf16[32,384]{1,0:T(8,128)(2,1)S(1)}, bf16[32,384]{1,0:T(8,128)(2,1)S(1)}, u32[]{:S(2)}, u32[]{:S(2)}) collective-permute-start(bf16[32,384]{1,0:T(8,128)(2,1)S(1)} %get-tuple-element.39), channel_id=1, source_target_pairs={{0,2},{1,3},{2,0},{3,1},{16,17},{17,16},{18,19},{19,18},{4,6},{5,7... | collective-permute-start | bytes 73736 | tf_op jit(solution)/shard_map/ppermute | solution.py:230
  14.0 4.5 %collective-permute-start.9 = (bf16[32,384]{1,0:T(8,128)(2,1)S(1)}, bf16[32,384]{1,0:T(8,128)(2,1)S(1)}, u32[]{:S(2)}, u32[]{:S(2)}) collective-permute-start(bf16[32,384]{1,0:T(8,128)(2,1)S(1)} %sum.1), channel_id=1, source_target_pairs={{0,4},{4,0},{8,12},{12,8},{1,5},{5,1},{9,13},{13,9},{2,6},{6,2},{1... | collective-permute-start | bytes 73736 | tf_op jit(solution)/shard_map/ppermute | solution.py:224
  15.6 6.4 %collective-permute-start.4 = (bf16[32,384]{1,0:T(8,128)(2,1)S(1)}, bf16[32,384]{1,0:T(8,128)(2,1)S(1)}, u32[]{:S(2)}, u32[]{:S(2)}) collective-permute-start(bf16[32,384]{1,0:T(8,128)(2,1)S(1)} %sum.1), channel_id=1, source_target_pairs={{0,8},{4,12},{8,0},{12,4},{1,9},{5,13},{9,1},{13,5},{2,10},{6,14},... | collective-permute-start | bytes 73736 | tf_op jit(solution)/shard_map/ppermute | solution.py:224
  18.2 5.6 %collective-permute-start.5 = (bf16[32,384]{1,0:T(8,128)(2,1)S(1)}, bf16[32,384]{1,0:T(8,128)(2,1)S(1)}, u32[]{:S(2)}, u32[]{:S(2)}) collective-permute-start(bf16[32,384]{1,0:T(8,128)(2,1)S(1)} %sum.1), channel_id=1, source_target_pairs={{0,12},{4,8},{8,4},{12,0},{1,13},{5,9},{9,5},{13,1},{2,14},{6,10},... | collective-permute-start | bytes 73736 | tf_op jit(solution)/shard_map/ppermute | solution.py:224
  18.4 7.4 %collective-permute-start.10 = (bf16[2,32,384]{2,1,0:T(8,128)(2,1)S(1)}, bf16[2,32,384]{2,1,0:T(8,128)(2,1)S(1)}, u32[]{:S(2)}, u32[]{:S(2)}) collective-permute-start(bf16[2,32,384]{2,1,0:T(8,128)(2,1)S(1)} %pad_maximum_fusion.1.refs_4_), channel_id=1, source_target_pairs={{0,3},{1,2},{2,1},{3,0},{16,19},{17,18},{18,17},{19,16},{4,7},{5,6... | collective-permute-start | bytes 147464 | tf_op jit(solution)/shard_map/ppermute | solution.py:230
  19.9 7.5 %collective-permute-start.11 = (bf16[2,32,384]{2,1,0:T(8,128)(2,1)S(1)}, bf16[2,32,384]{2,1,0:T(8,128)(2,1)S(1)}, u32[]{:S(2)}, u32[]{:S(2)}) collective-permute-start(bf16[2,32,384]{2,1,0:T(8,128)(2,1)S(1)} %pad_maximum_fusion.1.refs_4_), channel_id=1, source_target_pairs={{0,1},{1,0},{2,3},{3,2},{16,18},{17,19},{18,16},{19,17},{4,5},{5,4... | collective-permute-start | bytes 147464 | tf_op jit(solution)/shard_map/ppermute | solution.py:230
  20.3 7.1 %collective-permute-start.12 = (bf16[2,32,384]{2,1,0:T(8,128)(2,1)S(1)}, bf16[2,32,384]{2,1,0:T(8,128)(2,1)S(1)}, u32[]{:S(2)}, u32[]{:S(2)}) collective-permute-start(bf16[2,32,384]{2,1,0:T(8,128)(2,1)S(1)} %pad_maximum_fusion.1.refs_4_), channel_id=1, source_target_pairs={{0,2},{1,3},{2,0},{3,1},{16,17},{17,16},{18,19},{19,18},{4,6},{5,7... | collective-permute-start | bytes 147464 | tf_op jit(solution)/shard_map/ppermute | solution.py:230
  23.8 5.1 %collective-permute-start.6 = (bf16[2,32,384]{2,1,0:T(8,128)(2,1)S(1)}, bf16[2,32,384]{2,1,0:T(8,128)(2,1)S(1)}, u32[]{:S(2)}, u32[]{:S(2)}) collective-permute-start(bf16[2,32,384]{2,1,0:T(8,128)(2,1)S(1)} %pad_maximum_fusion.refs_0_), channel_id=1, source_target_pairs={{0,3},{1,2},{2,1},{3,0},{16,19},{17,18},{18,17},{19,16},{4,7},{5,6... | collective-permute-start | bytes 147464 | tf_op jit(solution)/shard_map/ppermute | solution.py:230
  25.3 4.1 %collective-permute-start.7 = (bf16[2,32,384]{2,1,0:T(8,128)(2,1)S(1)}, bf16[2,32,384]{2,1,0:T(8,128)(2,1)S(1)}, u32[]{:S(2)}, u32[]{:S(2)}) collective-permute-start(bf16[2,32,384]{2,1,0:T(8,128)(2,1)S(1)} %pad_maximum_fusion.refs_0_), channel_id=1, source_target_pairs={{0,1},{1,0},{2,3},{3,2},{16,18},{17,19},{18,16},{19,17},{4,5},{5,4... | collective-permute-start | bytes 147464 | tf_op jit(solution)/shard_map/ppermute | solution.py:230
  25.9 4.1 %collective-permute-start.8 = (bf16[2,32,384]{2,1,0:T(8,128)(2,1)S(1)}, bf16[2,32,384]{2,1,0:T(8,128)(2,1)S(1)}, u32[]{:S(2)}, u32[]{:S(2)}) collective-permute-start(bf16[2,32,384]{2,1,0:T(8,128)(2,1)S(1)} %pad_maximum_fusion.refs_0_), channel_id=1, source_target_pairs={{0,2},{1,3},{2,0},{3,1},{16,17},{17,16},{18,19},{19,18},{4,6},{5,7... | collective-permute-start | bytes 147464 | tf_op jit(solution)/shard_map/ppermute | solution.py:230
  27.4 2.6 %collective-permute-start.17 = (bf16[2,32,384]{2,1,0:T(8,128)(2,1)S(1)}, bf16[2,32,384]{2,1,0:T(8,128)(2,1)S(1)}, u32[]{:S(2)}, u32[]{:S(2)}) collective-permute-start(bf16[2,32,384]{2,1,0:T(8,128)(2,1)S(1)} %pad_maximum_fusion.1.refs_4_), channel_id=1, source_target_pairs={{0,16},{16,0},{1,17},{17,1},{2,18},{18,2},{3,19},{19,3},{4,20},{20... | collective-permute-start | bytes 147464 | tf_op jit(solution)/shard_map/ppermute | solution.py:224
  27.4 3.1 %collective-permute-start.13 = (bf16[2,32,384]{2,1,0:T(8,128)(2,1)S(1)}, bf16[2,32,384]{2,1,0:T(8,128)(2,1)S(1)}, u32[]{:S(2)}, u32[]{:S(2)}) collective-permute-start(bf16[2,32,384]{2,1,0:T(8,128)(2,1)S(1)} %pad_maximum_fusion.refs_0_), channel_id=1, source_target_pairs={{0,16},{16,0},{1,17},{17,1},{2,18},{18,2},{3,19},{19,3},{4,20},{20... | collective-permute-start | bytes 147464 | tf_op jit(solution)/shard_map/ppermute | solution.py:224
  29.4 2.2 %collective-permute-start.19 = (bf16[2,32,384]{2,1,0:T(8,128)(2,1)S(1)}, bf16[2,32,384]{2,1,0:T(8,128)(2,1)S(1)}, u32[]{:S(2)}, u32[]{:S(2)}) collective-permute-start(bf16[2,32,384]{2,1,0:T(8,128)(2,1)S(1)} %collective-permute-done.11.refs_6_), channel_id=1, source_target_pairs={{0,16},{16,0},{1,17},{17,1},{2,18},{18,2},{3,19},{19,3},{4,20},{20... | collective-permute-start | bytes 147464 | tf_op jit(solution)/shard_map/ppermute | solution.py:224
  34.9 6.5 %collective-permute-start.25 = (bf16[64,360]{1,0:T(8,128)(2,1)S(1)}, bf16[64,360]{1,0:T(8,128)(2,1)S(1)}, u32[]{:S(2)}, u32[]{:S(2)}) collective-permute-start(bf16[64,360]{1,0:T(8,128)(2,1)S(1)} %get-tuple-element.54), channel_id=1, source_target_pairs={{0,3},{1,2},{2,1},{3,0},{16,19},{17,18},{18,17},{19,16},{4,7},{5,6... | collective-permute-start | bytes 138248 | tf_op jit(solution)/shard_map/ppermute | solution.py:230
  37.4 4.5 %collective-permute-start.26 = (bf16[64,360]{1,0:T(8,128)(2,1)S(1)}, bf16[64,360]{1,0:T(8,128)(2,1)S(1)}, u32[]{:S(2)}, u32[]{:S(2)}) collective-permute-start(bf16[64,360]{1,0:T(8,128)(2,1)S(1)} %get-tuple-element.55), channel_id=1, source_target_pairs={{0,1},{1,0},{2,3},{3,2},{16,18},{17,19},{18,16},{19,17},{4,5},{5,4... | collective-permute-start | bytes 138248 | tf_op jit(solution)/shard_map/ppermute | solution.py:230
  38.0 4.1 %collective-permute-start.27 = (bf16[64,360]{1,0:T(8,128)(2,1)S(1)}, bf16[64,360]{1,0:T(8,128)(2,1)S(1)}, u32[]{:S(2)}, u32[]{:S(2)}) collective-permute-start(bf16[64,360]{1,0:T(8,128)(2,1)S(1)} %get-tuple-element.56), channel_id=1, source_target_pairs={{0,2},{1,3},{2,0},{3,1},{16,17},{17,16},{18,19},{19,18},{4,6},{5,7... | collective-permute-start | bytes 138248 | tf_op jit(solution)/shard_map/ppermute | solution.py:230
  38.5 5.8 %collective-permute-start.22 = (bf16[64,360]{1,0:T(8,128)(2,1)S(1)}, bf16[64,360]{1,0:T(8,128)(2,1)S(1)}, u32[]{:S(2)}, u32[]{:S(2)}) collective-permute-start(bf16[64,360]{1,0:T(8,128)(2,1)S(1)} %get-tuple-element.50), channel_id=1, source_target_pairs={{0,3},{1,2},{2,1},{3,0},{16,19},{17,18},{18,17},{19,16},{4,7},{5,6... | collective-permute-start | bytes 138248 | tf_op jit(solution)/shard_map/ppermute | solution.py:230
  40.9 4.1 %collective-permute-start.23 = (bf16[64,360]{1,0:T(8,128)(2,1)S(1)}, bf16[64,360]{1,0:T(8,128)(2,1)S(1)}, u32[]{:S(2)}, u32[]{:S(2)}) collective-permute-start(bf16[64,360]{1,0:T(8,128)(2,1)S(1)} %get-tuple-element.51), channel_id=1, source_target_pairs={{0,1},{1,0},{2,3},{3,2},{16,18},{17,19},{18,16},{19,17},{4,5},{5,4... | collective-permute-start | bytes 138248 | tf_op jit(solution)/shard_map/ppermute | solution.py:230
  41.5 4.1 %collective-permute-start.24 = (bf16[64,360]{1,0:T(8,128)(2,1)S(1)}, bf16[64,360]{1,0:T(8,128)(2,1)S(1)}, u32[]{:S(2)}, u32[]{:S(2)}) collective-permute-start(bf16[64,360]{1,0:T(8,128)(2,1)S(1)} %get-tuple-element.52), channel_id=1, source_target_pairs={{0,2},{1,3},{2,0},{3,1},{16,17},{17,16},{18,19},{19,18},{4,6},{5,7... | collective-permute-start | bytes 138248 | tf_op jit(solution)/shard_map/ppermute | solution.py:230
  42.1 5.7 %collective-permute-start.28 = (bf16[32,360]{1,0:T(8,128)(2,1)S(1)}, bf16[32,360]{1,0:T(8,128)(2,1)S(1)}, u32[]{:S(2)}, u32[]{:S(2)}) collective-permute-start(bf16[32,360]{1,0:T(8,128)(2,1)S(1)} %get-tuple-element.57), channel_id=1, source_target_pairs={{0,12},{4,8},{8,4},{12,0},{1,13},{5,9},{9,5},{13,1},{2,14},{6,10},... | collective-permute-start | bytes 69128 | tf_op jit(solution)/shard_map/ppermute | solution.py:224
  44.0 4.7 %collective-permute-start.29 = (bf16[32,360]{1,0:T(8,128)(2,1)S(1)}, bf16[32,360]{1,0:T(8,128)(2,1)S(1)}, u32[]{:S(2)}, u32[]{:S(2)}) collective-permute-start(bf16[32,360]{1,0:T(8,128)(2,1)S(1)} %get-tuple-element.58), channel_id=1, source_target_pairs={{0,8},{4,12},{8,0},{12,4},{1,9},{5,13},{9,1},{13,5},{2,10},{6,14},... | collective-permute-start | bytes 69128 | tf_op jit(solution)/shard_map/ppermute | solution.py:224
  45.6 3.9 %collective-permute-start.30 = (bf16[32,360]{1,0:T(8,128)(2,1)S(1)}, bf16[32,360]{1,0:T(8,128)(2,1)S(1)}, u32[]{:S(2)}, u32[]{:S(2)}) collective-permute-start(bf16[32,360]{1,0:T(8,128)(2,1)S(1)} %get-tuple-element.59), channel_id=1, source_target_pairs={{0,4},{4,0},{8,12},{12,8},{1,5},{5,1},{9,13},{13,9},{2,6},{6,2},{1... | collective-permute-start | bytes 69128 | tf_op jit(solution)/shard_map/ppermute | solution.py:224
  (11 other events, 118.4 us)

commit v8 on v7

--- a/solution.py
+++ b/solution.py
@@ -476,12 +476,11 @@
 
 
 def first_products(pieces, masks, side, x_ref, gain_ref, gate_ref, up_ref, gate_out, up_out, square_out):
-    width, lines = gate_ref.shape[1], x_ref.shape[0] // 2
+    width, lines = gate_ref.shape[1], x_ref.shape[0]
     tp = lax.axis_index("tp")
-    for n, piece in enumerate(pieces):
-        half, mask = 1 - n // len(masks), masks[n % len(masks)]
+    for mask, piece in zip(masks, pieces):
         at = pl.multiple_of(jnp.bitwise_xor(tp, mask) * LANES, LANES)
-        x_ref[half * lines:(half + 1) * lines, pl.ds(at, LANES)] = piece[...].reshape(lines, LANES)
+        x_ref[:, pl.ds(at, LANES)] = piece[...].reshape(lines, LANES)
     for at in range(2):
         start, stop = at * x_ref.shape[1], min((at + 1) * x_ref.shape[1], width)
 
@@ -545,8 +544,8 @@
 
 def experts(gain, w_gate, w_up, w_down, pieces, part):
     gain, w_gate, w_up = gain.reshape(1, -1), w_gate.swapaxes(0, 1), w_up.swapaxes(0, 1)
-    (hidden, width), tps, (groups, total_rows, _) = w_gate.shape, len(pieces) // 2, pieces[0].shape
-    lines = 2 * groups * total_rows
+    (hidden, width), tps, (groups, total_rows, _) = w_gate.shape, len(pieces), pieces[0].shape
+    lines = groups * total_rows
     far_pieces = [swap(piece, "sec", 1) for piece in pieces]
     halves = [shape_of((lines, tps * LANES)), shape_of((lines, hidden), jnp.float32), shape_of((lines, hidden), jnp.float32),
               shape_of((lines, 128), jnp.float32)]
@@ -586,13 +585,10 @@
     mine = call(own_projection_kernel, "own_projection", shape_of(other.shape, jnp.float32), mix, held, limit=12,
                 flops=mix.size * width)
     middle = call(sum_kernel, "sum", shape_of((steps * rows, LANES)), *scatter_shards(mine, come), own_x)
-    nearest, second, third = [swap(middle, "grp", m) for m in (1, 2, 3)]
-    near_rows = jnp.stack([middle, nearest])
-    first_pieces = [near_rows] + shard_swaps([near_rows] * (tps - 1))
-    far_rows = jnp.stack([second, third])
-    second_pieces = [far_rows] + shard_swaps([far_rows] * (tps - 1))
+    stacked = jnp.stack([middle] + [swap(middle, "grp", m) for m in range(1, groups)])
+    pieces = [stacked] + shard_swaps([stacked] * (tps - 1))
     part = width // (secs * tps)
-    mine, come, own_middle = experts(expert_gain, w_gate[0], w_up[0], w_down[0], second_pieces + first_pieces, part)
+    mine, come, own_middle = experts(expert_gain, w_gate[0], w_up[0], w_down[0], pieces, part)
     lines = steps * rows
     own, *parts = call(after_core_halves_kernel, "after_core_halves",
                        [shape_of((groups * lines, part), jnp.float32)] + [shape_of((groups // 2 * lines, part))] * 6, mine, come)

time: 50.3 us -> 50.2 us (level)
  starting transfers between devices: 28.8 us -> 21.7 us
  waiting for transfers between devices: 13.2 us -> 20.3 us
    ppermute x16 -> x12, waiting for transfers between devices: 6.08 us -> 10.3 us  [swap(): return lax.ppermute(value, axes, [(i, i ^ mask) for i in range(size)])]
    ppermute x15 -> x12, starting transfers between devices: 18.6 us -> 15 us  [swap_by_core(): return lax.ppermute(value, ('sec', axis), pairs)]
    ppermute x16 -> x12, starting transfers between devices: 10.2 us -> 6.68 us  [swap(): return lax.ppermute(value, axes, [(i, i ^ mask) for i in range(size)])]
    ppermute x15 -> x12, waiting for transfers between devices: 7.14 us -> 10 us  [swap_by_core(): return lax.ppermute(value, ('sec', axis), pairs)]
  transfers between devices with their start and end apart: 31 -> 24, of which waited for: 16 -> 18; matrix products, arithmetic and copies ran while one was open for 0% -> 0% of each run, Pallas kernels for 4% -> 4%
where the time goes in v8:
time: 50.2 us; the launch traced here: 50 us
  starting transfers between devices  21.7 us (43%)
  waiting for transfers between devices  20.3 us (40%)
  Pallas kernels  7.86 us (16%)
    ppermute x12, starting transfers between devices, swap_by_core(): return lax.ppermute(value, ('sec', axis), pairs)  15 us
    ppermute x12, waiting for transfers between devices, swap(): return lax.ppermute(value, axes, [(i, i ^ mask) for i in range(size)])  10.3 us
    ppermute x12, waiting for transfers between devices, swap_by_core(): return lax.ppermute(value, ('sec', axis), pairs)  10 us
    ppermute x12, starting transfers between devices, swap(): return lax.ppermute(value, axes, [(i, i ^ mask) for i in range(size)])  6.68 us
    pallas_call x1, Pallas kernels, attention_partial(): pl.pallas_call(attention_kernel, name='attention', out_shape=[shape_of((t...  4.19 us
    pallas_call x8, Pallas kernels, call(): pl.pallas_call(kernel, name=name, out_shape=outs, in_specs=[vmem()] * len...  1.94 us
    pallas_call x1, Pallas kernels, experts(): pl.pallas_call(far_kernel, name='far_columns', out_shape=[shape_of((tps,...  1.16 us
  transfers between devices with their start and end apart: 24, of which 18 were waited for; matrix products, arithmetic and copies ran while one was open for 0% of the time, Pallas kernels for 4%

profile of v8, /device:TPU:0, one launch (start us, length us, event | category | flops | bytes accessed | tf_op | source)
XLA Modules:
  0.0 50.0 jit_solution(4758501834038964007)
XLA Ops:
  0.0 4.2 %attention.1 = (bf16[4,32,384]{2,1,0:T(8,128)(2,1)S(1)}, f32[32,384]{1,0:T(8,128)S(1)}, bf16[32,512]{1,0:T(8,128)(2,1)S(1)}, bf16[2880,512]{1,0:T(8,128)(2,1)S(1)}) custom-call(s32[16]{0:T(128)} %lengths_hbm.1, f32[8]{0:T(128)} %sinks_hbm.1, s32[2,4,16]{2,1,0:T(4,128)} %bitcast.31, f32[2,4,16]{2,1,0:T(4,128)} %bitcast.32, f32[2880]{0:T(1024)} %gain_hbm.1, ...), custom_call_target="tpu_custom_call" | custom-call | tf_op jit(solution)/shard_map/attention/pallas_call | solution.py:391
  4.2 0.6 %collective-permute-start = (bf16[4,32,384]{2,1,0:T(8,128)(2,1)S(1)}, bf16[4,32,384]{2,1,0:T(8,128)(2,1)S(1)}, u32[]{:S(2)}, u32[]{:S(2)}) collective-permute-start(bf16[4,32,384]{2,1,0:T(8,128)(2,1)S(1)} %get-tuple-element.35), channel_id=1, source_target_pairs={{0,16},{16,0},{1,17},{17,1},{2,18},{18,2},{3,19},{19,3},{4,20},{20... | collective-permute-start | bytes 294920 | tf_op jit(solution)/shard_map/ppermute | solution.py:224
  5.8 3.8 %collective-permute-start.1 = (bf16[32,384]{1,0:T(8,128)(2,1)S(1)}, bf16[32,384]{1,0:T(8,128)(2,1)S(1)}, u32[]{:S(2)}, u32[]{:S(2)}) collective-permute-start(bf16[32,384]{1,0:T(8,128)(2,1)S(1)} %get-tuple-element.37), channel_id=1, source_target_pairs={{0,3},{1,2},{2,1},{3,0},{16,19},{17,18},{18,17},{19,16},{4,7},{5,6... | collective-permute-start | bytes 73736 | tf_op jit(solution)/shard_map/ppermute | solution.py:230
  10.2 1.2 %collective-permute-done.1.refs_1_ = bf16[32,384]{1,0:T(8,128)(2,1)S(1)} collective-permute-done((bf16[32,384]{1,0:T(8,128)(2,1)S(1)}, bf16[32,384]{1,0:T(8,128)(2,1)S(1)}, u32[]{:S(2)}, u32[]{:S(2)}) %collective-permute-start.1) | collective-permute-done | bytes 24608 | tf_op jit(solution)/shard_map/ppermute | solution.py:230
  11.4 2.0 %collective-permute-done.2.refs_2_ = bf16[32,384]{1,0:T(8,128)(2,1)S(1)} collective-permute-done((bf16[32,384]{1,0:T(8,128)(2,1)S(1)}, bf16[32,384]{1,0:T(8,128)(2,1)S(1)}, u32[]{:S(2)}, u32[]{:S(2)}) %collective-permute-start.2) | collective-permute-done | bytes 24608 | tf_op jit(solution)/shard_map/ppermute | solution.py:230
  14.0 1.6 %collective-permute-start.4 = (bf16[32,384]{1,0:T(8,128)(2,1)S(1)}, bf16[32,384]{1,0:T(8,128)(2,1)S(1)}, u32[]{:S(2)}, u32[]{:S(2)}) collective-permute-start(bf16[32,384]{1,0:T(8,128)(2,1)S(1)} %sum.1), channel_id=1, source_target_pairs={{0,4},{4,0},{8,12},{12,8},{1,5},{5,1},{9,13},{13,9},{2,6},{6,2},{1... | collective-permute-start | bytes 73736 | tf_op jit(solution)/shard_map/ppermute | solution.py:224
  15.6 2.6 %collective-permute-start.5 = (bf16[32,384]{1,0:T(8,128)(2,1)S(1)}, bf16[32,384]{1,0:T(8,128)(2,1)S(1)}, u32[]{:S(2)}, u32[]{:S(2)}) collective-permute-start(bf16[32,384]{1,0:T(8,128)(2,1)S(1)} %sum.1), channel_id=1, source_target_pairs={{0,8},{4,12},{8,0},{12,4},{1,9},{5,13},{9,1},{13,5},{2,10},{6,14},... | collective-permute-start | bytes 73736 | tf_op jit(solution)/shard_map/ppermute | solution.py:224
  18.4 2.3 %collective-permute-done.5 = bf16[32,384]{1,0:T(8,128)(2,1)S(1)} collective-permute-done((bf16[32,384]{1,0:T(8,128)(2,1)S(1)}, bf16[32,384]{1,0:T(8,128)(2,1)S(1)}, u32[]{:S(2)}, u32[]{:S(2)}) %collective-permute-start.5) | collective-permute-done | bytes 24608 | tf_op jit(solution)/shard_map/ppermute | solution.py:224
  20.8 3.1 %collective-permute-done.6 = bf16[32,384]{1,0:T(8,128)(2,1)S(1)} collective-permute-done((bf16[32,384]{1,0:T(8,128)(2,1)S(1)}, bf16[32,384]{1,0:T(8,128)(2,1)S(1)}, u32[]{:S(2)}, u32[]{:S(2)}) %collective-permute-start.6) | collective-permute-done | bytes 24608 | tf_op jit(solution)/shard_map/ppermute | solution.py:224
  23.9 1.5 %collective-permute-start.7 = (bf16[4,32,384]{2,1,0:T(8,128)(2,1)S(1)}, bf16[4,32,384]{2,1,0:T(8,128)(2,1)S(1)}, u32[]{:S(2)}, u32[]{:S(2)}) collective-permute-start(bf16[4,32,384]{2,1,0:T(8,128)(2,1)S(1)} %pad_maximum_fusion.refs_0_), channel_id=1, source_target_pairs={{0,3},{1,2},{2,1},{3,0},{16,19},{17,18},{18,17},{19,16},{4,7},{5,6... | collective-permute-start | bytes 294920 | tf_op jit(solution)/shard_map/ppermute | solution.py:230
  25.9 1.5 %collective-permute-start.9 = (bf16[4,32,384]{2,1,0:T(8,128)(2,1)S(1)}, bf16[4,32,384]{2,1,0:T(8,128)(2,1)S(1)}, u32[]{:S(2)}, u32[]{:S(2)}) collective-permute-start(bf16[4,32,384]{2,1,0:T(8,128)(2,1)S(1)} %pad_maximum_fusion.refs_0_), channel_id=1, source_target_pairs={{0,2},{1,3},{2,0},{3,1},{16,17},{17,16},{18,19},{19,18},{4,6},{5,7... | collective-permute-start | bytes 294920 | tf_op jit(solution)/shard_map/ppermute | solution.py:230
  27.4 2.0 %collective-permute-done.7.refs_1_ = bf16[4,32,384]{2,1,0:T(8,128)(2,1)S(1)} collective-permute-done((bf16[4,32,384]{2,1,0:T(8,128)(2,1)S(1)}, bf16[4,32,384]{2,1,0:T(8,128)(2,1)S(1)}, u32[]{:S(2)}, u32[]{:S(2)}) %collective-permute-start.7) | collective-permute-done | bytes 98336 | tf_op jit(solution)/shard_map/ppermute | solution.py:230
  30.5 0.6 %near_columns.1 = (bf16[128,1536]{1,0:T(8,128)(2,1)S(1)}, f32[128,180]{1,0:T(8,128)S(1)}, f32[128,180]{1,0:T(8,128)S(1)}, f32[128,128]{1,0:T(8,128)S(1)}) custom-call(f32[1,2880]{1,0:T(1,128)S(1)} %reshape.6.gain_ref, bf16[180,2880]{1,0:T(8,128)(2,1)S(1)} %bitcast.17, bf16[180,2880]{1,0:T(8,128)(2,1)S(1)} %bitcast.19, ...), custom_call_target="tpu_custom_call" | custom-call | flops 132710400 | bytes 3121408 | tf_op jit(solution)/shard_map/near_columns/pallas_call | solution.py:420
  31.8 1.2 %far_columns.1 = (bf16[4,128,360]{2,1,0:T(8,128)(2,1)S(1)}, bf16[128,180]{1,0:T(8,128)(2,1)S(1)}, bf16[128,1536]{1,0:T(8,128)(2,1)S(1)}) custom-call(f32[1,2880]{1,0:T(1,128)S(1)} %reshape.6.gain_ref, bf16[180,2880]{1,0:T(8,128)(2,1)S(1)} %bitcast.18, bf16[180,2880]{1,0:T(8,128)(2,1)S(1)} %bitcast.20, bf16[180,2880]{1,0:T(8,128)(2,1)S(1)} %bitcast.21, ...), custom_call_target="tpu_custom_call" | custom-call | tf_op jit(solution)/shard_map/far_columns/pallas_call | solution.py:553
  33.2 0.6 %own_columns.1 = (f32[4,128,360]{2,1,0:T(8,128)S(1)}, f32[32,360]{1,0:T(8,128)S(1)}) custom-call(bf16[128,180]{1,0:T(8,128)(2,1)S(1)} %get-tuple-element.45.act_ref, bf16[180,2880]{1,0:T(8,128)(2,1)S(1)} %bitcast.22, bf16[128,1536]{1,0:T(8,128)(2,1)S(1)} %get-tuple-element.41.near_x_ref, bf16[128,1536]{1,0:T(8,128)(2,1)S(1)} %get-tuple-element.46.far_x_ref), custom_call_target="tpu_custom_call" | custom-call | flops 66355200 | bytes 737280 | tf_op jit(solution)/shard_map/own_columns/pallas_call | solution.py:563
  33.8 1.0 %collective-permute-done.14.come_ref = bf16[4,128,360]{2,1,0:T(8,128)(2,1)S(1)} collective-permute-done((bf16[4,128,360]{2,1,0:T(8,128)(2,1)S(1)}, bf16[4,128,360]{2,1,0:T(8,128)(2,1)S(1)}, u32[]{:S(2)}, u32[]{:S(2)}) %collective-permute-start.14) | collective-permute-done | bytes 368672 | tf_op jit(solution)/shard_map/ppermute | solution.py:224
  34.8 2.5 %collective-permute-start.18 = (bf16[64,360]{1,0:T(8,128)(2,1)S(1)}, bf16[64,360]{1,0:T(8,128)(2,1)S(1)}, u32[]{:S(2)}, u32[]{:S(2)}) collective-permute-start(bf16[64,360]{1,0:T(8,128)(2,1)S(1)} %get-tuple-element.54), channel_id=1, source_target_pairs={{0,3},{1,2},{2,1},{3,0},{16,19},{17,18},{18,17},{19,16},{4,7},{5,6... | collective-permute-start | bytes 138248 | tf_op jit(solution)/shard_map/ppermute | solution.py:230
  38.4 2.5 %collective-permute-start.15 = (bf16[64,360]{1,0:T(8,128)(2,1)S(1)}, bf16[64,360]{1,0:T(8,128)(2,1)S(1)}, u32[]{:S(2)}, u32[]{:S(2)}) collective-permute-start(bf16[64,360]{1,0:T(8,128)(2,1)S(1)} %get-tuple-element.50), channel_id=1, source_target_pairs={{0,3},{1,2},{2,1},{3,0},{16,19},{17,18},{18,17},{19,16},{4,7},{5,6... | collective-permute-start | bytes 138248 | tf_op jit(solution)/shard_map/ppermute | solution.py:230
  42.4 1.1 %collective-permute-done.15.refs_0_ = bf16[64,360]{1,0:T(8,128)(2,1)S(1)} collective-permute-done((bf16[64,360]{1,0:T(8,128)(2,1)S(1)}, bf16[64,360]{1,0:T(8,128)(2,1)S(1)}, u32[]{:S(2)}, u32[]{:S(2)}) %collective-permute-start.15) | collective-permute-done | bytes 46112 | tf_op jit(solution)/shard_map/ppermute | solution.py:230
  43.4 1.5 %collective-permute-done.16.refs_1_ = bf16[64,360]{1,0:T(8,128)(2,1)S(1)} collective-permute-done((bf16[64,360]{1,0:T(8,128)(2,1)S(1)}, bf16[64,360]{1,0:T(8,128)(2,1)S(1)}, u32[]{:S(2)}, u32[]{:S(2)}) %collective-permute-start.16) | collective-permute-done | bytes 46112 | tf_op jit(solution)/shard_map/ppermute | solution.py:230
  45.5 1.1 %collective-permute-start.23 = (bf16[32,360]{1,0:T(8,128)(2,1)S(1)}, bf16[32,360]{1,0:T(8,128)(2,1)S(1)}, u32[]{:S(2)}, u32[]{:S(2)}) collective-permute-start(bf16[32,360]{1,0:T(8,128)(2,1)S(1)} %get-tuple-element.59), channel_id=1, source_target_pairs={{0,4},{4,0},{8,12},{12,8},{1,5},{5,1},{9,13},{13,9},{2,6},{6,2},{1... | collective-permute-start | bytes 69128 | tf_op jit(solution)/shard_map/ppermute | solution.py:224
  46.6 1.1 %collective-permute-done.21.refs_1_ = bf16[32,360]{1,0:T(8,128)(2,1)S(1)} collective-permute-done((bf16[32,360]{1,0:T(8,128)(2,1)S(1)}, bf16[32,360]{1,0:T(8,128)(2,1)S(1)}, u32[]{:S(2)}, u32[]{:S(2)}) %collective-permute-start.21) | collective-permute-done | bytes 23072 | tf_op jit(solution)/shard_map/ppermute | solution.py:224
  47.7 1.7 %collective-permute-done.23.refs_3_ = bf16[32,360]{1,0:T(8,128)(2,1)S(1)} collective-permute-done((bf16[32,360]{1,0:T(8,128)(2,1)S(1)}, bf16[32,360]{1,0:T(8,128)(2,1)S(1)}, u32[]{:S(2)}, u32[]{:S(2)}) %collective-permute-start.23) | collective-permute-done | bytes 23072 | tf_op jit(solution)/shard_map/ppermute | solution.py:224
  49.4 0.6 %combine.1 = bf16[2,16,360]{2,1,0:T(8,128)(2,1)} custom-call(f32[32,360]{1,0:T(8,128)S(1)} %get-tuple-element.53.refs_0_, bf16[32,360]{1,0:T(8,128)(2,1)S(1)} %collective-permute-done.21.refs_1_, bf16[32,360]{1,0:T(8,128)(2,1)S(1)} %collective-permute-done.22.refs_2_, bf16[32,360]{1,0:T(8,128)(2,1)S(1)} %collective-permute-done.23.refs_3_, ...), custom_call_target="tpu_custom_call" | custom-call | bytes 184320 | tf_op jit(solution)/shard_map/combine/pallas_call | solution.py:420
  (45 shorter events, 8.1 us)
Async XLA Ops:
  4.2 1.5 %collective-permute-start = (bf16[4,32,384]{2,1,0:T(8,128)(2,1)S(1)}, bf16[4,32,384]{2,1,0:T(8,128)(2,1)S(1)}, u32[]{:S(2)}, u32[]{:S(2)}) collective-permute-start(bf16[4,32,384]{2,1,0:T(8,128)(2,1)S(1)} %get-tuple-element.35), channel_id=1, source_target_pairs={{0,16},{16,0},{1,17},{17,1},{2,18},{18,2},{3,19},{19,3},{4,20},{20... | collective-permute-start | bytes 294920 | tf_op jit(solution)/shard_map/ppermute | solution.py:224
  5.8 5.6 %collective-permute-start.1 = (bf16[32,384]{1,0:T(8,128)(2,1)S(1)}, bf16[32,384]{1,0:T(8,128)(2,1)S(1)}, u32[]{:S(2)}, u32[]{:S(2)}) collective-permute-start(bf16[32,384]{1,0:T(8,128)(2,1)S(1)} %get-tuple-element.37), channel_id=1, source_target_pairs={{0,3},{1,2},{2,1},{3,0},{16,19},{17,18},{18,17},{19,16},{4,7},{5,6... | collective-permute-start | bytes 73736 | tf_op jit(solution)/shard_map/ppermute | solution.py:230
  9.6 3.8 %collective-permute-start.2 = (bf16[32,384]{1,0:T(8,128)(2,1)S(1)}, bf16[32,384]{1,0:T(8,128)(2,1)S(1)}, u32[]{:S(2)}, u32[]{:S(2)}) collective-permute-start(bf16[32,384]{1,0:T(8,128)(2,1)S(1)} %get-tuple-element.38), channel_id=1, source_target_pairs={{0,1},{1,0},{2,3},{3,2},{16,18},{17,19},{18,16},{19,17},{4,5},{5,4... | collective-permute-start | bytes 73736 | tf_op jit(solution)/shard_map/ppermute | solution.py:230
  10.1 3.8 %collective-permute-start.3 = (bf16[32,384]{1,0:T(8,128)(2,1)S(1)}, bf16[32,384]{1,0:T(8,128)(2,1)S(1)}, u32[]{:S(2)}, u32[]{:S(2)}) collective-permute-start(bf16[32,384]{1,0:T(8,128)(2,1)S(1)} %get-tuple-element.39), channel_id=1, source_target_pairs={{0,2},{1,3},{2,0},{3,1},{16,17},{17,16},{18,19},{19,18},{4,6},{5,7... | collective-permute-start | bytes 73736 | tf_op jit(solution)/shard_map/ppermute | solution.py:230
  14.0 4.5 %collective-permute-start.4 = (bf16[32,384]{1,0:T(8,128)(2,1)S(1)}, bf16[32,384]{1,0:T(8,128)(2,1)S(1)}, u32[]{:S(2)}, u32[]{:S(2)}) collective-permute-start(bf16[32,384]{1,0:T(8,128)(2,1)S(1)} %sum.1), channel_id=1, source_target_pairs={{0,4},{4,0},{8,12},{12,8},{1,5},{5,1},{9,13},{13,9},{2,6},{6,2},{1... | collective-permute-start | bytes 73736 | tf_op jit(solution)/shard_map/ppermute | solution.py:224
  15.6 5.1 %collective-permute-start.5 = (bf16[32,384]{1,0:T(8,128)(2,1)S(1)}, bf16[32,384]{1,0:T(8,128)(2,1)S(1)}, u32[]{:S(2)}, u32[]{:S(2)}) collective-permute-start(bf16[32,384]{1,0:T(8,128)(2,1)S(1)} %sum.1), channel_id=1, source_target_pairs={{0,8},{4,12},{8,0},{12,4},{1,9},{5,13},{9,1},{13,5},{2,10},{6,14},... | collective-permute-start | bytes 73736 | tf_op jit(solution)/shard_map/ppermute | solution.py:224
  18.2 5.6 %collective-permute-start.6 = (bf16[32,384]{1,0:T(8,128)(2,1)S(1)}, bf16[32,384]{1,0:T(8,128)(2,1)S(1)}, u32[]{:S(2)}, u32[]{:S(2)}) collective-permute-start(bf16[32,384]{1,0:T(8,128)(2,1)S(1)} %sum.1), channel_id=1, source_target_pairs={{0,12},{4,8},{8,4},{12,0},{1,13},{5,9},{9,5},{13,1},{2,14},{6,10},... | collective-permute-start | bytes 73736 | tf_op jit(solution)/shard_map/ppermute | solution.py:224
  23.9 5.6 %collective-permute-start.7 = (bf16[4,32,384]{2,1,0:T(8,128)(2,1)S(1)}, bf16[4,32,384]{2,1,0:T(8,128)(2,1)S(1)}, u32[]{:S(2)}, u32[]{:S(2)}) collective-permute-start(bf16[4,32,384]{2,1,0:T(8,128)(2,1)S(1)} %pad_maximum_fusion.refs_0_), channel_id=1, source_target_pairs={{0,3},{1,2},{2,1},{3,0},{16,19},{17,18},{18,17},{19,16},{4,7},{5,6... | collective-permute-start | bytes 294920 | tf_op jit(solution)/shard_map/ppermute | solution.py:230
  25.4 4.6 %collective-permute-start.8 = (bf16[4,32,384]{2,1,0:T(8,128)(2,1)S(1)}, bf16[4,32,384]{2,1,0:T(8,128)(2,1)S(1)}, u32[]{:S(2)}, u32[]{:S(2)}) collective-permute-start(bf16[4,32,384]{2,1,0:T(8,128)(2,1)S(1)} %pad_maximum_fusion.refs_0_), channel_id=1, source_target_pairs={{0,1},{1,0},{2,3},{3,2},{16,18},{17,19},{18,16},{19,17},{4,5},{5,4... | collective-permute-start | bytes 294920 | tf_op jit(solution)/shard_map/ppermute | solution.py:230
  25.9 4.6 %collective-permute-start.9 = (bf16[4,32,384]{2,1,0:T(8,128)(2,1)S(1)}, bf16[4,32,384]{2,1,0:T(8,128)(2,1)S(1)}, u32[]{:S(2)}, u32[]{:S(2)}) collective-permute-start(bf16[4,32,384]{2,1,0:T(8,128)(2,1)S(1)} %pad_maximum_fusion.refs_0_), channel_id=1, source_target_pairs={{0,2},{1,3},{2,0},{3,1},{16,17},{17,16},{18,19},{19,18},{4,6},{5,7... | collective-permute-start | bytes 294920 | tf_op jit(solution)/shard_map/ppermute | solution.py:230
  27.4 3.7 %collective-permute-start.10 = (bf16[4,32,384]{2,1,0:T(8,128)(2,1)S(1)}, bf16[4,32,384]{2,1,0:T(8,128)(2,1)S(1)}, u32[]{:S(2)}, u32[]{:S(2)}) collective-permute-start(bf16[4,32,384]{2,1,0:T(8,128)(2,1)S(1)} %pad_maximum_fusion.refs_0_), channel_id=1, source_target_pairs={{0,16},{16,0},{1,17},{17,1},{2,18},{18,2},{3,19},{19,3},{4,20},{20... | collective-permute-start | bytes 294920 | tf_op jit(solution)/shard_map/ppermute | solution.py:224
  29.4 1.7 %collective-permute-start.11 = (bf16[4,32,384]{2,1,0:T(8,128)(2,1)S(1)}, bf16[4,32,384]{2,1,0:T(8,128)(2,1)S(1)}, u32[]{:S(2)}, u32[]{:S(2)}) collective-permute-start(bf16[4,32,384]{2,1,0:T(8,128)(2,1)S(1)} %collective-permute-done.7.refs_1_), channel_id=1, source_target_pairs={{0,16},{16,0},{1,17},{17,1},{2,18},{18,2},{3,19},{19,3},{4,20},{20... | collective-permute-start | bytes 294920 | tf_op jit(solution)/shard_map/ppermute | solution.py:224
  30.0 1.3 %collective-permute-start.12 = (bf16[4,32,384]{2,1,0:T(8,128)(2,1)S(1)}, bf16[4,32,384]{2,1,0:T(8,128)(2,1)S(1)}, u32[]{:S(2)}, u32[]{:S(2)}) collective-permute-start(bf16[4,32,384]{2,1,0:T(8,128)(2,1)S(1)} %collective-permute-done.8.refs_2_), channel_id=1, source_target_pairs={{0,16},{16,0},{1,17},{17,1},{2,18},{18,2},{3,19},{19,3},{4,20},{20... | collective-permute-start | bytes 294920 | tf_op jit(solution)/shard_map/ppermute | solution.py:224
  30.5 1.3 %collective-permute-start.13 = (bf16[4,32,384]{2,1,0:T(8,128)(2,1)S(1)}, bf16[4,32,384]{2,1,0:T(8,128)(2,1)S(1)}, u32[]{:S(2)}, u32[]{:S(2)}) collective-permute-start(bf16[4,32,384]{2,1,0:T(8,128)(2,1)S(1)} %collective-permute-done.9.refs_3_), channel_id=1, source_target_pairs={{0,16},{16,0},{1,17},{17,1},{2,18},{18,2},{3,19},{19,3},{4,20},{20... | collective-permute-start | bytes 294920 | tf_op jit(solution)/shard_map/ppermute | solution.py:224
  33.0 1.8 %collective-permute-start.14 = (bf16[4,128,360]{2,1,0:T(8,128)(2,1)S(1)}, bf16[4,128,360]{2,1,0:T(8,128)(2,1)S(1)}, u32[]{:S(2)}, u32[]{:S(2)}) collective-permute-start(bf16[4,128,360]{2,1,0:T(8,128)(2,1)S(1)} %get-tuple-element.48), channel_id=1, source_target_pairs={{0,16},{16,0},{1,17},{17,1},{2,18},{18,2},{3,19},{19,3},{4,20},{20... | collective-permute-start | bytes 1105928 | tf_op jit(solution)/shard_map/ppermute | solution.py:224
  34.8 6.5 %collective-permute-start.18 = (bf16[64,360]{1,0:T(8,128)(2,1)S(1)}, bf16[64,360]{1,0:T(8,128)(2,1)S(1)}, u32[]{:S(2)}, u32[]{:S(2)}) collective-permute-start(bf16[64,360]{1,0:T(8,128)(2,1)S(1)} %get-tuple-element.54), channel_id=1, source_target_pairs={{0,3},{1,2},{2,1},{3,0},{16,19},{17,18},{18,17},{19,16},{4,7},{5,6... | collective-permute-start | bytes 138248 | tf_op jit(solution)/shard_map/ppermute | solution.py:230
  37.4 4.5 %collective-permute-start.19 = (bf16[64,360]{1,0:T(8,128)(2,1)S(1)}, bf16[64,360]{1,0:T(8,128)(2,1)S(1)}, u32[]{:S(2)}, u32[]{:S(2)}) collective-permute-start(bf16[64,360]{1,0:T(8,128)(2,1)S(1)} %get-tuple-element.55), channel_id=1, source_target_pairs={{0,1},{1,0},{2,3},{3,2},{16,18},{17,19},{18,16},{19,17},{4,5},{5,4... | collective-permute-start | bytes 138248 | tf_op jit(solution)/shard_map/ppermute | solution.py:230
  37.9 4.1 %collective-permute-start.20 = (bf16[64,360]{1,0:T(8,128)(2,1)S(1)}, bf16[64,360]{1,0:T(8,128)(2,1)S(1)}, u32[]{:S(2)}, u32[]{:S(2)}) collective-permute-start(bf16[64,360]{1,0:T(8,128)(2,1)S(1)} %get-tuple-element.56), channel_id=1, source_target_pairs={{0,2},{1,3},{2,0},{3,1},{16,17},{17,16},{18,19},{19,18},{4,6},{5,7... | collective-permute-start | bytes 138248 | tf_op jit(solution)/shard_map/ppermute | solution.py:230
  38.4 5.0 %collective-permute-start.15 = (bf16[64,360]{1,0:T(8,128)(2,1)S(1)}, bf16[64,360]{1,0:T(8,128)(2,1)S(1)}, u32[]{:S(2)}, u32[]{:S(2)}) collective-permute-start(bf16[64,360]{1,0:T(8,128)(2,1)S(1)} %get-tuple-element.50), channel_id=1, source_target_pairs={{0,3},{1,2},{2,1},{3,0},{16,19},{17,18},{18,17},{19,16},{4,7},{5,6... | collective-permute-start | bytes 138248 | tf_op jit(solution)/shard_map/ppermute | solution.py:230
  40.9 4.1 %collective-permute-start.16 = (bf16[64,360]{1,0:T(8,128)(2,1)S(1)}, bf16[64,360]{1,0:T(8,128)(2,1)S(1)}, u32[]{:S(2)}, u32[]{:S(2)}) collective-permute-start(bf16[64,360]{1,0:T(8,128)(2,1)S(1)} %get-tuple-element.51), channel_id=1, source_target_pairs={{0,1},{1,0},{2,3},{3,2},{16,18},{17,19},{18,16},{19,17},{4,5},{5,4... | collective-permute-start | bytes 138248 | tf_op jit(solution)/shard_map/ppermute | solution.py:230
  41.4 4.1 %collective-permute-start.17 = (bf16[64,360]{1,0:T(8,128)(2,1)S(1)}, bf16[64,360]{1,0:T(8,128)(2,1)S(1)}, u32[]{:S(2)}, u32[]{:S(2)}) collective-permute-start(bf16[64,360]{1,0:T(8,128)(2,1)S(1)} %get-tuple-element.52), channel_id=1, source_target_pairs={{0,2},{1,3},{2,0},{3,1},{16,17},{17,16},{18,19},{19,18},{4,6},{5,7... | collective-permute-start | bytes 138248 | tf_op jit(solution)/shard_map/ppermute | solution.py:230
  42.0 5.7 %collective-permute-start.21 = (bf16[32,360]{1,0:T(8,128)(2,1)S(1)}, bf16[32,360]{1,0:T(8,128)(2,1)S(1)}, u32[]{:S(2)}, u32[]{:S(2)}) collective-permute-start(bf16[32,360]{1,0:T(8,128)(2,1)S(1)} %get-tuple-element.57), channel_id=1, source_target_pairs={{0,12},{4,8},{8,4},{12,0},{1,13},{5,9},{9,5},{13,1},{2,14},{6,10},... | collective-permute-start | bytes 69128 | tf_op jit(solution)/shard_map/ppermute | solution.py:224
  42.4 5.4 %collective-permute-start.22 = (bf16[32,360]{1,0:T(8,128)(2,1)S(1)}, bf16[32,360]{1,0:T(8,128)(2,1)S(1)}, u32[]{:S(2)}, u32[]{:S(2)}) collective-permute-start(bf16[32,360]{1,0:T(8,128)(2,1)S(1)} %get-tuple-element.58), channel_id=1, source_target_pairs={{0,8},{4,12},{8,0},{12,4},{1,9},{5,13},{9,1},{13,5},{2,10},{6,14},... | collective-permute-start | bytes 69128 | tf_op jit(solution)/shard_map/ppermute | solution.py:224
  45.5 3.9 %collective-permute-start.23 = (bf16[32,360]{1,0:T(8,128)(2,1)S(1)}, bf16[32,360]{1,0:T(8,128)(2,1)S(1)}, u32[]{:S(2)}, u32[]{:S(2)}) collective-permute-start(bf16[32,360]{1,0:T(8,128)(2,1)S(1)} %get-tuple-element.59), channel_id=1, source_target_pairs={{0,4},{4,0},{8,12},{12,8},{1,5},{5,1},{9,13},{13,9},{2,6},{6,2},{1... | collective-permute-start | bytes 69128 | tf_op jit(solution)/shard_map/ppermute | solution.py:224
  (4 other events, 105.9 us)

commit v9 on v8

--- a/solution.py
+++ b/solution.py
@@ -194,9 +194,10 @@
     return jnp.stack(results, 0)
 
 
-LANES = 384
+LANES = 768
 BASE = 150000.0
 MIB = 1 << 20
+SHARD_MASKS = (3, 1, 2)
 
 
 def shape_of(shape, dtype=jnp.bfloat16):
@@ -219,24 +220,17 @@
     return lax.dot_general(left, right, (((1,), (1,)), ((), ())), preferred_element_type=jnp.float32)
 
 
-def swap(value, axes, mask):
-    size = lax.axis_size(axes)
-    return lax.ppermute(value, axes, [(i, i ^ mask) for i in range(size)])
-
-
-def swap_by_core(value, axis, masks):
+def swap(value, axis, mask):
     size = lax.axis_size(axis)
-    pairs = [(s * size + i, s * size + (i ^ masks[s])) for s in range(2) for i in range(size)]
-    return lax.ppermute(value, ("sec", axis), pairs)
+    return lax.ppermute(value, ("sec", axis), [(size + i, size + (i ^ mask)) for i in range(size)])
 
 
 def shard_swaps(parts):
-    return [swap_by_core(part, "tp", masks) for part, masks in zip(parts, ((3, 3), (1, 2), (2, 1)))]
-
-
-def shard_masks():
-    sec = lax.axis_index("sec")
-    return 3, 1 + sec, 2 - sec
+    return [swap(part, "tp", mask) for part, mask in zip(parts, SHARD_MASKS)]
+
+
+def hand_over(value, to):
+    return lax.ppermute(value, "sec", [(1 - to, to)])
 
 
 def split_width(width):
@@ -245,15 +239,15 @@
 
 
 def attention_kernel(lengths_hbm, sinks_hbm, routes_hbm, weights_hbm, gain_hbm, x_hbm, wq_hbm, wkv_hbm, cache_hbm, wo_hbm,
-                     other_ref, own_x_ref, mix_ref, wo_ref,
-                     lengths_ref, sinks_ref, routes_ref, weights_ref, gain_ref, x_ref, wq_ref, wkv_ref, cache_ref,
+                     keep_ref, send_ref, own_x_ref,
+                     lengths_ref, sinks_ref, routes_ref, weights_ref, gain_ref, x_ref, wq_ref, wkv_ref, cache_ref, wo_ref,
                      xs_ref, turned_ref, mixed_ref, sems):
     total_rows, width = x_ref.shape
     rows, slots, pair = cache_ref.shape
     steps = total_rows // rows
     heads = wq_ref.shape[1] // HEAD_SIZE
     per_row = heads * steps
-    tps = other_ref.shape[0]
+    tps = keep_ref.shape[0]
     cuts = split_width(width)
     small = [(lengths_hbm, lengths_ref), (x_hbm, x_ref), (gain_hbm, gain_ref), (routes_hbm, routes_ref), (weights_hbm, weights_ref),
              (sinks_hbm, sinks_ref)]
@@ -301,7 +295,7 @@
         tables.append(table)
     x = x_ref[...].astype(jnp.float32)
     xs_ref[...] = jnp.concatenate([x, jnp.concatenate(tables, axis=0)], axis=1)
-    own = (lax.axis_index("sec") * tps + lax.axis_index("tp")) * LANES
+    own = lax.axis_index("tp") * LANES
     own_x_ref[...] = xs_ref[:, pl.ds(pl.multiple_of(own, LANES), LANES)]
     scale = lax.rsqrt(jnp.mean(x * x, axis=-1, keepdims=True) + 1e-05)
     normed = (x * scale * gain_ref[...].reshape(1, width)).astype(jnp.bfloat16)
@@ -355,46 +349,31 @@
     def head(h):
         return jnp.concatenate([mixed_ref[pl.ds(h * steps + s, rows, stride=per_row), :] for s in range(steps)], axis=0)
 
-    mix_ref[...] = jnp.concatenate(
+    mix = jnp.concatenate(
         [jnp.where(is_key, pltpu.roll(head(2 * m), HEAD_SIZE, 1), head(2 * m + 1)) for m in range(heads // 2)], axis=1
     ).astype(jnp.bfloat16)
     copies[-1].wait()
-    project(mix_ref, wo_ref, other_ref, 1 - lax.axis_index("sec"))
-
-
-def project(mix_ref, wo_ref, out_ref, side):
-    width, (tps, total_rows, _) = wo_ref.shape[0], out_ref.shape
-    for at in range(2):
-        start, stop = at * tps * LANES, min((at + 1) * tps * LANES, width)
-
-        @pl.when(side == at)
-        def _(start=start, stop=stop):
-            partial = dot_last(mix_ref[...], wo_ref[start:stop, :])
-            for t in range(tps):
-                low, high = t * LANES, min((t + 1) * LANES, stop - start)
-                piece = partial[:, low:high]
-                if high - low < LANES:
-                    piece = jnp.concatenate([piece, jnp.zeros((total_rows, LANES - (high - low)), jnp.float32)], axis=1)
-                out_ref[t] = piece.astype(out_ref.dtype)
-
-
-def own_projection_kernel(mix_ref, wo_ref, mine_ref):
-    project(mix_ref, wo_ref, mine_ref, lax.axis_index("sec"))
-
-
-def attention_partial(flat, gain, w_query, key_value, sinks, w_output, cache, lengths, routes, weights, secs, tps):
+    for t in range(tps):
+        low, high = t * LANES, min((t + 1) * LANES, width)
+        piece = dot_last(mix, wo_ref[low:high, :])
+        if high - low < LANES:
+            piece = jnp.concatenate([piece, jnp.zeros((total_rows, LANES - (high - low)), jnp.float32)], axis=1)
+        keep_ref[t] = piece
+        send_ref[t] = piece.astype(jnp.bfloat16)
+
+
+def attention_partial(flat, gain, w_query, key_value, sinks, w_output, cache, lengths, routes, weights, tps):
     total_rows, width = flat.shape
     rows, slots, pair = cache.shape
     per_row = w_query.shape[1] // HEAD_SIZE * (total_rows // rows)
-    shards = secs * tps
     operands = (lengths, sinks, routes, weights, gain, flat, w_query, key_value, cache, w_output.swapaxes(0, 1))
     return pl.pallas_call(
         attention_kernel,
         name="attention",
-        out_shape=[shape_of((tps, total_rows, LANES)), shape_of((total_rows, LANES), jnp.float32),
-                   shape_of((total_rows, w_output.shape[0])), shape_of((width, w_output.shape[0]))],
+        out_shape=[shape_of((tps, total_rows, LANES), jnp.float32), shape_of((tps, total_rows, LANES)),
+                   shape_of((total_rows, LANES), jnp.float32)],
         in_specs=[outside()] * len(operands),
-        out_specs=[vmem()] * 4,
+        out_specs=[vmem()] * 3,
         scratch_shapes=[
             pltpu.SMEM(lengths.shape, jnp.int32),
             pltpu.SMEM(sinks.shape, jnp.float32),
@@ -405,7 +384,8 @@
             pltpu.VMEM(w_query.shape, jnp.bfloat16),
             pltpu.VMEM(key_value.shape, jnp.bfloat16),
             pltpu.VMEM(cache.shape, jnp.bfloat16),
-            pltpu.VMEM((total_rows, shards * LANES), jnp.float32),
+            pltpu.VMEM((width, w_output.shape[0]), jnp.bfloat16),
+            pltpu.VMEM((total_rows, tps * LANES), jnp.float32),
             pltpu.VMEM((rows * per_row, pair), jnp.float32),
             pltpu.VMEM((rows * per_row, pair), jnp.float32),
             pltpu.SemaphoreType.DMA((9 + len(split_width(width)),)),
@@ -429,22 +409,27 @@
     )(*operands)
 
 
-def after_core_kernel(mine_ref, come_ref, own_ref, *send_refs):
+def after_core_kernel(keep_ref, come_ref, own_x_ref, own_ref, *send_refs):
     tp = lax.axis_index("tp")
-    own_ref[...] = mine_ref[tp] + come_ref[tp].astype(jnp.float32)
-    for mask, ref in zip(shard_masks(), send_refs):
+    own_ref[...] = keep_ref[tp] + come_ref[tp].astype(jnp.float32) + own_x_ref[...]
+    for mask, ref in zip(SHARD_MASKS, send_refs):
         to = jnp.bitwise_xor(tp, mask)
-        ref[...] = (mine_ref[to] + come_ref[to].astype(jnp.float32)).astype(jnp.bfloat16)
-
-
-def after_core_halves_kernel(mine_ref, come_ref, own_ref, *send_refs):
-    tp, half = lax.axis_index("tp"), mine_ref.shape[1] // 2
-    own_ref[...] = mine_ref[tp] + come_ref[tp].astype(jnp.float32)
-    for mask, second, first in zip(shard_masks(), send_refs[:3], send_refs[3:]):
-        to = jnp.bitwise_xor(tp, mask)
-        part = (mine_ref[to] + come_ref[to].astype(jnp.float32)).astype(jnp.bfloat16)
-        second[...] = part[half:]
-        first[...] = part[:half]
+        ref[...] = (keep_ref[to] + come_ref[to].astype(jnp.float32)).astype(jnp.bfloat16)
+
+
+def after_core_halves_kernel(low_ref, high_ref, low_come_ref, high_come_ref, own_ref, *send_refs):
+    tp, half = lax.axis_index("tp"), low_ref.shape[2] // 2
+
+    def part(to):
+        at = jnp.bitwise_and(to, 1)
+        low = low_ref[at] + low_come_ref[at].astype(jnp.float32)
+        return jnp.where(to < 2, low, high_ref[at] + high_come_ref[at].astype(jnp.float32))
+
+    own_ref[...] = part(tp)
+    for mask, second, first in zip(SHARD_MASKS, send_refs[:3], send_refs[3:]):
+        whole = part(jnp.bitwise_xor(tp, mask)).astype(jnp.bfloat16)
+        second[...] = whole[:, half:]
+        first[...] = whole[:, :half]
 
 
 def add_all(*refs):
@@ -460,66 +445,83 @@
 
 def sum_rows_kernel(own_ref, *refs, line):
     come, outs = refs[:3], refs[3:]
-    lines = outs[0].shape[0]
-    total = own_ref[line:line + len(outs) * lines]
+    lines = outs[0].shape[1]
+    total = own_ref[:, line:line + len(outs) * lines]
     for ref in come:
         total = total + ref[...].astype(jnp.float32)
     for n, out in enumerate(outs):
-        out[...] = total[n * lines:(n + 1) * lines].astype(out.dtype)
-
-
-def scatter_shards(mine, come):
-    tps, lines, part = mine.shape
-    own, *parts = call(after_core_kernel, "after_core", [shape_of((lines, part), jnp.float32)] + [shape_of((lines, part))] * (tps - 1),
-                       mine, come)
-    return [own] + shard_swaps(parts)
-
-
-def first_products(pieces, masks, side, x_ref, gain_ref, gate_ref, up_ref, gate_out, up_out, square_out):
+        out[...] = total[:, n * lines:(n + 1) * lines].astype(out.dtype)
+
+
+def combine_kernel(*refs):
+    terms, outs = refs[:-2], refs[-2:]
+    total = add_all(*terms).astype(jnp.bfloat16)
+    for n, out in enumerate(outs):
+        out[...] = total[n]
+
+
+def choose_kernel(own_ref, come_ref, out_ref):
+    out_ref[...] = jnp.where(lax.axis_index("sec") == 1, own_ref[...].astype(jnp.float32),
+                             come_ref[...].astype(jnp.float32)).astype(jnp.bfloat16).reshape(out_ref.shape)
+
+
+def first_products(pieces, masks, outer, x_ref, gain_ref, gate_ref, up_ref, outs):
     width, lines = gate_ref.shape[1], x_ref.shape[0]
+    sec, tp = lax.axis_index("sec"), lax.axis_index("tp")
+    for mask, at_second, at_first in zip(masks, pieces[::2], pieces[1::2]):
+        at = pl.ds(pl.multiple_of(jnp.bitwise_xor(tp, mask) * LANES, LANES), LANES)
+
+        @pl.when(sec == 1)
+        def _(at=at, piece=at_second):
+            x_ref[:, at] = piece[...].reshape(lines, LANES)
+
+        @pl.when(sec == 0)
+        def _(at=at, piece=at_first):
+            x_ref[:, at] = piece[...].reshape(lines, LANES)
+
+    for where, cuts in ((outer, ((0, LANES), (3 * LANES, width))), (jnp.logical_not(outer), ((LANES, 3 * LANES),))):
+        @pl.when(where)
+        def _(cuts=cuts):
+            sums = None
+            for start, stop in cuts:
+                x = x_ref[:, start:stop].astype(jnp.float32)
+                scaled = (x * gain_ref[:, start:stop]).astype(jnp.bfloat16)
+                terms = (dot_last(scaled, gate_ref[:, start:stop]), dot_last(scaled, up_ref[:, start:stop]),
+                         jnp.sum(x * x, axis=-1, keepdims=True))
+                sums = terms if sums is None else [a + b for a, b in zip(sums, terms)]
+            for out, total in zip(outs, sums):
+                out[...] = jnp.broadcast_to(total, out.shape)
+
+
+def outer_chip():
     tp = lax.axis_index("tp")
-    for mask, piece in zip(masks, pieces):
-        at = pl.multiple_of(jnp.bitwise_xor(tp, mask) * LANES, LANES)
-        x_ref[:, pl.ds(at, LANES)] = piece[...].reshape(lines, LANES)
-    for at in range(2):
-        start, stop = at * x_ref.shape[1], min((at + 1) * x_ref.shape[1], width)
-
-        @pl.when(side == at)
-        def _(start=start, stop=stop):
-            x = x_ref[:, :stop - start].astype(jnp.float32)
-            square_out[...] = jnp.broadcast_to(jnp.sum(x * x, axis=-1, keepdims=True), square_out.shape)
-            scaled = (x * gain_ref[:, start:stop]).astype(jnp.bfloat16)
-            gate_out[...] = dot_last(scaled, gate_ref[:, start:stop])
-            up_out[...] = dot_last(scaled, up_ref[:, start:stop])
+    return (tp == 0) | (tp == 3)
 
 
 def near_kernel(gain_ref, gate_ref, up_ref, *refs):
-    pieces, (x_ref, gate_out, up_out, square_out) = refs[:-4], refs[-4:]
-    first_products(pieces, (0, *shard_masks()), lax.axis_index("sec"), x_ref, gain_ref, gate_ref, up_ref, gate_out, up_out,
-                   square_out)
-
-
-def second_product(act_ref, down_ref, out_ref, side):
-    width, (tps, lines, part) = down_ref.shape[1], out_ref.shape
-    for at in range(2):
-        start, stop = at * tps * part, (at + 1) * tps * part
+    pieces, (x_ref, *outs) = refs[:-4], refs[-4:]
+    first_products(pieces, (0, SHARD_MASKS[0]), outer_chip(), x_ref, gain_ref, gate_ref, up_ref, outs)
+
+
+def second_product(act_ref, down_ref, keep_ref, send_ref, first):
+    chips, secs, _, part = keep_ref.shape
+    for n in range(secs):
+        start = (n * 4 + first) * part
         shift = start % 128
-
-        @pl.when(side == at)
-        def _(start=start, stop=stop, shift=shift):
-            out = jnp.dot(act_ref[...], down_ref[:, start - shift:stop], preferred_element_type=jnp.float32)
-            for t in range(tps):
-                out_ref[t] = out[:, shift + t * part:shift + (t + 1) * part].astype(out_ref.dtype)
+        out = jnp.dot(act_ref[...], down_ref[:, start - shift:start + chips * part], preferred_element_type=jnp.float32)
+        for t in range(chips):
+            piece = out[:, shift + t * part:shift + (t + 1) * part]
+            keep_ref[t, n] = piece
+            send_ref[t, n] = piece.astype(jnp.bfloat16)
 
 
 def far_kernel(gain_ref, gate_ref, up_ref, down_ref, near_x_ref, near_gate_ref, near_up_ref, near_square_ref, *refs):
-    pieces, (other_ref, act_ref, far_x_ref, gate_out, up_out, square_out) = refs[:-6], refs[-6:]
-    sec, grp = lax.axis_index("sec"), lax.axis_index("grp")
-    masks = shard_masks()
-    first_products(pieces, (0, masks[0], masks[2], masks[1]), 1 - sec, far_x_ref, gain_ref, gate_ref, up_ref, gate_out, up_out,
-                   square_out)
-    width, half = gate_ref.shape[1], near_x_ref.shape[1]
-    spare = jnp.where(sec == 1, near_x_ref[:, width - half:], far_x_ref[:, width - half:]).astype(jnp.float32)
+    pieces, (keep_ref, send_ref, act_ref, far_x_ref, *outs) = refs[:4], refs[4:]
+    grp, outer = lax.axis_index("grp"), outer_chip()
+    first_products(pieces, SHARD_MASKS[1:], jnp.logical_not(outer), far_x_ref, gain_ref, gate_ref, up_ref, outs)
+    gate_out, up_out, square_out = outs
+    width = gate_ref.shape[1]
+    spare = jnp.where(outer, near_x_ref[:, width:].astype(jnp.float32), far_x_ref[:, width:].astype(jnp.float32))
     spare_at = lax.broadcasted_iota(jnp.int32, spare.shape, 1)
     weight = jnp.sum(jnp.where((spare_at == 2 * grp) | (spare_at == 2 * grp + 1), spare, 0.0), axis=1, keepdims=True)
     square = (near_square_ref[...] + square_out[...])[:, :1]
@@ -527,78 +529,84 @@
     gate_h = (near_gate_ref[...] + gate_out[...]) * scale
     up_h = (near_up_ref[...] + up_out[...]) * scale
     act_ref[...] = ((up_h + 1.0) * gate_h * jax.nn.sigmoid(1.702 * gate_h) * weight).astype(jnp.bfloat16)
-    second_product(act_ref, down_ref, other_ref, 1 - sec)
-
-
-def last_kernel(act_ref, down_ref, near_x_ref, far_x_ref, mine_ref, middle_ref, row_ref):
-    sec, tp = lax.axis_index("sec"), lax.axis_index("tp")
-    second_product(act_ref, down_ref, mine_ref, sec)
-    total_rows, part = middle_ref.shape
-    near, far = near_x_ref[:total_rows].astype(jnp.float32), far_x_ref[:total_rows].astype(jnp.float32)
-    first = sec == 0
-    x = jnp.concatenate([jnp.where(first, near, far), jnp.where(first, far, near)], axis=1)
+    second_product(act_ref, down_ref, keep_ref, send_ref, 0)
+
+
+def last_kernel(act_ref, down_ref, near_x_ref, far_x_ref, keep_ref, send_ref, middle_ref, row_ref):
+    second_product(act_ref, down_ref, keep_ref, send_ref, 2)
+    secs, total_rows, part = middle_ref.shape
+    outer, tp = outer_chip(), lax.axis_index("tp")
+    columns = []
+    for t in range(4):
+        at = slice(t * LANES, (t + 1) * LANES)
+        near, far = near_x_ref[:total_rows, at].astype(jnp.float32), far_x_ref[:total_rows, at].astype(jnp.float32)
+        columns.append(jnp.where(outer if t in (0, 3) else jnp.logical_not(outer), near, far))
+    x = jnp.concatenate(columns, axis=1)
     for c in range(row_ref.shape[0]):
         row_ref[c] = x[:, c * part:(c + 1) * part]
-    middle_ref[...] = row_ref[sec * mine_ref.shape[0] + tp]
+    for n in range(secs):
+        middle_ref[n] = row_ref[n * 4 + tp]
 
 
 def experts(gain, w_gate, w_up, w_down, pieces, part):
     gain, w_gate, w_up = gain.reshape(1, -1), w_gate.swapaxes(0, 1), w_up.swapaxes(0, 1)
     (hidden, width), tps, (groups, total_rows, _) = w_gate.shape, len(pieces), pieces[0].shape
     lines = groups * total_rows
-    far_pieces = [swap(piece, "sec", 1) for piece in pieces]
+    both = [copy for piece in pieces for copy in (piece, hand_over(piece, 0))]
     halves = [shape_of((lines, tps * LANES)), shape_of((lines, hidden), jnp.float32), shape_of((lines, hidden), jnp.float32),
               shape_of((lines, 128), jnp.float32)]
-    near = call(near_kernel, "near_columns", halves, gain, w_gate, w_up, *pieces, limit=12, flops=2 * lines * width * hidden)
-    other, act, far_x = pl.pallas_call(
+    near = call(near_kernel, "near_columns", halves, gain, w_gate, w_up, *both[:4], limit=16, flops=2 * lines * width * hidden)
+    outs = [shape_of((2, 2, lines, part), jnp.float32), shape_of((2, 2, lines, part))]
+    low, low_send, act, far_x = pl.pallas_call(
         far_kernel,
         name="far_columns",
-        out_shape=[shape_of((tps, lines, part)), shape_of((lines, hidden)), halves[0]],
-        in_specs=[vmem()] * (8 + len(far_pieces)),
+        out_shape=outs + [shape_of((lines, hidden)), halves[0]],
+        in_specs=[vmem()] * 12,
+        out_specs=[vmem()] * 4,
+        scratch_shapes=[pltpu.VMEM(half.shape, half.dtype) for half in halves[1:]],
+        compiler_params=pltpu.CompilerParams(vmem_limit_bytes=20 * MIB),
+    )(gain, w_gate, w_up, w_down, *near, *both[4:])
+    low_come = hand_over(low_send, 1)
+    high, high_send, middle = pl.pallas_call(
+        last_kernel,
+        name="last_columns",
+        out_shape=outs + [shape_of((2, total_rows, part), jnp.float32)],
+        in_specs=[vmem()] * 4,
         out_specs=[vmem()] * 3,
-        scratch_shapes=[pltpu.VMEM(half.shape, half.dtype) for half in halves[1:]],
+        scratch_shapes=[pltpu.VMEM((2 * tps, total_rows, part), jnp.float32)],
         compiler_params=pltpu.CompilerParams(vmem_limit_bytes=16 * MIB),
-    )(gain, w_gate, w_up, w_down, *near, *far_pieces)
-    come = swap(other, "sec", 1)
-    mine, middle = pl.pallas_call(
-        last_kernel,
-        name="own_columns",
-        out_shape=[shape_of((tps, lines, part), jnp.float32), shape_of((total_rows, part), jnp.float32)],
-        in_specs=[vmem()] * 4,
-        out_specs=[vmem()] * 2,
-        scratch_shapes=[pltpu.VMEM((2 * tps, total_rows, part), jnp.float32)],
-        compiler_params=pltpu.CompilerParams(vmem_limit_bytes=12 * MIB),
         cost_estimate=pl.CostEstimate(flops=lines * width * hidden, transcendentals=0, bytes_accessed=2 * lines * width),
     )(act, w_down, near[0], far_x)
-    return mine, come, middle
+    return low, high, low_come, hand_over(high_send, 1), middle
 
 
 def every_expert_body(inputs, attention_gain, w_query, key_value_weight, head_sink_logits, w_output, cache_pairs, lengths,
                       expert_gain, w_gate, w_up, w_down, routes, gate_weights):
-    secs, tps, groups = lax.axis_size("sec"), lax.axis_size("tp"), lax.axis_size("grp")
+    tps, groups = lax.axis_size("tp"), lax.axis_size("grp")
     steps, rows, width = inputs.shape
-    flat = inputs.reshape(steps * rows, width)
-    other, own_x, mix, held = attention_partial(
-        flat, attention_gain, w_query, key_value_weight[:, 0], head_sink_logits, w_output, cache_pairs[:, :, 0], lengths,
-        routes.swapaxes(1, 2), gate_weights.swapaxes(1, 2), secs, tps)
-    come = swap(other, "sec", 1)
-    mine = call(own_projection_kernel, "own_projection", shape_of(other.shape, jnp.float32), mix, held, limit=12,
-                flops=mix.size * width)
-    middle = call(sum_kernel, "sum", shape_of((steps * rows, LANES)), *scatter_shards(mine, come), own_x)
+    lines = steps * rows
+    keep, send, own_x = attention_partial(
+        inputs.reshape(lines, width), attention_gain, w_query, key_value_weight[:, 0], head_sink_logits, w_output,
+        cache_pairs[:, :, 0], lengths, routes.swapaxes(1, 2), gate_weights.swapaxes(1, 2), tps)
+    own, *parts = call(after_core_kernel, "after_core", [shape_of((lines, LANES), jnp.float32)] + [shape_of((lines, LANES))] * 3,
+                       keep, hand_over(send, 1), own_x)
+    middle = call(sum_kernel, "sum", shape_of((lines, LANES)), own, *shard_swaps(parts))
     stacked = jnp.stack([middle] + [swap(middle, "grp", m) for m in range(1, groups)])
-    pieces = [stacked] + shard_swaps([stacked] * (tps - 1))
-    part = width // (secs * tps)
-    mine, come, own_middle = experts(expert_gain, w_gate[0], w_up[0], w_down[0], pieces, part)
-    lines = steps * rows
+    pieces = [stacked] + shard_swaps([stacked] * 3)
+    part = width // (2 * tps)
+    *terms, own_middle = experts(expert_gain, w_gate[0], w_up[0], w_down[0], pieces, part)
     own, *parts = call(after_core_halves_kernel, "after_core_halves",
-                       [shape_of((groups * lines, part), jnp.float32)] + [shape_of((groups // 2 * lines, part))] * 6, mine, come)
+                       [shape_of((2, groups * lines, part), jnp.float32)] + [shape_of((2, groups // 2 * lines, part))] * 6, *terms,
+                       limit=12)
     second_come, first_come = shard_swaps(parts[:3]), shard_swaps(parts[3:])
-    second, third = call(functools.partial(sum_rows_kernel, line=2 * lines), "sum_far_rows", [shape_of((lines, part))] * 2,
+    second, third = call(functools.partial(sum_rows_kernel, line=2 * lines), "sum_far_rows", [shape_of((2, lines, part))] * 2,
                          own, *second_come)
     third, second = swap(third, "grp", 3), swap(second, "grp", 2)
     own, nearest = call(functools.partial(sum_rows_kernel, line=0), "sum_near_rows",
-                        [shape_of((lines, part), jnp.float32), shape_of((lines, part))], own, *first_come)
-    return call(sum_kernel, "combine", shape_of((steps, rows, part)), own, third, second, swap(nearest, "grp", 1), own_middle)
+                        [shape_of((2, lines, part), jnp.float32), shape_of((2, lines, part))], own, *first_come)
+    first_core, second_core = call(combine_kernel, "combine", [shape_of((lines, part))] * 2, own, third, second,
+                                   swap(nearest, "grp", 1), own_middle)
+    return call(choose_kernel, "choose", shape_of((steps, rows, part)), second_core, hand_over(first_core, 0))
 
 
 def body(*args):

time: 50.2 us -> 88.7 us (1.77)
  waiting for transfers between devices: 20.3 us -> 54.3 us
  starting transfers between devices: 21.7 us -> 24.6 us
    ppermute x24 -> x26, waiting for transfers between devices: 20.3 us -> 54.3 us  [the longest x8 54.3 us: hand_over(): return lax.ppermute(value, 'sec', [(1 - to, to)])]
    ppermute x24 -> x26, starting transfers between devices: 21.7 us -> 24.6 us  [the longest x8 12.6 us: hand_over(): return lax.ppermute(value, 'sec', [(1 - to, to)])]
  transfers between devices with their start and end apart: 24 -> 26, of which waited for: 18 -> 7; matrix products, arithmetic and copies ran while one was open for 0% -> 0% of each run, Pallas kernels for 4% -> 2%
where the time goes in v9:
time: 88.7 us; the launch traced here: 88 us
  waiting for transfers between devices  54.3 us (61%)
  starting transfers between devices  24.6 us (28%)
  Pallas kernels  8.54 us (10%)
    ppermute x8, waiting for transfers between devices, hand_over(): return lax.ppermute(value, 'sec', [(1 - to, to)])  54.3 us
    ppermute x8, starting transfers between devices, hand_over(): return lax.ppermute(value, 'sec', [(1 - to, to)])  12.6 us
    ppermute x18, starting transfers between devices, swap(): lax.ppermute(value, ('sec', axis), [(size + i, size + (i ^ mask)) for i i...  12 us
    pallas_call x1, Pallas kernels, attention_partial(): pl.pallas_call(attention_kernel, name='attention', out_shape=[shape_of((t...  4.77 us
    pallas_call x8, Pallas kernels, call(): pl.pallas_call(kernel, name=name, out_shape=outs, in_specs=[vmem()] * len...  1.8 us
  transfers between devices with their start and end apart: 26, of which 7 were waited for; matrix products, arithmetic and copies ran while one was open for 0% of the time, Pallas kernels for 2%

profile of v9, /device:TPU:0, one launch (start us, length us, event | category | flops | bytes accessed | tf_op | source)
XLA Modules:
  0.0 88.0 jit_solution(3832947348352080309)
XLA Ops:
  0.0 4.8 %attention.1 = (f32[4,32,768]{2,1,0:T(8,128)S(1)}, bf16[4,32,768]{2,1,0:T(8,128)(2,1)S(1)}, f32[32,768]{1,0:T(8,128)S(1)}) custom-call(s32[16]{0:T(128)} %lengths_hbm.1, f32[8]{0:T(128)} %sinks_hbm.1, s32[2,4,16]{2,1,0:T(4,128)} %bitcast.31, f32[2,4,16]{2,1,0:T(4,128)} %bitcast.32, f32[2880]{0:T(1024)} %gain_hbm.1, bf16[32,2880]{1,0:T(8,128)(2,1)} %bitcast.27, ...), custom_call_target="tpu_custom_call" | custom-call | tf_op jit(solution)/shard_map/attention/pallas_call | solution.py:370
  4.8 2.5 %collective-permute-start = (bf16[4,32,768]{2,1,0:T(8,128)(2,1)S(1)}, bf16[4,32,768]{2,1,0:T(8,128)(2,1)S(1)}, u32[]{:S(2)}, u32[]{:S(2)}) collective-permute-start(bf16[4,32,768]{2,1,0:T(8,128)(2,1)S(1)} %get-tuple-element.37), channel_id=1, source_target_pairs={{0,16},{1,17},{2,18},{3,19},{4,20},{5,21},{6,22},{7,23},{8,24},{9,... | collective-permute-start | bytes 589832 | tf_op jit(solution)/shard_map/ppermute | solution.py:233
  7.3 1.0 %collective-permute-done.come_ref = bf16[4,32,768]{2,1,0:T(8,128)(2,1)S(1)} collective-permute-done((bf16[4,32,768]{2,1,0:T(8,128)(2,1)S(1)}, bf16[4,32,768]{2,1,0:T(8,128)(2,1)S(1)}, u32[]{:S(2)}, u32[]{:S(2)}) %collective-permute-start) | collective-permute-done | bytes 196640 | tf_op jit(solution)/shard_map/ppermute | solution.py:233
  12.6 0.7 collective-permute-start.8
  13.2 0.7 collective-permute-start.12
  13.9 0.7 collective-permute-start.10
  14.6 1.3 %collective-permute-start.7 = (bf16[4,32,768]{2,1,0:T(8,128)(2,1)S(1)}, bf16[4,32,768]{2,1,0:T(8,128)(2,1)S(1)}, u32[]{:S(2)}, u32[]{:S(2)}) collective-permute-start(bf16[4,32,768]{2,1,0:T(8,128)(2,1)S(1)} %pad_maximum_fusion.refs_0_), channel_id=1, source_target_pairs={{16,0},{17,1},{18,2},{19,3},{20,4},{21,5},{22,6},{23,7},{24,8},{25... | collective-permute-start | bytes 589832 | tf_op jit(solution)/shard_map/ppermute | solution.py:233
  15.9 1.3 %collective-permute-start.9 = (bf16[4,32,768]{2,1,0:T(8,128)(2,1)S(1)}, bf16[4,32,768]{2,1,0:T(8,128)(2,1)S(1)}, u32[]{:S(2)}, u32[]{:S(2)}) collective-permute-start(bf16[4,32,768]{2,1,0:T(8,128)(2,1)S(1)} %collective-permute-done.8.refs_2_), channel_id=1, source_target_pairs={{16,0},{17,1},{18,2},{19,3},{20,4},{21,5},{22,6},{23,7},{24,8},{25... | collective-permute-start | bytes 589832 | tf_op jit(solution)/shard_map/ppermute | solution.py:233
  17.2 1.3 %collective-permute-start.13 = (bf16[4,32,768]{2,1,0:T(8,128)(2,1)S(1)}, bf16[4,32,768]{2,1,0:T(8,128)(2,1)S(1)}, u32[]{:S(2)}, u32[]{:S(2)}) collective-permute-start(bf16[4,32,768]{2,1,0:T(8,128)(2,1)S(1)} %collective-permute-done.12.refs_2_), channel_id=1, source_target_pairs={{16,0},{17,1},{18,2},{19,3},{20,4},{21,5},{22,6},{23,7},{24,8},{25... | collective-permute-start | bytes 589832 | tf_op jit(solution)/shard_map/ppermute | solution.py:233
  18.5 1.3 %collective-permute-start.11 = (bf16[4,32,768]{2,1,0:T(8,128)(2,1)S(1)}, bf16[4,32,768]{2,1,0:T(8,128)(2,1)S(1)}, u32[]{:S(2)}, u32[]{:S(2)}) collective-permute-start(bf16[4,32,768]{2,1,0:T(8,128)(2,1)S(1)} %collective-permute-done.10.refs_0_), channel_id=1, source_target_pairs={{16,0},{17,1},{18,2},{19,3},{20,4},{21,5},{22,6},{23,7},{24,8},{25... | collective-permute-start | bytes 589832 | tf_op jit(solution)/shard_map/ppermute | solution.py:233
  19.9 23.5 %collective-permute-done.7.refs_1_ = bf16[4,32,768]{2,1,0:T(8,128)(2,1)S(1)} collective-permute-done((bf16[4,32,768]{2,1,0:T(8,128)(2,1)S(1)}, bf16[4,32,768]{2,1,0:T(8,128)(2,1)S(1)}, u32[]{:S(2)}, u32[]{:S(2)}) %collective-permute-start.7) | collective-permute-done | bytes 196640 | tf_op jit(solution)/shard_map/ppermute | solution.py:233
  43.4 1.3 %collective-permute-done.9.refs_3_ = bf16[4,32,768]{2,1,0:T(8,128)(2,1)S(1)} collective-permute-done((bf16[4,32,768]{2,1,0:T(8,128)(2,1)S(1)}, bf16[4,32,768]{2,1,0:T(8,128)(2,1)S(1)}, u32[]{:S(2)}, u32[]{:S(2)}) %collective-permute-start.9) | collective-permute-done | bytes 196640 | tf_op jit(solution)/shard_map/ppermute | solution.py:233
  45.3 0.7 collective-permute-done.13.refs_3_
  46.0 1.6 %collective-permute-done.11.refs_1_ = bf16[4,32,768]{2,1,0:T(8,128)(2,1)S(1)} collective-permute-done((bf16[4,32,768]{2,1,0:T(8,128)(2,1)S(1)}, bf16[4,32,768]{2,1,0:T(8,128)(2,1)S(1)}, u32[]{:S(2)}, u32[]{:S(2)}) %collective-permute-start.11) | collective-permute-done | bytes 196640 | tf_op jit(solution)/shard_map/ppermute | solution.py:233
  47.6 1.3 %far_columns.1 = (f32[2,2,128,360]{3,2,1,0:T(8,128)S(1)}, bf16[2,2,128,360]{3,2,1,0:T(8,128)(2,1)S(1)}, bf16[128,180]{1,0:T(8,128)(2,1)S(1)}, bf16[128,3072]{1,0:T(8,128)(2,1)S(1)}) custom-call(f32[1,2880]{1,0:T(1,128)S(1)} %reshape.6.gain_ref, bf16[180,2880]{1,0:T(8,128)(2,1)S(1)} %bitcast.20, bf16[180,2880]{1,0:T(8,128)(2,1)S(1)} %bitcast.22, ...), custom_call_target="tpu_custom_call" | custom-call | tf_op jit(solution)/shard_map/far_columns/pallas_call | solution.py:560
  48.8 2.3 %collective-permute-start.14 = (bf16[2,2,128,360]{3,2,1,0:T(8,128)(2,1)S(1)}, bf16[2,2,128,360]{3,2,1,0:T(8,128)(2,1)S(1)}, u32[]{:S(2)}, u32[]{:S(2)}) collective-permute-start(bf16[2,2,128,360]{3,2,1,0:T(8,128)(2,1)S(1)} %get-tuple-element.51), channel_id=1, source_target_pairs={{0,16},{1,17},{2,18},{3,19},{4,20},{5,21},{6,22},{7,23},{8,24},{9,... | collective-permute-start | bytes 1105928 | tf_op jit(solution)/shard_map/ppermute | solution.py:233
  51.2 0.7 last_columns.1
  51.9 1.3 %collective-permute-start.15 = (bf16[2,2,128,360]{3,2,1,0:T(8,128)(2,1)S(1)}, bf16[2,2,128,360]{3,2,1,0:T(8,128)(2,1)S(1)}, u32[]{:S(2)}, u32[]{:S(2)}) collective-permute-start(bf16[2,2,128,360]{3,2,1,0:T(8,128)(2,1)S(1)} %get-tuple-element.52), channel_id=1, source_target_pairs={{0,16},{1,17},{2,18},{3,19},{4,20},{5,21},{6,22},{7,23},{8,24},{9,... | collective-permute-start | bytes 1105928 | tf_op jit(solution)/shard_map/ppermute | solution.py:233
  53.2 1.3 %collective-permute-done.15.high_come_ref = bf16[2,2,128,360]{3,2,1,0:T(8,128)(2,1)S(1)} collective-permute-done((bf16[2,2,128,360]{3,2,1,0:T(8,128)(2,1)S(1)}, bf16[2,2,128,360]{3,2,1,0:T(8,128)(2,1)S(1)}, u32[]{:S(2)}, u32[]{:S(2)}) %collective-permute-start.15) | collective-permute-done | bytes 368672 | tf_op jit(solution)/shard_map/ppermute | solution.py:233
  54.9 0.7 collective-permute-start.16
  55.6 0.7 collective-permute-start.17
  56.3 0.7 collective-permute-start.18
  61.2 1.3 %collective-permute-start.25 = (bf16[32,360]{1,0:T(8,128)(2,1)S(1)}, bf16[32,360]{1,0:T(8,128)(2,1)S(1)}, u32[]{:S(2)}, u32[]{:S(2)}) collective-permute-start(bf16[32,360]{1,0:T(8,128)(2,1)S(1)} %get-tuple-element.66), channel_id=1, source_target_pairs={{16,0},{17,1},{18,2},{19,3},{20,4},{21,5},{22,6},{23,7},{24,8},{25... | collective-permute-start | bytes 69128 | tf_op jit(solution)/shard_map/ppermute | solution.py:233
  62.5 24.8 %collective-permute-done.25.come_ref = bf16[32,360]{1,0:T(8,128)(2,1)S(1)} collective-permute-done((bf16[32,360]{1,0:T(8,128)(2,1)S(1)}, bf16[32,360]{1,0:T(8,128)(2,1)S(1)}, u32[]{:S(2)}, u32[]{:S(2)}) %collective-permute-start.25) | collective-permute-done | bytes 23072 | tf_op jit(solution)/shard_map/ppermute | solution.py:233
  (49 shorter events, 9.9 us)
Async XLA Ops:
  4.8 3.5 %collective-permute-start = (bf16[4,32,768]{2,1,0:T(8,128)(2,1)S(1)}, bf16[4,32,768]{2,1,0:T(8,128)(2,1)S(1)}, u32[]{:S(2)}, u32[]{:S(2)}) collective-permute-start(bf16[4,32,768]{2,1,0:T(8,128)(2,1)S(1)} %get-tuple-element.37), channel_id=1, source_target_pairs={{0,16},{1,17},{2,18},{3,19},{4,20},{5,21},{6,22},{7,23},{8,24},{9,... | collective-permute-start | bytes 589832 | tf_op jit(solution)/shard_map/ppermute | solution.py:233
  8.4 2.0 %collective-permute-start.1 = (bf16[32,768]{1,0:T(8,128)(2,1)S(1)}, bf16[32,768]{1,0:T(8,128)(2,1)S(1)}, u32[]{:S(2)}, u32[]{:S(2)}) collective-permute-start(bf16[32,768]{1,0:T(8,128)(2,1)S(1)} %get-tuple-element.40), channel_id=1, source_target_pairs={{16,19},{17,18},{18,17},{19,16},{20,23},{21,22},{22,21},{23,20},{2... | collective-permute-start | bytes 147464 | tf_op jit(solution)/shard_map/ppermute | solution.py:225
  9.1 1.4 %collective-permute-start.2 = (bf16[32,768]{1,0:T(8,128)(2,1)S(1)}, bf16[32,768]{1,0:T(8,128)(2,1)S(1)}, u32[]{:S(2)}, u32[]{:S(2)}) collective-permute-start(bf16[32,768]{1,0:T(8,128)(2,1)S(1)} %get-tuple-element.41), channel_id=1, source_target_pairs={{16,17},{17,16},{18,19},{19,18},{20,21},{21,20},{22,23},{23,22},{2... | collective-permute-start | bytes 147464 | tf_op jit(solution)/shard_map/ppermute | solution.py:225
  9.7 0.7 collective-permute-start.3
  10.5 2.0 %collective-permute-start.6 = (bf16[32,768]{1,0:T(8,128)(2,1)S(1)}, bf16[32,768]{1,0:T(8,128)(2,1)S(1)}, u32[]{:S(2)}, u32[]{:S(2)}) collective-permute-start(bf16[32,768]{1,0:T(8,128)(2,1)S(1)} %sum.1), channel_id=1, source_target_pairs={{16,28},{20,24},{24,20},{28,16},{17,29},{21,25},{25,21},{29,17},{1... | collective-permute-start | bytes 147464 | tf_op jit(solution)/shard_map/ppermute | solution.py:225
  11.1 1.4 %collective-permute-start.5 = (bf16[32,768]{1,0:T(8,128)(2,1)S(1)}, bf16[32,768]{1,0:T(8,128)(2,1)S(1)}, u32[]{:S(2)}, u32[]{:S(2)}) collective-permute-start(bf16[32,768]{1,0:T(8,128)(2,1)S(1)} %sum.1), channel_id=1, source_target_pairs={{16,24},{20,28},{24,16},{28,20},{17,25},{21,29},{25,17},{29,21},{1... | collective-permute-start | bytes 147464 | tf_op jit(solution)/shard_map/ppermute | solution.py:225
  12.6 3.3 %collective-permute-start.8 = (bf16[4,32,768]{2,1,0:T(8,128)(2,1)S(1)}, bf16[4,32,768]{2,1,0:T(8,128)(2,1)S(1)}, u32[]{:S(2)}, u32[]{:S(2)}) collective-permute-start(bf16[4,32,768]{2,1,0:T(8,128)(2,1)S(1)} %pad_maximum_fusion.refs_0_), channel_id=1, source_target_pairs={{16,19},{17,18},{18,17},{19,16},{20,23},{21,22},{22,21},{23,20},{2... | collective-permute-start | bytes 589832 | tf_op jit(solution)/shard_map/ppermute | solution.py:225
  13.2 4.0 %collective-permute-start.12 = (bf16[4,32,768]{2,1,0:T(8,128)(2,1)S(1)}, bf16[4,32,768]{2,1,0:T(8,128)(2,1)S(1)}, u32[]{:S(2)}, u32[]{:S(2)}) collective-permute-start(bf16[4,32,768]{2,1,0:T(8,128)(2,1)S(1)} %pad_maximum_fusion.refs_0_), channel_id=1, source_target_pairs={{16,18},{17,19},{18,16},{19,17},{20,22},{21,23},{22,20},{23,21},{2... | collective-permute-start | bytes 589832 | tf_op jit(solution)/shard_map/ppermute | solution.py:225
  13.9 4.6 %collective-permute-start.10 = (bf16[4,32,768]{2,1,0:T(8,128)(2,1)S(1)}, bf16[4,32,768]{2,1,0:T(8,128)(2,1)S(1)}, u32[]{:S(2)}, u32[]{:S(2)}) collective-permute-start(bf16[4,32,768]{2,1,0:T(8,128)(2,1)S(1)} %pad_maximum_fusion.refs_0_), channel_id=1, source_target_pairs={{16,17},{17,16},{18,19},{19,18},{20,21},{21,20},{22,23},{23,22},{2... | collective-permute-start | bytes 589832 | tf_op jit(solution)/shard_map/ppermute | solution.py:225
  14.6 28.8 %collective-permute-start.7 = (bf16[4,32,768]{2,1,0:T(8,128)(2,1)S(1)}, bf16[4,32,768]{2,1,0:T(8,128)(2,1)S(1)}, u32[]{:S(2)}, u32[]{:S(2)}) collective-permute-start(bf16[4,32,768]{2,1,0:T(8,128)(2,1)S(1)} %pad_maximum_fusion.refs_0_), channel_id=1, source_target_pairs={{16,0},{17,1},{18,2},{19,3},{20,4},{21,5},{22,6},{23,7},{24,8},{25... | collective-permute-start | bytes 589832 | tf_op jit(solution)/shard_map/ppermute | solution.py:233
  15.9 28.8 %collective-permute-start.9 = (bf16[4,32,768]{2,1,0:T(8,128)(2,1)S(1)}, bf16[4,32,768]{2,1,0:T(8,128)(2,1)S(1)}, u32[]{:S(2)}, u32[]{:S(2)}) collective-permute-start(bf16[4,32,768]{2,1,0:T(8,128)(2,1)S(1)} %collective-permute-done.8.refs_2_), channel_id=1, source_target_pairs={{16,0},{17,1},{18,2},{19,3},{20,4},{21,5},{22,6},{23,7},{24,8},{25... | collective-permute-start | bytes 589832 | tf_op jit(solution)/shard_map/ppermute | solution.py:233
  17.2 28.8 %collective-permute-start.13 = (bf16[4,32,768]{2,1,0:T(8,128)(2,1)S(1)}, bf16[4,32,768]{2,1,0:T(8,128)(2,1)S(1)}, u32[]{:S(2)}, u32[]{:S(2)}) collective-permute-start(bf16[4,32,768]{2,1,0:T(8,128)(2,1)S(1)} %collective-permute-done.12.refs_2_), channel_id=1, source_target_pairs={{16,0},{17,1},{18,2},{19,3},{20,4},{21,5},{22,6},{23,7},{24,8},{25... | collective-permute-start | bytes 589832 | tf_op jit(solution)/shard_map/ppermute | solution.py:233
  18.5 29.0 %collective-permute-start.11 = (bf16[4,32,768]{2,1,0:T(8,128)(2,1)S(1)}, bf16[4,32,768]{2,1,0:T(8,128)(2,1)S(1)}, u32[]{:S(2)}, u32[]{:S(2)}) collective-permute-start(bf16[4,32,768]{2,1,0:T(8,128)(2,1)S(1)} %collective-permute-done.10.refs_0_), channel_id=1, source_target_pairs={{16,0},{17,1},{18,2},{19,3},{20,4},{21,5},{22,6},{23,7},{24,8},{25... | collective-permute-start | bytes 589832 | tf_op jit(solution)/shard_map/ppermute | solution.py:233
  48.8 4.4 %collective-permute-start.14 = (bf16[2,2,128,360]{3,2,1,0:T(8,128)(2,1)S(1)}, bf16[2,2,128,360]{3,2,1,0:T(8,128)(2,1)S(1)}, u32[]{:S(2)}, u32[]{:S(2)}) collective-permute-start(bf16[2,2,128,360]{3,2,1,0:T(8,128)(2,1)S(1)} %get-tuple-element.51), channel_id=1, source_target_pairs={{0,16},{1,17},{2,18},{3,19},{4,20},{5,21},{6,22},{7,23},{8,24},{9,... | collective-permute-start | bytes 1105928 | tf_op jit(solution)/shard_map/ppermute | solution.py:233
  51.9 2.6 %collective-permute-start.15 = (bf16[2,2,128,360]{3,2,1,0:T(8,128)(2,1)S(1)}, bf16[2,2,128,360]{3,2,1,0:T(8,128)(2,1)S(1)}, u32[]{:S(2)}, u32[]{:S(2)}) collective-permute-start(bf16[2,2,128,360]{3,2,1,0:T(8,128)(2,1)S(1)} %get-tuple-element.52), channel_id=1, source_target_pairs={{0,16},{1,17},{2,18},{3,19},{4,20},{5,21},{6,22},{7,23},{8,24},{9,... | collective-permute-start | bytes 1105928 | tf_op jit(solution)/shard_map/ppermute | solution.py:233
  54.9 3.4 %collective-permute-start.16 = (bf16[2,64,360]{2,1,0:T(8,128)(2,1)S(1)}, bf16[2,64,360]{2,1,0:T(8,128)(2,1)S(1)}, u32[]{:S(2)}, u32[]{:S(2)}) collective-permute-start(bf16[2,64,360]{2,1,0:T(8,128)(2,1)S(1)} %get-tuple-element.54), channel_id=1, source_target_pairs={{16,19},{17,18},{18,17},{19,16},{20,23},{21,22},{22,21},{23,20},{2... | collective-permute-start | bytes 276488 | tf_op jit(solution)/shard_map/ppermute | solution.py:225
  55.6 3.4 %collective-permute-start.17 = (bf16[2,64,360]{2,1,0:T(8,128)(2,1)S(1)}, bf16[2,64,360]{2,1,0:T(8,128)(2,1)S(1)}, u32[]{:S(2)}, u32[]{:S(2)}) collective-permute-start(bf16[2,64,360]{2,1,0:T(8,128)(2,1)S(1)} %get-tuple-element.55), channel_id=1, source_target_pairs={{16,17},{17,16},{18,19},{19,18},{20,21},{21,20},{22,23},{23,22},{2... | collective-permute-start | bytes 276488 | tf_op jit(solution)/shard_map/ppermute | solution.py:225
  56.3 2.7 %collective-permute-start.18 = (bf16[2,64,360]{2,1,0:T(8,128)(2,1)S(1)}, bf16[2,64,360]{2,1,0:T(8,128)(2,1)S(1)}, u32[]{:S(2)}, u32[]{:S(2)}) collective-permute-start(bf16[2,64,360]{2,1,0:T(8,128)(2,1)S(1)} %get-tuple-element.56), channel_id=1, source_target_pairs={{16,18},{17,19},{18,16},{19,17},{20,22},{21,23},{22,20},{23,21},{2... | collective-permute-start | bytes 276488 | tf_op jit(solution)/shard_map/ppermute | solution.py:225
  56.9 2.8 %collective-permute-start.19 = (bf16[2,64,360]{2,1,0:T(8,128)(2,1)S(1)}, bf16[2,64,360]{2,1,0:T(8,128)(2,1)S(1)}, u32[]{:S(2)}, u32[]{:S(2)}) collective-permute-start(bf16[2,64,360]{2,1,0:T(8,128)(2,1)S(1)} %get-tuple-element.58), channel_id=1, source_target_pairs={{16,19},{17,18},{18,17},{19,16},{20,23},{21,22},{22,21},{23,20},{2... | collective-permute-start | bytes 276488 | tf_op jit(solution)/shard_map/ppermute | solution.py:225
  57.6 2.1 %collective-permute-start.20 = (bf16[2,64,360]{2,1,0:T(8,128)(2,1)S(1)}, bf16[2,64,360]{2,1,0:T(8,128)(2,1)S(1)}, u32[]{:S(2)}, u32[]{:S(2)}) collective-permute-start(bf16[2,64,360]{2,1,0:T(8,128)(2,1)S(1)} %get-tuple-element.59), channel_id=1, source_target_pairs={{16,17},{17,16},{18,19},{19,18},{20,21},{21,20},{22,23},{23,22},{2... | collective-permute-start | bytes 276488 | tf_op jit(solution)/shard_map/ppermute | solution.py:225
  58.3 1.4 %collective-permute-start.21 = (bf16[2,64,360]{2,1,0:T(8,128)(2,1)S(1)}, bf16[2,64,360]{2,1,0:T(8,128)(2,1)S(1)}, u32[]{:S(2)}, u32[]{:S(2)}) collective-permute-start(bf16[2,64,360]{2,1,0:T(8,128)(2,1)S(1)} %get-tuple-element.60), channel_id=1, source_target_pairs={{16,18},{17,19},{18,16},{19,17},{20,22},{21,23},{22,20},{23,21},{2... | collective-permute-start | bytes 276488 | tf_op jit(solution)/shard_map/ppermute | solution.py:225
  59.1 2.1 %collective-permute-start.24 = (bf16[2,32,360]{2,1,0:T(8,128)(2,1)S(1)}, bf16[2,32,360]{2,1,0:T(8,128)(2,1)S(1)}, u32[]{:S(2)}, u32[]{:S(2)}) collective-permute-start(bf16[2,32,360]{2,1,0:T(8,128)(2,1)S(1)} %get-tuple-element.63), channel_id=1, source_target_pairs={{16,20},{20,16},{24,28},{28,24},{17,21},{21,17},{25,29},{29,25},{1... | collective-permute-start | bytes 138248 | tf_op jit(solution)/shard_map/ppermute | solution.py:225
  59.8 1.4 %collective-permute-start.22 = (bf16[2,32,360]{2,1,0:T(8,128)(2,1)S(1)}, bf16[2,32,360]{2,1,0:T(8,128)(2,1)S(1)}, u32[]{:S(2)}, u32[]{:S(2)}) collective-permute-start(bf16[2,32,360]{2,1,0:T(8,128)(2,1)S(1)} %get-tuple-element.61), channel_id=1, source_target_pairs={{16,28},{20,24},{24,20},{28,16},{17,29},{21,25},{25,21},{29,17},{1... | collective-permute-start | bytes 138248 | tf_op jit(solution)/shard_map/ppermute | solution.py:225
  61.2 26.1 %collective-permute-start.25 = (bf16[32,360]{1,0:T(8,128)(2,1)S(1)}, bf16[32,360]{1,0:T(8,128)(2,1)S(1)}, u32[]{:S(2)}, u32[]{:S(2)}) collective-permute-start(bf16[32,360]{1,0:T(8,128)(2,1)S(1)} %get-tuple-element.66), channel_id=1, source_target_pairs={{16,0},{17,1},{18,2},{19,3},{20,4},{21,5},{22,6},{23,7},{24,8},{25... | collective-permute-start | bytes 69128 | tf_op jit(solution)/shard_map/ppermute | solution.py:233
  (6 other events, 103.9 us)

commit v10 on v9

--- a/solution.py
+++ b/solution.py
@@ -222,15 +222,15 @@
 
 def swap(value, axis, mask):
     size = lax.axis_size(axis)
-    return lax.ppermute(value, ("sec", axis), [(size + i, size + (i ^ mask)) for i in range(size)])
+    return lax.ppermute(value, ("sec", axis), [(i, i if i < size else size + (i - size ^ mask)) for i in range(2 * size)])
 
 
 def shard_swaps(parts):
     return [swap(part, "tp", mask) for part, mask in zip(parts, SHARD_MASKS)]
 
 
-def hand_over(value, to):
-    return lax.ppermute(value, "sec", [(1 - to, to)])
+def hand_over(value):
+    return lax.ppermute(value, "sec", [(0, 1), (1, 0)])
 
 
 def split_width(width):
@@ -552,7 +552,7 @@
     gain, w_gate, w_up = gain.reshape(1, -1), w_gate.swapaxes(0, 1), w_up.swapaxes(0, 1)
     (hidden, width), tps, (groups, total_rows, _) = w_gate.shape, len(pieces), pieces[0].shape
     lines = groups * total_rows
-    both = [copy for piece in pieces for copy in (piece, hand_over(piece, 0))]
+    both = [copy for piece in pieces for copy in (piece, hand_over(piece))]
     halves = [shape_of((lines, tps * LANES)), shape_of((lines, hidden), jnp.float32), shape_of((lines, hidden), jnp.float32),
               shape_of((lines, 128), jnp.float32)]
     near = call(near_kernel, "near_columns", halves, gain, w_gate, w_up, *both[:4], limit=16, flops=2 * lines * width * hidden)
@@ -566,7 +566,7 @@
         scratch_shapes=[pltpu.VMEM(half.shape, half.dtype) for half in halves[1:]],
         compiler_params=pltpu.CompilerParams(vmem_limit_bytes=20 * MIB),
     )(gain, w_gate, w_up, w_down, *near, *both[4:])
-    low_come = hand_over(low_send, 1)
+    low_come = hand_over(low_send)
     high, high_send, middle = pl.pallas_call(
         last_kernel,
         name="last_columns",
@@ -577,7 +577,7 @@
         compiler_params=pltpu.CompilerParams(vmem_limit_bytes=16 * MIB),
         cost_estimate=pl.CostEstimate(flops=lines * width * hidden, transcendentals=0, bytes_accessed=2 * lines * width),
     )(act, w_down, near[0], far_x)
-    return low, high, low_come, hand_over(high_send, 1), middle
+    return low, high, low_come, hand_over(high_send), middle
 
 
 def every_expert_body(inputs, attention_gain, w_query, key_value_weight, head_sink_logits, w_output, cache_pairs, lengths,
@@ -589,7 +589,7 @@
         inputs.reshape(lines, width), attention_gain, w_query, key_value_weight[:, 0], head_sink_logits, w_output,
         cache_pairs[:, :, 0], lengths, routes.swapaxes(1, 2), gate_weights.swapaxes(1, 2), tps)
     own, *parts = call(after_core_kernel, "after_core", [shape_of((lines, LANES), jnp.float32)] + [shape_of((lines, LANES))] * 3,
-                       keep, hand_over(send, 1), own_x)
+                       keep, hand_over(send), own_x)
     middle = call(sum_kernel, "sum", shape_of((lines, LANES)), own, *shard_swaps(parts))
     stacked = jnp.stack([middle] + [swap(middle, "grp", m) for m in range(1, groups)])
     pieces = [stacked] + shard_swaps([stacked] * 3)
@@ -606,7 +606,7 @@
                         [shape_of((2, lines, part), jnp.float32), shape_of((2, lines, part))], own, *first_come)
     first_core, second_core = call(combine_kernel, "combine", [shape_of((lines, part))] * 2, own, third, second,
                                    swap(nearest, "grp", 1), own_middle)
-    return call(choose_kernel, "choose", shape_of((steps, rows, part)), second_core, hand_over(first_core, 0))
+    return call(choose_kernel, "choose", shape_of((steps, rows, part)), second_core, hand_over(first_core))
 
 
 def body(*args):

time: 88.7 us -> 81.9 us (0.923)
  waiting for transfers between devices: 54.3 us -> 3.7 us
  starting transfers between devices: 24.6 us -> 68.4 us
    ppermute x26, waiting for transfers between devices: 54.3 us -> 3.7 us  [the longest x8 3.65 us: hand_over(): return lax.ppermute(value, 'sec', [(0, 1), (1, 0)])]
    ppermute x26, starting transfers between devices: 24.6 us -> 68.4 us  [the longest x8 56.5 us: hand_over(): return lax.ppermute(value, 'sec', [(0, 1), (1, 0)])]
  transfers between devices with their start and end apart: 26 -> 26, of which waited for: 7 -> 5; matrix products, arithmetic and copies ran while one was open for 0% -> 0% of each run, Pallas kernels for 2% -> 2%
where the time goes in v10:
time: 81.9 us; the launch traced here: 81.4 us
  starting transfers between devices  68.4 us (84%)
  Pallas kernels  8.54 us (10%)
  waiting for transfers between devices  3.7 us (5%)
    ppermute x8, starting transfers between devices, hand_over(): return lax.ppermute(value, 'sec', [(0, 1), (1, 0)])  56.5 us
    ppermute x18, starting transfers between devices, swap(): lax.ppermute(value, ('sec', axis), [(i, i if i < size else size + (i - si...  12 us
    pallas_call x1, Pallas kernels, attention_partial(): pl.pallas_call(attention_kernel, name='attention', out_shape=[shape_of((t...  4.77 us
    ppermute x8, waiting for transfers between devices, hand_over(): return lax.ppermute(value, 'sec', [(0, 1), (1, 0)])  3.65 us
    pallas_call x8, Pallas kernels, call(): pl.pallas_call(kernel, name=name, out_shape=outs, in_specs=[vmem()] * len...  1.8 us
  transfers between devices with their start and end apart: 26, of which 5 were waited for; matrix products, arithmetic and copies ran while one was open for 0% of the time, Pallas kernels for 2%

profile of v10, /device:TPU:0, one launch (start us, length us, event | category | flops | bytes accessed | tf_op | source)
XLA Modules:
  0.0 81.4 jit_solution(9834859600751681305)
XLA Ops:
  0.0 4.8 %attention.1 = (f32[4,32,768]{2,1,0:T(8,128)S(1)}, bf16[4,32,768]{2,1,0:T(8,128)(2,1)S(1)}, f32[32,768]{1,0:T(8,128)S(1)}) custom-call(s32[16]{0:T(128)} %lengths_hbm.1, f32[8]{0:T(128)} %sinks_hbm.1, s32[2,4,16]{2,1,0:T(4,128)} %bitcast.31, f32[2,4,16]{2,1,0:T(4,128)} %bitcast.32, f32[2880]{0:T(1024)} %gain_hbm.1, bf16[32,2880]{1,0:T(8,128)(2,1)} %bitcast.27, ...), custom_call_target="tpu_custom_call" | custom-call | tf_op jit(solution)/shard_map/attention/pallas_call | solution.py:370
  5.3 1.1 %collective-permute-done.come_ref = bf16[4,32,768]{2,1,0:T(8,128)(2,1)S(1)} collective-permute-done((bf16[4,32,768]{2,1,0:T(8,128)(2,1)S(1)}, bf16[4,32,768]{2,1,0:T(8,128)(2,1)S(1)}, u32[]{:S(2)}, u32[]{:S(2)}) %collective-permute-start) | collective-permute-done | bytes 196640 | tf_op jit(solution)/shard_map/ppermute | solution.py:233
  6.4 0.7 collective-permute-start.1
  7.1 0.7 collective-permute-start.2
  7.8 0.7 collective-permute-start.3
  8.5 0.7 collective-permute-start.6
  10.6 0.7 collective-permute-start.8
  11.3 0.7 collective-permute-start.12
  12.0 0.7 collective-permute-start.10
  12.6 26.9 %collective-permute-start.7 = (bf16[4,32,768]{2,1,0:T(8,128)(2,1)S(1)}, bf16[4,32,768]{2,1,0:T(8,128)(2,1)S(1)}, u32[]{:S(2)}, u32[]{:S(2)}) collective-permute-start(bf16[4,32,768]{2,1,0:T(8,128)(2,1)S(1)} %pad_maximum_fusion.refs_0_), channel_id=1, source_target_pairs={{0,16},{16,0},{1,17},{17,1},{2,18},{18,2},{3,19},{19,3},{4,20},{20... | collective-permute-start | bytes 589832 | tf_op jit(solution)/shard_map/ppermute | solution.py:233
  39.6 0.9 %collective-permute-start.13 = (bf16[4,32,768]{2,1,0:T(8,128)(2,1)S(1)}, bf16[4,32,768]{2,1,0:T(8,128)(2,1)S(1)}, u32[]{:S(2)}, u32[]{:S(2)}) collective-permute-start(bf16[4,32,768]{2,1,0:T(8,128)(2,1)S(1)} %collective-permute-done.12.refs_2_), channel_id=1, source_target_pairs={{0,16},{16,0},{1,17},{17,1},{2,18},{18,2},{3,19},{19,3},{4,20},{20... | collective-permute-start | bytes 589832 | tf_op jit(solution)/shard_map/ppermute | solution.py:233
  40.6 3.2 %collective-permute-start.11 = (bf16[4,32,768]{2,1,0:T(8,128)(2,1)S(1)}, bf16[4,32,768]{2,1,0:T(8,128)(2,1)S(1)}, u32[]{:S(2)}, u32[]{:S(2)}) collective-permute-start(bf16[4,32,768]{2,1,0:T(8,128)(2,1)S(1)} %collective-permute-done.10.refs_0_), channel_id=1, source_target_pairs={{0,16},{16,0},{1,17},{17,1},{2,18},{18,2},{3,19},{19,3},{4,20},{20... | collective-permute-start | bytes 589832 | tf_op jit(solution)/shard_map/ppermute | solution.py:233
  45.0 1.3 %far_columns.1 = (f32[2,2,128,360]{3,2,1,0:T(8,128)S(1)}, bf16[2,2,128,360]{3,2,1,0:T(8,128)(2,1)S(1)}, bf16[128,180]{1,0:T(8,128)(2,1)S(1)}, bf16[128,3072]{1,0:T(8,128)(2,1)S(1)}) custom-call(f32[1,2880]{1,0:T(1,128)S(1)} %reshape.6.gain_ref, bf16[180,2880]{1,0:T(8,128)(2,1)S(1)} %bitcast.20, bf16[180,2880]{1,0:T(8,128)(2,1)S(1)} %bitcast.22, ...), custom_call_target="tpu_custom_call" | custom-call | tf_op jit(solution)/shard_map/far_columns/pallas_call | solution.py:560
  46.5 0.7 last_columns.1
  48.1 0.9 %collective-permute-done.15.high_come_ref = bf16[2,2,128,360]{3,2,1,0:T(8,128)(2,1)S(1)} collective-permute-done((bf16[2,2,128,360]{3,2,1,0:T(8,128)(2,1)S(1)}, bf16[2,2,128,360]{3,2,1,0:T(8,128)(2,1)S(1)}, u32[]{:S(2)}, u32[]{:S(2)}) %collective-permute-start.15) | collective-permute-done | bytes 368672 | tf_op jit(solution)/shard_map/ppermute | solution.py:233
  49.4 0.7 collective-permute-start.16
  50.1 0.7 collective-permute-start.17
  50.7 0.7 collective-permute-start.18
  51.4 0.7 collective-permute-start.19
  52.1 0.7 collective-permute-start.20
  52.8 0.7 collective-permute-start.21
  55.0 0.7 collective-permute-start.23
  55.7 24.2 %collective-permute-start.25 = (bf16[32,360]{1,0:T(8,128)(2,1)S(1)}, bf16[32,360]{1,0:T(8,128)(2,1)S(1)}, u32[]{:S(2)}, u32[]{:S(2)}) collective-permute-start(bf16[32,360]{1,0:T(8,128)(2,1)S(1)} %get-tuple-element.66), channel_id=1, source_target_pairs={{0,16},{16,0},{1,17},{17,1},{2,18},{18,2},{3,19},{19,3},{4,20},{20... | collective-permute-start | bytes 69128 | tf_op jit(solution)/shard_map/ppermute | solution.py:233
  79.9 0.8 %collective-permute-done.25.come_ref = bf16[32,360]{1,0:T(8,128)(2,1)S(1)} collective-permute-done((bf16[32,360]{1,0:T(8,128)(2,1)S(1)}, bf16[32,360]{1,0:T(8,128)(2,1)S(1)}, u32[]{:S(2)}, u32[]{:S(2)}) %collective-permute-start.25) | collective-permute-done | bytes 23072 | tf_op jit(solution)/shard_map/ppermute | solution.py:233
  (49 shorter events, 6.8 us)
Async XLA Ops:
  4.8 1.6 %collective-permute-start = (bf16[4,32,768]{2,1,0:T(8,128)(2,1)S(1)}, bf16[4,32,768]{2,1,0:T(8,128)(2,1)S(1)}, u32[]{:S(2)}, u32[]{:S(2)}) collective-permute-start(bf16[4,32,768]{2,1,0:T(8,128)(2,1)S(1)} %get-tuple-element.37), channel_id=1, source_target_pairs={{0,16},{16,0},{1,17},{17,1},{2,18},{18,2},{3,19},{19,3},{4,20},{20... | collective-permute-start | bytes 589832 | tf_op jit(solution)/shard_map/ppermute | solution.py:233
  6.4 2.0 %collective-permute-start.1 = (bf16[32,768]{1,0:T(8,128)(2,1)S(1)}, bf16[32,768]{1,0:T(8,128)(2,1)S(1)}, u32[]{:S(2)}, u32[]{:S(2)}) collective-permute-start(bf16[32,768]{1,0:T(8,128)(2,1)S(1)} %get-tuple-element.40), channel_id=1, source_target_pairs={{0,0},{1,1},{2,2},{3,3},{16,19},{17,18},{18,17},{19,16},{4,4},{5,5... | collective-permute-start | bytes 147464 | tf_op jit(solution)/shard_map/ppermute | solution.py:225
  7.1 1.4 %collective-permute-start.2 = (bf16[32,768]{1,0:T(8,128)(2,1)S(1)}, bf16[32,768]{1,0:T(8,128)(2,1)S(1)}, u32[]{:S(2)}, u32[]{:S(2)}) collective-permute-start(bf16[32,768]{1,0:T(8,128)(2,1)S(1)} %get-tuple-element.41), channel_id=1, source_target_pairs={{0,0},{1,1},{2,2},{3,3},{16,17},{17,16},{18,19},{19,18},{4,4},{5,5... | collective-permute-start | bytes 147464 | tf_op jit(solution)/shard_map/ppermute | solution.py:225
  8.5 2.0 %collective-permute-start.6 = (bf16[32,768]{1,0:T(8,128)(2,1)S(1)}, bf16[32,768]{1,0:T(8,128)(2,1)S(1)}, u32[]{:S(2)}, u32[]{:S(2)}) collective-permute-start(bf16[32,768]{1,0:T(8,128)(2,1)S(1)} %sum.1), channel_id=1, source_target_pairs={{0,0},{4,4},{8,8},{12,12},{16,28},{20,24},{24,20},{28,16},{1,1},{5... | collective-permute-start | bytes 147464 | tf_op jit(solution)/shard_map/ppermute | solution.py:225
  9.2 1.4 %collective-permute-start.5 = (bf16[32,768]{1,0:T(8,128)(2,1)S(1)}, bf16[32,768]{1,0:T(8,128)(2,1)S(1)}, u32[]{:S(2)}, u32[]{:S(2)}) collective-permute-start(bf16[32,768]{1,0:T(8,128)(2,1)S(1)} %sum.1), channel_id=1, source_target_pairs={{0,0},{4,4},{8,8},{12,12},{16,24},{20,28},{24,16},{28,20},{1,1},{5... | collective-permute-start | bytes 147464 | tf_op jit(solution)/shard_map/ppermute | solution.py:225
  10.6 29.0 %collective-permute-start.8 = (bf16[4,32,768]{2,1,0:T(8,128)(2,1)S(1)}, bf16[4,32,768]{2,1,0:T(8,128)(2,1)S(1)}, u32[]{:S(2)}, u32[]{:S(2)}) collective-permute-start(bf16[4,32,768]{2,1,0:T(8,128)(2,1)S(1)} %pad_maximum_fusion.refs_0_), channel_id=1, source_target_pairs={{0,0},{1,1},{2,2},{3,3},{16,19},{17,18},{18,17},{19,16},{4,4},{5,5... | collective-permute-start | bytes 589832 | tf_op jit(solution)/shard_map/ppermute | solution.py:225
  11.3 28.4 %collective-permute-start.12 = (bf16[4,32,768]{2,1,0:T(8,128)(2,1)S(1)}, bf16[4,32,768]{2,1,0:T(8,128)(2,1)S(1)}, u32[]{:S(2)}, u32[]{:S(2)}) collective-permute-start(bf16[4,32,768]{2,1,0:T(8,128)(2,1)S(1)} %pad_maximum_fusion.refs_0_), channel_id=1, source_target_pairs={{0,0},{1,1},{2,2},{3,3},{16,18},{17,19},{18,16},{19,17},{4,4},{5,5... | collective-permute-start | bytes 589832 | tf_op jit(solution)/shard_map/ppermute | solution.py:225
  12.0 28.6 %collective-permute-start.10 = (bf16[4,32,768]{2,1,0:T(8,128)(2,1)S(1)}, bf16[4,32,768]{2,1,0:T(8,128)(2,1)S(1)}, u32[]{:S(2)}, u32[]{:S(2)}) collective-permute-start(bf16[4,32,768]{2,1,0:T(8,128)(2,1)S(1)} %pad_maximum_fusion.refs_0_), channel_id=1, source_target_pairs={{0,0},{1,1},{2,2},{3,3},{16,17},{17,16},{18,19},{19,18},{4,4},{5,5... | collective-permute-start | bytes 589832 | tf_op jit(solution)/shard_map/ppermute | solution.py:225
  12.6 31.1 %collective-permute-start.7 = (bf16[4,32,768]{2,1,0:T(8,128)(2,1)S(1)}, bf16[4,32,768]{2,1,0:T(8,128)(2,1)S(1)}, u32[]{:S(2)}, u32[]{:S(2)}) collective-permute-start(bf16[4,32,768]{2,1,0:T(8,128)(2,1)S(1)} %pad_maximum_fusion.refs_0_), channel_id=1, source_target_pairs={{0,16},{16,0},{1,17},{17,1},{2,18},{18,2},{3,19},{19,3},{4,20},{20... | collective-permute-start | bytes 589832 | tf_op jit(solution)/shard_map/ppermute | solution.py:233
  39.6 4.2 %collective-permute-start.9 = (bf16[4,32,768]{2,1,0:T(8,128)(2,1)S(1)}, bf16[4,32,768]{2,1,0:T(8,128)(2,1)S(1)}, u32[]{:S(2)}, u32[]{:S(2)}) collective-permute-start(bf16[4,32,768]{2,1,0:T(8,128)(2,1)S(1)} %collective-permute-done.8.refs_2_), channel_id=1, source_target_pairs={{0,16},{16,0},{1,17},{17,1},{2,18},{18,2},{3,19},{19,3},{4,20},{20... | collective-permute-start | bytes 589832 | tf_op jit(solution)/shard_map/ppermute | solution.py:233
  39.6 4.8 %collective-permute-start.13 = (bf16[4,32,768]{2,1,0:T(8,128)(2,1)S(1)}, bf16[4,32,768]{2,1,0:T(8,128)(2,1)S(1)}, u32[]{:S(2)}, u32[]{:S(2)}) collective-permute-start(bf16[4,32,768]{2,1,0:T(8,128)(2,1)S(1)} %collective-permute-done.12.refs_2_), channel_id=1, source_target_pairs={{0,16},{16,0},{1,17},{17,1},{2,18},{18,2},{3,19},{19,3},{4,20},{20... | collective-permute-start | bytes 589832 | tf_op jit(solution)/shard_map/ppermute | solution.py:233
  40.6 4.2 %collective-permute-start.11 = (bf16[4,32,768]{2,1,0:T(8,128)(2,1)S(1)}, bf16[4,32,768]{2,1,0:T(8,128)(2,1)S(1)}, u32[]{:S(2)}, u32[]{:S(2)}) collective-permute-start(bf16[4,32,768]{2,1,0:T(8,128)(2,1)S(1)} %collective-permute-done.10.refs_0_), channel_id=1, source_target_pairs={{0,16},{16,0},{1,17},{17,1},{2,18},{18,2},{3,19},{19,3},{4,20},{20... | collective-permute-start | bytes 589832 | tf_op jit(solution)/shard_map/ppermute | solution.py:233
  46.3 1.8 %collective-permute-start.14 = (bf16[2,2,128,360]{3,2,1,0:T(8,128)(2,1)S(1)}, bf16[2,2,128,360]{3,2,1,0:T(8,128)(2,1)S(1)}, u32[]{:S(2)}, u32[]{:S(2)}) collective-permute-start(bf16[2,2,128,360]{3,2,1,0:T(8,128)(2,1)S(1)} %get-tuple-element.51), channel_id=1, source_target_pairs={{0,16},{16,0},{1,17},{17,1},{2,18},{18,2},{3,19},{19,3},{4,20},{20... | collective-permute-start | bytes 1105928 | tf_op jit(solution)/shard_map/ppermute | solution.py:233
  47.2 1.8 %collective-permute-start.15 = (bf16[2,2,128,360]{3,2,1,0:T(8,128)(2,1)S(1)}, bf16[2,2,128,360]{3,2,1,0:T(8,128)(2,1)S(1)}, u32[]{:S(2)}, u32[]{:S(2)}) collective-permute-start(bf16[2,2,128,360]{3,2,1,0:T(8,128)(2,1)S(1)} %get-tuple-element.52), channel_id=1, source_target_pairs={{0,16},{16,0},{1,17},{17,1},{2,18},{18,2},{3,19},{19,3},{4,20},{20... | collective-permute-start | bytes 1105928 | tf_op jit(solution)/shard_map/ppermute | solution.py:233
  49.4 3.4 %collective-permute-start.16 = (bf16[2,64,360]{2,1,0:T(8,128)(2,1)S(1)}, bf16[2,64,360]{2,1,0:T(8,128)(2,1)S(1)}, u32[]{:S(2)}, u32[]{:S(2)}) collective-permute-start(bf16[2,64,360]{2,1,0:T(8,128)(2,1)S(1)} %get-tuple-element.54), channel_id=1, source_target_pairs={{0,0},{1,1},{2,2},{3,3},{16,19},{17,18},{18,17},{19,16},{4,4},{5,5... | collective-permute-start | bytes 276488 | tf_op jit(solution)/shard_map/ppermute | solution.py:225
  50.1 3.4 %collective-permute-start.17 = (bf16[2,64,360]{2,1,0:T(8,128)(2,1)S(1)}, bf16[2,64,360]{2,1,0:T(8,128)(2,1)S(1)}, u32[]{:S(2)}, u32[]{:S(2)}) collective-permute-start(bf16[2,64,360]{2,1,0:T(8,128)(2,1)S(1)} %get-tuple-element.55), channel_id=1, source_target_pairs={{0,0},{1,1},{2,2},{3,3},{16,17},{17,16},{18,19},{19,18},{4,4},{5,5... | collective-permute-start | bytes 276488 | tf_op jit(solution)/shard_map/ppermute | solution.py:225
  50.7 2.7 %collective-permute-start.18 = (bf16[2,64,360]{2,1,0:T(8,128)(2,1)S(1)}, bf16[2,64,360]{2,1,0:T(8,128)(2,1)S(1)}, u32[]{:S(2)}, u32[]{:S(2)}) collective-permute-start(bf16[2,64,360]{2,1,0:T(8,128)(2,1)S(1)} %get-tuple-element.56), channel_id=1, source_target_pairs={{0,0},{1,1},{2,2},{3,3},{16,18},{17,19},{18,16},{19,17},{4,4},{5,5... | collective-permute-start | bytes 276488 | tf_op jit(solution)/shard_map/ppermute | solution.py:225
  51.4 2.8 %collective-permute-start.19 = (bf16[2,64,360]{2,1,0:T(8,128)(2,1)S(1)}, bf16[2,64,360]{2,1,0:T(8,128)(2,1)S(1)}, u32[]{:S(2)}, u32[]{:S(2)}) collective-permute-start(bf16[2,64,360]{2,1,0:T(8,128)(2,1)S(1)} %get-tuple-element.58), channel_id=1, source_target_pairs={{0,0},{1,1},{2,2},{3,3},{16,19},{17,18},{18,17},{19,16},{4,4},{5,5... | collective-permute-start | bytes 276488 | tf_op jit(solution)/shard_map/ppermute | solution.py:225
  52.1 2.1 %collective-permute-start.20 = (bf16[2,64,360]{2,1,0:T(8,128)(2,1)S(1)}, bf16[2,64,360]{2,1,0:T(8,128)(2,1)S(1)}, u32[]{:S(2)}, u32[]{:S(2)}) collective-permute-start(bf16[2,64,360]{2,1,0:T(8,128)(2,1)S(1)} %get-tuple-element.59), channel_id=1, source_target_pairs={{0,0},{1,1},{2,2},{3,3},{16,17},{17,16},{18,19},{19,18},{4,4},{5,5... | collective-permute-start | bytes 276488 | tf_op jit(solution)/shard_map/ppermute | solution.py:225
  52.8 1.4 %collective-permute-start.21 = (bf16[2,64,360]{2,1,0:T(8,128)(2,1)S(1)}, bf16[2,64,360]{2,1,0:T(8,128)(2,1)S(1)}, u32[]{:S(2)}, u32[]{:S(2)}) collective-permute-start(bf16[2,64,360]{2,1,0:T(8,128)(2,1)S(1)} %get-tuple-element.60), channel_id=1, source_target_pairs={{0,0},{1,1},{2,2},{3,3},{16,18},{17,19},{18,16},{19,17},{4,4},{5,5... | collective-permute-start | bytes 276488 | tf_op jit(solution)/shard_map/ppermute | solution.py:225
  53.5 2.1 %collective-permute-start.24 = (bf16[2,32,360]{2,1,0:T(8,128)(2,1)S(1)}, bf16[2,32,360]{2,1,0:T(8,128)(2,1)S(1)}, u32[]{:S(2)}, u32[]{:S(2)}) collective-permute-start(bf16[2,32,360]{2,1,0:T(8,128)(2,1)S(1)} %get-tuple-element.63), channel_id=1, source_target_pairs={{0,0},{4,4},{8,8},{12,12},{16,20},{20,16},{24,28},{28,24},{1,1},{5... | collective-permute-start | bytes 138248 | tf_op jit(solution)/shard_map/ppermute | solution.py:225
  54.3 1.4 %collective-permute-start.22 = (bf16[2,32,360]{2,1,0:T(8,128)(2,1)S(1)}, bf16[2,32,360]{2,1,0:T(8,128)(2,1)S(1)}, u32[]{:S(2)}, u32[]{:S(2)}) collective-permute-start(bf16[2,32,360]{2,1,0:T(8,128)(2,1)S(1)} %get-tuple-element.61), channel_id=1, source_target_pairs={{0,0},{4,4},{8,8},{12,12},{16,28},{20,24},{24,20},{28,16},{1,1},{5... | collective-permute-start | bytes 138248 | tf_op jit(solution)/shard_map/ppermute | solution.py:225
  55.0 0.7 collective-permute-start.23
  55.7 25.1 %collective-permute-start.25 = (bf16[32,360]{1,0:T(8,128)(2,1)S(1)}, bf16[32,360]{1,0:T(8,128)(2,1)S(1)}, u32[]{:S(2)}, u32[]{:S(2)}) collective-permute-start(bf16[32,360]{1,0:T(8,128)(2,1)S(1)} %get-tuple-element.66), channel_id=1, source_target_pairs={{0,16},{16,0},{1,17},{17,1},{2,18},{18,2},{3,19},{19,3},{4,20},{20... | collective-permute-start | bytes 69128 | tf_op jit(solution)/shard_map/ppermute | solution.py:233
  (6 other events, 124.3 us)

commit v11 on v8

--- a/solution.py
+++ b/solution.py
@@ -266,7 +266,20 @@
     copies.append(pltpu.make_async_copy(wo_hbm, wo_ref, sems.at[8]))
     for copy in small + copies:
         copy.start()
-    small[0].wait()
+    small[1].wait()
+    small[2].wait()
+    x = x_ref[...].astype(jnp.float32)
+    scale = lax.rsqrt(jnp.mean(x * x, axis=-1, keepdims=True) + 1e-05)
+    normed = (x * scale * gain_ref[...].reshape(1, width)).astype(jnp.bfloat16)
+    copies[0].wait()
+    pairs = jnp.dot(normed, wkv_ref[...], preferred_element_type=jnp.float32)
+    query = jnp.zeros((total_rows, wq_ref.shape[1]), jnp.float32)
+    for n, (low, high) in enumerate(cuts[:-1]):
+        copies[1 + n].wait()
+        query = query + jnp.dot(normed[:, low:high], wq_ref[low:high, :], preferred_element_type=jnp.float32)
+    for copy in (small[0], *small[3:], copies[len(cuts)]):
+        copy.wait()
+    query = query + jnp.dot(normed[:, cuts[-1][0]:], wq_ref[cuts[-1][0]:, :], preferred_element_type=jnp.float32)
 
     lane = lax.broadcasted_iota(jnp.int32, (total_rows, pair), 1)
     line = lax.broadcasted_iota(jnp.int32, (total_rows, pair), 0)
@@ -285,8 +298,6 @@
     def turn(two):
         return two * cosine + jnp.where(low_half, pltpu.roll(two, pair - half, 1), pltpu.roll(two, half, 1)) * sine
 
-    for copy in small[1:]:
-        copy.wait()
     spare = xs_ref.shape[1] - width
     spare_at = lax.broadcasted_iota(jnp.int32, (rows, spare), 1)
     corner = lax.broadcasted_iota(jnp.int32, (rows, rows), 0) == lax.broadcasted_iota(jnp.int32, (rows, rows), 1)
@@ -299,20 +310,9 @@
             high_part = column.astype(jnp.bfloat16).astype(jnp.float32)
             table = jnp.where(spare_at == 2 * e, high_part, jnp.where(spare_at == 2 * e + 1, column - high_part, table))
         tables.append(table)
-    x = x_ref[...].astype(jnp.float32)
     xs_ref[...] = jnp.concatenate([x, jnp.concatenate(tables, axis=0)], axis=1)
     own = (lax.axis_index("sec") * tps + lax.axis_index("tp")) * LANES
     own_x_ref[...] = xs_ref[:, pl.ds(pl.multiple_of(own, LANES), LANES)]
-    scale = lax.rsqrt(jnp.mean(x * x, axis=-1, keepdims=True) + 1e-05)
-    normed = (x * scale * gain_ref[...].reshape(1, width)).astype(jnp.bfloat16)
-    copies[0].wait()
-    pairs = jnp.dot(normed, wkv_ref[...], preferred_element_type=jnp.float32)
-    query = None
-    for n, (low, high) in enumerate(cuts):
-        copies[1 + n].wait()
-        term = jnp.dot(normed[:, low:high], wq_ref[low:high, :], preferred_element_type=jnp.float32)
-        query = term if query is None else query + term
-
     is_key = lane < HEAD_SIZE
     fresh = jnp.where(is_key, turn(pairs), pairs).astype(jnp.bfloat16)
     for m in range(heads // 2):

time: 50.2 us -> 50.2 us (level)
  no operation moved by 1% of the time
where the time goes in v11:
time: 50.2 us; the launch traced here: 50.1 us
  starting transfers between devices  21.7 us (43%)
  waiting for transfers between devices  20.3 us (40%)
  Pallas kernels  7.91 us (16%)
    ppermute x12, starting transfers between devices, swap_by_core(): return lax.ppermute(value, ('sec', axis), pairs)  15 us
    ppermute x12, waiting for transfers between devices, swap(): return lax.ppermute(value, axes, [(i, i ^ mask) for i in range(size)])  10.3 us
    ppermute x12, waiting for transfers between devices, swap_by_core(): return lax.ppermute(value, ('sec', axis), pairs)  10 us
    ppermute x12, starting transfers between devices, swap(): return lax.ppermute(value, axes, [(i, i ^ mask) for i in range(size)])  6.67 us
    pallas_call x1, Pallas kernels, attention_partial(): pl.pallas_call(attention_kernel, name='attention', out_shape=[shape_of((t...  4.24 us
    pallas_call x8, Pallas kernels, call(): pl.pallas_call(kernel, name=name, out_shape=outs, in_specs=[vmem()] * len...  1.94 us
    pallas_call x1, Pallas kernels, experts(): pl.pallas_call(far_kernel, name='far_columns', out_shape=[shape_of((tps,...  1.16 us
  transfers between devices with their start and end apart: 24, of which 18 were waited for; matrix products, arithmetic and copies ran while one was open for 0% of the time, Pallas kernels for 4%

profile of v11, /device:TPU:0, one launch (start us, length us, event | category | flops | bytes accessed | tf_op | source)
XLA Modules:
  0.0 50.1 jit_solution(8698012279263625154)
XLA Ops:
  0.0 4.2 %attention.1 = (bf16[4,32,384]{2,1,0:T(8,128)(2,1)S(1)}, f32[32,384]{1,0:T(8,128)S(1)}, bf16[32,512]{1,0:T(8,128)(2,1)S(1)}, bf16[2880,512]{1,0:T(8,128)(2,1)S(1)}) custom-call(s32[16]{0:T(128)} %lengths_hbm.1, f32[8]{0:T(128)} %sinks_hbm.1, s32[2,4,16]{2,1,0:T(4,128)} %bitcast.31, f32[2,4,16]{2,1,0:T(4,128)} %bitcast.32, f32[2880]{0:T(1024)} %gain_hbm.1, ...), custom_call_target="tpu_custom_call" | custom-call | tf_op jit(solution)/shard_map/attention/pallas_call | solution.py:391
  4.3 0.6 %collective-permute-start = (bf16[4,32,384]{2,1,0:T(8,128)(2,1)S(1)}, bf16[4,32,384]{2,1,0:T(8,128)(2,1)S(1)}, u32[]{:S(2)}, u32[]{:S(2)}) collective-permute-start(bf16[4,32,384]{2,1,0:T(8,128)(2,1)S(1)} %get-tuple-element.35), channel_id=1, source_target_pairs={{0,16},{16,0},{1,17},{17,1},{2,18},{18,2},{3,19},{19,3},{4,20},{20... | collective-permute-start | bytes 294920 | tf_op jit(solution)/shard_map/ppermute | solution.py:224
  5.8 3.8 %collective-permute-start.1 = (bf16[32,384]{1,0:T(8,128)(2,1)S(1)}, bf16[32,384]{1,0:T(8,128)(2,1)S(1)}, u32[]{:S(2)}, u32[]{:S(2)}) collective-permute-start(bf16[32,384]{1,0:T(8,128)(2,1)S(1)} %get-tuple-element.37), channel_id=1, source_target_pairs={{0,3},{1,2},{2,1},{3,0},{16,19},{17,18},{18,17},{19,16},{4,7},{5,6... | collective-permute-start | bytes 73736 | tf_op jit(solution)/shard_map/ppermute | solution.py:230
  10.3 1.2 %collective-permute-done.1.refs_1_ = bf16[32,384]{1,0:T(8,128)(2,1)S(1)} collective-permute-done((bf16[32,384]{1,0:T(8,128)(2,1)S(1)}, bf16[32,384]{1,0:T(8,128)(2,1)S(1)}, u32[]{:S(2)}, u32[]{:S(2)}) %collective-permute-start.1) | collective-permute-done | bytes 24608 | tf_op jit(solution)/shard_map/ppermute | solution.py:230
  11.4 2.0 %collective-permute-done.2.refs_2_ = bf16[32,384]{1,0:T(8,128)(2,1)S(1)} collective-permute-done((bf16[32,384]{1,0:T(8,128)(2,1)S(1)}, bf16[32,384]{1,0:T(8,128)(2,1)S(1)}, u32[]{:S(2)}, u32[]{:S(2)}) %collective-permute-start.2) | collective-permute-done | bytes 24608 | tf_op jit(solution)/shard_map/ppermute | solution.py:230
  14.0 1.6 %collective-permute-start.4 = (bf16[32,384]{1,0:T(8,128)(2,1)S(1)}, bf16[32,384]{1,0:T(8,128)(2,1)S(1)}, u32[]{:S(2)}, u32[]{:S(2)}) collective-permute-start(bf16[32,384]{1,0:T(8,128)(2,1)S(1)} %sum.1), channel_id=1, source_target_pairs={{0,4},{4,0},{8,12},{12,8},{1,5},{5,1},{9,13},{13,9},{2,6},{6,2},{1... | collective-permute-start | bytes 73736 | tf_op jit(solution)/shard_map/ppermute | solution.py:224
  15.7 2.6 %collective-permute-start.5 = (bf16[32,384]{1,0:T(8,128)(2,1)S(1)}, bf16[32,384]{1,0:T(8,128)(2,1)S(1)}, u32[]{:S(2)}, u32[]{:S(2)}) collective-permute-start(bf16[32,384]{1,0:T(8,128)(2,1)S(1)} %sum.1), channel_id=1, source_target_pairs={{0,8},{4,12},{8,0},{12,4},{1,9},{5,13},{9,1},{13,5},{2,10},{6,14},... | collective-permute-start | bytes 73736 | tf_op jit(solution)/shard_map/ppermute | solution.py:224
  18.5 2.3 %collective-permute-done.5 = bf16[32,384]{1,0:T(8,128)(2,1)S(1)} collective-permute-done((bf16[32,384]{1,0:T(8,128)(2,1)S(1)}, bf16[32,384]{1,0:T(8,128)(2,1)S(1)}, u32[]{:S(2)}, u32[]{:S(2)}) %collective-permute-start.5) | collective-permute-done | bytes 24608 | tf_op jit(solution)/shard_map/ppermute | solution.py:224
  20.8 3.1 %collective-permute-done.6 = bf16[32,384]{1,0:T(8,128)(2,1)S(1)} collective-permute-done((bf16[32,384]{1,0:T(8,128)(2,1)S(1)}, bf16[32,384]{1,0:T(8,128)(2,1)S(1)}, u32[]{:S(2)}, u32[]{:S(2)}) %collective-permute-start.6) | collective-permute-done | bytes 24608 | tf_op jit(solution)/shard_map/ppermute | solution.py:224
  23.9 1.5 %collective-permute-start.7 = (bf16[4,32,384]{2,1,0:T(8,128)(2,1)S(1)}, bf16[4,32,384]{2,1,0:T(8,128)(2,1)S(1)}, u32[]{:S(2)}, u32[]{:S(2)}) collective-permute-start(bf16[4,32,384]{2,1,0:T(8,128)(2,1)S(1)} %pad_maximum_fusion.refs_0_), channel_id=1, source_target_pairs={{0,3},{1,2},{2,1},{3,0},{16,19},{17,18},{18,17},{19,16},{4,7},{5,6... | collective-permute-start | bytes 294920 | tf_op jit(solution)/shard_map/ppermute | solution.py:230
  25.9 1.5 %collective-permute-start.9 = (bf16[4,32,384]{2,1,0:T(8,128)(2,1)S(1)}, bf16[4,32,384]{2,1,0:T(8,128)(2,1)S(1)}, u32[]{:S(2)}, u32[]{:S(2)}) collective-permute-start(bf16[4,32,384]{2,1,0:T(8,128)(2,1)S(1)} %pad_maximum_fusion.refs_0_), channel_id=1, source_target_pairs={{0,2},{1,3},{2,0},{3,1},{16,17},{17,16},{18,19},{19,18},{4,6},{5,7... | collective-permute-start | bytes 294920 | tf_op jit(solution)/shard_map/ppermute | solution.py:230
  27.5 2.0 %collective-permute-done.7.refs_1_ = bf16[4,32,384]{2,1,0:T(8,128)(2,1)S(1)} collective-permute-done((bf16[4,32,384]{2,1,0:T(8,128)(2,1)S(1)}, bf16[4,32,384]{2,1,0:T(8,128)(2,1)S(1)}, u32[]{:S(2)}, u32[]{:S(2)}) %collective-permute-start.7) | collective-permute-done | bytes 98336 | tf_op jit(solution)/shard_map/ppermute | solution.py:230
  30.6 0.6 %near_columns.1 = (bf16[128,1536]{1,0:T(8,128)(2,1)S(1)}, f32[128,180]{1,0:T(8,128)S(1)}, f32[128,180]{1,0:T(8,128)S(1)}, f32[128,128]{1,0:T(8,128)S(1)}) custom-call(f32[1,2880]{1,0:T(1,128)S(1)} %reshape.6.gain_ref, bf16[180,2880]{1,0:T(8,128)(2,1)S(1)} %bitcast.17, bf16[180,2880]{1,0:T(8,128)(2,1)S(1)} %bitcast.19, ...), custom_call_target="tpu_custom_call" | custom-call | flops 132710400 | bytes 3121408 | tf_op jit(solution)/shard_map/near_columns/pallas_call | solution.py:420
  31.9 1.2 %far_columns.1 = (bf16[4,128,360]{2,1,0:T(8,128)(2,1)S(1)}, bf16[128,180]{1,0:T(8,128)(2,1)S(1)}, bf16[128,1536]{1,0:T(8,128)(2,1)S(1)}) custom-call(f32[1,2880]{1,0:T(1,128)S(1)} %reshape.6.gain_ref, bf16[180,2880]{1,0:T(8,128)(2,1)S(1)} %bitcast.18, bf16[180,2880]{1,0:T(8,128)(2,1)S(1)} %bitcast.20, bf16[180,2880]{1,0:T(8,128)(2,1)S(1)} %bitcast.21, ...), custom_call_target="tpu_custom_call" | custom-call | tf_op jit(solution)/shard_map/far_columns/pallas_call | solution.py:553
  33.2 0.6 %own_columns.1 = (f32[4,128,360]{2,1,0:T(8,128)S(1)}, f32[32,360]{1,0:T(8,128)S(1)}) custom-call(bf16[128,180]{1,0:T(8,128)(2,1)S(1)} %get-tuple-element.45.act_ref, bf16[180,2880]{1,0:T(8,128)(2,1)S(1)} %bitcast.22, bf16[128,1536]{1,0:T(8,128)(2,1)S(1)} %get-tuple-element.41.near_x_ref, bf16[128,1536]{1,0:T(8,128)(2,1)S(1)} %get-tuple-element.46.far_x_ref), custom_call_target="tpu_custom_call" | custom-call | flops 66355200 | bytes 737280 | tf_op jit(solution)/shard_map/own_columns/pallas_call | solution.py:563
  33.8 1.0 %collective-permute-done.14.come_ref = bf16[4,128,360]{2,1,0:T(8,128)(2,1)S(1)} collective-permute-done((bf16[4,128,360]{2,1,0:T(8,128)(2,1)S(1)}, bf16[4,128,360]{2,1,0:T(8,128)(2,1)S(1)}, u32[]{:S(2)}, u32[]{:S(2)}) %collective-permute-start.14) | collective-permute-done | bytes 368672 | tf_op jit(solution)/shard_map/ppermute | solution.py:224
  34.9 2.5 %collective-permute-start.18 = (bf16[64,360]{1,0:T(8,128)(2,1)S(1)}, bf16[64,360]{1,0:T(8,128)(2,1)S(1)}, u32[]{:S(2)}, u32[]{:S(2)}) collective-permute-start(bf16[64,360]{1,0:T(8,128)(2,1)S(1)} %get-tuple-element.54), channel_id=1, source_target_pairs={{0,3},{1,2},{2,1},{3,0},{16,19},{17,18},{18,17},{19,16},{4,7},{5,6... | collective-permute-start | bytes 138248 | tf_op jit(solution)/shard_map/ppermute | solution.py:230
  38.4 2.5 %collective-permute-start.15 = (bf16[64,360]{1,0:T(8,128)(2,1)S(1)}, bf16[64,360]{1,0:T(8,128)(2,1)S(1)}, u32[]{:S(2)}, u32[]{:S(2)}) collective-permute-start(bf16[64,360]{1,0:T(8,128)(2,1)S(1)} %get-tuple-element.50), channel_id=1, source_target_pairs={{0,3},{1,2},{2,1},{3,0},{16,19},{17,18},{18,17},{19,16},{4,7},{5,6... | collective-permute-start | bytes 138248 | tf_op jit(solution)/shard_map/ppermute | solution.py:230
  42.4 1.1 %collective-permute-done.15.refs_0_ = bf16[64,360]{1,0:T(8,128)(2,1)S(1)} collective-permute-done((bf16[64,360]{1,0:T(8,128)(2,1)S(1)}, bf16[64,360]{1,0:T(8,128)(2,1)S(1)}, u32[]{:S(2)}, u32[]{:S(2)}) %collective-permute-start.15) | collective-permute-done | bytes 46112 | tf_op jit(solution)/shard_map/ppermute | solution.py:230
  43.5 1.5 %collective-permute-done.16.refs_1_ = bf16[64,360]{1,0:T(8,128)(2,1)S(1)} collective-permute-done((bf16[64,360]{1,0:T(8,128)(2,1)S(1)}, bf16[64,360]{1,0:T(8,128)(2,1)S(1)}, u32[]{:S(2)}, u32[]{:S(2)}) %collective-permute-start.16) | collective-permute-done | bytes 46112 | tf_op jit(solution)/shard_map/ppermute | solution.py:230
  45.6 1.1 %collective-permute-start.23 = (bf16[32,360]{1,0:T(8,128)(2,1)S(1)}, bf16[32,360]{1,0:T(8,128)(2,1)S(1)}, u32[]{:S(2)}, u32[]{:S(2)}) collective-permute-start(bf16[32,360]{1,0:T(8,128)(2,1)S(1)} %get-tuple-element.59), channel_id=1, source_target_pairs={{0,4},{4,0},{8,12},{12,8},{1,5},{5,1},{9,13},{13,9},{2,6},{6,2},{1... | collective-permute-start | bytes 69128 | tf_op jit(solution)/shard_map/ppermute | solution.py:224
  46.6 1.1 %collective-permute-done.21.refs_1_ = bf16[32,360]{1,0:T(8,128)(2,1)S(1)} collective-permute-done((bf16[32,360]{1,0:T(8,128)(2,1)S(1)}, bf16[32,360]{1,0:T(8,128)(2,1)S(1)}, u32[]{:S(2)}, u32[]{:S(2)}) %collective-permute-start.21) | collective-permute-done | bytes 23072 | tf_op jit(solution)/shard_map/ppermute | solution.py:224
  47.8 1.7 %collective-permute-done.23.refs_3_ = bf16[32,360]{1,0:T(8,128)(2,1)S(1)} collective-permute-done((bf16[32,360]{1,0:T(8,128)(2,1)S(1)}, bf16[32,360]{1,0:T(8,128)(2,1)S(1)}, u32[]{:S(2)}, u32[]{:S(2)}) %collective-permute-start.23) | collective-permute-done | bytes 23072 | tf_op jit(solution)/shard_map/ppermute | solution.py:224
  49.5 0.6 %combine.1 = bf16[2,16,360]{2,1,0:T(8,128)(2,1)} custom-call(f32[32,360]{1,0:T(8,128)S(1)} %get-tuple-element.53.refs_0_, bf16[32,360]{1,0:T(8,128)(2,1)S(1)} %collective-permute-done.21.refs_1_, bf16[32,360]{1,0:T(8,128)(2,1)S(1)} %collective-permute-done.22.refs_2_, bf16[32,360]{1,0:T(8,128)(2,1)S(1)} %collective-permute-done.23.refs_3_, ...), custom_call_target="tpu_custom_call" | custom-call | bytes 184320 | tf_op jit(solution)/shard_map/combine/pallas_call | solution.py:420
  (45 shorter events, 8.1 us)
Async XLA Ops:
  4.3 1.5 %collective-permute-start = (bf16[4,32,384]{2,1,0:T(8,128)(2,1)S(1)}, bf16[4,32,384]{2,1,0:T(8,128)(2,1)S(1)}, u32[]{:S(2)}, u32[]{:S(2)}) collective-permute-start(bf16[4,32,384]{2,1,0:T(8,128)(2,1)S(1)} %get-tuple-element.35), channel_id=1, source_target_pairs={{0,16},{16,0},{1,17},{17,1},{2,18},{18,2},{3,19},{19,3},{4,20},{20... | collective-permute-start | bytes 294920 | tf_op jit(solution)/shard_map/ppermute | solution.py:224
  5.8 5.6 %collective-permute-start.1 = (bf16[32,384]{1,0:T(8,128)(2,1)S(1)}, bf16[32,384]{1,0:T(8,128)(2,1)S(1)}, u32[]{:S(2)}, u32[]{:S(2)}) collective-permute-start(bf16[32,384]{1,0:T(8,128)(2,1)S(1)} %get-tuple-element.37), channel_id=1, source_target_pairs={{0,3},{1,2},{2,1},{3,0},{16,19},{17,18},{18,17},{19,16},{4,7},{5,6... | collective-permute-start | bytes 73736 | tf_op jit(solution)/shard_map/ppermute | solution.py:230
  9.6 3.8 %collective-permute-start.2 = (bf16[32,384]{1,0:T(8,128)(2,1)S(1)}, bf16[32,384]{1,0:T(8,128)(2,1)S(1)}, u32[]{:S(2)}, u32[]{:S(2)}) collective-permute-start(bf16[32,384]{1,0:T(8,128)(2,1)S(1)} %get-tuple-element.38), channel_id=1, source_target_pairs={{0,1},{1,0},{2,3},{3,2},{16,18},{17,19},{18,16},{19,17},{4,5},{5,4... | collective-permute-start | bytes 73736 | tf_op jit(solution)/shard_map/ppermute | solution.py:230
  10.2 3.8 %collective-permute-start.3 = (bf16[32,384]{1,0:T(8,128)(2,1)S(1)}, bf16[32,384]{1,0:T(8,128)(2,1)S(1)}, u32[]{:S(2)}, u32[]{:S(2)}) collective-permute-start(bf16[32,384]{1,0:T(8,128)(2,1)S(1)} %get-tuple-element.39), channel_id=1, source_target_pairs={{0,2},{1,3},{2,0},{3,1},{16,17},{17,16},{18,19},{19,18},{4,6},{5,7... | collective-permute-start | bytes 73736 | tf_op jit(solution)/shard_map/ppermute | solution.py:230
  14.0 4.5 %collective-permute-start.4 = (bf16[32,384]{1,0:T(8,128)(2,1)S(1)}, bf16[32,384]{1,0:T(8,128)(2,1)S(1)}, u32[]{:S(2)}, u32[]{:S(2)}) collective-permute-start(bf16[32,384]{1,0:T(8,128)(2,1)S(1)} %sum.1), channel_id=1, source_target_pairs={{0,4},{4,0},{8,12},{12,8},{1,5},{5,1},{9,13},{13,9},{2,6},{6,2},{1... | collective-permute-start | bytes 73736 | tf_op jit(solution)/shard_map/ppermute | solution.py:224
  15.7 5.1 %collective-permute-start.5 = (bf16[32,384]{1,0:T(8,128)(2,1)S(1)}, bf16[32,384]{1,0:T(8,128)(2,1)S(1)}, u32[]{:S(2)}, u32[]{:S(2)}) collective-permute-start(bf16[32,384]{1,0:T(8,128)(2,1)S(1)} %sum.1), channel_id=1, source_target_pairs={{0,8},{4,12},{8,0},{12,4},{1,9},{5,13},{9,1},{13,5},{2,10},{6,14},... | collective-permute-start | bytes 73736 | tf_op jit(solution)/shard_map/ppermute | solution.py:224
  18.3 5.6 %collective-permute-start.6 = (bf16[32,384]{1,0:T(8,128)(2,1)S(1)}, bf16[32,384]{1,0:T(8,128)(2,1)S(1)}, u32[]{:S(2)}, u32[]{:S(2)}) collective-permute-start(bf16[32,384]{1,0:T(8,128)(2,1)S(1)} %sum.1), channel_id=1, source_target_pairs={{0,12},{4,8},{8,4},{12,0},{1,13},{5,9},{9,5},{13,1},{2,14},{6,10},... | collective-permute-start | bytes 73736 | tf_op jit(solution)/shard_map/ppermute | solution.py:224
  23.9 5.6 %collective-permute-start.7 = (bf16[4,32,384]{2,1,0:T(8,128)(2,1)S(1)}, bf16[4,32,384]{2,1,0:T(8,128)(2,1)S(1)}, u32[]{:S(2)}, u32[]{:S(2)}) collective-permute-start(bf16[4,32,384]{2,1,0:T(8,128)(2,1)S(1)} %pad_maximum_fusion.refs_0_), channel_id=1, source_target_pairs={{0,3},{1,2},{2,1},{3,0},{16,19},{17,18},{18,17},{19,16},{4,7},{5,6... | collective-permute-start | bytes 294920 | tf_op jit(solution)/shard_map/ppermute | solution.py:230
  25.4 4.6 %collective-permute-start.8 = (bf16[4,32,384]{2,1,0:T(8,128)(2,1)S(1)}, bf16[4,32,384]{2,1,0:T(8,128)(2,1)S(1)}, u32[]{:S(2)}, u32[]{:S(2)}) collective-permute-start(bf16[4,32,384]{2,1,0:T(8,128)(2,1)S(1)} %pad_maximum_fusion.refs_0_), channel_id=1, source_target_pairs={{0,1},{1,0},{2,3},{3,2},{16,18},{17,19},{18,16},{19,17},{4,5},{5,4... | collective-permute-start | bytes 294920 | tf_op jit(solution)/shard_map/ppermute | solution.py:230
  25.9 4.6 %collective-permute-start.9 = (bf16[4,32,384]{2,1,0:T(8,128)(2,1)S(1)}, bf16[4,32,384]{2,1,0:T(8,128)(2,1)S(1)}, u32[]{:S(2)}, u32[]{:S(2)}) collective-permute-start(bf16[4,32,384]{2,1,0:T(8,128)(2,1)S(1)} %pad_maximum_fusion.refs_0_), channel_id=1, source_target_pairs={{0,2},{1,3},{2,0},{3,1},{16,17},{17,16},{18,19},{19,18},{4,6},{5,7... | collective-permute-start | bytes 294920 | tf_op jit(solution)/shard_map/ppermute | solution.py:230
  27.5 3.7 %collective-permute-start.10 = (bf16[4,32,384]{2,1,0:T(8,128)(2,1)S(1)}, bf16[4,32,384]{2,1,0:T(8,128)(2,1)S(1)}, u32[]{:S(2)}, u32[]{:S(2)}) collective-permute-start(bf16[4,32,384]{2,1,0:T(8,128)(2,1)S(1)} %pad_maximum_fusion.refs_0_), channel_id=1, source_target_pairs={{0,16},{16,0},{1,17},{17,1},{2,18},{18,2},{3,19},{19,3},{4,20},{20... | collective-permute-start | bytes 294920 | tf_op jit(solution)/shard_map/ppermute | solution.py:224
  29.5 1.7 %collective-permute-start.11 = (bf16[4,32,384]{2,1,0:T(8,128)(2,1)S(1)}, bf16[4,32,384]{2,1,0:T(8,128)(2,1)S(1)}, u32[]{:S(2)}, u32[]{:S(2)}) collective-permute-start(bf16[4,32,384]{2,1,0:T(8,128)(2,1)S(1)} %collective-permute-done.7.refs_1_), channel_id=1, source_target_pairs={{0,16},{16,0},{1,17},{17,1},{2,18},{18,2},{3,19},{19,3},{4,20},{20... | collective-permute-start | bytes 294920 | tf_op jit(solution)/shard_map/ppermute | solution.py:224
  30.0 1.3 %collective-permute-start.12 = (bf16[4,32,384]{2,1,0:T(8,128)(2,1)S(1)}, bf16[4,32,384]{2,1,0:T(8,128)(2,1)S(1)}, u32[]{:S(2)}, u32[]{:S(2)}) collective-permute-start(bf16[4,32,384]{2,1,0:T(8,128)(2,1)S(1)} %collective-permute-done.8.refs_2_), channel_id=1, source_target_pairs={{0,16},{16,0},{1,17},{17,1},{2,18},{18,2},{3,19},{19,3},{4,20},{20... | collective-permute-start | bytes 294920 | tf_op jit(solution)/shard_map/ppermute | solution.py:224
  30.6 1.3 %collective-permute-start.13 = (bf16[4,32,384]{2,1,0:T(8,128)(2,1)S(1)}, bf16[4,32,384]{2,1,0:T(8,128)(2,1)S(1)}, u32[]{:S(2)}, u32[]{:S(2)}) collective-permute-start(bf16[4,32,384]{2,1,0:T(8,128)(2,1)S(1)} %collective-permute-done.9.refs_3_), channel_id=1, source_target_pairs={{0,16},{16,0},{1,17},{17,1},{2,18},{18,2},{3,19},{19,3},{4,20},{20... | collective-permute-start | bytes 294920 | tf_op jit(solution)/shard_map/ppermute | solution.py:224
  33.0 1.8 %collective-permute-start.14 = (bf16[4,128,360]{2,1,0:T(8,128)(2,1)S(1)}, bf16[4,128,360]{2,1,0:T(8,128)(2,1)S(1)}, u32[]{:S(2)}, u32[]{:S(2)}) collective-permute-start(bf16[4,128,360]{2,1,0:T(8,128)(2,1)S(1)} %get-tuple-element.48), channel_id=1, source_target_pairs={{0,16},{16,0},{1,17},{17,1},{2,18},{18,2},{3,19},{19,3},{4,20},{20... | collective-permute-start | bytes 1105928 | tf_op jit(solution)/shard_map/ppermute | solution.py:224
  34.9 6.6 %collective-permute-start.18 = (bf16[64,360]{1,0:T(8,128)(2,1)S(1)}, bf16[64,360]{1,0:T(8,128)(2,1)S(1)}, u32[]{:S(2)}, u32[]{:S(2)}) collective-permute-start(bf16[64,360]{1,0:T(8,128)(2,1)S(1)} %get-tuple-element.54), channel_id=1, source_target_pairs={{0,3},{1,2},{2,1},{3,0},{16,19},{17,18},{18,17},{19,16},{4,7},{5,6... | collective-permute-start | bytes 138248 | tf_op jit(solution)/shard_map/ppermute | solution.py:230
  37.4 4.5 %collective-permute-start.19 = (bf16[64,360]{1,0:T(8,128)(2,1)S(1)}, bf16[64,360]{1,0:T(8,128)(2,1)S(1)}, u32[]{:S(2)}, u32[]{:S(2)}) collective-permute-start(bf16[64,360]{1,0:T(8,128)(2,1)S(1)} %get-tuple-element.55), channel_id=1, source_target_pairs={{0,1},{1,0},{2,3},{3,2},{16,18},{17,19},{18,16},{19,17},{4,5},{5,4... | collective-permute-start | bytes 138248 | tf_op jit(solution)/shard_map/ppermute | solution.py:230
  38.0 4.1 %collective-permute-start.20 = (bf16[64,360]{1,0:T(8,128)(2,1)S(1)}, bf16[64,360]{1,0:T(8,128)(2,1)S(1)}, u32[]{:S(2)}, u32[]{:S(2)}) collective-permute-start(bf16[64,360]{1,0:T(8,128)(2,1)S(1)} %get-tuple-element.56), channel_id=1, source_target_pairs={{0,2},{1,3},{2,0},{3,1},{16,17},{17,16},{18,19},{19,18},{4,6},{5,7... | collective-permute-start | bytes 138248 | tf_op jit(solution)/shard_map/ppermute | solution.py:230
  38.4 5.0 %collective-permute-start.15 = (bf16[64,360]{1,0:T(8,128)(2,1)S(1)}, bf16[64,360]{1,0:T(8,128)(2,1)S(1)}, u32[]{:S(2)}, u32[]{:S(2)}) collective-permute-start(bf16[64,360]{1,0:T(8,128)(2,1)S(1)} %get-tuple-element.50), channel_id=1, source_target_pairs={{0,3},{1,2},{2,1},{3,0},{16,19},{17,18},{18,17},{19,16},{4,7},{5,6... | collective-permute-start | bytes 138248 | tf_op jit(solution)/shard_map/ppermute | solution.py:230
  40.9 4.1 %collective-permute-start.16 = (bf16[64,360]{1,0:T(8,128)(2,1)S(1)}, bf16[64,360]{1,0:T(8,128)(2,1)S(1)}, u32[]{:S(2)}, u32[]{:S(2)}) collective-permute-start(bf16[64,360]{1,0:T(8,128)(2,1)S(1)} %get-tuple-element.51), channel_id=1, source_target_pairs={{0,1},{1,0},{2,3},{3,2},{16,18},{17,19},{18,16},{19,17},{4,5},{5,4... | collective-permute-start | bytes 138248 | tf_op jit(solution)/shard_map/ppermute | solution.py:230
  41.4 4.1 %collective-permute-start.17 = (bf16[64,360]{1,0:T(8,128)(2,1)S(1)}, bf16[64,360]{1,0:T(8,128)(2,1)S(1)}, u32[]{:S(2)}, u32[]{:S(2)}) collective-permute-start(bf16[64,360]{1,0:T(8,128)(2,1)S(1)} %get-tuple-element.52), channel_id=1, source_target_pairs={{0,2},{1,3},{2,0},{3,1},{16,17},{17,16},{18,19},{19,18},{4,6},{5,7... | collective-permute-start | bytes 138248 | tf_op jit(solution)/shard_map/ppermute | solution.py:230
  42.1 5.7 %collective-permute-start.21 = (bf16[32,360]{1,0:T(8,128)(2,1)S(1)}, bf16[32,360]{1,0:T(8,128)(2,1)S(1)}, u32[]{:S(2)}, u32[]{:S(2)}) collective-permute-start(bf16[32,360]{1,0:T(8,128)(2,1)S(1)} %get-tuple-element.57), channel_id=1, source_target_pairs={{0,12},{4,8},{8,4},{12,0},{1,13},{5,9},{9,5},{13,1},{2,14},{6,10},... | collective-permute-start | bytes 69128 | tf_op jit(solution)/shard_map/ppermute | solution.py:224
  42.4 5.4 %collective-permute-start.22 = (bf16[32,360]{1,0:T(8,128)(2,1)S(1)}, bf16[32,360]{1,0:T(8,128)(2,1)S(1)}, u32[]{:S(2)}, u32[]{:S(2)}) collective-permute-start(bf16[32,360]{1,0:T(8,128)(2,1)S(1)} %get-tuple-element.58), channel_id=1, source_target_pairs={{0,8},{4,12},{8,0},{12,4},{1,9},{5,13},{9,1},{13,5},{2,10},{6,14},... | collective-permute-start | bytes 69128 | tf_op jit(solution)/shard_map/ppermute | solution.py:224
  45.6 3.9 %collective-permute-start.23 = (bf16[32,360]{1,0:T(8,128)(2,1)S(1)}, bf16[32,360]{1,0:T(8,128)(2,1)S(1)}, u32[]{:S(2)}, u32[]{:S(2)}) collective-permute-start(bf16[32,360]{1,0:T(8,128)(2,1)S(1)} %get-tuple-element.59), channel_id=1, source_target_pairs={{0,4},{4,0},{8,12},{12,8},{1,5},{5,1},{9,13},{13,9},{2,6},{6,2},{1... | collective-permute-start | bytes 69128 | tf_op jit(solution)/shard_map/ppermute | solution.py:224
  (4 other events, 105.9 us)

commit v12 on v11

--- a/solution.py
+++ b/solution.py
@@ -224,19 +224,36 @@
     return lax.ppermute(value, axes, [(i, i ^ mask) for i in range(size)])
 
 
-def swap_by_core(value, axis, masks):
-    size = lax.axis_size(axis)
-    pairs = [(s * size + i, s * size + (i ^ masks[s])) for s in range(2) for i in range(size)]
-    return lax.ppermute(value, ("sec", axis), pairs)
-
-
-def shard_swaps(parts):
-    return [swap_by_core(part, "tp", masks) for part, masks in zip(parts, ((3, 3), (1, 2), (2, 1)))]
-
-
-def shard_masks():
-    sec = lax.axis_index("sec")
-    return 3, 1 + sec, 2 - sec
+def lane_of(by_group):
+    tp = lax.axis_index("tp")
+    number = lax.axis_index("sec") ^ (tp & 1) ^ (tp >> 1)
+    return number ^ (lax.axis_index("grp") & 1) if by_group else number
+
+
+def lane_swap(value, mask, shard_masks_by_lane, by_group):
+    groups, tps = lax.axis_size("grp"), lax.axis_size("tp")
+
+    def parity(group, shard):
+        return (shard & 1) ^ (shard >> 1) ^ (group & 1 if by_group else 0)
+
+    pairs = []
+    for core in range(2):
+        for group in range(groups):
+            for shard in range(tps):
+                number = core ^ parity(group, shard)
+                to_group, to_shard = group ^ mask, shard ^ shard_masks_by_lane[number]
+                to_core = number ^ parity(to_group, to_shard)
+                pairs.append(((core * groups + group) * tps + shard, (to_core * groups + to_group) * tps + to_shard))
+    return lax.ppermute(value, ("sec", "grp", "tp"), pairs)
+
+
+def shard_swaps(parts, by_group):
+    return [lane_swap(part, 0, masks, by_group) for part, masks in zip(parts, ((3, 3), (1, 2), (2, 1)))]
+
+
+def shard_masks(by_group):
+    number = lane_of(by_group)
+    return 3, 1 + number, 2 - number
 
 
 def split_width(width):
@@ -311,7 +328,7 @@
             table = jnp.where(spare_at == 2 * e, high_part, jnp.where(spare_at == 2 * e + 1, column - high_part, table))
         tables.append(table)
     xs_ref[...] = jnp.concatenate([x, jnp.concatenate(tables, axis=0)], axis=1)
-    own = (lax.axis_index("sec") * tps + lax.axis_index("tp")) * LANES
+    own = (lane_of(True) * tps + lax.axis_index("tp")) * LANES
     own_x_ref[...] = xs_ref[:, pl.ds(pl.multiple_of(own, LANES), LANES)]
     is_key = lane < HEAD_SIZE
     fresh = jnp.where(is_key, turn(pairs), pairs).astype(jnp.bfloat16)
@@ -359,7 +376,7 @@
         [jnp.where(is_key, pltpu.roll(head(2 * m), HEAD_SIZE, 1), head(2 * m + 1)) for m in range(heads // 2)], axis=1
     ).astype(jnp.bfloat16)
     copies[-1].wait()
-    project(mix_ref, wo_ref, other_ref, 1 - lax.axis_index("sec"))
+    project(mix_ref, wo_ref, other_ref, 1 - lane_of(True))
 
 
 def project(mix_ref, wo_ref, out_ref, side):
@@ -379,7 +396,7 @@
 
 
 def own_projection_kernel(mix_ref, wo_ref, mine_ref):
-    project(mix_ref, wo_ref, mine_ref, lax.axis_index("sec"))
+    project(mix_ref, wo_ref, mine_ref, lane_of(True))
 
 
 def attention_partial(flat, gain, w_query, key_value, sinks, w_output, cache, lengths, routes, weights, secs, tps):
@@ -432,7 +449,7 @@
 def after_core_kernel(mine_ref, come_ref, own_ref, *send_refs):
     tp = lax.axis_index("tp")
     own_ref[...] = mine_ref[tp] + come_ref[tp].astype(jnp.float32)
-    for mask, ref in zip(shard_masks(), send_refs):
+    for mask, ref in zip(shard_masks(True), send_refs):
         to = jnp.bitwise_xor(tp, mask)
         ref[...] = (mine_ref[to] + come_ref[to].astype(jnp.float32)).astype(jnp.bfloat16)
 
@@ -440,7 +457,7 @@
 def after_core_halves_kernel(mine_ref, come_ref, own_ref, *send_refs):
     tp, half = lax.axis_index("tp"), mine_ref.shape[1] // 2
     own_ref[...] = mine_ref[tp] + come_ref[tp].astype(jnp.float32)
-    for mask, second, first in zip(shard_masks(), send_refs[:3], send_refs[3:]):
+    for mask, second, first in zip(shard_masks(False), send_refs[:3], send_refs[3:]):
         to = jnp.bitwise_xor(tp, mask)
         part = (mine_ref[to] + come_ref[to].astype(jnp.float32)).astype(jnp.bfloat16)
         second[...] = part[half:]
@@ -472,7 +489,7 @@
     tps, lines, part = mine.shape
     own, *parts = call(after_core_kernel, "after_core", [shape_of((lines, part), jnp.float32)] + [shape_of((lines, part))] * (tps - 1),
                        mine, come)
-    return [own] + shard_swaps(parts)
+    return [own] + shard_swaps(parts, True)
 
 
 def first_products(pieces, masks, side, x_ref, gain_ref, gate_ref, up_ref, gate_out, up_out, square_out):
@@ -495,31 +512,34 @@
 
 def near_kernel(gain_ref, gate_ref, up_ref, *refs):
     pieces, (x_ref, gate_out, up_out, square_out) = refs[:-4], refs[-4:]
-    first_products(pieces, (0, *shard_masks()), lax.axis_index("sec"), x_ref, gain_ref, gate_ref, up_ref, gate_out, up_out,
+    first_products(pieces, (0, *shard_masks(True)), lane_of(True), x_ref, gain_ref, gate_ref, up_ref, gate_out, up_out,
                    square_out)
 
 
-def second_product(act_ref, down_ref, out_ref, side):
-    width, (tps, lines, part) = down_ref.shape[1], out_ref.shape
+def second_product(act_ref, down_ref, out_ref, number):
+    tps, _, part = out_ref.shape
+
     for at in range(2):
-        start, stop = at * tps * part, (at + 1) * tps * part
-        shift = start % 128
-
-        @pl.when(side == at)
-        def _(start=start, stop=stop, shift=shift):
-            out = jnp.dot(act_ref[...], down_ref[:, start - shift:stop], preferred_element_type=jnp.float32)
-            for t in range(tps):
-                out_ref[t] = out[:, shift + t * part:shift + (t + 1) * part].astype(out_ref.dtype)
+        starts = [((at ^ (t & 1) ^ (t >> 1)) * tps + t) * part for t in range(tps)]
+
+        @pl.when(number == at)
+        def _(starts=starts):
+            for first, last in ((0, 0), (1, 2), (3, 3)):
+                shift = starts[first] % 128
+                out = jnp.dot(act_ref[...], down_ref[:, starts[first] - shift:starts[last] + part],
+                              preferred_element_type=jnp.float32)
+                for n, t in enumerate(range(first, last + 1)):
+                    out_ref[t] = out[:, shift + n * part:shift + (n + 1) * part].astype(out_ref.dtype)
 
 
 def far_kernel(gain_ref, gate_ref, up_ref, down_ref, near_x_ref, near_gate_ref, near_up_ref, near_square_ref, *refs):
     pieces, (other_ref, act_ref, far_x_ref, gate_out, up_out, square_out) = refs[:-6], refs[-6:]
-    sec, grp = lax.axis_index("sec"), lax.axis_index("grp")
-    masks = shard_masks()
-    first_products(pieces, (0, masks[0], masks[2], masks[1]), 1 - sec, far_x_ref, gain_ref, gate_ref, up_ref, gate_out, up_out,
+    side, grp = lane_of(True), lax.axis_index("grp")
+    masks = shard_masks(True)
+    first_products(pieces, (0, masks[0], masks[2], masks[1]), 1 - side, far_x_ref, gain_ref, gate_ref, up_ref, gate_out, up_out,
                    square_out)
     width, half = gate_ref.shape[1], near_x_ref.shape[1]
-    spare = jnp.where(sec == 1, near_x_ref[:, width - half:], far_x_ref[:, width - half:]).astype(jnp.float32)
+    spare = jnp.where(side == 1, near_x_ref[:, width - half:], far_x_ref[:, width - half:]).astype(jnp.float32)
     spare_at = lax.broadcasted_iota(jnp.int32, spare.shape, 1)
     weight = jnp.sum(jnp.where((spare_at == 2 * grp) | (spare_at == 2 * grp + 1), spare, 0.0), axis=1, keepdims=True)
     square = (near_square_ref[...] + square_out[...])[:, :1]
@@ -527,15 +547,15 @@
     gate_h = (near_gate_ref[...] + gate_out[...]) * scale
     up_h = (near_up_ref[...] + up_out[...]) * scale
     act_ref[...] = ((up_h + 1.0) * gate_h * jax.nn.sigmoid(1.702 * gate_h) * weight).astype(jnp.bfloat16)
-    second_product(act_ref, down_ref, other_ref, 1 - sec)
+    second_product(act_ref, down_ref, other_ref, 1 - lane_of(False))
 
 
 def last_kernel(act_ref, down_ref, near_x_ref, far_x_ref, mine_ref, middle_ref, row_ref):
     sec, tp = lax.axis_index("sec"), lax.axis_index("tp")
-    second_product(act_ref, down_ref, mine_ref, sec)
+    second_product(act_ref, down_ref, mine_ref, lane_of(False))
     total_rows, part = middle_ref.shape
     near, far = near_x_ref[:total_rows].astype(jnp.float32), far_x_ref[:total_rows].astype(jnp.float32)
-    first = sec == 0
+    first = lane_of(True) == 0
     x = jnp.concatenate([jnp.where(first, near, far), jnp.where(first, far, near)], axis=1)
     for c in range(row_ref.shape[0]):
         row_ref[c] = x[:, c * part:(c + 1) * part]
@@ -585,14 +605,14 @@
     mine = call(own_projection_kernel, "own_projection", shape_of(other.shape, jnp.float32), mix, held, limit=12,
                 flops=mix.size * width)
     middle = call(sum_kernel, "sum", shape_of((steps * rows, LANES)), *scatter_shards(mine, come), own_x)
-    stacked = jnp.stack([middle] + [swap(middle, "grp", m) for m in range(1, groups)])
-    pieces = [stacked] + shard_swaps([stacked] * (tps - 1))
+    stacked = jnp.stack([middle] + [lane_swap(middle, m, (0, 0), True) for m in range(1, groups)])
+    pieces = [stacked] + shard_swaps([stacked] * (tps - 1), True)
     part = width // (secs * tps)
     mine, come, own_middle = experts(expert_gain, w_gate[0], w_up[0], w_down[0], pieces, part)
     lines = steps * rows
     own, *parts = call(after_core_halves_kernel, "after_core_halves",
                        [shape_of((groups * lines, part), jnp.float32)] + [shape_of((groups // 2 * lines, part))] * 6, mine, come)
-    second_come, first_come = shard_swaps(parts[:3]), shard_swaps(parts[3:])
+    second_come, first_come = shard_swaps(parts[:3], False), shard_swaps(parts[3:], False)
     second, third = call(functools.partial(sum_rows_kernel, line=2 * lines), "sum_far_rows", [shape_of((lines, part))] * 2,
                          own, *second_come)
     third, second = swap(third, "grp", 3), swap(second, "grp", 2)

time: 50.2 us -> 48.8 us (0.972)
  waiting for transfers between devices: 20.3 us -> 18.2 us
  starting transfers between devices: 21.7 us -> 22.3 us
    ppermute x12 -> x9, waiting for transfers between devices: 10.3 us -> 3.85 us  [swap(): return lax.ppermute(value, axes, [(i, i ^ mask) for i in range(size)])]
    ppermute x12 -> x15, waiting for transfers between devices: 10 us -> 14.3 us  [lane_swap(): return lax.ppermute(value, ('sec', 'grp', 'tp'), pairs)]
    ppermute x12 -> x15, starting transfers between devices: 15 us -> 17.6 us  [lane_swap(): return lax.ppermute(value, ('sec', 'grp', 'tp'), pairs)]
    ppermute x12 -> x9, starting transfers between devices: 6.67 us -> 4.66 us  [swap(): return lax.ppermute(value, axes, [(i, i ^ mask) for i in range(size)])]
  transfers between devices with their start and end apart: 24 -> 24, of which waited for: 18 -> 16; matrix products, arithmetic and copies ran while one was open for 0% -> 0% of each run, Pallas kernels for 4% -> 4%
where the time goes in v12:
time: 48.8 us; the launch traced here: 48.6 us
  starting transfers between devices  22.3 us (46%)
  waiting for transfers between devices  18.2 us (37%)
  Pallas kernels  7.97 us (16%)
    ppermute x15, starting transfers between devices, lane_swap(): return lax.ppermute(value, ('sec', 'grp', 'tp'), pairs)  17.6 us
    ppermute x15, waiting for transfers between devices, lane_swap(): return lax.ppermute(value, ('sec', 'grp', 'tp'), pairs)  14.3 us
    ppermute x9, starting transfers between devices, swap(): return lax.ppermute(value, axes, [(i, i ^ mask) for i in range(size)])  4.66 us
    pallas_call x1, Pallas kernels, attention_partial(): pl.pallas_call(attention_kernel, name='attention', out_shape=[shape_of((t...  4.24 us
    ppermute x9, waiting for transfers between devices, swap(): return lax.ppermute(value, axes, [(i, i ^ mask) for i in range(size)])  3.85 us
    pallas_call x8, Pallas kernels, call(): pl.pallas_call(kernel, name=name, out_shape=outs, in_specs=[vmem()] * len...  1.96 us
    pallas_call x1, Pallas kernels, experts(): pl.pallas_call(far_kernel, name='far_columns', out_shape=[shape_of((tps,...  1.17 us
  transfers between devices with their start and end apart: 24, of which 16 were waited for; matrix products, arithmetic and copies ran while one was open for 0% of the time, Pallas kernels for 4%

profile of v12, /device:TPU:0, one launch (start us, length us, event | category | flops | bytes accessed | tf_op | source)
XLA Modules:
  0.0 48.6 jit_solution(4980581880214722726)
XLA Ops:
  0.0 4.2 %attention.1 = (bf16[4,32,384]{2,1,0:T(8,128)(2,1)S(1)}, f32[32,384]{1,0:T(8,128)S(1)}, bf16[32,512]{1,0:T(8,128)(2,1)S(1)}, bf16[2880,512]{1,0:T(8,128)(2,1)S(1)}) custom-call(s32[16]{0:T(128)} %lengths_hbm.1, f32[8]{0:T(128)} %sinks_hbm.1, s32[2,4,16]{2,1,0:T(4,128)} %bitcast.31, f32[2,4,16]{2,1,0:T(4,128)} %bitcast.32, f32[2880]{0:T(1024)} %gain_hbm.1, ...), custom_call_target="tpu_custom_call" | custom-call | tf_op jit(solution)/shard_map/attention/pallas_call | solution.py:408
  5.8 3.8 %collective-permute-start.1 = (bf16[32,384]{1,0:T(8,128)(2,1)S(1)}, bf16[32,384]{1,0:T(8,128)(2,1)S(1)}, u32[]{:S(2)}, u32[]{:S(2)}) collective-permute-start(bf16[32,384]{1,0:T(8,128)(2,1)S(1)} %get-tuple-element.37), channel_id=1, source_target_pairs={{0,3},{1,2},{2,1},{3,0},{4,7},{5,6},{6,5},{7,4},{8,11},{9,10},{10,... | collective-permute-start | bytes 73736 | tf_op jit(solution)/shard_map/ppermute | solution.py:247
  10.0 1.4 %collective-permute-done.1.refs_1_ = bf16[32,384]{1,0:T(8,128)(2,1)S(1)} collective-permute-done((bf16[32,384]{1,0:T(8,128)(2,1)S(1)}, bf16[32,384]{1,0:T(8,128)(2,1)S(1)}, u32[]{:S(2)}, u32[]{:S(2)}) %collective-permute-start.1) | collective-permute-done | bytes 24608 | tf_op jit(solution)/shard_map/ppermute | solution.py:247
  11.4 1.4 %collective-permute-done.2.refs_2_ = bf16[32,384]{1,0:T(8,128)(2,1)S(1)} collective-permute-done((bf16[32,384]{1,0:T(8,128)(2,1)S(1)}, bf16[32,384]{1,0:T(8,128)(2,1)S(1)}, u32[]{:S(2)}, u32[]{:S(2)}) %collective-permute-start.2) | collective-permute-done | bytes 24608 | tf_op jit(solution)/shard_map/ppermute | solution.py:247
  13.2 1.6 %collective-permute-start.4 = (bf16[32,384]{1,0:T(8,128)(2,1)S(1)}, bf16[32,384]{1,0:T(8,128)(2,1)S(1)}, u32[]{:S(2)}, u32[]{:S(2)}) collective-permute-start(bf16[32,384]{1,0:T(8,128)(2,1)S(1)} %sum.1), channel_id=1, source_target_pairs={{0,20},{1,21},{2,22},{3,23},{4,16},{5,17},{6,18},{7,19},{8,28},{9,... | collective-permute-start | bytes 73736 | tf_op jit(solution)/shard_map/ppermute | solution.py:247
  14.8 2.6 %collective-permute-start.5 = (bf16[32,384]{1,0:T(8,128)(2,1)S(1)}, bf16[32,384]{1,0:T(8,128)(2,1)S(1)}, u32[]{:S(2)}, u32[]{:S(2)}) collective-permute-start(bf16[32,384]{1,0:T(8,128)(2,1)S(1)} %sum.1), channel_id=1, source_target_pairs={{0,8},{1,9},{2,10},{3,11},{4,12},{5,13},{6,14},{7,15},{8,0},{9,1},... | collective-permute-start | bytes 73736 | tf_op jit(solution)/shard_map/ppermute | solution.py:247
  17.4 2.3 %collective-permute-done.5 = bf16[32,384]{1,0:T(8,128)(2,1)S(1)} collective-permute-done((bf16[32,384]{1,0:T(8,128)(2,1)S(1)}, bf16[32,384]{1,0:T(8,128)(2,1)S(1)}, u32[]{:S(2)}, u32[]{:S(2)}) %collective-permute-start.5) | collective-permute-done | bytes 24608 | tf_op jit(solution)/shard_map/ppermute | solution.py:247
  19.7 2.9 %collective-permute-done.6 = bf16[32,384]{1,0:T(8,128)(2,1)S(1)} collective-permute-done((bf16[32,384]{1,0:T(8,128)(2,1)S(1)}, bf16[32,384]{1,0:T(8,128)(2,1)S(1)}, u32[]{:S(2)}, u32[]{:S(2)}) %collective-permute-start.6) | collective-permute-done | bytes 24608 | tf_op jit(solution)/shard_map/ppermute | solution.py:247
  22.7 1.5 %collective-permute-start.7 = (bf16[4,32,384]{2,1,0:T(8,128)(2,1)S(1)}, bf16[4,32,384]{2,1,0:T(8,128)(2,1)S(1)}, u32[]{:S(2)}, u32[]{:S(2)}) collective-permute-start(bf16[4,32,384]{2,1,0:T(8,128)(2,1)S(1)} %pad_maximum_fusion.refs_0_), channel_id=1, source_target_pairs={{0,3},{1,2},{2,1},{3,0},{4,7},{5,6},{6,5},{7,4},{8,11},{9,10},{10,... | collective-permute-start | bytes 294920 | tf_op jit(solution)/shard_map/ppermute | solution.py:247
  24.2 1.8 %collective-permute-start.9 = (bf16[4,32,384]{2,1,0:T(8,128)(2,1)S(1)}, bf16[4,32,384]{2,1,0:T(8,128)(2,1)S(1)}, u32[]{:S(2)}, u32[]{:S(2)}) collective-permute-start(bf16[4,32,384]{2,1,0:T(8,128)(2,1)S(1)} %pad_maximum_fusion.refs_0_), channel_id=1, source_target_pairs={{0,18},{1,16},{2,19},{3,17},{4,21},{5,23},{6,20},{7,22},{8,26},{9,... | collective-permute-start | bytes 294920 | tf_op jit(solution)/shard_map/ppermute | solution.py:247
  26.0 2.9 %collective-permute-done.7.refs_1_ = bf16[4,32,384]{2,1,0:T(8,128)(2,1)S(1)} collective-permute-done((bf16[4,32,384]{2,1,0:T(8,128)(2,1)S(1)}, bf16[4,32,384]{2,1,0:T(8,128)(2,1)S(1)}, u32[]{:S(2)}, u32[]{:S(2)}) %collective-permute-start.7) | collective-permute-done | bytes 98336 | tf_op jit(solution)/shard_map/ppermute | solution.py:247
  29.3 1.4 %collective-permute-start.12 = (bf16[4,32,384]{2,1,0:T(8,128)(2,1)S(1)}, bf16[4,32,384]{2,1,0:T(8,128)(2,1)S(1)}, u32[]{:S(2)}, u32[]{:S(2)}) collective-permute-start(bf16[4,32,384]{2,1,0:T(8,128)(2,1)S(1)} %collective-permute-done.8.refs_2_), channel_id=1, source_target_pairs={{0,16},{16,0},{1,17},{17,1},{2,18},{18,2},{3,19},{19,3},{4,20},{20... | collective-permute-start | bytes 294920 | tf_op jit(solution)/shard_map/ppermute | solution.py:224
  30.7 0.6 %near_columns.1 = (bf16[128,1536]{1,0:T(8,128)(2,1)S(1)}, f32[128,180]{1,0:T(8,128)S(1)}, f32[128,180]{1,0:T(8,128)S(1)}, f32[128,128]{1,0:T(8,128)S(1)}) custom-call(f32[1,2880]{1,0:T(1,128)S(1)} %reshape.6.gain_ref, bf16[180,2880]{1,0:T(8,128)(2,1)S(1)} %bitcast.17, bf16[180,2880]{1,0:T(8,128)(2,1)S(1)} %bitcast.19, ...), custom_call_target="tpu_custom_call" | custom-call | flops 132710400 | bytes 3121408 | tf_op jit(solution)/shard_map/near_columns/pallas_call | solution.py:437
  32.0 1.2 %far_columns.1 = (bf16[4,128,360]{2,1,0:T(8,128)(2,1)S(1)}, bf16[128,180]{1,0:T(8,128)(2,1)S(1)}, bf16[128,1536]{1,0:T(8,128)(2,1)S(1)}) custom-call(f32[1,2880]{1,0:T(1,128)S(1)} %reshape.6.gain_ref, bf16[180,2880]{1,0:T(8,128)(2,1)S(1)} %bitcast.18, bf16[180,2880]{1,0:T(8,128)(2,1)S(1)} %bitcast.20, bf16[180,2880]{1,0:T(8,128)(2,1)S(1)} %bitcast.21, ...), custom_call_target="tpu_custom_call" | custom-call | tf_op jit(solution)/shard_map/far_columns/pallas_call | solution.py:573
  34.0 1.0 %collective-permute-done.14.come_ref = bf16[4,128,360]{2,1,0:T(8,128)(2,1)S(1)} collective-permute-done((bf16[4,128,360]{2,1,0:T(8,128)(2,1)S(1)}, bf16[4,128,360]{2,1,0:T(8,128)(2,1)S(1)}, u32[]{:S(2)}, u32[]{:S(2)}) %collective-permute-start.14) | collective-permute-done | bytes 368672 | tf_op jit(solution)/shard_map/ppermute | solution.py:224
  35.0 1.5 %collective-permute-start.18 = (bf16[64,360]{1,0:T(8,128)(2,1)S(1)}, bf16[64,360]{1,0:T(8,128)(2,1)S(1)}, u32[]{:S(2)}, u32[]{:S(2)}) collective-permute-start(bf16[64,360]{1,0:T(8,128)(2,1)S(1)} %get-tuple-element.54), channel_id=1, source_target_pairs={{0,3},{1,2},{2,1},{3,0},{4,7},{5,6},{6,5},{7,4},{8,11},{9,10},{10,... | collective-permute-start | bytes 138248 | tf_op jit(solution)/shard_map/ppermute | solution.py:247
  36.5 1.8 %collective-permute-start.20 = (bf16[64,360]{1,0:T(8,128)(2,1)S(1)}, bf16[64,360]{1,0:T(8,128)(2,1)S(1)}, u32[]{:S(2)}, u32[]{:S(2)}) collective-permute-start(bf16[64,360]{1,0:T(8,128)(2,1)S(1)} %get-tuple-element.56), channel_id=1, source_target_pairs={{0,18},{1,16},{2,19},{3,17},{4,22},{5,20},{6,23},{7,21},{8,26},{9,... | collective-permute-start | bytes 138248 | tf_op jit(solution)/shard_map/ppermute | solution.py:247
  38.3 1.4 %collective-permute-start.15 = (bf16[64,360]{1,0:T(8,128)(2,1)S(1)}, bf16[64,360]{1,0:T(8,128)(2,1)S(1)}, u32[]{:S(2)}, u32[]{:S(2)}) collective-permute-start(bf16[64,360]{1,0:T(8,128)(2,1)S(1)} %get-tuple-element.50), channel_id=1, source_target_pairs={{0,3},{1,2},{2,1},{3,0},{4,7},{5,6},{6,5},{7,4},{8,11},{9,10},{10,... | collective-permute-start | bytes 138248 | tf_op jit(solution)/shard_map/ppermute | solution.py:247
  40.2 1.3 %collective-permute-start.17 = (bf16[64,360]{1,0:T(8,128)(2,1)S(1)}, bf16[64,360]{1,0:T(8,128)(2,1)S(1)}, u32[]{:S(2)}, u32[]{:S(2)}) collective-permute-start(bf16[64,360]{1,0:T(8,128)(2,1)S(1)} %get-tuple-element.52), channel_id=1, source_target_pairs={{0,18},{1,16},{2,19},{3,17},{4,22},{5,20},{6,23},{7,21},{8,26},{9,... | collective-permute-start | bytes 138248 | tf_op jit(solution)/shard_map/ppermute | solution.py:247
  42.0 1.4 %collective-permute-done.15.refs_0_ = bf16[64,360]{1,0:T(8,128)(2,1)S(1)} collective-permute-done((bf16[64,360]{1,0:T(8,128)(2,1)S(1)}, bf16[64,360]{1,0:T(8,128)(2,1)S(1)}, u32[]{:S(2)}, u32[]{:S(2)}) %collective-permute-start.15) | collective-permute-done | bytes 46112 | tf_op jit(solution)/shard_map/ppermute | solution.py:247
  43.4 0.6 %collective-permute-done.17.refs_2_ = bf16[64,360]{1,0:T(8,128)(2,1)S(1)} collective-permute-done((bf16[64,360]{1,0:T(8,128)(2,1)S(1)}, bf16[64,360]{1,0:T(8,128)(2,1)S(1)}, u32[]{:S(2)}, u32[]{:S(2)}) %collective-permute-start.17) | collective-permute-done | bytes 46112 | tf_op jit(solution)/shard_map/ppermute | solution.py:247
  44.1 2.0 %collective-permute-start.23 = (bf16[32,360]{1,0:T(8,128)(2,1)S(1)}, bf16[32,360]{1,0:T(8,128)(2,1)S(1)}, u32[]{:S(2)}, u32[]{:S(2)}) collective-permute-start(bf16[32,360]{1,0:T(8,128)(2,1)S(1)} %get-tuple-element.59), channel_id=1, source_target_pairs={{0,4},{4,0},{8,12},{12,8},{1,5},{5,1},{9,13},{13,9},{2,6},{6,2},{1... | collective-permute-start | bytes 69128 | tf_op jit(solution)/shard_map/ppermute | solution.py:224
  46.1 1.4 %collective-permute-done.21.refs_1_ = bf16[32,360]{1,0:T(8,128)(2,1)S(1)} collective-permute-done((bf16[32,360]{1,0:T(8,128)(2,1)S(1)}, bf16[32,360]{1,0:T(8,128)(2,1)S(1)}, u32[]{:S(2)}, u32[]{:S(2)}) %collective-permute-start.21) | collective-permute-done | bytes 23072 | tf_op jit(solution)/shard_map/ppermute | solution.py:224
  48.0 0.6 %combine.1 = bf16[2,16,360]{2,1,0:T(8,128)(2,1)} custom-call(f32[32,360]{1,0:T(8,128)S(1)} %get-tuple-element.53.refs_0_, bf16[32,360]{1,0:T(8,128)(2,1)S(1)} %collective-permute-done.21.refs_1_, bf16[32,360]{1,0:T(8,128)(2,1)S(1)} %collective-permute-done.22.refs_2_, bf16[32,360]{1,0:T(8,128)(2,1)S(1)} %collective-permute-done.23.refs_3_, ...), custom_call_target="tpu_custom_call" | custom-call | bytes 184320 | tf_op jit(solution)/shard_map/combine/pallas_call | solution.py:437
  (45 shorter events, 5.6 us)
Async XLA Ops:
  4.3 1.5 %collective-permute-start = (bf16[4,32,384]{2,1,0:T(8,128)(2,1)S(1)}, bf16[4,32,384]{2,1,0:T(8,128)(2,1)S(1)}, u32[]{:S(2)}, u32[]{:S(2)}) collective-permute-start(bf16[4,32,384]{2,1,0:T(8,128)(2,1)S(1)} %get-tuple-element.35), channel_id=1, source_target_pairs={{0,16},{16,0},{1,17},{17,1},{2,18},{18,2},{3,19},{19,3},{4,20},{20... | collective-permute-start | bytes 294920 | tf_op jit(solution)/shard_map/ppermute | solution.py:224
  5.8 5.6 %collective-permute-start.1 = (bf16[32,384]{1,0:T(8,128)(2,1)S(1)}, bf16[32,384]{1,0:T(8,128)(2,1)S(1)}, u32[]{:S(2)}, u32[]{:S(2)}) collective-permute-start(bf16[32,384]{1,0:T(8,128)(2,1)S(1)} %get-tuple-element.37), channel_id=1, source_target_pairs={{0,3},{1,2},{2,1},{3,0},{4,7},{5,6},{6,5},{7,4},{8,11},{9,10},{10,... | collective-permute-start | bytes 73736 | tf_op jit(solution)/shard_map/ppermute | solution.py:247
  9.6 3.3 %collective-permute-start.2 = (bf16[32,384]{1,0:T(8,128)(2,1)S(1)}, bf16[32,384]{1,0:T(8,128)(2,1)S(1)}, u32[]{:S(2)}, u32[]{:S(2)}) collective-permute-start(bf16[32,384]{1,0:T(8,128)(2,1)S(1)} %get-tuple-element.38), channel_id=1, source_target_pairs={{0,17},{1,19},{2,16},{3,18},{4,22},{5,20},{6,23},{7,21},{8,25},{9,... | collective-permute-start | bytes 73736 | tf_op jit(solution)/shard_map/ppermute | solution.py:247
  9.7 3.5 %collective-permute-start.3 = (bf16[32,384]{1,0:T(8,128)(2,1)S(1)}, bf16[32,384]{1,0:T(8,128)(2,1)S(1)}, u32[]{:S(2)}, u32[]{:S(2)}) collective-permute-start(bf16[32,384]{1,0:T(8,128)(2,1)S(1)} %get-tuple-element.39), channel_id=1, source_target_pairs={{0,18},{1,16},{2,19},{3,17},{4,21},{5,23},{6,20},{7,22},{8,26},{9,... | collective-permute-start | bytes 73736 | tf_op jit(solution)/shard_map/ppermute | solution.py:247
  13.2 4.2 %collective-permute-start.4 = (bf16[32,384]{1,0:T(8,128)(2,1)S(1)}, bf16[32,384]{1,0:T(8,128)(2,1)S(1)}, u32[]{:S(2)}, u32[]{:S(2)}) collective-permute-start(bf16[32,384]{1,0:T(8,128)(2,1)S(1)} %sum.1), channel_id=1, source_target_pairs={{0,20},{1,21},{2,22},{3,23},{4,16},{5,17},{6,18},{7,19},{8,28},{9,... | collective-permute-start | bytes 73736 | tf_op jit(solution)/shard_map/ppermute | solution.py:247
  14.8 4.9 %collective-permute-start.5 = (bf16[32,384]{1,0:T(8,128)(2,1)S(1)}, bf16[32,384]{1,0:T(8,128)(2,1)S(1)}, u32[]{:S(2)}, u32[]{:S(2)}) collective-permute-start(bf16[32,384]{1,0:T(8,128)(2,1)S(1)} %sum.1), channel_id=1, source_target_pairs={{0,8},{1,9},{2,10},{3,11},{4,12},{5,13},{6,14},{7,15},{8,0},{9,1},... | collective-permute-start | bytes 73736 | tf_op jit(solution)/shard_map/ppermute | solution.py:247
  17.4 5.3 %collective-permute-start.6 = (bf16[32,384]{1,0:T(8,128)(2,1)S(1)}, bf16[32,384]{1,0:T(8,128)(2,1)S(1)}, u32[]{:S(2)}, u32[]{:S(2)}) collective-permute-start(bf16[32,384]{1,0:T(8,128)(2,1)S(1)} %sum.1), channel_id=1, source_target_pairs={{0,28},{1,29},{2,30},{3,31},{4,24},{5,25},{6,26},{7,27},{8,20},{9,... | collective-permute-start | bytes 73736 | tf_op jit(solution)/shard_map/ppermute | solution.py:247
  22.7 6.2 %collective-permute-start.7 = (bf16[4,32,384]{2,1,0:T(8,128)(2,1)S(1)}, bf16[4,32,384]{2,1,0:T(8,128)(2,1)S(1)}, u32[]{:S(2)}, u32[]{:S(2)}) collective-permute-start(bf16[4,32,384]{2,1,0:T(8,128)(2,1)S(1)} %pad_maximum_fusion.refs_0_), channel_id=1, source_target_pairs={{0,3},{1,2},{2,1},{3,0},{4,7},{5,6},{6,5},{7,4},{8,11},{9,10},{10,... | collective-permute-start | bytes 294920 | tf_op jit(solution)/shard_map/ppermute | solution.py:247
  24.2 5.1 %collective-permute-start.8 = (bf16[4,32,384]{2,1,0:T(8,128)(2,1)S(1)}, bf16[4,32,384]{2,1,0:T(8,128)(2,1)S(1)}, u32[]{:S(2)}, u32[]{:S(2)}) collective-permute-start(bf16[4,32,384]{2,1,0:T(8,128)(2,1)S(1)} %pad_maximum_fusion.refs_0_), channel_id=1, source_target_pairs={{0,17},{1,19},{2,16},{3,18},{4,22},{5,20},{6,23},{7,21},{8,25},{9,... | collective-permute-start | bytes 294920 | tf_op jit(solution)/shard_map/ppermute | solution.py:247
  24.2 6.5 %collective-permute-start.9 = (bf16[4,32,384]{2,1,0:T(8,128)(2,1)S(1)}, bf16[4,32,384]{2,1,0:T(8,128)(2,1)S(1)}, u32[]{:S(2)}, u32[]{:S(2)}) collective-permute-start(bf16[4,32,384]{2,1,0:T(8,128)(2,1)S(1)} %pad_maximum_fusion.refs_0_), channel_id=1, source_target_pairs={{0,18},{1,16},{2,19},{3,17},{4,21},{5,23},{6,20},{7,22},{8,26},{9,... | collective-permute-start | bytes 294920 | tf_op jit(solution)/shard_map/ppermute | solution.py:247
  26.0 5.4 %collective-permute-start.10 = (bf16[4,32,384]{2,1,0:T(8,128)(2,1)S(1)}, bf16[4,32,384]{2,1,0:T(8,128)(2,1)S(1)}, u32[]{:S(2)}, u32[]{:S(2)}) collective-permute-start(bf16[4,32,384]{2,1,0:T(8,128)(2,1)S(1)} %pad_maximum_fusion.refs_0_), channel_id=1, source_target_pairs={{0,16},{16,0},{1,17},{17,1},{2,18},{18,2},{3,19},{19,3},{4,20},{20... | collective-permute-start | bytes 294920 | tf_op jit(solution)/shard_map/ppermute | solution.py:224
  28.9 2.5 %collective-permute-start.11 = (bf16[4,32,384]{2,1,0:T(8,128)(2,1)S(1)}, bf16[4,32,384]{2,1,0:T(8,128)(2,1)S(1)}, u32[]{:S(2)}, u32[]{:S(2)}) collective-permute-start(bf16[4,32,384]{2,1,0:T(8,128)(2,1)S(1)} %collective-permute-done.7.refs_1_), channel_id=1, source_target_pairs={{0,16},{16,0},{1,17},{17,1},{2,18},{18,2},{3,19},{19,3},{4,20},{20... | collective-permute-start | bytes 294920 | tf_op jit(solution)/shard_map/ppermute | solution.py:224
  29.3 2.4 %collective-permute-start.12 = (bf16[4,32,384]{2,1,0:T(8,128)(2,1)S(1)}, bf16[4,32,384]{2,1,0:T(8,128)(2,1)S(1)}, u32[]{:S(2)}, u32[]{:S(2)}) collective-permute-start(bf16[4,32,384]{2,1,0:T(8,128)(2,1)S(1)} %collective-permute-done.8.refs_2_), channel_id=1, source_target_pairs={{0,16},{16,0},{1,17},{17,1},{2,18},{18,2},{3,19},{19,3},{4,20},{20... | collective-permute-start | bytes 294920 | tf_op jit(solution)/shard_map/ppermute | solution.py:224
  30.7 1.3 %collective-permute-start.13 = (bf16[4,32,384]{2,1,0:T(8,128)(2,1)S(1)}, bf16[4,32,384]{2,1,0:T(8,128)(2,1)S(1)}, u32[]{:S(2)}, u32[]{:S(2)}) collective-permute-start(bf16[4,32,384]{2,1,0:T(8,128)(2,1)S(1)} %collective-permute-done.9.refs_3_), channel_id=1, source_target_pairs={{0,16},{16,0},{1,17},{17,1},{2,18},{18,2},{3,19},{19,3},{4,20},{20... | collective-permute-start | bytes 294920 | tf_op jit(solution)/shard_map/ppermute | solution.py:224
  33.2 1.8 %collective-permute-start.14 = (bf16[4,128,360]{2,1,0:T(8,128)(2,1)S(1)}, bf16[4,128,360]{2,1,0:T(8,128)(2,1)S(1)}, u32[]{:S(2)}, u32[]{:S(2)}) collective-permute-start(bf16[4,128,360]{2,1,0:T(8,128)(2,1)S(1)} %get-tuple-element.48), channel_id=1, source_target_pairs={{0,16},{16,0},{1,17},{17,1},{2,18},{18,2},{3,19},{19,3},{4,20},{20... | collective-permute-start | bytes 1105928 | tf_op jit(solution)/shard_map/ppermute | solution.py:224
  35.0 5.2 %collective-permute-start.18 = (bf16[64,360]{1,0:T(8,128)(2,1)S(1)}, bf16[64,360]{1,0:T(8,128)(2,1)S(1)}, u32[]{:S(2)}, u32[]{:S(2)}) collective-permute-start(bf16[64,360]{1,0:T(8,128)(2,1)S(1)} %get-tuple-element.54), channel_id=1, source_target_pairs={{0,3},{1,2},{2,1},{3,0},{4,7},{5,6},{6,5},{7,4},{8,11},{9,10},{10,... | collective-permute-start | bytes 138248 | tf_op jit(solution)/shard_map/ppermute | solution.py:247
  36.5 5.0 %collective-permute-start.19 = (bf16[64,360]{1,0:T(8,128)(2,1)S(1)}, bf16[64,360]{1,0:T(8,128)(2,1)S(1)}, u32[]{:S(2)}, u32[]{:S(2)}) collective-permute-start(bf16[64,360]{1,0:T(8,128)(2,1)S(1)} %get-tuple-element.55), channel_id=1, source_target_pairs={{0,17},{1,19},{2,16},{3,18},{4,21},{5,23},{6,20},{7,22},{8,25},{9,... | collective-permute-start | bytes 138248 | tf_op jit(solution)/shard_map/ppermute | solution.py:247
  36.5 5.0 %collective-permute-start.20 = (bf16[64,360]{1,0:T(8,128)(2,1)S(1)}, bf16[64,360]{1,0:T(8,128)(2,1)S(1)}, u32[]{:S(2)}, u32[]{:S(2)}) collective-permute-start(bf16[64,360]{1,0:T(8,128)(2,1)S(1)} %get-tuple-element.56), channel_id=1, source_target_pairs={{0,18},{1,16},{2,19},{3,17},{4,22},{5,20},{6,23},{7,21},{8,26},{9,... | collective-permute-start | bytes 138248 | tf_op jit(solution)/shard_map/ppermute | solution.py:247
  38.3 5.1 %collective-permute-start.15 = (bf16[64,360]{1,0:T(8,128)(2,1)S(1)}, bf16[64,360]{1,0:T(8,128)(2,1)S(1)}, u32[]{:S(2)}, u32[]{:S(2)}) collective-permute-start(bf16[64,360]{1,0:T(8,128)(2,1)S(1)} %get-tuple-element.50), channel_id=1, source_target_pairs={{0,3},{1,2},{2,1},{3,0},{4,7},{5,6},{6,5},{7,4},{8,11},{9,10},{10,... | collective-permute-start | bytes 138248 | tf_op jit(solution)/shard_map/ppermute | solution.py:247
  39.7 3.7 %collective-permute-start.16 = (bf16[64,360]{1,0:T(8,128)(2,1)S(1)}, bf16[64,360]{1,0:T(8,128)(2,1)S(1)}, u32[]{:S(2)}, u32[]{:S(2)}) collective-permute-start(bf16[64,360]{1,0:T(8,128)(2,1)S(1)} %get-tuple-element.51), channel_id=1, source_target_pairs={{0,17},{1,19},{2,16},{3,18},{4,21},{5,23},{6,20},{7,22},{8,25},{9,... | collective-permute-start | bytes 138248 | tf_op jit(solution)/shard_map/ppermute | solution.py:247
  40.2 3.9 %collective-permute-start.17 = (bf16[64,360]{1,0:T(8,128)(2,1)S(1)}, bf16[64,360]{1,0:T(8,128)(2,1)S(1)}, u32[]{:S(2)}, u32[]{:S(2)}) collective-permute-start(bf16[64,360]{1,0:T(8,128)(2,1)S(1)} %get-tuple-element.52), channel_id=1, source_target_pairs={{0,18},{1,16},{2,19},{3,17},{4,22},{5,20},{6,23},{7,21},{8,26},{9,... | collective-permute-start | bytes 138248 | tf_op jit(solution)/shard_map/ppermute | solution.py:247
  41.6 5.9 %collective-permute-start.21 = (bf16[32,360]{1,0:T(8,128)(2,1)S(1)}, bf16[32,360]{1,0:T(8,128)(2,1)S(1)}, u32[]{:S(2)}, u32[]{:S(2)}) collective-permute-start(bf16[32,360]{1,0:T(8,128)(2,1)S(1)} %get-tuple-element.57), channel_id=1, source_target_pairs={{0,12},{4,8},{8,4},{12,0},{1,13},{5,9},{9,5},{13,1},{2,14},{6,10},... | collective-permute-start | bytes 69128 | tf_op jit(solution)/shard_map/ppermute | solution.py:224
  42.0 5.5 %collective-permute-start.22 = (bf16[32,360]{1,0:T(8,128)(2,1)S(1)}, bf16[32,360]{1,0:T(8,128)(2,1)S(1)}, u32[]{:S(2)}, u32[]{:S(2)}) collective-permute-start(bf16[32,360]{1,0:T(8,128)(2,1)S(1)} %get-tuple-element.58), channel_id=1, source_target_pairs={{0,8},{4,12},{8,0},{12,4},{1,9},{5,13},{9,1},{13,5},{2,10},{6,14},... | collective-permute-start | bytes 69128 | tf_op jit(solution)/shard_map/ppermute | solution.py:224
  44.1 3.9 %collective-permute-start.23 = (bf16[32,360]{1,0:T(8,128)(2,1)S(1)}, bf16[32,360]{1,0:T(8,128)(2,1)S(1)}, u32[]{:S(2)}, u32[]{:S(2)}) collective-permute-start(bf16[32,360]{1,0:T(8,128)(2,1)S(1)} %get-tuple-element.59), channel_id=1, source_target_pairs={{0,4},{4,0},{8,12},{12,8},{1,5},{5,1},{9,13},{13,9},{2,6},{6,2},{1... | collective-permute-start | bytes 69128 | tf_op jit(solution)/shard_map/ppermute | solution.py:224
  (4 other events, 106.5 us)

commit v13 on v12

--- a/solution.py
+++ b/solution.py
@@ -280,9 +280,17 @@
         part = pl.ds(low, high - low)
         copies.append(pltpu.make_async_copy(wq_hbm.at[part], wq_ref.at[part], sems.at[9 + n]))
     copies.append(pltpu.make_async_copy(cache_hbm, cache_ref, sems.at[7]))
-    copies.append(pltpu.make_async_copy(wo_hbm, wo_ref, sems.at[8]))
     for copy in small + copies:
         copy.start()
+    middle = tps * LANES
+    halves = [pltpu.make_async_copy(wo_hbm.at[part], wo_ref.at[part], sems.at[sem])
+              for part, sem in ((pl.ds(0, middle), 8), (pl.ds(middle, width - middle), 9 + len(cuts)))]
+    for at in range(2):
+        @pl.when(lane_of(True) == at)
+        def _(at=at):
+            halves[1 - at].start()
+            halves[at].start()
+
     small[1].wait()
     small[2].wait()
     x = x_ref[...].astype(jnp.float32)
@@ -342,7 +350,7 @@
                 turned_ref[pl.ds(slot, rows, stride=per_row), :] = one[s * rows:(s + 1) * rows]
     turned = turned_ref[...].astype(jnp.bfloat16)
 
-    copies[-2].wait()
+    copies[-1].wait()
     place = lax.broadcasted_iota(jnp.int32, (per_row, slots), 1)
     scores = []
     for r in range(rows):
@@ -375,17 +383,22 @@
     mix_ref[...] = jnp.concatenate(
         [jnp.where(is_key, pltpu.roll(head(2 * m), HEAD_SIZE, 1), head(2 * m + 1)) for m in range(heads // 2)], axis=1
     ).astype(jnp.bfloat16)
-    copies[-1].wait()
-    project(mix_ref, wo_ref, other_ref, 1 - lane_of(True))
-
-
-def project(mix_ref, wo_ref, out_ref, side):
+    project(mix_ref, wo_ref, other_ref, 1 - lane_of(True), halves)
+    for at in range(2):
+        @pl.when(lane_of(True) == at)
+        def _(at=at):
+            halves[at].wait()
+
+
+def project(mix_ref, wo_ref, out_ref, side, halves=None):
     width, (tps, total_rows, _) = wo_ref.shape[0], out_ref.shape
     for at in range(2):
         start, stop = at * tps * LANES, min((at + 1) * tps * LANES, width)
 
         @pl.when(side == at)
-        def _(start=start, stop=stop):
+        def _(at=at, start=start, stop=stop):
+            if halves is not None:
+                halves[at].wait()
             partial = dot_last(mix_ref[...], wo_ref[start:stop, :])
             for t in range(tps):
                 low, high = t * LANES, min((t + 1) * LANES, stop - start)
@@ -425,7 +438,7 @@
             pltpu.VMEM((total_rows, shards * LANES), jnp.float32),
             pltpu.VMEM((rows * per_row, pair), jnp.float32),
             pltpu.VMEM((rows * per_row, pair), jnp.float32),
-            pltpu.SemaphoreType.DMA((9 + len(split_width(width)),)),
+            pltpu.SemaphoreType.DMA((10 + len(split_width(width)),)),
         ],
         compiler_params=pltpu.CompilerParams(vmem_limit_bytes=24 * MIB),
     )(*[pltpu.with_memory_space_constraint(operand, pltpu.HBM) for operand in operands])
@@ -601,6 +614,7 @@
     other, own_x, mix, held = attention_partial(
         flat, attention_gain, w_query, key_value_weight[:, 0], head_sink_logits, w_output, cache_pairs[:, :, 0], lengths,
         routes.swapaxes(1, 2), gate_weights.swapaxes(1, 2), secs, tps)
+    w_gate, w_up, w_down, other = lax.optimization_barrier((w_gate, w_up, w_down, other))
     come = swap(other, "sec", 1)
     mine = call(own_projection_kernel, "own_projection", shape_of(other.shape, jnp.float32), mix, held, limit=12,
                 flops=mix.size * width)

time: 48.8 us -> 48.8 us (level)
  no operation moved by 1% of the time
where the time goes in v13:
time: 48.8 us; the launch traced here: 48.6 us
  starting transfers between devices  22.3 us (46%)
  waiting for transfers between devices  18.2 us (37%)
  Pallas kernels  7.98 us (16%)
    ppermute x15, starting transfers between devices, lane_swap(): return lax.ppermute(value, ('sec', 'grp', 'tp'), pairs)  17.6 us
    ppermute x15, waiting for transfers between devices, lane_swap(): return lax.ppermute(value, ('sec', 'grp', 'tp'), pairs)  14.3 us
    ppermute x9, starting transfers between devices, swap(): return lax.ppermute(value, axes, [(i, i ^ mask) for i in range(size)])  4.63 us
    pallas_call x1, Pallas kernels, attention_partial(): pl.pallas_call(attention_kernel, name='attention', out_shape=[shape_of((t...  4.26 us
    ppermute x9, waiting for transfers between devices, swap(): return lax.ppermute(value, axes, [(i, i ^ mask) for i in range(size)])  3.86 us
    pallas_call x8, Pallas kernels, call(): pl.pallas_call(kernel, name=name, out_shape=outs, in_specs=[vmem()] * len...  1.95 us
    pallas_call x1, Pallas kernels, experts(): pl.pallas_call(far_kernel, name='far_columns', out_shape=[shape_of((tps,...  1.18 us
  transfers between devices with their start and end apart: 24, of which 16 were waited for; matrix products, arithmetic and copies ran while one was open for 0% of the time, Pallas kernels for 4%

profile of v13, /device:TPU:0, one launch (start us, length us, event | category | flops | bytes accessed | tf_op | source)
XLA Modules:
  0.0 48.6 jit_solution(4858053653937792702)
XLA Ops:
  0.0 4.3 %attention.1 = (bf16[4,32,384]{2,1,0:T(8,128)(2,1)S(1)}, f32[32,384]{1,0:T(8,128)S(1)}, bf16[32,512]{1,0:T(8,128)(2,1)S(1)}, bf16[2880,512]{1,0:T(8,128)(2,1)S(1)}) custom-call(s32[16]{0:T(128)} %lengths_hbm.1, f32[8]{0:T(128)} %sinks_hbm.1, s32[2,4,16]{2,1,0:T(4,128)} %bitcast.31, f32[2,4,16]{2,1,0:T(4,128)} %bitcast.32, f32[2880]{0:T(1024)} %gain_hbm.1, ...), custom_call_target="tpu_custom_call" | custom-call | tf_op jit(solution)/shard_map/attention/pallas_call | solution.py:421
  5.8 3.8 %collective-permute-start.1 = (bf16[32,384]{1,0:T(8,128)(2,1)S(1)}, bf16[32,384]{1,0:T(8,128)(2,1)S(1)}, u32[]{:S(2)}, u32[]{:S(2)}) collective-permute-start(bf16[32,384]{1,0:T(8,128)(2,1)S(1)} %get-tuple-element.45), channel_id=1, source_target_pairs={{0,3},{1,2},{2,1},{3,0},{4,7},{5,6},{6,5},{7,4},{8,11},{9,10},{10,... | collective-permute-start | bytes 73736 | tf_op jit(solution)/shard_map/ppermute | solution.py:247
  10.0 1.4 %collective-permute-done.1.refs_1_ = bf16[32,384]{1,0:T(8,128)(2,1)S(1)} collective-permute-done((bf16[32,384]{1,0:T(8,128)(2,1)S(1)}, bf16[32,384]{1,0:T(8,128)(2,1)S(1)}, u32[]{:S(2)}, u32[]{:S(2)}) %collective-permute-start.1) | collective-permute-done | bytes 24608 | tf_op jit(solution)/shard_map/ppermute | solution.py:247
  11.5 1.4 %collective-permute-done.2.refs_2_ = bf16[32,384]{1,0:T(8,128)(2,1)S(1)} collective-permute-done((bf16[32,384]{1,0:T(8,128)(2,1)S(1)}, bf16[32,384]{1,0:T(8,128)(2,1)S(1)}, u32[]{:S(2)}, u32[]{:S(2)}) %collective-permute-start.2) | collective-permute-done | bytes 24608 | tf_op jit(solution)/shard_map/ppermute | solution.py:247
  13.3 1.6 %collective-permute-start.4 = (bf16[32,384]{1,0:T(8,128)(2,1)S(1)}, bf16[32,384]{1,0:T(8,128)(2,1)S(1)}, u32[]{:S(2)}, u32[]{:S(2)}) collective-permute-start(bf16[32,384]{1,0:T(8,128)(2,1)S(1)} %sum.1), channel_id=1, source_target_pairs={{0,20},{1,21},{2,22},{3,23},{4,16},{5,17},{6,18},{7,19},{8,28},{9,... | collective-permute-start | bytes 73736 | tf_op jit(solution)/shard_map/ppermute | solution.py:247
  14.8 2.6 %collective-permute-start.5 = (bf16[32,384]{1,0:T(8,128)(2,1)S(1)}, bf16[32,384]{1,0:T(8,128)(2,1)S(1)}, u32[]{:S(2)}, u32[]{:S(2)}) collective-permute-start(bf16[32,384]{1,0:T(8,128)(2,1)S(1)} %sum.1), channel_id=1, source_target_pairs={{0,8},{1,9},{2,10},{3,11},{4,12},{5,13},{6,14},{7,15},{8,0},{9,1},... | collective-permute-start | bytes 73736 | tf_op jit(solution)/shard_map/ppermute | solution.py:247
  17.4 2.3 %collective-permute-done.5 = bf16[32,384]{1,0:T(8,128)(2,1)S(1)} collective-permute-done((bf16[32,384]{1,0:T(8,128)(2,1)S(1)}, bf16[32,384]{1,0:T(8,128)(2,1)S(1)}, u32[]{:S(2)}, u32[]{:S(2)}) %collective-permute-start.5) | collective-permute-done | bytes 24608 | tf_op jit(solution)/shard_map/ppermute | solution.py:247
  19.7 3.0 %collective-permute-done.6 = bf16[32,384]{1,0:T(8,128)(2,1)S(1)} collective-permute-done((bf16[32,384]{1,0:T(8,128)(2,1)S(1)}, bf16[32,384]{1,0:T(8,128)(2,1)S(1)}, u32[]{:S(2)}, u32[]{:S(2)}) %collective-permute-start.6) | collective-permute-done | bytes 24608 | tf_op jit(solution)/shard_map/ppermute | solution.py:247
  22.7 1.5 %collective-permute-start.7 = (bf16[4,32,384]{2,1,0:T(8,128)(2,1)S(1)}, bf16[4,32,384]{2,1,0:T(8,128)(2,1)S(1)}, u32[]{:S(2)}, u32[]{:S(2)}) collective-permute-start(bf16[4,32,384]{2,1,0:T(8,128)(2,1)S(1)} %pad_maximum_fusion.refs_0_), channel_id=1, source_target_pairs={{0,3},{1,2},{2,1},{3,0},{4,7},{5,6},{6,5},{7,4},{8,11},{9,10},{10,... | collective-permute-start | bytes 294920 | tf_op jit(solution)/shard_map/ppermute | solution.py:247
  24.2 1.8 %collective-permute-start.9 = (bf16[4,32,384]{2,1,0:T(8,128)(2,1)S(1)}, bf16[4,32,384]{2,1,0:T(8,128)(2,1)S(1)}, u32[]{:S(2)}, u32[]{:S(2)}) collective-permute-start(bf16[4,32,384]{2,1,0:T(8,128)(2,1)S(1)} %pad_maximum_fusion.refs_0_), channel_id=1, source_target_pairs={{0,18},{1,16},{2,19},{3,17},{4,21},{5,23},{6,20},{7,22},{8,26},{9,... | collective-permute-start | bytes 294920 | tf_op jit(solution)/shard_map/ppermute | solution.py:247
  26.0 2.9 %collective-permute-done.7.refs_1_ = bf16[4,32,384]{2,1,0:T(8,128)(2,1)S(1)} collective-permute-done((bf16[4,32,384]{2,1,0:T(8,128)(2,1)S(1)}, bf16[4,32,384]{2,1,0:T(8,128)(2,1)S(1)}, u32[]{:S(2)}, u32[]{:S(2)}) %collective-permute-start.7) | collective-permute-done | bytes 98336 | tf_op jit(solution)/shard_map/ppermute | solution.py:247
  29.3 1.4 %collective-permute-start.12 = (bf16[4,32,384]{2,1,0:T(8,128)(2,1)S(1)}, bf16[4,32,384]{2,1,0:T(8,128)(2,1)S(1)}, u32[]{:S(2)}, u32[]{:S(2)}) collective-permute-start(bf16[4,32,384]{2,1,0:T(8,128)(2,1)S(1)} %collective-permute-done.8.refs_2_), channel_id=1, source_target_pairs={{0,16},{16,0},{1,17},{17,1},{2,18},{18,2},{3,19},{19,3},{4,20},{20... | collective-permute-start | bytes 294920 | tf_op jit(solution)/shard_map/ppermute | solution.py:224
  30.8 0.6 %near_columns.1 = (bf16[128,1536]{1,0:T(8,128)(2,1)S(1)}, f32[128,180]{1,0:T(8,128)S(1)}, f32[128,180]{1,0:T(8,128)S(1)}, f32[128,128]{1,0:T(8,128)S(1)}) custom-call(f32[1,2880]{1,0:T(1,128)S(1)} %reshape.6.gain_ref, bf16[180,2880]{1,0:T(8,128)(2,1)S(1)} %bitcast.17, bf16[180,2880]{1,0:T(8,128)(2,1)S(1)} %bitcast.19, ...), custom_call_target="tpu_custom_call" | custom-call | flops 132710400 | bytes 3121408 | tf_op jit(solution)/shard_map/near_columns/pallas_call | solution.py:450
  32.0 1.2 %far_columns.1 = (bf16[4,128,360]{2,1,0:T(8,128)(2,1)S(1)}, bf16[128,180]{1,0:T(8,128)(2,1)S(1)}, bf16[128,1536]{1,0:T(8,128)(2,1)S(1)}) custom-call(f32[1,2880]{1,0:T(1,128)S(1)} %reshape.6.gain_ref, bf16[180,2880]{1,0:T(8,128)(2,1)S(1)} %bitcast.18, bf16[180,2880]{1,0:T(8,128)(2,1)S(1)} %bitcast.20, bf16[180,2880]{1,0:T(8,128)(2,1)S(1)} %bitcast.21, ...), custom_call_target="tpu_custom_call" | custom-call | tf_op jit(solution)/shard_map/far_columns/pallas_call | solution.py:586
  34.0 1.0 %collective-permute-done.14.come_ref = bf16[4,128,360]{2,1,0:T(8,128)(2,1)S(1)} collective-permute-done((bf16[4,128,360]{2,1,0:T(8,128)(2,1)S(1)}, bf16[4,128,360]{2,1,0:T(8,128)(2,1)S(1)}, u32[]{:S(2)}, u32[]{:S(2)}) %collective-permute-start.14) | collective-permute-done | bytes 368672 | tf_op jit(solution)/shard_map/ppermute | solution.py:224
  35.1 1.5 %collective-permute-start.18 = (bf16[64,360]{1,0:T(8,128)(2,1)S(1)}, bf16[64,360]{1,0:T(8,128)(2,1)S(1)}, u32[]{:S(2)}, u32[]{:S(2)}) collective-permute-start(bf16[64,360]{1,0:T(8,128)(2,1)S(1)} %get-tuple-element.62), channel_id=1, source_target_pairs={{0,3},{1,2},{2,1},{3,0},{4,7},{5,6},{6,5},{7,4},{8,11},{9,10},{10,... | collective-permute-start | bytes 138248 | tf_op jit(solution)/shard_map/ppermute | solution.py:247
  36.5 1.8 %collective-permute-start.20 = (bf16[64,360]{1,0:T(8,128)(2,1)S(1)}, bf16[64,360]{1,0:T(8,128)(2,1)S(1)}, u32[]{:S(2)}, u32[]{:S(2)}) collective-permute-start(bf16[64,360]{1,0:T(8,128)(2,1)S(1)} %get-tuple-element.64), channel_id=1, source_target_pairs={{0,18},{1,16},{2,19},{3,17},{4,22},{5,20},{6,23},{7,21},{8,26},{9,... | collective-permute-start | bytes 138248 | tf_op jit(solution)/shard_map/ppermute | solution.py:247
  38.3 1.4 %collective-permute-start.15 = (bf16[64,360]{1,0:T(8,128)(2,1)S(1)}, bf16[64,360]{1,0:T(8,128)(2,1)S(1)}, u32[]{:S(2)}, u32[]{:S(2)}) collective-permute-start(bf16[64,360]{1,0:T(8,128)(2,1)S(1)} %get-tuple-element.58), channel_id=1, source_target_pairs={{0,3},{1,2},{2,1},{3,0},{4,7},{5,6},{6,5},{7,4},{8,11},{9,10},{10,... | collective-permute-start | bytes 138248 | tf_op jit(solution)/shard_map/ppermute | solution.py:247
  40.2 1.3 %collective-permute-start.17 = (bf16[64,360]{1,0:T(8,128)(2,1)S(1)}, bf16[64,360]{1,0:T(8,128)(2,1)S(1)}, u32[]{:S(2)}, u32[]{:S(2)}) collective-permute-start(bf16[64,360]{1,0:T(8,128)(2,1)S(1)} %get-tuple-element.60), channel_id=1, source_target_pairs={{0,18},{1,16},{2,19},{3,17},{4,22},{5,20},{6,23},{7,21},{8,26},{9,... | collective-permute-start | bytes 138248 | tf_op jit(solution)/shard_map/ppermute | solution.py:247
  42.0 1.4 %collective-permute-done.15.refs_0_ = bf16[64,360]{1,0:T(8,128)(2,1)S(1)} collective-permute-done((bf16[64,360]{1,0:T(8,128)(2,1)S(1)}, bf16[64,360]{1,0:T(8,128)(2,1)S(1)}, u32[]{:S(2)}, u32[]{:S(2)}) %collective-permute-start.15) | collective-permute-done | bytes 46112 | tf_op jit(solution)/shard_map/ppermute | solution.py:247
  43.4 0.6 %collective-permute-done.17.refs_2_ = bf16[64,360]{1,0:T(8,128)(2,1)S(1)} collective-permute-done((bf16[64,360]{1,0:T(8,128)(2,1)S(1)}, bf16[64,360]{1,0:T(8,128)(2,1)S(1)}, u32[]{:S(2)}, u32[]{:S(2)}) %collective-permute-start.17) | collective-permute-done | bytes 46112 | tf_op jit(solution)/shard_map/ppermute | solution.py:247
  44.1 2.0 %collective-permute-start.23 = (bf16[32,360]{1,0:T(8,128)(2,1)S(1)}, bf16[32,360]{1,0:T(8,128)(2,1)S(1)}, u32[]{:S(2)}, u32[]{:S(2)}) collective-permute-start(bf16[32,360]{1,0:T(8,128)(2,1)S(1)} %get-tuple-element.67), channel_id=1, source_target_pairs={{0,4},{4,0},{8,12},{12,8},{1,5},{5,1},{9,13},{13,9},{2,6},{6,2},{1... | collective-permute-start | bytes 69128 | tf_op jit(solution)/shard_map/ppermute | solution.py:224
  46.2 1.3 %collective-permute-done.21.refs_1_ = bf16[32,360]{1,0:T(8,128)(2,1)S(1)} collective-permute-done((bf16[32,360]{1,0:T(8,128)(2,1)S(1)}, bf16[32,360]{1,0:T(8,128)(2,1)S(1)}, u32[]{:S(2)}, u32[]{:S(2)}) %collective-permute-start.21) | collective-permute-done | bytes 23072 | tf_op jit(solution)/shard_map/ppermute | solution.py:224
  48.0 0.6 %combine.1 = bf16[2,16,360]{2,1,0:T(8,128)(2,1)} custom-call(f32[32,360]{1,0:T(8,128)S(1)} %get-tuple-element.61.refs_0_, bf16[32,360]{1,0:T(8,128)(2,1)S(1)} %collective-permute-done.21.refs_1_, bf16[32,360]{1,0:T(8,128)(2,1)S(1)} %collective-permute-done.22.refs_2_, bf16[32,360]{1,0:T(8,128)(2,1)S(1)} %collective-permute-done.23.refs_3_, ...), custom_call_target="tpu_custom_call" | custom-call | bytes 184320 | tf_op jit(solution)/shard_map/combine/pallas_call | solution.py:450
  (45 shorter events, 5.7 us)
Async XLA Ops:
  4.3 1.5 %collective-permute-start = (bf16[4,32,384]{2,1,0:T(8,128)(2,1)S(1)}, bf16[4,32,384]{2,1,0:T(8,128)(2,1)S(1)}, u32[]{:S(2)}, u32[]{:S(2)}) collective-permute-start(bf16[4,32,384]{2,1,0:T(8,128)(2,1)S(1)} %get-tuple-element.43), channel_id=1, source_target_pairs={{0,16},{16,0},{1,17},{17,1},{2,18},{18,2},{3,19},{19,3},{4,20},{20... | collective-permute-start | bytes 294920 | tf_op jit(solution)/shard_map/ppermute | solution.py:224
  5.8 5.6 %collective-permute-start.1 = (bf16[32,384]{1,0:T(8,128)(2,1)S(1)}, bf16[32,384]{1,0:T(8,128)(2,1)S(1)}, u32[]{:S(2)}, u32[]{:S(2)}) collective-permute-start(bf16[32,384]{1,0:T(8,128)(2,1)S(1)} %get-tuple-element.45), channel_id=1, source_target_pairs={{0,3},{1,2},{2,1},{3,0},{4,7},{5,6},{6,5},{7,4},{8,11},{9,10},{10,... | collective-permute-start | bytes 73736 | tf_op jit(solution)/shard_map/ppermute | solution.py:247
  9.7 3.3 %collective-permute-start.2 = (bf16[32,384]{1,0:T(8,128)(2,1)S(1)}, bf16[32,384]{1,0:T(8,128)(2,1)S(1)}, u32[]{:S(2)}, u32[]{:S(2)}) collective-permute-start(bf16[32,384]{1,0:T(8,128)(2,1)S(1)} %get-tuple-element.46), channel_id=1, source_target_pairs={{0,17},{1,19},{2,16},{3,18},{4,22},{5,20},{6,23},{7,21},{8,25},{9,... | collective-permute-start | bytes 73736 | tf_op jit(solution)/shard_map/ppermute | solution.py:247
  9.7 3.5 %collective-permute-start.3 = (bf16[32,384]{1,0:T(8,128)(2,1)S(1)}, bf16[32,384]{1,0:T(8,128)(2,1)S(1)}, u32[]{:S(2)}, u32[]{:S(2)}) collective-permute-start(bf16[32,384]{1,0:T(8,128)(2,1)S(1)} %get-tuple-element.47), channel_id=1, source_target_pairs={{0,18},{1,16},{2,19},{3,17},{4,21},{5,23},{6,20},{7,22},{8,26},{9,... | collective-permute-start | bytes 73736 | tf_op jit(solution)/shard_map/ppermute | solution.py:247
  13.3 4.2 %collective-permute-start.4 = (bf16[32,384]{1,0:T(8,128)(2,1)S(1)}, bf16[32,384]{1,0:T(8,128)(2,1)S(1)}, u32[]{:S(2)}, u32[]{:S(2)}) collective-permute-start(bf16[32,384]{1,0:T(8,128)(2,1)S(1)} %sum.1), channel_id=1, source_target_pairs={{0,20},{1,21},{2,22},{3,23},{4,16},{5,17},{6,18},{7,19},{8,28},{9,... | collective-permute-start | bytes 73736 | tf_op jit(solution)/shard_map/ppermute | solution.py:247
  14.8 4.9 %collective-permute-start.5 = (bf16[32,384]{1,0:T(8,128)(2,1)S(1)}, bf16[32,384]{1,0:T(8,128)(2,1)S(1)}, u32[]{:S(2)}, u32[]{:S(2)}) collective-permute-start(bf16[32,384]{1,0:T(8,128)(2,1)S(1)} %sum.1), channel_id=1, source_target_pairs={{0,8},{1,9},{2,10},{3,11},{4,12},{5,13},{6,14},{7,15},{8,0},{9,1},... | collective-permute-start | bytes 73736 | tf_op jit(solution)/shard_map/ppermute | solution.py:247
  17.4 5.3 %collective-permute-start.6 = (bf16[32,384]{1,0:T(8,128)(2,1)S(1)}, bf16[32,384]{1,0:T(8,128)(2,1)S(1)}, u32[]{:S(2)}, u32[]{:S(2)}) collective-permute-start(bf16[32,384]{1,0:T(8,128)(2,1)S(1)} %sum.1), channel_id=1, source_target_pairs={{0,28},{1,29},{2,30},{3,31},{4,24},{5,25},{6,26},{7,27},{8,20},{9,... | collective-permute-start | bytes 73736 | tf_op jit(solution)/shard_map/ppermute | solution.py:247
  22.7 6.2 %collective-permute-start.7 = (bf16[4,32,384]{2,1,0:T(8,128)(2,1)S(1)}, bf16[4,32,384]{2,1,0:T(8,128)(2,1)S(1)}, u32[]{:S(2)}, u32[]{:S(2)}) collective-permute-start(bf16[4,32,384]{2,1,0:T(8,128)(2,1)S(1)} %pad_maximum_fusion.refs_0_), channel_id=1, source_target_pairs={{0,3},{1,2},{2,1},{3,0},{4,7},{5,6},{6,5},{7,4},{8,11},{9,10},{10,... | collective-permute-start | bytes 294920 | tf_op jit(solution)/shard_map/ppermute | solution.py:247
  24.2 5.1 %collective-permute-start.8 = (bf16[4,32,384]{2,1,0:T(8,128)(2,1)S(1)}, bf16[4,32,384]{2,1,0:T(8,128)(2,1)S(1)}, u32[]{:S(2)}, u32[]{:S(2)}) collective-permute-start(bf16[4,32,384]{2,1,0:T(8,128)(2,1)S(1)} %pad_maximum_fusion.refs_0_), channel_id=1, source_target_pairs={{0,17},{1,19},{2,16},{3,18},{4,22},{5,20},{6,23},{7,21},{8,25},{9,... | collective-permute-start | bytes 294920 | tf_op jit(solution)/shard_map/ppermute | solution.py:247
  24.2 6.5 %collective-permute-start.9 = (bf16[4,32,384]{2,1,0:T(8,128)(2,1)S(1)}, bf16[4,32,384]{2,1,0:T(8,128)(2,1)S(1)}, u32[]{:S(2)}, u32[]{:S(2)}) collective-permute-start(bf16[4,32,384]{2,1,0:T(8,128)(2,1)S(1)} %pad_maximum_fusion.refs_0_), channel_id=1, source_target_pairs={{0,18},{1,16},{2,19},{3,17},{4,21},{5,23},{6,20},{7,22},{8,26},{9,... | collective-permute-start | bytes 294920 | tf_op jit(solution)/shard_map/ppermute | solution.py:247
  26.0 5.4 %collective-permute-start.10 = (bf16[4,32,384]{2,1,0:T(8,128)(2,1)S(1)}, bf16[4,32,384]{2,1,0:T(8,128)(2,1)S(1)}, u32[]{:S(2)}, u32[]{:S(2)}) collective-permute-start(bf16[4,32,384]{2,1,0:T(8,128)(2,1)S(1)} %pad_maximum_fusion.refs_0_), channel_id=1, source_target_pairs={{0,16},{16,0},{1,17},{17,1},{2,18},{18,2},{3,19},{19,3},{4,20},{20... | collective-permute-start | bytes 294920 | tf_op jit(solution)/shard_map/ppermute | solution.py:224
  28.9 2.5 %collective-permute-start.11 = (bf16[4,32,384]{2,1,0:T(8,128)(2,1)S(1)}, bf16[4,32,384]{2,1,0:T(8,128)(2,1)S(1)}, u32[]{:S(2)}, u32[]{:S(2)}) collective-permute-start(bf16[4,32,384]{2,1,0:T(8,128)(2,1)S(1)} %collective-permute-done.7.refs_1_), channel_id=1, source_target_pairs={{0,16},{16,0},{1,17},{17,1},{2,18},{18,2},{3,19},{19,3},{4,20},{20... | collective-permute-start | bytes 294920 | tf_op jit(solution)/shard_map/ppermute | solution.py:224
  29.3 2.4 %collective-permute-start.12 = (bf16[4,32,384]{2,1,0:T(8,128)(2,1)S(1)}, bf16[4,32,384]{2,1,0:T(8,128)(2,1)S(1)}, u32[]{:S(2)}, u32[]{:S(2)}) collective-permute-start(bf16[4,32,384]{2,1,0:T(8,128)(2,1)S(1)} %collective-permute-done.8.refs_2_), channel_id=1, source_target_pairs={{0,16},{16,0},{1,17},{17,1},{2,18},{18,2},{3,19},{19,3},{4,20},{20... | collective-permute-start | bytes 294920 | tf_op jit(solution)/shard_map/ppermute | solution.py:224
  30.7 1.3 %collective-permute-start.13 = (bf16[4,32,384]{2,1,0:T(8,128)(2,1)S(1)}, bf16[4,32,384]{2,1,0:T(8,128)(2,1)S(1)}, u32[]{:S(2)}, u32[]{:S(2)}) collective-permute-start(bf16[4,32,384]{2,1,0:T(8,128)(2,1)S(1)} %collective-permute-done.9.refs_3_), channel_id=1, source_target_pairs={{0,16},{16,0},{1,17},{17,1},{2,18},{18,2},{3,19},{19,3},{4,20},{20... | collective-permute-start | bytes 294920 | tf_op jit(solution)/shard_map/ppermute | solution.py:224
  33.2 1.8 %collective-permute-start.14 = (bf16[4,128,360]{2,1,0:T(8,128)(2,1)S(1)}, bf16[4,128,360]{2,1,0:T(8,128)(2,1)S(1)}, u32[]{:S(2)}, u32[]{:S(2)}) collective-permute-start(bf16[4,128,360]{2,1,0:T(8,128)(2,1)S(1)} %get-tuple-element.56), channel_id=1, source_target_pairs={{0,16},{16,0},{1,17},{17,1},{2,18},{18,2},{3,19},{19,3},{4,20},{20... | collective-permute-start | bytes 1105928 | tf_op jit(solution)/shard_map/ppermute | solution.py:224
  35.1 5.2 %collective-permute-start.18 = (bf16[64,360]{1,0:T(8,128)(2,1)S(1)}, bf16[64,360]{1,0:T(8,128)(2,1)S(1)}, u32[]{:S(2)}, u32[]{:S(2)}) collective-permute-start(bf16[64,360]{1,0:T(8,128)(2,1)S(1)} %get-tuple-element.62), channel_id=1, source_target_pairs={{0,3},{1,2},{2,1},{3,0},{4,7},{5,6},{6,5},{7,4},{8,11},{9,10},{10,... | collective-permute-start | bytes 138248 | tf_op jit(solution)/shard_map/ppermute | solution.py:247
  36.5 5.0 %collective-permute-start.19 = (bf16[64,360]{1,0:T(8,128)(2,1)S(1)}, bf16[64,360]{1,0:T(8,128)(2,1)S(1)}, u32[]{:S(2)}, u32[]{:S(2)}) collective-permute-start(bf16[64,360]{1,0:T(8,128)(2,1)S(1)} %get-tuple-element.63), channel_id=1, source_target_pairs={{0,17},{1,19},{2,16},{3,18},{4,21},{5,23},{6,20},{7,22},{8,25},{9,... | collective-permute-start | bytes 138248 | tf_op jit(solution)/shard_map/ppermute | solution.py:247
  36.5 5.0 %collective-permute-start.20 = (bf16[64,360]{1,0:T(8,128)(2,1)S(1)}, bf16[64,360]{1,0:T(8,128)(2,1)S(1)}, u32[]{:S(2)}, u32[]{:S(2)}) collective-permute-start(bf16[64,360]{1,0:T(8,128)(2,1)S(1)} %get-tuple-element.64), channel_id=1, source_target_pairs={{0,18},{1,16},{2,19},{3,17},{4,22},{5,20},{6,23},{7,21},{8,26},{9,... | collective-permute-start | bytes 138248 | tf_op jit(solution)/shard_map/ppermute | solution.py:247
  38.3 5.1 %collective-permute-start.15 = (bf16[64,360]{1,0:T(8,128)(2,1)S(1)}, bf16[64,360]{1,0:T(8,128)(2,1)S(1)}, u32[]{:S(2)}, u32[]{:S(2)}) collective-permute-start(bf16[64,360]{1,0:T(8,128)(2,1)S(1)} %get-tuple-element.58), channel_id=1, source_target_pairs={{0,3},{1,2},{2,1},{3,0},{4,7},{5,6},{6,5},{7,4},{8,11},{9,10},{10,... | collective-permute-start | bytes 138248 | tf_op jit(solution)/shard_map/ppermute | solution.py:247
  39.8 3.7 %collective-permute-start.16 = (bf16[64,360]{1,0:T(8,128)(2,1)S(1)}, bf16[64,360]{1,0:T(8,128)(2,1)S(1)}, u32[]{:S(2)}, u32[]{:S(2)}) collective-permute-start(bf16[64,360]{1,0:T(8,128)(2,1)S(1)} %get-tuple-element.59), channel_id=1, source_target_pairs={{0,17},{1,19},{2,16},{3,18},{4,21},{5,23},{6,20},{7,22},{8,25},{9,... | collective-permute-start | bytes 138248 | tf_op jit(solution)/shard_map/ppermute | solution.py:247
  40.2 3.9 %collective-permute-start.17 = (bf16[64,360]{1,0:T(8,128)(2,1)S(1)}, bf16[64,360]{1,0:T(8,128)(2,1)S(1)}, u32[]{:S(2)}, u32[]{:S(2)}) collective-permute-start(bf16[64,360]{1,0:T(8,128)(2,1)S(1)} %get-tuple-element.60), channel_id=1, source_target_pairs={{0,18},{1,16},{2,19},{3,17},{4,22},{5,20},{6,23},{7,21},{8,26},{9,... | collective-permute-start | bytes 138248 | tf_op jit(solution)/shard_map/ppermute | solution.py:247
  41.6 5.9 %collective-permute-start.21 = (bf16[32,360]{1,0:T(8,128)(2,1)S(1)}, bf16[32,360]{1,0:T(8,128)(2,1)S(1)}, u32[]{:S(2)}, u32[]{:S(2)}) collective-permute-start(bf16[32,360]{1,0:T(8,128)(2,1)S(1)} %get-tuple-element.65), channel_id=1, source_target_pairs={{0,12},{4,8},{8,4},{12,0},{1,13},{5,9},{9,5},{13,1},{2,14},{6,10},... | collective-permute-start | bytes 69128 | tf_op jit(solution)/shard_map/ppermute | solution.py:224
  42.0 5.5 %collective-permute-start.22 = (bf16[32,360]{1,0:T(8,128)(2,1)S(1)}, bf16[32,360]{1,0:T(8,128)(2,1)S(1)}, u32[]{:S(2)}, u32[]{:S(2)}) collective-permute-start(bf16[32,360]{1,0:T(8,128)(2,1)S(1)} %get-tuple-element.66), channel_id=1, source_target_pairs={{0,8},{4,12},{8,0},{12,4},{1,9},{5,13},{9,1},{13,5},{2,10},{6,14},... | collective-permute-start | bytes 69128 | tf_op jit(solution)/shard_map/ppermute | solution.py:224
  44.1 3.9 %collective-permute-start.23 = (bf16[32,360]{1,0:T(8,128)(2,1)S(1)}, bf16[32,360]{1,0:T(8,128)(2,1)S(1)}, u32[]{:S(2)}, u32[]{:S(2)}) collective-permute-start(bf16[32,360]{1,0:T(8,128)(2,1)S(1)} %get-tuple-element.67), channel_id=1, source_target_pairs={{0,4},{4,0},{8,12},{12,8},{1,5},{5,1},{9,13},{13,9},{2,6},{6,2},{1... | collective-permute-start | bytes 69128 | tf_op jit(solution)/shard_map/ppermute | solution.py:224
  (4 other events, 106.5 us)

commit v14 on v12

--- a/solution.py
+++ b/solution.py
@@ -457,11 +457,11 @@
 def after_core_halves_kernel(mine_ref, come_ref, own_ref, *send_refs):
     tp, half = lax.axis_index("tp"), mine_ref.shape[1] // 2
     own_ref[...] = mine_ref[tp] + come_ref[tp].astype(jnp.float32)
-    for mask, second, first in zip(shard_masks(False), send_refs[:3], send_refs[3:]):
+    for mask, first, second in zip(shard_masks(False), send_refs[:3], send_refs[3:]):
         to = jnp.bitwise_xor(tp, mask)
         part = (mine_ref[to] + come_ref[to].astype(jnp.float32)).astype(jnp.bfloat16)
+        first[...] = part[:half]
         second[...] = part[half:]
-        first[...] = part[:half]
 
 
 def add_all(*refs):
@@ -554,7 +554,7 @@
     sec, tp = lax.axis_index("sec"), lax.axis_index("tp")
     second_product(act_ref, down_ref, mine_ref, lane_of(False))
     total_rows, part = middle_ref.shape
-    near, far = near_x_ref[:total_rows].astype(jnp.float32), far_x_ref[:total_rows].astype(jnp.float32)
+    near, far = near_x_ref[-total_rows:].astype(jnp.float32), far_x_ref[-total_rows:].astype(jnp.float32)
     first = lane_of(True) == 0
     x = jnp.concatenate([jnp.where(first, near, far), jnp.where(first, far, near)], axis=1)
     for c in range(row_ref.shape[0]):
@@ -605,19 +605,19 @@
     mine = call(own_projection_kernel, "own_projection", shape_of(other.shape, jnp.float32), mix, held, limit=12,
                 flops=mix.size * width)
     middle = call(sum_kernel, "sum", shape_of((steps * rows, LANES)), *scatter_shards(mine, come), own_x)
-    stacked = jnp.stack([middle] + [lane_swap(middle, m, (0, 0), True) for m in range(1, groups)])
+    stacked = jnp.stack([lane_swap(middle, m, (0, 0), True) for m in reversed(range(1, groups))] + [middle])
     pieces = [stacked] + shard_swaps([stacked] * (tps - 1), True)
     part = width // (secs * tps)
     mine, come, own_middle = experts(expert_gain, w_gate[0], w_up[0], w_down[0], pieces, part)
     lines = steps * rows
     own, *parts = call(after_core_halves_kernel, "after_core_halves",
                        [shape_of((groups * lines, part), jnp.float32)] + [shape_of((groups // 2 * lines, part))] * 6, mine, come)
-    second_come, first_come = shard_swaps(parts[:3], False), shard_swaps(parts[3:], False)
-    second, third = call(functools.partial(sum_rows_kernel, line=2 * lines), "sum_far_rows", [shape_of((lines, part))] * 2,
-                         own, *second_come)
+    far_come, near_come = shard_swaps(parts[:3], False), shard_swaps(parts[3:], False)
+    third, second = call(functools.partial(sum_rows_kernel, line=0), "sum_far_rows", [shape_of((lines, part))] * 2,
+                         own, *far_come)
     third, second = swap(third, "grp", 3), swap(second, "grp", 2)
-    own, nearest = call(functools.partial(sum_rows_kernel, line=0), "sum_near_rows",
-                        [shape_of((lines, part), jnp.float32), shape_of((lines, part))], own, *first_come)
+    nearest, own = call(functools.partial(sum_rows_kernel, line=2 * lines), "sum_near_rows",
+                        [shape_of((lines, part)), shape_of((lines, part), jnp.float32)], own, *near_come)
     return call(sum_kernel, "combine", shape_of((steps, rows, part)), own, third, second, swap(nearest, "grp", 1), own_middle)
 
 

time: 48.8 us -> 47.4 us (0.971)
  waiting for transfers between devices: 18.2 us -> 15.3 us
  starting transfers between devices: 22.3 us -> 23.9 us
    ppermute x15, waiting for transfers between devices: 14.3 us -> 11.2 us  [lane_swap(): return lax.ppermute(value, ('sec', 'grp', 'tp'), pairs)]
    ppermute x9, starting transfers between devices: 4.66 us -> 5.96 us  [swap(): return lax.ppermute(value, axes, [(i, i ^ mask) for i in range(size)])]
  transfers between devices with their start and end apart: 24 -> 24, of which waited for: 16 -> 15; matrix products, arithmetic and copies ran while one was open for 0% -> 0% of each run, Pallas kernels for 4% -> 4%
where the time goes in v14:
time: 47.4 us; the launch traced here: 47.3 us
  starting transfers between devices  23.9 us (50%)
  waiting for transfers between devices  15.3 us (32%)
  Pallas kernels  7.95 us (17%)
    ppermute x15, starting transfers between devices, lane_swap(): return lax.ppermute(value, ('sec', 'grp', 'tp'), pairs)  17.9 us
    ppermute x15, waiting for transfers between devices, lane_swap(): return lax.ppermute(value, ('sec', 'grp', 'tp'), pairs)  11.2 us
    ppermute x9, starting transfers between devices, swap(): return lax.ppermute(value, axes, [(i, i ^ mask) for i in range(size)])  5.96 us
    pallas_call x1, Pallas kernels, attention_partial(): pl.pallas_call(attention_kernel, name='attention', out_shape=[shape_of((t...  4.24 us
    ppermute x9, waiting for transfers between devices, swap(): return lax.ppermute(value, axes, [(i, i ^ mask) for i in range(size)])  4.06 us
    pallas_call x8, Pallas kernels, call(): pl.pallas_call(kernel, name=name, out_shape=outs, in_specs=[vmem()] * len...  1.96 us
    pallas_call x1, Pallas kernels, experts(): pl.pallas_call(far_kernel, name='far_columns', out_shape=[shape_of((tps,...  1.17 us
  transfers between devices with their start and end apart: 24, of which 15 were waited for; matrix products, arithmetic and copies ran while one was open for 0% of the time, Pallas kernels for 4%

profile of v14, /device:TPU:0, one launch (start us, length us, event | category | flops | bytes accessed | tf_op | source)
XLA Modules:
  0.0 47.3 jit_solution(4809952862685799881)
XLA Ops:
  0.0 4.2 %attention.1 = (bf16[4,32,384]{2,1,0:T(8,128)(2,1)S(1)}, f32[32,384]{1,0:T(8,128)S(1)}, bf16[32,512]{1,0:T(8,128)(2,1)S(1)}, bf16[2880,512]{1,0:T(8,128)(2,1)S(1)}) custom-call(s32[16]{0:T(128)} %lengths_hbm.1, f32[8]{0:T(128)} %sinks_hbm.1, s32[2,4,16]{2,1,0:T(4,128)} %bitcast.31, f32[2,4,16]{2,1,0:T(4,128)} %bitcast.32, f32[2880]{0:T(1024)} %gain_hbm.1, ...), custom_call_target="tpu_custom_call" | custom-call | tf_op jit(solution)/shard_map/attention/pallas_call | solution.py:408
  5.8 3.8 %collective-permute-start.1 = (bf16[32,384]{1,0:T(8,128)(2,1)S(1)}, bf16[32,384]{1,0:T(8,128)(2,1)S(1)}, u32[]{:S(2)}, u32[]{:S(2)}) collective-permute-start(bf16[32,384]{1,0:T(8,128)(2,1)S(1)} %get-tuple-element.37), channel_id=1, source_target_pairs={{0,3},{1,2},{2,1},{3,0},{4,7},{5,6},{6,5},{7,4},{8,11},{9,10},{10,... | collective-permute-start | bytes 73736 | tf_op jit(solution)/shard_map/ppermute | solution.py:247
  10.0 1.4 %collective-permute-done.1.refs_1_ = bf16[32,384]{1,0:T(8,128)(2,1)S(1)} collective-permute-done((bf16[32,384]{1,0:T(8,128)(2,1)S(1)}, bf16[32,384]{1,0:T(8,128)(2,1)S(1)}, u32[]{:S(2)}, u32[]{:S(2)}) %collective-permute-start.1) | collective-permute-done | bytes 24608 | tf_op jit(solution)/shard_map/ppermute | solution.py:247
  11.4 1.4 %collective-permute-done.2.refs_2_ = bf16[32,384]{1,0:T(8,128)(2,1)S(1)} collective-permute-done((bf16[32,384]{1,0:T(8,128)(2,1)S(1)}, bf16[32,384]{1,0:T(8,128)(2,1)S(1)}, u32[]{:S(2)}, u32[]{:S(2)}) %collective-permute-start.2) | collective-permute-done | bytes 24608 | tf_op jit(solution)/shard_map/ppermute | solution.py:247
  13.2 3.6 %collective-permute-start.4 = (bf16[32,384]{1,0:T(8,128)(2,1)S(1)}, bf16[32,384]{1,0:T(8,128)(2,1)S(1)}, u32[]{:S(2)}, u32[]{:S(2)}) collective-permute-start(bf16[32,384]{1,0:T(8,128)(2,1)S(1)} %sum.1), channel_id=1, source_target_pairs={{0,28},{1,29},{2,30},{3,31},{4,24},{5,25},{6,26},{7,27},{8,20},{9,... | collective-permute-start | bytes 73736 | tf_op jit(solution)/shard_map/ppermute | solution.py:247
  17.2 1.2 %collective-permute-done.4 = bf16[32,384]{1,0:T(8,128)(2,1)S(1)} collective-permute-done((bf16[32,384]{1,0:T(8,128)(2,1)S(1)}, bf16[32,384]{1,0:T(8,128)(2,1)S(1)}, u32[]{:S(2)}, u32[]{:S(2)}) %collective-permute-start.4) | collective-permute-done | bytes 24608 | tf_op jit(solution)/shard_map/ppermute | solution.py:247
  18.4 3.2 %collective-permute-done.5 = bf16[32,384]{1,0:T(8,128)(2,1)S(1)} collective-permute-done((bf16[32,384]{1,0:T(8,128)(2,1)S(1)}, bf16[32,384]{1,0:T(8,128)(2,1)S(1)}, u32[]{:S(2)}, u32[]{:S(2)}) %collective-permute-start.5) | collective-permute-done | bytes 24608 | tf_op jit(solution)/shard_map/ppermute | solution.py:247
  21.6 1.5 %collective-permute-start.7 = (bf16[4,32,384]{2,1,0:T(8,128)(2,1)S(1)}, bf16[4,32,384]{2,1,0:T(8,128)(2,1)S(1)}, u32[]{:S(2)}, u32[]{:S(2)}) collective-permute-start(bf16[4,32,384]{2,1,0:T(8,128)(2,1)S(1)} %pad_maximum_fusion.refs_0_), channel_id=1, source_target_pairs={{0,3},{1,2},{2,1},{3,0},{4,7},{5,6},{6,5},{7,4},{8,11},{9,10},{10,... | collective-permute-start | bytes 294920 | tf_op jit(solution)/shard_map/ppermute | solution.py:247
  23.1 1.8 %collective-permute-start.9 = (bf16[4,32,384]{2,1,0:T(8,128)(2,1)S(1)}, bf16[4,32,384]{2,1,0:T(8,128)(2,1)S(1)}, u32[]{:S(2)}, u32[]{:S(2)}) collective-permute-start(bf16[4,32,384]{2,1,0:T(8,128)(2,1)S(1)} %pad_maximum_fusion.refs_0_), channel_id=1, source_target_pairs={{0,18},{1,16},{2,19},{3,17},{4,21},{5,23},{6,20},{7,22},{8,26},{9,... | collective-permute-start | bytes 294920 | tf_op jit(solution)/shard_map/ppermute | solution.py:247
  24.9 2.4 %collective-permute-done.7.refs_1_ = bf16[4,32,384]{2,1,0:T(8,128)(2,1)S(1)} collective-permute-done((bf16[4,32,384]{2,1,0:T(8,128)(2,1)S(1)}, bf16[4,32,384]{2,1,0:T(8,128)(2,1)S(1)}, u32[]{:S(2)}, u32[]{:S(2)}) %collective-permute-start.7) | collective-permute-done | bytes 98336 | tf_op jit(solution)/shard_map/ppermute | solution.py:247
  27.3 0.8 %collective-permute-done.8.refs_2_ = bf16[4,32,384]{2,1,0:T(8,128)(2,1)S(1)} collective-permute-done((bf16[4,32,384]{2,1,0:T(8,128)(2,1)S(1)}, bf16[4,32,384]{2,1,0:T(8,128)(2,1)S(1)}, u32[]{:S(2)}, u32[]{:S(2)}) %collective-permute-start.8) | collective-permute-done | bytes 98336 | tf_op jit(solution)/shard_map/ppermute | solution.py:247
  29.1 0.6 %near_columns.1 = (bf16[128,1536]{1,0:T(8,128)(2,1)S(1)}, f32[128,180]{1,0:T(8,128)S(1)}, f32[128,180]{1,0:T(8,128)S(1)}, f32[128,128]{1,0:T(8,128)S(1)}) custom-call(f32[1,2880]{1,0:T(1,128)S(1)} %reshape.6.gain_ref, bf16[180,2880]{1,0:T(8,128)(2,1)S(1)} %bitcast.17, bf16[180,2880]{1,0:T(8,128)(2,1)S(1)} %bitcast.19, ...), custom_call_target="tpu_custom_call" | custom-call | flops 132710400 | bytes 3121408 | tf_op jit(solution)/shard_map/near_columns/pallas_call | solution.py:437
  30.1 1.2 %far_columns.1 = (bf16[4,128,360]{2,1,0:T(8,128)(2,1)S(1)}, bf16[128,180]{1,0:T(8,128)(2,1)S(1)}, bf16[128,1536]{1,0:T(8,128)(2,1)S(1)}) custom-call(f32[1,2880]{1,0:T(1,128)S(1)} %reshape.6.gain_ref, bf16[180,2880]{1,0:T(8,128)(2,1)S(1)} %bitcast.18, bf16[180,2880]{1,0:T(8,128)(2,1)S(1)} %bitcast.20, bf16[180,2880]{1,0:T(8,128)(2,1)S(1)} %bitcast.21, ...), custom_call_target="tpu_custom_call" | custom-call | tf_op jit(solution)/shard_map/far_columns/pallas_call | solution.py:573
  31.6 0.6 %own_columns.1 = (f32[4,128,360]{2,1,0:T(8,128)S(1)}, f32[32,360]{1,0:T(8,128)S(1)}) custom-call(bf16[128,180]{1,0:T(8,128)(2,1)S(1)} %get-tuple-element.45.act_ref, bf16[180,2880]{1,0:T(8,128)(2,1)S(1)} %bitcast.22, bf16[128,1536]{1,0:T(8,128)(2,1)S(1)} %get-tuple-element.41.near_x_ref, bf16[128,1536]{1,0:T(8,128)(2,1)S(1)} %get-tuple-element.46.far_x_ref), custom_call_target="tpu_custom_call" | custom-call | flops 66355200 | bytes 737280 | tf_op jit(solution)/shard_map/own_columns/pallas_call | solution.py:583
  32.2 0.9 %collective-permute-done.14.come_ref = bf16[4,128,360]{2,1,0:T(8,128)(2,1)S(1)} collective-permute-done((bf16[4,128,360]{2,1,0:T(8,128)(2,1)S(1)}, bf16[4,128,360]{2,1,0:T(8,128)(2,1)S(1)}, u32[]{:S(2)}, u32[]{:S(2)}) %collective-permute-start.14) | collective-permute-done | bytes 368672 | tf_op jit(solution)/shard_map/ppermute | solution.py:224
  33.1 2.1 %collective-permute-start.18 = (bf16[64,360]{1,0:T(8,128)(2,1)S(1)}, bf16[64,360]{1,0:T(8,128)(2,1)S(1)}, u32[]{:S(2)}, u32[]{:S(2)}) collective-permute-start(bf16[64,360]{1,0:T(8,128)(2,1)S(1)} %get-tuple-element.54), channel_id=1, source_target_pairs={{0,3},{1,2},{2,1},{3,0},{4,7},{5,6},{6,5},{7,4},{8,11},{9,10},{10,... | collective-permute-start | bytes 138248 | tf_op jit(solution)/shard_map/ppermute | solution.py:247
  35.6 0.8 %collective-permute-start.20 = (bf16[64,360]{1,0:T(8,128)(2,1)S(1)}, bf16[64,360]{1,0:T(8,128)(2,1)S(1)}, u32[]{:S(2)}, u32[]{:S(2)}) collective-permute-start(bf16[64,360]{1,0:T(8,128)(2,1)S(1)} %get-tuple-element.56), channel_id=1, source_target_pairs={{0,18},{1,16},{2,19},{3,17},{4,22},{5,20},{6,23},{7,21},{8,26},{9,... | collective-permute-start | bytes 138248 | tf_op jit(solution)/shard_map/ppermute | solution.py:247
  36.4 2.0 %collective-permute-start.15 = (bf16[64,360]{1,0:T(8,128)(2,1)S(1)}, bf16[64,360]{1,0:T(8,128)(2,1)S(1)}, u32[]{:S(2)}, u32[]{:S(2)}) collective-permute-start(bf16[64,360]{1,0:T(8,128)(2,1)S(1)} %get-tuple-element.50), channel_id=1, source_target_pairs={{0,3},{1,2},{2,1},{3,0},{4,7},{5,6},{6,5},{7,4},{8,11},{9,10},{10,... | collective-permute-start | bytes 138248 | tf_op jit(solution)/shard_map/ppermute | solution.py:247
  38.6 1.1 %collective-permute-start.17 = (bf16[64,360]{1,0:T(8,128)(2,1)S(1)}, bf16[64,360]{1,0:T(8,128)(2,1)S(1)}, u32[]{:S(2)}, u32[]{:S(2)}) collective-permute-start(bf16[64,360]{1,0:T(8,128)(2,1)S(1)} %get-tuple-element.52), channel_id=1, source_target_pairs={{0,18},{1,16},{2,19},{3,17},{4,22},{5,20},{6,23},{7,21},{8,26},{9,... | collective-permute-start | bytes 138248 | tf_op jit(solution)/shard_map/ppermute | solution.py:247
  39.7 2.0 %collective-permute-start.21 = (bf16[32,360]{1,0:T(8,128)(2,1)S(1)}, bf16[32,360]{1,0:T(8,128)(2,1)S(1)}, u32[]{:S(2)}, u32[]{:S(2)}) collective-permute-start(bf16[32,360]{1,0:T(8,128)(2,1)S(1)} %get-tuple-element.57), channel_id=1, source_target_pairs={{0,12},{4,8},{8,4},{12,0},{1,13},{5,9},{9,5},{13,1},{2,14},{6,10},... | collective-permute-start | bytes 69128 | tf_op jit(solution)/shard_map/ppermute | solution.py:224
  42.5 1.7 %collective-permute-start.23 = (bf16[32,360]{1,0:T(8,128)(2,1)S(1)}, bf16[32,360]{1,0:T(8,128)(2,1)S(1)}, u32[]{:S(2)}, u32[]{:S(2)}) collective-permute-start(bf16[32,360]{1,0:T(8,128)(2,1)S(1)} %get-tuple-element.59), channel_id=1, source_target_pairs={{0,4},{4,0},{8,12},{12,8},{1,5},{5,1},{9,13},{13,9},{2,6},{6,2},{1... | collective-permute-start | bytes 69128 | tf_op jit(solution)/shard_map/ppermute | solution.py:224
  44.2 1.4 %collective-permute-done.21.refs_1_ = bf16[32,360]{1,0:T(8,128)(2,1)S(1)} collective-permute-done((bf16[32,360]{1,0:T(8,128)(2,1)S(1)}, bf16[32,360]{1,0:T(8,128)(2,1)S(1)}, u32[]{:S(2)}, u32[]{:S(2)}) %collective-permute-start.21) | collective-permute-done | bytes 23072 | tf_op jit(solution)/shard_map/ppermute | solution.py:224
  45.6 0.8 %collective-permute-done.22.refs_2_ = bf16[32,360]{1,0:T(8,128)(2,1)S(1)} collective-permute-done((bf16[32,360]{1,0:T(8,128)(2,1)S(1)}, bf16[32,360]{1,0:T(8,128)(2,1)S(1)}, u32[]{:S(2)}, u32[]{:S(2)}) %collective-permute-start.22) | collective-permute-done | bytes 23072 | tf_op jit(solution)/shard_map/ppermute | solution.py:224
  46.7 0.6 %combine.1 = bf16[2,16,360]{2,1,0:T(8,128)(2,1)} custom-call(f32[32,360]{1,0:T(8,128)S(1)} %get-tuple-element.53.refs_0_, bf16[32,360]{1,0:T(8,128)(2,1)S(1)} %collective-permute-done.21.refs_1_, bf16[32,360]{1,0:T(8,128)(2,1)S(1)} %collective-permute-done.22.refs_2_, bf16[32,360]{1,0:T(8,128)(2,1)S(1)} %collective-permute-done.23.refs_3_, ...), custom_call_target="tpu_custom_call" | custom-call | bytes 184320 | tf_op jit(solution)/shard_map/combine/pallas_call | solution.py:437
  (45 shorter events, 6.0 us)
Async XLA Ops:
  4.3 1.5 %collective-permute-start = (bf16[4,32,384]{2,1,0:T(8,128)(2,1)S(1)}, bf16[4,32,384]{2,1,0:T(8,128)(2,1)S(1)}, u32[]{:S(2)}, u32[]{:S(2)}) collective-permute-start(bf16[4,32,384]{2,1,0:T(8,128)(2,1)S(1)} %get-tuple-element.35), channel_id=1, source_target_pairs={{0,16},{16,0},{1,17},{17,1},{2,18},{18,2},{3,19},{19,3},{4,20},{20... | collective-permute-start | bytes 294920 | tf_op jit(solution)/shard_map/ppermute | solution.py:224
  5.8 5.6 %collective-permute-start.1 = (bf16[32,384]{1,0:T(8,128)(2,1)S(1)}, bf16[32,384]{1,0:T(8,128)(2,1)S(1)}, u32[]{:S(2)}, u32[]{:S(2)}) collective-permute-start(bf16[32,384]{1,0:T(8,128)(2,1)S(1)} %get-tuple-element.37), channel_id=1, source_target_pairs={{0,3},{1,2},{2,1},{3,0},{4,7},{5,6},{6,5},{7,4},{8,11},{9,10},{10,... | collective-permute-start | bytes 73736 | tf_op jit(solution)/shard_map/ppermute | solution.py:247
  9.6 3.3 %collective-permute-start.2 = (bf16[32,384]{1,0:T(8,128)(2,1)S(1)}, bf16[32,384]{1,0:T(8,128)(2,1)S(1)}, u32[]{:S(2)}, u32[]{:S(2)}) collective-permute-start(bf16[32,384]{1,0:T(8,128)(2,1)S(1)} %get-tuple-element.38), channel_id=1, source_target_pairs={{0,17},{1,19},{2,16},{3,18},{4,22},{5,20},{6,23},{7,21},{8,25},{9,... | collective-permute-start | bytes 73736 | tf_op jit(solution)/shard_map/ppermute | solution.py:247
  9.7 3.5 %collective-permute-start.3 = (bf16[32,384]{1,0:T(8,128)(2,1)S(1)}, bf16[32,384]{1,0:T(8,128)(2,1)S(1)}, u32[]{:S(2)}, u32[]{:S(2)}) collective-permute-start(bf16[32,384]{1,0:T(8,128)(2,1)S(1)} %get-tuple-element.39), channel_id=1, source_target_pairs={{0,18},{1,16},{2,19},{3,17},{4,21},{5,23},{6,20},{7,22},{8,26},{9,... | collective-permute-start | bytes 73736 | tf_op jit(solution)/shard_map/ppermute | solution.py:247
  13.2 5.1 %collective-permute-start.4 = (bf16[32,384]{1,0:T(8,128)(2,1)S(1)}, bf16[32,384]{1,0:T(8,128)(2,1)S(1)}, u32[]{:S(2)}, u32[]{:S(2)}) collective-permute-start(bf16[32,384]{1,0:T(8,128)(2,1)S(1)} %sum.1), channel_id=1, source_target_pairs={{0,28},{1,29},{2,30},{3,31},{4,24},{5,25},{6,26},{7,27},{8,20},{9,... | collective-permute-start | bytes 73736 | tf_op jit(solution)/shard_map/ppermute | solution.py:247
  16.8 4.7 %collective-permute-start.5 = (bf16[32,384]{1,0:T(8,128)(2,1)S(1)}, bf16[32,384]{1,0:T(8,128)(2,1)S(1)}, u32[]{:S(2)}, u32[]{:S(2)}) collective-permute-start(bf16[32,384]{1,0:T(8,128)(2,1)S(1)} %sum.1), channel_id=1, source_target_pairs={{0,8},{1,9},{2,10},{3,11},{4,12},{5,13},{6,14},{7,15},{8,0},{9,1},... | collective-permute-start | bytes 73736 | tf_op jit(solution)/shard_map/ppermute | solution.py:247
  16.8 4.7 %collective-permute-start.6 = (bf16[32,384]{1,0:T(8,128)(2,1)S(1)}, bf16[32,384]{1,0:T(8,128)(2,1)S(1)}, u32[]{:S(2)}, u32[]{:S(2)}) collective-permute-start(bf16[32,384]{1,0:T(8,128)(2,1)S(1)} %sum.1), channel_id=1, source_target_pairs={{0,20},{1,21},{2,22},{3,23},{4,16},{5,17},{6,18},{7,19},{8,28},{9,... | collective-permute-start | bytes 73736 | tf_op jit(solution)/shard_map/ppermute | solution.py:247
  21.6 5.7 %collective-permute-start.7 = (bf16[4,32,384]{2,1,0:T(8,128)(2,1)S(1)}, bf16[4,32,384]{2,1,0:T(8,128)(2,1)S(1)}, u32[]{:S(2)}, u32[]{:S(2)}) collective-permute-start(bf16[4,32,384]{2,1,0:T(8,128)(2,1)S(1)} %pad_maximum_fusion.refs_0_), channel_id=1, source_target_pairs={{0,3},{1,2},{2,1},{3,0},{4,7},{5,6},{6,5},{7,4},{8,11},{9,10},{10,... | collective-permute-start | bytes 294920 | tf_op jit(solution)/shard_map/ppermute | solution.py:247
  23.1 5.0 %collective-permute-start.8 = (bf16[4,32,384]{2,1,0:T(8,128)(2,1)S(1)}, bf16[4,32,384]{2,1,0:T(8,128)(2,1)S(1)}, u32[]{:S(2)}, u32[]{:S(2)}) collective-permute-start(bf16[4,32,384]{2,1,0:T(8,128)(2,1)S(1)} %pad_maximum_fusion.refs_0_), channel_id=1, source_target_pairs={{0,17},{1,19},{2,16},{3,18},{4,22},{5,20},{6,23},{7,21},{8,25},{9,... | collective-permute-start | bytes 294920 | tf_op jit(solution)/shard_map/ppermute | solution.py:247
  23.1 5.7 %collective-permute-start.9 = (bf16[4,32,384]{2,1,0:T(8,128)(2,1)S(1)}, bf16[4,32,384]{2,1,0:T(8,128)(2,1)S(1)}, u32[]{:S(2)}, u32[]{:S(2)}) collective-permute-start(bf16[4,32,384]{2,1,0:T(8,128)(2,1)S(1)} %pad_maximum_fusion.refs_0_), channel_id=1, source_target_pairs={{0,18},{1,16},{2,19},{3,17},{4,21},{5,23},{6,20},{7,22},{8,26},{9,... | collective-permute-start | bytes 294920 | tf_op jit(solution)/shard_map/ppermute | solution.py:247
  24.9 4.8 %collective-permute-start.10 = (bf16[4,32,384]{2,1,0:T(8,128)(2,1)S(1)}, bf16[4,32,384]{2,1,0:T(8,128)(2,1)S(1)}, u32[]{:S(2)}, u32[]{:S(2)}) collective-permute-start(bf16[4,32,384]{2,1,0:T(8,128)(2,1)S(1)} %pad_maximum_fusion.refs_0_), channel_id=1, source_target_pairs={{0,16},{16,0},{1,17},{17,1},{2,18},{18,2},{3,19},{19,3},{4,20},{20... | collective-permute-start | bytes 294920 | tf_op jit(solution)/shard_map/ppermute | solution.py:224
  27.3 2.4 %collective-permute-start.11 = (bf16[4,32,384]{2,1,0:T(8,128)(2,1)S(1)}, bf16[4,32,384]{2,1,0:T(8,128)(2,1)S(1)}, u32[]{:S(2)}, u32[]{:S(2)}) collective-permute-start(bf16[4,32,384]{2,1,0:T(8,128)(2,1)S(1)} %collective-permute-done.7.refs_1_), channel_id=1, source_target_pairs={{0,16},{16,0},{1,17},{17,1},{2,18},{18,2},{3,19},{19,3},{4,20},{20... | collective-permute-start | bytes 294920 | tf_op jit(solution)/shard_map/ppermute | solution.py:224
  28.1 1.7 %collective-permute-start.12 = (bf16[4,32,384]{2,1,0:T(8,128)(2,1)S(1)}, bf16[4,32,384]{2,1,0:T(8,128)(2,1)S(1)}, u32[]{:S(2)}, u32[]{:S(2)}) collective-permute-start(bf16[4,32,384]{2,1,0:T(8,128)(2,1)S(1)} %collective-permute-done.8.refs_2_), channel_id=1, source_target_pairs={{0,16},{16,0},{1,17},{17,1},{2,18},{18,2},{3,19},{19,3},{4,20},{20... | collective-permute-start | bytes 294920 | tf_op jit(solution)/shard_map/ppermute | solution.py:224
  28.8 1.3 %collective-permute-start.13 = (bf16[4,32,384]{2,1,0:T(8,128)(2,1)S(1)}, bf16[4,32,384]{2,1,0:T(8,128)(2,1)S(1)}, u32[]{:S(2)}, u32[]{:S(2)}) collective-permute-start(bf16[4,32,384]{2,1,0:T(8,128)(2,1)S(1)} %collective-permute-done.9.refs_3_), channel_id=1, source_target_pairs={{0,16},{16,0},{1,17},{17,1},{2,18},{18,2},{3,19},{19,3},{4,20},{20... | collective-permute-start | bytes 294920 | tf_op jit(solution)/shard_map/ppermute | solution.py:224
  31.3 1.8 %collective-permute-start.14 = (bf16[4,128,360]{2,1,0:T(8,128)(2,1)S(1)}, bf16[4,128,360]{2,1,0:T(8,128)(2,1)S(1)}, u32[]{:S(2)}, u32[]{:S(2)}) collective-permute-start(bf16[4,128,360]{2,1,0:T(8,128)(2,1)S(1)} %get-tuple-element.48), channel_id=1, source_target_pairs={{0,16},{16,0},{1,17},{17,1},{2,18},{18,2},{3,19},{19,3},{4,20},{20... | collective-permute-start | bytes 1105928 | tf_op jit(solution)/shard_map/ppermute | solution.py:224
  33.1 5.4 %collective-permute-start.18 = (bf16[64,360]{1,0:T(8,128)(2,1)S(1)}, bf16[64,360]{1,0:T(8,128)(2,1)S(1)}, u32[]{:S(2)}, u32[]{:S(2)}) collective-permute-start(bf16[64,360]{1,0:T(8,128)(2,1)S(1)} %get-tuple-element.54), channel_id=1, source_target_pairs={{0,3},{1,2},{2,1},{3,0},{4,7},{5,6},{6,5},{7,4},{8,11},{9,10},{10,... | collective-permute-start | bytes 138248 | tf_op jit(solution)/shard_map/ppermute | solution.py:247
  35.2 4.4 %collective-permute-start.19 = (bf16[64,360]{1,0:T(8,128)(2,1)S(1)}, bf16[64,360]{1,0:T(8,128)(2,1)S(1)}, u32[]{:S(2)}, u32[]{:S(2)}) collective-permute-start(bf16[64,360]{1,0:T(8,128)(2,1)S(1)} %get-tuple-element.55), channel_id=1, source_target_pairs={{0,17},{1,19},{2,16},{3,18},{4,21},{5,23},{6,20},{7,22},{8,25},{9,... | collective-permute-start | bytes 138248 | tf_op jit(solution)/shard_map/ppermute | solution.py:247
  35.6 4.0 %collective-permute-start.20 = (bf16[64,360]{1,0:T(8,128)(2,1)S(1)}, bf16[64,360]{1,0:T(8,128)(2,1)S(1)}, u32[]{:S(2)}, u32[]{:S(2)}) collective-permute-start(bf16[64,360]{1,0:T(8,128)(2,1)S(1)} %get-tuple-element.56), channel_id=1, source_target_pairs={{0,18},{1,16},{2,19},{3,17},{4,22},{5,20},{6,23},{7,21},{8,26},{9,... | collective-permute-start | bytes 138248 | tf_op jit(solution)/shard_map/ppermute | solution.py:247
  36.4 5.9 %collective-permute-start.15 = (bf16[64,360]{1,0:T(8,128)(2,1)S(1)}, bf16[64,360]{1,0:T(8,128)(2,1)S(1)}, u32[]{:S(2)}, u32[]{:S(2)}) collective-permute-start(bf16[64,360]{1,0:T(8,128)(2,1)S(1)} %get-tuple-element.50), channel_id=1, source_target_pairs={{0,3},{1,2},{2,1},{3,0},{4,7},{5,6},{6,5},{7,4},{8,11},{9,10},{10,... | collective-permute-start | bytes 138248 | tf_op jit(solution)/shard_map/ppermute | solution.py:247
  38.4 3.8 %collective-permute-start.16 = (bf16[64,360]{1,0:T(8,128)(2,1)S(1)}, bf16[64,360]{1,0:T(8,128)(2,1)S(1)}, u32[]{:S(2)}, u32[]{:S(2)}) collective-permute-start(bf16[64,360]{1,0:T(8,128)(2,1)S(1)} %get-tuple-element.51), channel_id=1, source_target_pairs={{0,17},{1,19},{2,16},{3,18},{4,21},{5,23},{6,20},{7,22},{8,25},{9,... | collective-permute-start | bytes 138248 | tf_op jit(solution)/shard_map/ppermute | solution.py:247
  38.6 3.9 %collective-permute-start.17 = (bf16[64,360]{1,0:T(8,128)(2,1)S(1)}, bf16[64,360]{1,0:T(8,128)(2,1)S(1)}, u32[]{:S(2)}, u32[]{:S(2)}) collective-permute-start(bf16[64,360]{1,0:T(8,128)(2,1)S(1)} %get-tuple-element.52), channel_id=1, source_target_pairs={{0,18},{1,16},{2,19},{3,17},{4,22},{5,20},{6,23},{7,21},{8,26},{9,... | collective-permute-start | bytes 138248 | tf_op jit(solution)/shard_map/ppermute | solution.py:247
  39.7 5.9 %collective-permute-start.21 = (bf16[32,360]{1,0:T(8,128)(2,1)S(1)}, bf16[32,360]{1,0:T(8,128)(2,1)S(1)}, u32[]{:S(2)}, u32[]{:S(2)}) collective-permute-start(bf16[32,360]{1,0:T(8,128)(2,1)S(1)} %get-tuple-element.57), channel_id=1, source_target_pairs={{0,12},{4,8},{8,4},{12,0},{1,13},{5,9},{9,5},{13,1},{2,14},{6,10},... | collective-permute-start | bytes 69128 | tf_op jit(solution)/shard_map/ppermute | solution.py:224
  41.7 4.8 %collective-permute-start.22 = (bf16[32,360]{1,0:T(8,128)(2,1)S(1)}, bf16[32,360]{1,0:T(8,128)(2,1)S(1)}, u32[]{:S(2)}, u32[]{:S(2)}) collective-permute-start(bf16[32,360]{1,0:T(8,128)(2,1)S(1)} %get-tuple-element.58), channel_id=1, source_target_pairs={{0,8},{4,12},{8,0},{12,4},{1,9},{5,13},{9,1},{13,5},{2,10},{6,14},... | collective-permute-start | bytes 69128 | tf_op jit(solution)/shard_map/ppermute | solution.py:224
  42.5 4.2 %collective-permute-start.23 = (bf16[32,360]{1,0:T(8,128)(2,1)S(1)}, bf16[32,360]{1,0:T(8,128)(2,1)S(1)}, u32[]{:S(2)}, u32[]{:S(2)}) collective-permute-start(bf16[32,360]{1,0:T(8,128)(2,1)S(1)} %get-tuple-element.59), channel_id=1, source_target_pairs={{0,4},{4,0},{8,12},{12,8},{1,5},{5,1},{9,13},{13,9},{2,6},{6,2},{1... | collective-permute-start | bytes 69128 | tf_op jit(solution)/shard_map/ppermute | solution.py:224
  (4 other events, 99.7 us)

commit v15 on v14

--- a/solution.py
+++ b/solution.py
@@ -605,7 +605,7 @@
     mine = call(own_projection_kernel, "own_projection", shape_of(other.shape, jnp.float32), mix, held, limit=12,
                 flops=mix.size * width)
     middle = call(sum_kernel, "sum", shape_of((steps * rows, LANES)), *scatter_shards(mine, come), own_x)
-    stacked = jnp.stack([lane_swap(middle, m, (0, 0), True) for m in reversed(range(1, groups))] + [middle])
+    stacked = jnp.stack([lane_swap(middle, m, (0, 0), True) for m in (2, 3, 1)] + [middle])
     pieces = [stacked] + shard_swaps([stacked] * (tps - 1), True)
     part = width // (secs * tps)
     mine, come, own_middle = experts(expert_gain, w_gate[0], w_up[0], w_down[0], pieces, part)
@@ -613,7 +613,7 @@
     own, *parts = call(after_core_halves_kernel, "after_core_halves",
                        [shape_of((groups * lines, part), jnp.float32)] + [shape_of((groups // 2 * lines, part))] * 6, mine, come)
     far_come, near_come = shard_swaps(parts[:3], False), shard_swaps(parts[3:], False)
-    third, second = call(functools.partial(sum_rows_kernel, line=0), "sum_far_rows", [shape_of((lines, part))] * 2,
+    second, third = call(functools.partial(sum_rows_kernel, line=0), "sum_far_rows", [shape_of((lines, part))] * 2,
                          own, *far_come)
     third, second = swap(third, "grp", 3), swap(second, "grp", 2)
     nearest, own = call(functools.partial(sum_rows_kernel, line=2 * lines), "sum_near_rows",

time: 47.4 us -> 47.5 us (level)
  transfers between devices with their start and end apart: 24 -> 24, of which waited for: 15 -> 16; matrix products, arithmetic and copies ran while one was open for 0% -> 0% of each run, Pallas kernels for 4% -> 4%
where the time goes in v15:
time: 47.5 us; the launch traced here: 47.4 us
  starting transfers between devices  23.5 us (49%)
  waiting for transfers between devices  15.7 us (33%)
  Pallas kernels  7.97 us (17%)
    ppermute x15, starting transfers between devices, lane_swap(): return lax.ppermute(value, ('sec', 'grp', 'tp'), pairs)  17.5 us
    ppermute x15, waiting for transfers between devices, lane_swap(): return lax.ppermute(value, ('sec', 'grp', 'tp'), pairs)  11.5 us
    ppermute x9, starting transfers between devices, swap(): return lax.ppermute(value, axes, [(i, i ^ mask) for i in range(size)])  6.06 us
    pallas_call x1, Pallas kernels, attention_partial(): pl.pallas_call(attention_kernel, name='attention', out_shape=[shape_of((t...  4.24 us
    ppermute x9, waiting for transfers between devices, swap(): return lax.ppermute(value, axes, [(i, i ^ mask) for i in range(size)])  4.23 us
    pallas_call x8, Pallas kernels, call(): pl.pallas_call(kernel, name=name, out_shape=outs, in_specs=[vmem()] * len...  1.95 us
    pallas_call x1, Pallas kernels, experts(): pl.pallas_call(far_kernel, name='far_columns', out_shape=[shape_of((tps,...  1.19 us
  transfers between devices with their start and end apart: 24, of which 16 were waited for; matrix products, arithmetic and copies ran while one was open for 0% of the time, Pallas kernels for 4%

profile of v15, /device:TPU:0, one launch (start us, length us, event | category | flops | bytes accessed | tf_op | source)
XLA Modules:
  0.0 47.4 jit_solution(6317355090348908660)
XLA Ops:
  0.0 4.2 %attention.1 = (bf16[4,32,384]{2,1,0:T(8,128)(2,1)S(1)}, f32[32,384]{1,0:T(8,128)S(1)}, bf16[32,512]{1,0:T(8,128)(2,1)S(1)}, bf16[2880,512]{1,0:T(8,128)(2,1)S(1)}) custom-call(s32[16]{0:T(128)} %lengths_hbm.1, f32[8]{0:T(128)} %sinks_hbm.1, s32[2,4,16]{2,1,0:T(4,128)} %bitcast.31, f32[2,4,16]{2,1,0:T(4,128)} %bitcast.32, f32[2880]{0:T(1024)} %gain_hbm.1, ...), custom_call_target="tpu_custom_call" | custom-call | tf_op jit(solution)/shard_map/attention/pallas_call | solution.py:408
  5.8 3.8 %collective-permute-start.1 = (bf16[32,384]{1,0:T(8,128)(2,1)S(1)}, bf16[32,384]{1,0:T(8,128)(2,1)S(1)}, u32[]{:S(2)}, u32[]{:S(2)}) collective-permute-start(bf16[32,384]{1,0:T(8,128)(2,1)S(1)} %get-tuple-element.37), channel_id=1, source_target_pairs={{0,3},{1,2},{2,1},{3,0},{4,7},{5,6},{6,5},{7,4},{8,11},{9,10},{10,... | collective-permute-start | bytes 73736 | tf_op jit(solution)/shard_map/ppermute | solution.py:247
  10.0 1.4 %collective-permute-done.1.refs_1_ = bf16[32,384]{1,0:T(8,128)(2,1)S(1)} collective-permute-done((bf16[32,384]{1,0:T(8,128)(2,1)S(1)}, bf16[32,384]{1,0:T(8,128)(2,1)S(1)}, u32[]{:S(2)}, u32[]{:S(2)}) %collective-permute-start.1) | collective-permute-done | bytes 24608 | tf_op jit(solution)/shard_map/ppermute | solution.py:247
  11.4 1.4 %collective-permute-done.2.refs_2_ = bf16[32,384]{1,0:T(8,128)(2,1)S(1)} collective-permute-done((bf16[32,384]{1,0:T(8,128)(2,1)S(1)}, bf16[32,384]{1,0:T(8,128)(2,1)S(1)}, u32[]{:S(2)}, u32[]{:S(2)}) %collective-permute-start.2) | collective-permute-done | bytes 24608 | tf_op jit(solution)/shard_map/ppermute | solution.py:247
  13.2 2.7 %collective-permute-start.4 = (bf16[32,384]{1,0:T(8,128)(2,1)S(1)}, bf16[32,384]{1,0:T(8,128)(2,1)S(1)}, u32[]{:S(2)}, u32[]{:S(2)}) collective-permute-start(bf16[32,384]{1,0:T(8,128)(2,1)S(1)} %sum.1), channel_id=1, source_target_pairs={{0,8},{1,9},{2,10},{3,11},{4,12},{5,13},{6,14},{7,15},{8,0},{9,1},... | collective-permute-start | bytes 73736 | tf_op jit(solution)/shard_map/ppermute | solution.py:247
  15.9 1.0 %collective-permute-start.5 = (bf16[32,384]{1,0:T(8,128)(2,1)S(1)}, bf16[32,384]{1,0:T(8,128)(2,1)S(1)}, u32[]{:S(2)}, u32[]{:S(2)}) collective-permute-start(bf16[32,384]{1,0:T(8,128)(2,1)S(1)} %sum.1), channel_id=1, source_target_pairs={{0,28},{1,29},{2,30},{3,31},{4,24},{5,25},{6,26},{7,27},{8,20},{9,... | collective-permute-start | bytes 73736 | tf_op jit(solution)/shard_map/ppermute | solution.py:247
  17.1 0.9 %collective-permute-done.4 = bf16[32,384]{1,0:T(8,128)(2,1)S(1)} collective-permute-done((bf16[32,384]{1,0:T(8,128)(2,1)S(1)}, bf16[32,384]{1,0:T(8,128)(2,1)S(1)}, u32[]{:S(2)}, u32[]{:S(2)}) %collective-permute-start.4) | collective-permute-done | bytes 24608 | tf_op jit(solution)/shard_map/ppermute | solution.py:247
  18.0 3.0 %collective-permute-done.5 = bf16[32,384]{1,0:T(8,128)(2,1)S(1)} collective-permute-done((bf16[32,384]{1,0:T(8,128)(2,1)S(1)}, bf16[32,384]{1,0:T(8,128)(2,1)S(1)}, u32[]{:S(2)}, u32[]{:S(2)}) %collective-permute-start.5) | collective-permute-done | bytes 24608 | tf_op jit(solution)/shard_map/ppermute | solution.py:247
  21.1 1.5 %collective-permute-start.7 = (bf16[4,32,384]{2,1,0:T(8,128)(2,1)S(1)}, bf16[4,32,384]{2,1,0:T(8,128)(2,1)S(1)}, u32[]{:S(2)}, u32[]{:S(2)}) collective-permute-start(bf16[4,32,384]{2,1,0:T(8,128)(2,1)S(1)} %pad_maximum_fusion.refs_0_), channel_id=1, source_target_pairs={{0,3},{1,2},{2,1},{3,0},{4,7},{5,6},{6,5},{7,4},{8,11},{9,10},{10,... | collective-permute-start | bytes 294920 | tf_op jit(solution)/shard_map/ppermute | solution.py:247
  23.1 1.3 %collective-permute-start.9 = (bf16[4,32,384]{2,1,0:T(8,128)(2,1)S(1)}, bf16[4,32,384]{2,1,0:T(8,128)(2,1)S(1)}, u32[]{:S(2)}, u32[]{:S(2)}) collective-permute-start(bf16[4,32,384]{2,1,0:T(8,128)(2,1)S(1)} %pad_maximum_fusion.refs_0_), channel_id=1, source_target_pairs={{0,18},{1,16},{2,19},{3,17},{4,21},{5,23},{6,20},{7,22},{8,26},{9,... | collective-permute-start | bytes 294920 | tf_op jit(solution)/shard_map/ppermute | solution.py:247
  24.4 2.8 %collective-permute-done.7.refs_1_ = bf16[4,32,384]{2,1,0:T(8,128)(2,1)S(1)} collective-permute-done((bf16[4,32,384]{2,1,0:T(8,128)(2,1)S(1)}, bf16[4,32,384]{2,1,0:T(8,128)(2,1)S(1)}, u32[]{:S(2)}, u32[]{:S(2)}) %collective-permute-start.7) | collective-permute-done | bytes 98336 | tf_op jit(solution)/shard_map/ppermute | solution.py:247
  27.7 1.5 %collective-permute-start.12 = (bf16[4,32,384]{2,1,0:T(8,128)(2,1)S(1)}, bf16[4,32,384]{2,1,0:T(8,128)(2,1)S(1)}, u32[]{:S(2)}, u32[]{:S(2)}) collective-permute-start(bf16[4,32,384]{2,1,0:T(8,128)(2,1)S(1)} %collective-permute-done.8.refs_2_), channel_id=1, source_target_pairs={{0,16},{16,0},{1,17},{17,1},{2,18},{18,2},{3,19},{19,3},{4,20},{20... | collective-permute-start | bytes 294920 | tf_op jit(solution)/shard_map/ppermute | solution.py:224
  30.4 1.2 %far_columns.1 = (bf16[4,128,360]{2,1,0:T(8,128)(2,1)S(1)}, bf16[128,180]{1,0:T(8,128)(2,1)S(1)}, bf16[128,1536]{1,0:T(8,128)(2,1)S(1)}) custom-call(f32[1,2880]{1,0:T(1,128)S(1)} %reshape.6.gain_ref, bf16[180,2880]{1,0:T(8,128)(2,1)S(1)} %bitcast.18, bf16[180,2880]{1,0:T(8,128)(2,1)S(1)} %bitcast.20, bf16[180,2880]{1,0:T(8,128)(2,1)S(1)} %bitcast.21, ...), custom_call_target="tpu_custom_call" | custom-call | tf_op jit(solution)/shard_map/far_columns/pallas_call | solution.py:573
  32.4 1.0 %collective-permute-done.14.come_ref = bf16[4,128,360]{2,1,0:T(8,128)(2,1)S(1)} collective-permute-done((bf16[4,128,360]{2,1,0:T(8,128)(2,1)S(1)}, bf16[4,128,360]{2,1,0:T(8,128)(2,1)S(1)}, u32[]{:S(2)}, u32[]{:S(2)}) %collective-permute-start.14) | collective-permute-done | bytes 368672 | tf_op jit(solution)/shard_map/ppermute | solution.py:224
  33.5 1.5 %collective-permute-start.18 = (bf16[64,360]{1,0:T(8,128)(2,1)S(1)}, bf16[64,360]{1,0:T(8,128)(2,1)S(1)}, u32[]{:S(2)}, u32[]{:S(2)}) collective-permute-start(bf16[64,360]{1,0:T(8,128)(2,1)S(1)} %get-tuple-element.54), channel_id=1, source_target_pairs={{0,3},{1,2},{2,1},{3,0},{4,7},{5,6},{6,5},{7,4},{8,11},{9,10},{10,... | collective-permute-start | bytes 138248 | tf_op jit(solution)/shard_map/ppermute | solution.py:247
  35.1 1.6 %collective-permute-start.20 = (bf16[64,360]{1,0:T(8,128)(2,1)S(1)}, bf16[64,360]{1,0:T(8,128)(2,1)S(1)}, u32[]{:S(2)}, u32[]{:S(2)}) collective-permute-start(bf16[64,360]{1,0:T(8,128)(2,1)S(1)} %get-tuple-element.56), channel_id=1, source_target_pairs={{0,18},{1,16},{2,19},{3,17},{4,22},{5,20},{6,23},{7,21},{8,26},{9,... | collective-permute-start | bytes 138248 | tf_op jit(solution)/shard_map/ppermute | solution.py:247
  36.8 1.5 %collective-permute-start.15 = (bf16[64,360]{1,0:T(8,128)(2,1)S(1)}, bf16[64,360]{1,0:T(8,128)(2,1)S(1)}, u32[]{:S(2)}, u32[]{:S(2)}) collective-permute-start(bf16[64,360]{1,0:T(8,128)(2,1)S(1)} %get-tuple-element.50), channel_id=1, source_target_pairs={{0,3},{1,2},{2,1},{3,0},{4,7},{5,6},{6,5},{7,4},{8,11},{9,10},{10,... | collective-permute-start | bytes 138248 | tf_op jit(solution)/shard_map/ppermute | solution.py:247
  38.6 1.4 %collective-permute-start.17 = (bf16[64,360]{1,0:T(8,128)(2,1)S(1)}, bf16[64,360]{1,0:T(8,128)(2,1)S(1)}, u32[]{:S(2)}, u32[]{:S(2)}) collective-permute-start(bf16[64,360]{1,0:T(8,128)(2,1)S(1)} %get-tuple-element.52), channel_id=1, source_target_pairs={{0,18},{1,16},{2,19},{3,17},{4,22},{5,20},{6,23},{7,21},{8,26},{9,... | collective-permute-start | bytes 138248 | tf_op jit(solution)/shard_map/ppermute | solution.py:247
  40.0 1.9 %collective-permute-start.21 = (bf16[32,360]{1,0:T(8,128)(2,1)S(1)}, bf16[32,360]{1,0:T(8,128)(2,1)S(1)}, u32[]{:S(2)}, u32[]{:S(2)}) collective-permute-start(bf16[32,360]{1,0:T(8,128)(2,1)S(1)} %get-tuple-element.57), channel_id=1, source_target_pairs={{0,12},{4,8},{8,4},{12,0},{1,13},{5,9},{9,5},{13,1},{2,14},{6,10},... | collective-permute-start | bytes 69128 | tf_op jit(solution)/shard_map/ppermute | solution.py:224
  41.9 0.7 %collective-permute-done.17.refs_2_ = bf16[64,360]{1,0:T(8,128)(2,1)S(1)} collective-permute-done((bf16[64,360]{1,0:T(8,128)(2,1)S(1)}, bf16[64,360]{1,0:T(8,128)(2,1)S(1)}, u32[]{:S(2)}, u32[]{:S(2)}) %collective-permute-start.17) | collective-permute-done | bytes 46112 | tf_op jit(solution)/shard_map/ppermute | solution.py:247
  42.6 2.0 %collective-permute-start.23 = (bf16[32,360]{1,0:T(8,128)(2,1)S(1)}, bf16[32,360]{1,0:T(8,128)(2,1)S(1)}, u32[]{:S(2)}, u32[]{:S(2)}) collective-permute-start(bf16[32,360]{1,0:T(8,128)(2,1)S(1)} %get-tuple-element.59), channel_id=1, source_target_pairs={{0,4},{4,0},{8,12},{12,8},{1,5},{5,1},{9,13},{13,9},{2,6},{6,2},{1... | collective-permute-start | bytes 69128 | tf_op jit(solution)/shard_map/ppermute | solution.py:224
  44.6 1.1 %collective-permute-done.21.refs_1_ = bf16[32,360]{1,0:T(8,128)(2,1)S(1)} collective-permute-done((bf16[32,360]{1,0:T(8,128)(2,1)S(1)}, bf16[32,360]{1,0:T(8,128)(2,1)S(1)}, u32[]{:S(2)}, u32[]{:S(2)}) %collective-permute-start.21) | collective-permute-done | bytes 23072 | tf_op jit(solution)/shard_map/ppermute | solution.py:224
  45.7 0.9 %collective-permute-done.22.refs_2_ = bf16[32,360]{1,0:T(8,128)(2,1)S(1)} collective-permute-done((bf16[32,360]{1,0:T(8,128)(2,1)S(1)}, bf16[32,360]{1,0:T(8,128)(2,1)S(1)}, u32[]{:S(2)}, u32[]{:S(2)}) %collective-permute-start.22) | collective-permute-done | bytes 23072 | tf_op jit(solution)/shard_map/ppermute | solution.py:224
  46.8 0.6 %combine.1 = bf16[2,16,360]{2,1,0:T(8,128)(2,1)} custom-call(f32[32,360]{1,0:T(8,128)S(1)} %get-tuple-element.53.refs_0_, bf16[32,360]{1,0:T(8,128)(2,1)S(1)} %collective-permute-done.21.refs_1_, bf16[32,360]{1,0:T(8,128)(2,1)S(1)} %collective-permute-done.22.refs_2_, bf16[32,360]{1,0:T(8,128)(2,1)S(1)} %collective-permute-done.23.refs_3_, ...), custom_call_target="tpu_custom_call" | custom-call | bytes 184320 | tf_op jit(solution)/shard_map/combine/pallas_call | solution.py:437
  (45 shorter events, 6.2 us)
Async XLA Ops:
  4.3 1.5 %collective-permute-start = (bf16[4,32,384]{2,1,0:T(8,128)(2,1)S(1)}, bf16[4,32,384]{2,1,0:T(8,128)(2,1)S(1)}, u32[]{:S(2)}, u32[]{:S(2)}) collective-permute-start(bf16[4,32,384]{2,1,0:T(8,128)(2,1)S(1)} %get-tuple-element.35), channel_id=1, source_target_pairs={{0,16},{16,0},{1,17},{17,1},{2,18},{18,2},{3,19},{19,3},{4,20},{20... | collective-permute-start | bytes 294920 | tf_op jit(solution)/shard_map/ppermute | solution.py:224
  5.8 5.6 %collective-permute-start.1 = (bf16[32,384]{1,0:T(8,128)(2,1)S(1)}, bf16[32,384]{1,0:T(8,128)(2,1)S(1)}, u32[]{:S(2)}, u32[]{:S(2)}) collective-permute-start(bf16[32,384]{1,0:T(8,128)(2,1)S(1)} %get-tuple-element.37), channel_id=1, source_target_pairs={{0,3},{1,2},{2,1},{3,0},{4,7},{5,6},{6,5},{7,4},{8,11},{9,10},{10,... | collective-permute-start | bytes 73736 | tf_op jit(solution)/shard_map/ppermute | solution.py:247
  9.6 3.3 %collective-permute-start.2 = (bf16[32,384]{1,0:T(8,128)(2,1)S(1)}, bf16[32,384]{1,0:T(8,128)(2,1)S(1)}, u32[]{:S(2)}, u32[]{:S(2)}) collective-permute-start(bf16[32,384]{1,0:T(8,128)(2,1)S(1)} %get-tuple-element.38), channel_id=1, source_target_pairs={{0,17},{1,19},{2,16},{3,18},{4,22},{5,20},{6,23},{7,21},{8,25},{9,... | collective-permute-start | bytes 73736 | tf_op jit(solution)/shard_map/ppermute | solution.py:247
  9.7 3.5 %collective-permute-start.3 = (bf16[32,384]{1,0:T(8,128)(2,1)S(1)}, bf16[32,384]{1,0:T(8,128)(2,1)S(1)}, u32[]{:S(2)}, u32[]{:S(2)}) collective-permute-start(bf16[32,384]{1,0:T(8,128)(2,1)S(1)} %get-tuple-element.39), channel_id=1, source_target_pairs={{0,18},{1,16},{2,19},{3,17},{4,21},{5,23},{6,20},{7,22},{8,26},{9,... | collective-permute-start | bytes 73736 | tf_op jit(solution)/shard_map/ppermute | solution.py:247
  13.2 4.8 %collective-permute-start.4 = (bf16[32,384]{1,0:T(8,128)(2,1)S(1)}, bf16[32,384]{1,0:T(8,128)(2,1)S(1)}, u32[]{:S(2)}, u32[]{:S(2)}) collective-permute-start(bf16[32,384]{1,0:T(8,128)(2,1)S(1)} %sum.1), channel_id=1, source_target_pairs={{0,8},{1,9},{2,10},{3,11},{4,12},{5,13},{6,14},{7,15},{8,0},{9,1},... | collective-permute-start | bytes 73736 | tf_op jit(solution)/shard_map/ppermute | solution.py:247
  15.9 5.2 %collective-permute-start.5 = (bf16[32,384]{1,0:T(8,128)(2,1)S(1)}, bf16[32,384]{1,0:T(8,128)(2,1)S(1)}, u32[]{:S(2)}, u32[]{:S(2)}) collective-permute-start(bf16[32,384]{1,0:T(8,128)(2,1)S(1)} %sum.1), channel_id=1, source_target_pairs={{0,28},{1,29},{2,30},{3,31},{4,24},{5,25},{6,26},{7,27},{8,20},{9,... | collective-permute-start | bytes 73736 | tf_op jit(solution)/shard_map/ppermute | solution.py:247
  16.9 4.1 %collective-permute-start.6 = (bf16[32,384]{1,0:T(8,128)(2,1)S(1)}, bf16[32,384]{1,0:T(8,128)(2,1)S(1)}, u32[]{:S(2)}, u32[]{:S(2)}) collective-permute-start(bf16[32,384]{1,0:T(8,128)(2,1)S(1)} %sum.1), channel_id=1, source_target_pairs={{0,20},{1,21},{2,22},{3,23},{4,16},{5,17},{6,18},{7,19},{8,28},{9,... | collective-permute-start | bytes 73736 | tf_op jit(solution)/shard_map/ppermute | solution.py:247
  21.1 6.1 %collective-permute-start.7 = (bf16[4,32,384]{2,1,0:T(8,128)(2,1)S(1)}, bf16[4,32,384]{2,1,0:T(8,128)(2,1)S(1)}, u32[]{:S(2)}, u32[]{:S(2)}) collective-permute-start(bf16[4,32,384]{2,1,0:T(8,128)(2,1)S(1)} %pad_maximum_fusion.refs_0_), channel_id=1, source_target_pairs={{0,3},{1,2},{2,1},{3,0},{4,7},{5,6},{6,5},{7,4},{8,11},{9,10},{10,... | collective-permute-start | bytes 294920 | tf_op jit(solution)/shard_map/ppermute | solution.py:247
  22.6 5.1 %collective-permute-start.8 = (bf16[4,32,384]{2,1,0:T(8,128)(2,1)S(1)}, bf16[4,32,384]{2,1,0:T(8,128)(2,1)S(1)}, u32[]{:S(2)}, u32[]{:S(2)}) collective-permute-start(bf16[4,32,384]{2,1,0:T(8,128)(2,1)S(1)} %pad_maximum_fusion.refs_0_), channel_id=1, source_target_pairs={{0,17},{1,19},{2,16},{3,18},{4,22},{5,20},{6,23},{7,21},{8,25},{9,... | collective-permute-start | bytes 294920 | tf_op jit(solution)/shard_map/ppermute | solution.py:247
  23.1 6.0 %collective-permute-start.9 = (bf16[4,32,384]{2,1,0:T(8,128)(2,1)S(1)}, bf16[4,32,384]{2,1,0:T(8,128)(2,1)S(1)}, u32[]{:S(2)}, u32[]{:S(2)}) collective-permute-start(bf16[4,32,384]{2,1,0:T(8,128)(2,1)S(1)} %pad_maximum_fusion.refs_0_), channel_id=1, source_target_pairs={{0,18},{1,16},{2,19},{3,17},{4,21},{5,23},{6,20},{7,22},{8,26},{9,... | collective-permute-start | bytes 294920 | tf_op jit(solution)/shard_map/ppermute | solution.py:247
  24.4 5.4 %collective-permute-start.10 = (bf16[4,32,384]{2,1,0:T(8,128)(2,1)S(1)}, bf16[4,32,384]{2,1,0:T(8,128)(2,1)S(1)}, u32[]{:S(2)}, u32[]{:S(2)}) collective-permute-start(bf16[4,32,384]{2,1,0:T(8,128)(2,1)S(1)} %pad_maximum_fusion.refs_0_), channel_id=1, source_target_pairs={{0,16},{16,0},{1,17},{17,1},{2,18},{18,2},{3,19},{19,3},{4,20},{20... | collective-permute-start | bytes 294920 | tf_op jit(solution)/shard_map/ppermute | solution.py:224
  27.2 2.6 %collective-permute-start.11 = (bf16[4,32,384]{2,1,0:T(8,128)(2,1)S(1)}, bf16[4,32,384]{2,1,0:T(8,128)(2,1)S(1)}, u32[]{:S(2)}, u32[]{:S(2)}) collective-permute-start(bf16[4,32,384]{2,1,0:T(8,128)(2,1)S(1)} %collective-permute-done.7.refs_1_), channel_id=1, source_target_pairs={{0,16},{16,0},{1,17},{17,1},{2,18},{18,2},{3,19},{19,3},{4,20},{20... | collective-permute-start | bytes 294920 | tf_op jit(solution)/shard_map/ppermute | solution.py:224
  27.7 2.4 %collective-permute-start.12 = (bf16[4,32,384]{2,1,0:T(8,128)(2,1)S(1)}, bf16[4,32,384]{2,1,0:T(8,128)(2,1)S(1)}, u32[]{:S(2)}, u32[]{:S(2)}) collective-permute-start(bf16[4,32,384]{2,1,0:T(8,128)(2,1)S(1)} %collective-permute-done.8.refs_2_), channel_id=1, source_target_pairs={{0,16},{16,0},{1,17},{17,1},{2,18},{18,2},{3,19},{19,3},{4,20},{20... | collective-permute-start | bytes 294920 | tf_op jit(solution)/shard_map/ppermute | solution.py:224
  29.1 1.3 %collective-permute-start.13 = (bf16[4,32,384]{2,1,0:T(8,128)(2,1)S(1)}, bf16[4,32,384]{2,1,0:T(8,128)(2,1)S(1)}, u32[]{:S(2)}, u32[]{:S(2)}) collective-permute-start(bf16[4,32,384]{2,1,0:T(8,128)(2,1)S(1)} %collective-permute-done.9.refs_3_), channel_id=1, source_target_pairs={{0,16},{16,0},{1,17},{17,1},{2,18},{18,2},{3,19},{19,3},{4,20},{20... | collective-permute-start | bytes 294920 | tf_op jit(solution)/shard_map/ppermute | solution.py:224
  31.6 1.8 %collective-permute-start.14 = (bf16[4,128,360]{2,1,0:T(8,128)(2,1)S(1)}, bf16[4,128,360]{2,1,0:T(8,128)(2,1)S(1)}, u32[]{:S(2)}, u32[]{:S(2)}) collective-permute-start(bf16[4,128,360]{2,1,0:T(8,128)(2,1)S(1)} %get-tuple-element.48), channel_id=1, source_target_pairs={{0,16},{16,0},{1,17},{17,1},{2,18},{18,2},{3,19},{19,3},{4,20},{20... | collective-permute-start | bytes 1105928 | tf_op jit(solution)/shard_map/ppermute | solution.py:224
  33.5 5.1 %collective-permute-start.18 = (bf16[64,360]{1,0:T(8,128)(2,1)S(1)}, bf16[64,360]{1,0:T(8,128)(2,1)S(1)}, u32[]{:S(2)}, u32[]{:S(2)}) collective-permute-start(bf16[64,360]{1,0:T(8,128)(2,1)S(1)} %get-tuple-element.54), channel_id=1, source_target_pairs={{0,3},{1,2},{2,1},{3,0},{4,7},{5,6},{6,5},{7,4},{8,11},{9,10},{10,... | collective-permute-start | bytes 138248 | tf_op jit(solution)/shard_map/ppermute | solution.py:247
  35.0 4.9 %collective-permute-start.19 = (bf16[64,360]{1,0:T(8,128)(2,1)S(1)}, bf16[64,360]{1,0:T(8,128)(2,1)S(1)}, u32[]{:S(2)}, u32[]{:S(2)}) collective-permute-start(bf16[64,360]{1,0:T(8,128)(2,1)S(1)} %get-tuple-element.55), channel_id=1, source_target_pairs={{0,17},{1,19},{2,16},{3,18},{4,21},{5,23},{6,20},{7,22},{8,25},{9,... | collective-permute-start | bytes 138248 | tf_op jit(solution)/shard_map/ppermute | solution.py:247
  35.1 4.9 %collective-permute-start.20 = (bf16[64,360]{1,0:T(8,128)(2,1)S(1)}, bf16[64,360]{1,0:T(8,128)(2,1)S(1)}, u32[]{:S(2)}, u32[]{:S(2)}) collective-permute-start(bf16[64,360]{1,0:T(8,128)(2,1)S(1)} %get-tuple-element.56), channel_id=1, source_target_pairs={{0,18},{1,16},{2,19},{3,17},{4,22},{5,20},{6,23},{7,21},{8,26},{9,... | collective-permute-start | bytes 138248 | tf_op jit(solution)/shard_map/ppermute | solution.py:247
  36.8 5.1 %collective-permute-start.15 = (bf16[64,360]{1,0:T(8,128)(2,1)S(1)}, bf16[64,360]{1,0:T(8,128)(2,1)S(1)}, u32[]{:S(2)}, u32[]{:S(2)}) collective-permute-start(bf16[64,360]{1,0:T(8,128)(2,1)S(1)} %get-tuple-element.50), channel_id=1, source_target_pairs={{0,3},{1,2},{2,1},{3,0},{4,7},{5,6},{6,5},{7,4},{8,11},{9,10},{10,... | collective-permute-start | bytes 138248 | tf_op jit(solution)/shard_map/ppermute | solution.py:247
  38.2 3.7 %collective-permute-start.16 = (bf16[64,360]{1,0:T(8,128)(2,1)S(1)}, bf16[64,360]{1,0:T(8,128)(2,1)S(1)}, u32[]{:S(2)}, u32[]{:S(2)}) collective-permute-start(bf16[64,360]{1,0:T(8,128)(2,1)S(1)} %get-tuple-element.51), channel_id=1, source_target_pairs={{0,17},{1,19},{2,16},{3,18},{4,21},{5,23},{6,20},{7,22},{8,25},{9,... | collective-permute-start | bytes 138248 | tf_op jit(solution)/shard_map/ppermute | solution.py:247
  38.6 4.0 %collective-permute-start.17 = (bf16[64,360]{1,0:T(8,128)(2,1)S(1)}, bf16[64,360]{1,0:T(8,128)(2,1)S(1)}, u32[]{:S(2)}, u32[]{:S(2)}) collective-permute-start(bf16[64,360]{1,0:T(8,128)(2,1)S(1)} %get-tuple-element.52), channel_id=1, source_target_pairs={{0,18},{1,16},{2,19},{3,17},{4,22},{5,20},{6,23},{7,21},{8,26},{9,... | collective-permute-start | bytes 138248 | tf_op jit(solution)/shard_map/ppermute | solution.py:247
  40.0 5.7 %collective-permute-start.21 = (bf16[32,360]{1,0:T(8,128)(2,1)S(1)}, bf16[32,360]{1,0:T(8,128)(2,1)S(1)}, u32[]{:S(2)}, u32[]{:S(2)}) collective-permute-start(bf16[32,360]{1,0:T(8,128)(2,1)S(1)} %get-tuple-element.57), channel_id=1, source_target_pairs={{0,12},{4,8},{8,4},{12,0},{1,13},{5,9},{9,5},{13,1},{2,14},{6,10},... | collective-permute-start | bytes 69128 | tf_op jit(solution)/shard_map/ppermute | solution.py:224
  41.9 4.8 %collective-permute-start.22 = (bf16[32,360]{1,0:T(8,128)(2,1)S(1)}, bf16[32,360]{1,0:T(8,128)(2,1)S(1)}, u32[]{:S(2)}, u32[]{:S(2)}) collective-permute-start(bf16[32,360]{1,0:T(8,128)(2,1)S(1)} %get-tuple-element.58), channel_id=1, source_target_pairs={{0,8},{4,12},{8,0},{12,4},{1,9},{5,13},{9,1},{13,5},{2,10},{6,14},... | collective-permute-start | bytes 69128 | tf_op jit(solution)/shard_map/ppermute | solution.py:224
  42.6 4.2 %collective-permute-start.23 = (bf16[32,360]{1,0:T(8,128)(2,1)S(1)}, bf16[32,360]{1,0:T(8,128)(2,1)S(1)}, u32[]{:S(2)}, u32[]{:S(2)}) collective-permute-start(bf16[32,360]{1,0:T(8,128)(2,1)S(1)} %get-tuple-element.59), channel_id=1, source_target_pairs={{0,4},{4,0},{8,12},{12,8},{1,5},{5,1},{9,13},{13,9},{2,6},{6,2},{1... | collective-permute-start | bytes 69128 | tf_op jit(solution)/shard_map/ppermute | solution.py:224
  (4 other events, 100.2 us)

commit v16 on v14

--- a/solution.py
+++ b/solution.py
@@ -248,12 +248,12 @@
 
 
 def shard_swaps(parts, by_group):
-    return [lane_swap(part, 0, masks, by_group) for part, masks in zip(parts, ((3, 3), (1, 2), (2, 1)))]
+    return [lane_swap(part, 0, masks, by_group) for part, masks in zip(parts, ((1, 2), (3, 3), (2, 1)))]
 
 
 def shard_masks(by_group):
     number = lane_of(by_group)
-    return 3, 1 + number, 2 - number
+    return 1 + number, 3, 2 - number
 
 
 def split_width(width):
@@ -536,7 +536,7 @@
     pieces, (other_ref, act_ref, far_x_ref, gate_out, up_out, square_out) = refs[:-6], refs[-6:]
     side, grp = lane_of(True), lax.axis_index("grp")
     masks = shard_masks(True)
-    first_products(pieces, (0, masks[0], masks[2], masks[1]), 1 - side, far_x_ref, gain_ref, gate_ref, up_ref, gate_out, up_out,
+    first_products(pieces, (0, masks[2], masks[1], masks[0]), 1 - side, far_x_ref, gain_ref, gate_ref, up_ref, gate_out, up_out,
                    square_out)
     width, half = gate_ref.shape[1], near_x_ref.shape[1]
     spare = jnp.where(side == 1, near_x_ref[:, width - half:], far_x_ref[:, width - half:]).astype(jnp.float32)

time: 47.4 us -> 47.6 us (level)
  waiting for transfers between devices: 15.3 us -> 17.4 us
  starting transfers between devices: 23.9 us -> 21.9 us
    ppermute x15, waiting for transfers between devices: 11.2 us -> 13.1 us  [lane_swap(): return lax.ppermute(value, ('sec', 'grp', 'tp'), pairs)]
    ppermute x9, starting transfers between devices: 5.96 us -> 4.93 us  [swap(): return lax.ppermute(value, axes, [(i, i ^ mask) for i in range(size)])]
    ppermute x15, starting transfers between devices: 17.9 us -> 17 us  [lane_swap(): return lax.ppermute(value, ('sec', 'grp', 'tp'), pairs)]
where the time goes in v16:
time: 47.6 us; the launch traced here: 47.5 us
  starting transfers between devices  21.9 us (46%)
  waiting for transfers between devices  17.4 us (37%)
  Pallas kernels  7.96 us (17%)
    ppermute x15, starting transfers between devices, lane_swap(): return lax.ppermute(value, ('sec', 'grp', 'tp'), pairs)  17 us
    ppermute x15, waiting for transfers between devices, lane_swap(): return lax.ppermute(value, ('sec', 'grp', 'tp'), pairs)  13.1 us
    ppermute x9, starting transfers between devices, swap(): return lax.ppermute(value, axes, [(i, i ^ mask) for i in range(size)])  4.93 us
    ppermute x9, waiting for transfers between devices, swap(): return lax.ppermute(value, axes, [(i, i ^ mask) for i in range(size)])  4.34 us
    pallas_call x1, Pallas kernels, attention_partial(): pl.pallas_call(attention_kernel, name='attention', out_shape=[shape_of((t...  4.24 us
    pallas_call x8, Pallas kernels, call(): pl.pallas_call(kernel, name=name, out_shape=outs, in_specs=[vmem()] * len...  1.95 us
    pallas_call x1, Pallas kernels, experts(): pl.pallas_call(far_kernel, name='far_columns', out_shape=[shape_of((tps,...  1.19 us
  transfers between devices with their start and end apart: 24, of which 15 were waited for; matrix products, arithmetic and copies ran while one was open for 0% of the time, Pallas kernels for 4%

profile of v16, /device:TPU:0, one launch (start us, length us, event | category | flops | bytes accessed | tf_op | source)
XLA Modules:
  0.0 47.5 jit_solution(4491100640217658810)
XLA Ops:
  0.0 4.2 %attention.1 = (bf16[4,32,384]{2,1,0:T(8,128)(2,1)S(1)}, f32[32,384]{1,0:T(8,128)S(1)}, bf16[32,512]{1,0:T(8,128)(2,1)S(1)}, bf16[2880,512]{1,0:T(8,128)(2,1)S(1)}) custom-call(s32[16]{0:T(128)} %lengths_hbm.1, f32[8]{0:T(128)} %sinks_hbm.1, s32[2,4,16]{2,1,0:T(4,128)} %bitcast.31, f32[2,4,16]{2,1,0:T(4,128)} %bitcast.32, f32[2880]{0:T(1024)} %gain_hbm.1, ...), custom_call_target="tpu_custom_call" | custom-call | tf_op jit(solution)/shard_map/attention/pallas_call | solution.py:408
  5.8 2.7 %collective-permute-start.1 = (bf16[32,384]{1,0:T(8,128)(2,1)S(1)}, bf16[32,384]{1,0:T(8,128)(2,1)S(1)}, u32[]{:S(2)}, u32[]{:S(2)}) collective-permute-start(bf16[32,384]{1,0:T(8,128)(2,1)S(1)} %get-tuple-element.37), channel_id=1, source_target_pairs={{0,17},{1,19},{2,16},{3,18},{4,22},{5,20},{6,23},{7,21},{8,25},{9,... | collective-permute-start | bytes 73736 | tf_op jit(solution)/shard_map/ppermute | solution.py:247
  8.5 1.5 %collective-permute-start.2 = (bf16[32,384]{1,0:T(8,128)(2,1)S(1)}, bf16[32,384]{1,0:T(8,128)(2,1)S(1)}, u32[]{:S(2)}, u32[]{:S(2)}) collective-permute-start(bf16[32,384]{1,0:T(8,128)(2,1)S(1)} %get-tuple-element.38), channel_id=1, source_target_pairs={{0,3},{1,2},{2,1},{3,0},{4,7},{5,6},{6,5},{7,4},{8,11},{9,10},{10,... | collective-permute-start | bytes 73736 | tf_op jit(solution)/shard_map/ppermute | solution.py:247
  10.0 3.3 %collective-permute-done.2.refs_2_ = bf16[32,384]{1,0:T(8,128)(2,1)S(1)} collective-permute-done((bf16[32,384]{1,0:T(8,128)(2,1)S(1)}, bf16[32,384]{1,0:T(8,128)(2,1)S(1)}, u32[]{:S(2)}, u32[]{:S(2)}) %collective-permute-start.2) | collective-permute-done | bytes 24608 | tf_op jit(solution)/shard_map/ppermute | solution.py:247
  13.5 3.2 %collective-permute-start.4 = (bf16[32,384]{1,0:T(8,128)(2,1)S(1)}, bf16[32,384]{1,0:T(8,128)(2,1)S(1)}, u32[]{:S(2)}, u32[]{:S(2)}) collective-permute-start(bf16[32,384]{1,0:T(8,128)(2,1)S(1)} %sum.1), channel_id=1, source_target_pairs={{0,28},{1,29},{2,30},{3,31},{4,24},{5,25},{6,26},{7,27},{8,20},{9,... | collective-permute-start | bytes 73736 | tf_op jit(solution)/shard_map/ppermute | solution.py:247
  16.8 0.7 %collective-permute-start.6 = (bf16[32,384]{1,0:T(8,128)(2,1)S(1)}, bf16[32,384]{1,0:T(8,128)(2,1)S(1)}, u32[]{:S(2)}, u32[]{:S(2)}) collective-permute-start(bf16[32,384]{1,0:T(8,128)(2,1)S(1)} %sum.1), channel_id=1, source_target_pairs={{0,20},{1,21},{2,22},{3,23},{4,16},{5,17},{6,18},{7,19},{8,28},{9,... | collective-permute-start | bytes 73736 | tf_op jit(solution)/shard_map/ppermute | solution.py:247
  17.4 1.2 %collective-permute-done.4 = bf16[32,384]{1,0:T(8,128)(2,1)S(1)} collective-permute-done((bf16[32,384]{1,0:T(8,128)(2,1)S(1)}, bf16[32,384]{1,0:T(8,128)(2,1)S(1)}, u32[]{:S(2)}, u32[]{:S(2)}) %collective-permute-start.4) | collective-permute-done | bytes 24608 | tf_op jit(solution)/shard_map/ppermute | solution.py:247
  18.6 2.8 %collective-permute-done.5 = bf16[32,384]{1,0:T(8,128)(2,1)S(1)} collective-permute-done((bf16[32,384]{1,0:T(8,128)(2,1)S(1)}, bf16[32,384]{1,0:T(8,128)(2,1)S(1)}, u32[]{:S(2)}, u32[]{:S(2)}) %collective-permute-start.5) | collective-permute-done | bytes 24608 | tf_op jit(solution)/shard_map/ppermute | solution.py:247
  22.0 1.5 %collective-permute-start.8 = (bf16[4,32,384]{2,1,0:T(8,128)(2,1)S(1)}, bf16[4,32,384]{2,1,0:T(8,128)(2,1)S(1)}, u32[]{:S(2)}, u32[]{:S(2)}) collective-permute-start(bf16[4,32,384]{2,1,0:T(8,128)(2,1)S(1)} %pad_maximum_fusion.refs_0_), channel_id=1, source_target_pairs={{0,3},{1,2},{2,1},{3,0},{4,7},{5,6},{6,5},{7,4},{8,11},{9,10},{10,... | collective-permute-start | bytes 294920 | tf_op jit(solution)/shard_map/ppermute | solution.py:247
  23.5 1.0 %collective-permute-start.9 = (bf16[4,32,384]{2,1,0:T(8,128)(2,1)S(1)}, bf16[4,32,384]{2,1,0:T(8,128)(2,1)S(1)}, u32[]{:S(2)}, u32[]{:S(2)}) collective-permute-start(bf16[4,32,384]{2,1,0:T(8,128)(2,1)S(1)} %pad_maximum_fusion.refs_0_), channel_id=1, source_target_pairs={{0,18},{1,16},{2,19},{3,17},{4,21},{5,23},{6,20},{7,22},{8,26},{9,... | collective-permute-start | bytes 294920 | tf_op jit(solution)/shard_map/ppermute | solution.py:247
  24.8 0.8 %collective-permute-done.7.refs_1_ = bf16[4,32,384]{2,1,0:T(8,128)(2,1)S(1)} collective-permute-done((bf16[4,32,384]{2,1,0:T(8,128)(2,1)S(1)}, bf16[4,32,384]{2,1,0:T(8,128)(2,1)S(1)}, u32[]{:S(2)}, u32[]{:S(2)}) %collective-permute-start.7) | collective-permute-done | bytes 98336 | tf_op jit(solution)/shard_map/ppermute | solution.py:247
  25.7 2.7 %collective-permute-done.8.refs_2_ = bf16[4,32,384]{2,1,0:T(8,128)(2,1)S(1)} collective-permute-done((bf16[4,32,384]{2,1,0:T(8,128)(2,1)S(1)}, bf16[4,32,384]{2,1,0:T(8,128)(2,1)S(1)}, u32[]{:S(2)}, u32[]{:S(2)}) %collective-permute-start.8) | collective-permute-done | bytes 98336 | tf_op jit(solution)/shard_map/ppermute | solution.py:247
  28.5 1.1 %collective-permute-done.9.refs_3_ = bf16[4,32,384]{2,1,0:T(8,128)(2,1)S(1)} collective-permute-done((bf16[4,32,384]{2,1,0:T(8,128)(2,1)S(1)}, bf16[4,32,384]{2,1,0:T(8,128)(2,1)S(1)}, u32[]{:S(2)}, u32[]{:S(2)}) %collective-permute-start.9) | collective-permute-done | bytes 98336 | tf_op jit(solution)/shard_map/ppermute | solution.py:247
  30.9 1.2 %far_columns.1 = (bf16[4,128,360]{2,1,0:T(8,128)(2,1)S(1)}, bf16[128,180]{1,0:T(8,128)(2,1)S(1)}, bf16[128,1536]{1,0:T(8,128)(2,1)S(1)}) custom-call(f32[1,2880]{1,0:T(1,128)S(1)} %reshape.6.gain_ref, bf16[180,2880]{1,0:T(8,128)(2,1)S(1)} %bitcast.18, bf16[180,2880]{1,0:T(8,128)(2,1)S(1)} %bitcast.20, bf16[180,2880]{1,0:T(8,128)(2,1)S(1)} %bitcast.21, ...), custom_call_target="tpu_custom_call" | custom-call | tf_op jit(solution)/shard_map/far_columns/pallas_call | solution.py:573
  32.9 1.0 %collective-permute-done.14.come_ref = bf16[4,128,360]{2,1,0:T(8,128)(2,1)S(1)} collective-permute-done((bf16[4,128,360]{2,1,0:T(8,128)(2,1)S(1)}, bf16[4,128,360]{2,1,0:T(8,128)(2,1)S(1)}, u32[]{:S(2)}, u32[]{:S(2)}) %collective-permute-start.14) | collective-permute-done | bytes 368672 | tf_op jit(solution)/shard_map/ppermute | solution.py:224
  34.1 1.8 %collective-permute-start.19 = (bf16[64,360]{1,0:T(8,128)(2,1)S(1)}, bf16[64,360]{1,0:T(8,128)(2,1)S(1)}, u32[]{:S(2)}, u32[]{:S(2)}) collective-permute-start(bf16[64,360]{1,0:T(8,128)(2,1)S(1)} %get-tuple-element.55), channel_id=1, source_target_pairs={{0,3},{1,2},{2,1},{3,0},{4,7},{5,6},{6,5},{7,4},{8,11},{9,10},{10,... | collective-permute-start | bytes 138248 | tf_op jit(solution)/shard_map/ppermute | solution.py:247
  35.9 1.1 %collective-permute-start.20 = (bf16[64,360]{1,0:T(8,128)(2,1)S(1)}, bf16[64,360]{1,0:T(8,128)(2,1)S(1)}, u32[]{:S(2)}, u32[]{:S(2)}) collective-permute-start(bf16[64,360]{1,0:T(8,128)(2,1)S(1)} %get-tuple-element.56), channel_id=1, source_target_pairs={{0,18},{1,16},{2,19},{3,17},{4,22},{5,20},{6,23},{7,21},{8,26},{9,... | collective-permute-start | bytes 138248 | tf_op jit(solution)/shard_map/ppermute | solution.py:247
  37.3 1.7 %collective-permute-start.16 = (bf16[64,360]{1,0:T(8,128)(2,1)S(1)}, bf16[64,360]{1,0:T(8,128)(2,1)S(1)}, u32[]{:S(2)}, u32[]{:S(2)}) collective-permute-start(bf16[64,360]{1,0:T(8,128)(2,1)S(1)} %get-tuple-element.51), channel_id=1, source_target_pairs={{0,3},{1,2},{2,1},{3,0},{4,7},{5,6},{6,5},{7,4},{8,11},{9,10},{10,... | collective-permute-start | bytes 138248 | tf_op jit(solution)/shard_map/ppermute | solution.py:247
  39.1 0.8 %collective-permute-start.17 = (bf16[64,360]{1,0:T(8,128)(2,1)S(1)}, bf16[64,360]{1,0:T(8,128)(2,1)S(1)}, u32[]{:S(2)}, u32[]{:S(2)}) collective-permute-start(bf16[64,360]{1,0:T(8,128)(2,1)S(1)} %get-tuple-element.52), channel_id=1, source_target_pairs={{0,18},{1,16},{2,19},{3,17},{4,22},{5,20},{6,23},{7,21},{8,26},{9,... | collective-permute-start | bytes 138248 | tf_op jit(solution)/shard_map/ppermute | solution.py:247
  40.0 1.6 %collective-permute-start.21 = (bf16[32,360]{1,0:T(8,128)(2,1)S(1)}, bf16[32,360]{1,0:T(8,128)(2,1)S(1)}, u32[]{:S(2)}, u32[]{:S(2)}) collective-permute-start(bf16[32,360]{1,0:T(8,128)(2,1)S(1)} %get-tuple-element.57), channel_id=1, source_target_pairs={{0,12},{4,8},{8,4},{12,0},{1,13},{5,9},{9,5},{13,1},{2,14},{6,10},... | collective-permute-start | bytes 69128 | tf_op jit(solution)/shard_map/ppermute | solution.py:224
  42.9 1.6 %collective-permute-start.23 = (bf16[32,360]{1,0:T(8,128)(2,1)S(1)}, bf16[32,360]{1,0:T(8,128)(2,1)S(1)}, u32[]{:S(2)}, u32[]{:S(2)}) collective-permute-start(bf16[32,360]{1,0:T(8,128)(2,1)S(1)} %get-tuple-element.59), channel_id=1, source_target_pairs={{0,4},{4,0},{8,12},{12,8},{1,5},{5,1},{9,13},{13,9},{2,6},{6,2},{1... | collective-permute-start | bytes 69128 | tf_op jit(solution)/shard_map/ppermute | solution.py:224
  44.5 1.2 %collective-permute-done.21.refs_1_ = bf16[32,360]{1,0:T(8,128)(2,1)S(1)} collective-permute-done((bf16[32,360]{1,0:T(8,128)(2,1)S(1)}, bf16[32,360]{1,0:T(8,128)(2,1)S(1)}, u32[]{:S(2)}, u32[]{:S(2)}) %collective-permute-start.21) | collective-permute-done | bytes 23072 | tf_op jit(solution)/shard_map/ppermute | solution.py:224
  45.7 1.0 %collective-permute-done.22.refs_2_ = bf16[32,360]{1,0:T(8,128)(2,1)S(1)} collective-permute-done((bf16[32,360]{1,0:T(8,128)(2,1)S(1)}, bf16[32,360]{1,0:T(8,128)(2,1)S(1)}, u32[]{:S(2)}, u32[]{:S(2)}) %collective-permute-start.22) | collective-permute-done | bytes 23072 | tf_op jit(solution)/shard_map/ppermute | solution.py:224
  46.8 0.6 %combine.1 = bf16[2,16,360]{2,1,0:T(8,128)(2,1)} custom-call(f32[32,360]{1,0:T(8,128)S(1)} %get-tuple-element.53.refs_0_, bf16[32,360]{1,0:T(8,128)(2,1)S(1)} %collective-permute-done.21.refs_1_, bf16[32,360]{1,0:T(8,128)(2,1)S(1)} %collective-permute-done.22.refs_2_, bf16[32,360]{1,0:T(8,128)(2,1)S(1)} %collective-permute-done.23.refs_3_, ...), custom_call_target="tpu_custom_call" | custom-call | bytes 184320 | tf_op jit(solution)/shard_map/combine/pallas_call | solution.py:437
  (45 shorter events, 6.8 us)
Async XLA Ops:
  4.3 1.5 %collective-permute-start = (bf16[4,32,384]{2,1,0:T(8,128)(2,1)S(1)}, bf16[4,32,384]{2,1,0:T(8,128)(2,1)S(1)}, u32[]{:S(2)}, u32[]{:S(2)}) collective-permute-start(bf16[4,32,384]{2,1,0:T(8,128)(2,1)S(1)} %get-tuple-element.35), channel_id=1, source_target_pairs={{0,16},{16,0},{1,17},{17,1},{2,18},{18,2},{3,19},{19,3},{4,20},{20... | collective-permute-start | bytes 294920 | tf_op jit(solution)/shard_map/ppermute | solution.py:224
  5.8 4.2 %collective-permute-start.1 = (bf16[32,384]{1,0:T(8,128)(2,1)S(1)}, bf16[32,384]{1,0:T(8,128)(2,1)S(1)}, u32[]{:S(2)}, u32[]{:S(2)}) collective-permute-start(bf16[32,384]{1,0:T(8,128)(2,1)S(1)} %get-tuple-element.37), channel_id=1, source_target_pairs={{0,17},{1,19},{2,16},{3,18},{4,22},{5,20},{6,23},{7,21},{8,25},{9,... | collective-permute-start | bytes 73736 | tf_op jit(solution)/shard_map/ppermute | solution.py:247
  8.5 4.9 %collective-permute-start.2 = (bf16[32,384]{1,0:T(8,128)(2,1)S(1)}, bf16[32,384]{1,0:T(8,128)(2,1)S(1)}, u32[]{:S(2)}, u32[]{:S(2)}) collective-permute-start(bf16[32,384]{1,0:T(8,128)(2,1)S(1)} %get-tuple-element.38), channel_id=1, source_target_pairs={{0,3},{1,2},{2,1},{3,0},{4,7},{5,6},{6,5},{7,4},{8,11},{9,10},{10,... | collective-permute-start | bytes 73736 | tf_op jit(solution)/shard_map/ppermute | solution.py:247
  10.0 3.5 %collective-permute-start.3 = (bf16[32,384]{1,0:T(8,128)(2,1)S(1)}, bf16[32,384]{1,0:T(8,128)(2,1)S(1)}, u32[]{:S(2)}, u32[]{:S(2)}) collective-permute-start(bf16[32,384]{1,0:T(8,128)(2,1)S(1)} %get-tuple-element.39), channel_id=1, source_target_pairs={{0,18},{1,16},{2,19},{3,17},{4,21},{5,23},{6,20},{7,22},{8,26},{9,... | collective-permute-start | bytes 73736 | tf_op jit(solution)/shard_map/ppermute | solution.py:247
  13.5 5.1 %collective-permute-start.4 = (bf16[32,384]{1,0:T(8,128)(2,1)S(1)}, bf16[32,384]{1,0:T(8,128)(2,1)S(1)}, u32[]{:S(2)}, u32[]{:S(2)}) collective-permute-start(bf16[32,384]{1,0:T(8,128)(2,1)S(1)} %sum.1), channel_id=1, source_target_pairs={{0,28},{1,29},{2,30},{3,31},{4,24},{5,25},{6,26},{7,27},{8,20},{9,... | collective-permute-start | bytes 73736 | tf_op jit(solution)/shard_map/ppermute | solution.py:247
  16.8 4.7 %collective-permute-start.5 = (bf16[32,384]{1,0:T(8,128)(2,1)S(1)}, bf16[32,384]{1,0:T(8,128)(2,1)S(1)}, u32[]{:S(2)}, u32[]{:S(2)}) collective-permute-start(bf16[32,384]{1,0:T(8,128)(2,1)S(1)} %sum.1), channel_id=1, source_target_pairs={{0,8},{1,9},{2,10},{3,11},{4,12},{5,13},{6,14},{7,15},{8,0},{9,1},... | collective-permute-start | bytes 73736 | tf_op jit(solution)/shard_map/ppermute | solution.py:247
  16.8 4.7 %collective-permute-start.6 = (bf16[32,384]{1,0:T(8,128)(2,1)S(1)}, bf16[32,384]{1,0:T(8,128)(2,1)S(1)}, u32[]{:S(2)}, u32[]{:S(2)}) collective-permute-start(bf16[32,384]{1,0:T(8,128)(2,1)S(1)} %sum.1), channel_id=1, source_target_pairs={{0,20},{1,21},{2,22},{3,23},{4,16},{5,17},{6,18},{7,19},{8,28},{9,... | collective-permute-start | bytes 73736 | tf_op jit(solution)/shard_map/ppermute | solution.py:247
  21.5 4.1 %collective-permute-start.7 = (bf16[4,32,384]{2,1,0:T(8,128)(2,1)S(1)}, bf16[4,32,384]{2,1,0:T(8,128)(2,1)S(1)}, u32[]{:S(2)}, u32[]{:S(2)}) collective-permute-start(bf16[4,32,384]{2,1,0:T(8,128)(2,1)S(1)} %pad_maximum_fusion.refs_0_), channel_id=1, source_target_pairs={{0,17},{1,19},{2,16},{3,18},{4,22},{5,20},{6,23},{7,21},{8,25},{9,... | collective-permute-start | bytes 294920 | tf_op jit(solution)/shard_map/ppermute | solution.py:247
  22.0 6.4 %collective-permute-start.8 = (bf16[4,32,384]{2,1,0:T(8,128)(2,1)S(1)}, bf16[4,32,384]{2,1,0:T(8,128)(2,1)S(1)}, u32[]{:S(2)}, u32[]{:S(2)}) collective-permute-start(bf16[4,32,384]{2,1,0:T(8,128)(2,1)S(1)} %pad_maximum_fusion.refs_0_), channel_id=1, source_target_pairs={{0,3},{1,2},{2,1},{3,0},{4,7},{5,6},{6,5},{7,4},{8,11},{9,10},{10,... | collective-permute-start | bytes 294920 | tf_op jit(solution)/shard_map/ppermute | solution.py:247
  23.5 6.1 %collective-permute-start.9 = (bf16[4,32,384]{2,1,0:T(8,128)(2,1)S(1)}, bf16[4,32,384]{2,1,0:T(8,128)(2,1)S(1)}, u32[]{:S(2)}, u32[]{:S(2)}) collective-permute-start(bf16[4,32,384]{2,1,0:T(8,128)(2,1)S(1)} %pad_maximum_fusion.refs_0_), channel_id=1, source_target_pairs={{0,18},{1,16},{2,19},{3,17},{4,21},{5,23},{6,20},{7,22},{8,26},{9,... | collective-permute-start | bytes 294920 | tf_op jit(solution)/shard_map/ppermute | solution.py:247
  24.5 5.8 %collective-permute-start.10 = (bf16[4,32,384]{2,1,0:T(8,128)(2,1)S(1)}, bf16[4,32,384]{2,1,0:T(8,128)(2,1)S(1)}, u32[]{:S(2)}, u32[]{:S(2)}) collective-permute-start(bf16[4,32,384]{2,1,0:T(8,128)(2,1)S(1)} %pad_maximum_fusion.refs_0_), channel_id=1, source_target_pairs={{0,16},{16,0},{1,17},{17,1},{2,18},{18,2},{3,19},{19,3},{4,20},{20... | collective-permute-start | bytes 294920 | tf_op jit(solution)/shard_map/ppermute | solution.py:224
  25.6 4.7 %collective-permute-start.11 = (bf16[4,32,384]{2,1,0:T(8,128)(2,1)S(1)}, bf16[4,32,384]{2,1,0:T(8,128)(2,1)S(1)}, u32[]{:S(2)}, u32[]{:S(2)}) collective-permute-start(bf16[4,32,384]{2,1,0:T(8,128)(2,1)S(1)} %collective-permute-done.7.refs_1_), channel_id=1, source_target_pairs={{0,16},{16,0},{1,17},{17,1},{2,18},{18,2},{3,19},{19,3},{4,20},{20... | collective-permute-start | bytes 294920 | tf_op jit(solution)/shard_map/ppermute | solution.py:224
  28.4 1.9 %collective-permute-start.12 = (bf16[4,32,384]{2,1,0:T(8,128)(2,1)S(1)}, bf16[4,32,384]{2,1,0:T(8,128)(2,1)S(1)}, u32[]{:S(2)}, u32[]{:S(2)}) collective-permute-start(bf16[4,32,384]{2,1,0:T(8,128)(2,1)S(1)} %collective-permute-done.8.refs_2_), channel_id=1, source_target_pairs={{0,16},{16,0},{1,17},{17,1},{2,18},{18,2},{3,19},{19,3},{4,20},{20... | collective-permute-start | bytes 294920 | tf_op jit(solution)/shard_map/ppermute | solution.py:224
  29.6 1.3 %collective-permute-start.13 = (bf16[4,32,384]{2,1,0:T(8,128)(2,1)S(1)}, bf16[4,32,384]{2,1,0:T(8,128)(2,1)S(1)}, u32[]{:S(2)}, u32[]{:S(2)}) collective-permute-start(bf16[4,32,384]{2,1,0:T(8,128)(2,1)S(1)} %collective-permute-done.9.refs_3_), channel_id=1, source_target_pairs={{0,16},{16,0},{1,17},{17,1},{2,18},{18,2},{3,19},{19,3},{4,20},{20... | collective-permute-start | bytes 294920 | tf_op jit(solution)/shard_map/ppermute | solution.py:224
  32.1 1.8 %collective-permute-start.14 = (bf16[4,128,360]{2,1,0:T(8,128)(2,1)S(1)}, bf16[4,128,360]{2,1,0:T(8,128)(2,1)S(1)}, u32[]{:S(2)}, u32[]{:S(2)}) collective-permute-start(bf16[4,128,360]{2,1,0:T(8,128)(2,1)S(1)} %get-tuple-element.48), channel_id=1, source_target_pairs={{0,16},{16,0},{1,17},{17,1},{2,18},{18,2},{3,19},{19,3},{4,20},{20... | collective-permute-start | bytes 1105928 | tf_op jit(solution)/shard_map/ppermute | solution.py:224
  34.0 5.1 %collective-permute-start.18 = (bf16[64,360]{1,0:T(8,128)(2,1)S(1)}, bf16[64,360]{1,0:T(8,128)(2,1)S(1)}, u32[]{:S(2)}, u32[]{:S(2)}) collective-permute-start(bf16[64,360]{1,0:T(8,128)(2,1)S(1)} %get-tuple-element.54), channel_id=1, source_target_pairs={{0,17},{1,19},{2,16},{3,18},{4,21},{5,23},{6,20},{7,22},{8,25},{9,... | collective-permute-start | bytes 138248 | tf_op jit(solution)/shard_map/ppermute | solution.py:247
  34.1 5.9 %collective-permute-start.19 = (bf16[64,360]{1,0:T(8,128)(2,1)S(1)}, bf16[64,360]{1,0:T(8,128)(2,1)S(1)}, u32[]{:S(2)}, u32[]{:S(2)}) collective-permute-start(bf16[64,360]{1,0:T(8,128)(2,1)S(1)} %get-tuple-element.55), channel_id=1, source_target_pairs={{0,3},{1,2},{2,1},{3,0},{4,7},{5,6},{6,5},{7,4},{8,11},{9,10},{10,... | collective-permute-start | bytes 138248 | tf_op jit(solution)/shard_map/ppermute | solution.py:247
  35.9 4.0 %collective-permute-start.20 = (bf16[64,360]{1,0:T(8,128)(2,1)S(1)}, bf16[64,360]{1,0:T(8,128)(2,1)S(1)}, u32[]{:S(2)}, u32[]{:S(2)}) collective-permute-start(bf16[64,360]{1,0:T(8,128)(2,1)S(1)} %get-tuple-element.56), channel_id=1, source_target_pairs={{0,18},{1,16},{2,19},{3,17},{4,22},{5,20},{6,23},{7,21},{8,26},{9,... | collective-permute-start | bytes 138248 | tf_op jit(solution)/shard_map/ppermute | solution.py:247
  37.0 5.0 %collective-permute-start.15 = (bf16[64,360]{1,0:T(8,128)(2,1)S(1)}, bf16[64,360]{1,0:T(8,128)(2,1)S(1)}, u32[]{:S(2)}, u32[]{:S(2)}) collective-permute-start(bf16[64,360]{1,0:T(8,128)(2,1)S(1)} %get-tuple-element.50), channel_id=1, source_target_pairs={{0,17},{1,19},{2,16},{3,18},{4,21},{5,23},{6,20},{7,22},{8,25},{9,... | collective-permute-start | bytes 138248 | tf_op jit(solution)/shard_map/ppermute | solution.py:247
  37.3 5.0 %collective-permute-start.16 = (bf16[64,360]{1,0:T(8,128)(2,1)S(1)}, bf16[64,360]{1,0:T(8,128)(2,1)S(1)}, u32[]{:S(2)}, u32[]{:S(2)}) collective-permute-start(bf16[64,360]{1,0:T(8,128)(2,1)S(1)} %get-tuple-element.51), channel_id=1, source_target_pairs={{0,3},{1,2},{2,1},{3,0},{4,7},{5,6},{6,5},{7,4},{8,11},{9,10},{10,... | collective-permute-start | bytes 138248 | tf_op jit(solution)/shard_map/ppermute | solution.py:247
  39.1 3.8 %collective-permute-start.17 = (bf16[64,360]{1,0:T(8,128)(2,1)S(1)}, bf16[64,360]{1,0:T(8,128)(2,1)S(1)}, u32[]{:S(2)}, u32[]{:S(2)}) collective-permute-start(bf16[64,360]{1,0:T(8,128)(2,1)S(1)} %get-tuple-element.52), channel_id=1, source_target_pairs={{0,18},{1,16},{2,19},{3,17},{4,22},{5,20},{6,23},{7,21},{8,26},{9,... | collective-permute-start | bytes 138248 | tf_op jit(solution)/shard_map/ppermute | solution.py:247
  40.0 5.7 %collective-permute-start.21 = (bf16[32,360]{1,0:T(8,128)(2,1)S(1)}, bf16[32,360]{1,0:T(8,128)(2,1)S(1)}, u32[]{:S(2)}, u32[]{:S(2)}) collective-permute-start(bf16[32,360]{1,0:T(8,128)(2,1)S(1)} %get-tuple-element.57), channel_id=1, source_target_pairs={{0,12},{4,8},{8,4},{12,0},{1,13},{5,9},{9,5},{13,1},{2,14},{6,10},... | collective-permute-start | bytes 69128 | tf_op jit(solution)/shard_map/ppermute | solution.py:224
  41.6 5.1 %collective-permute-start.22 = (bf16[32,360]{1,0:T(8,128)(2,1)S(1)}, bf16[32,360]{1,0:T(8,128)(2,1)S(1)}, u32[]{:S(2)}, u32[]{:S(2)}) collective-permute-start(bf16[32,360]{1,0:T(8,128)(2,1)S(1)} %get-tuple-element.58), channel_id=1, source_target_pairs={{0,8},{4,12},{8,0},{12,4},{1,9},{5,13},{9,1},{13,5},{2,10},{6,14},... | collective-permute-start | bytes 69128 | tf_op jit(solution)/shard_map/ppermute | solution.py:224
  42.9 3.9 %collective-permute-start.23 = (bf16[32,360]{1,0:T(8,128)(2,1)S(1)}, bf16[32,360]{1,0:T(8,128)(2,1)S(1)}, u32[]{:S(2)}, u32[]{:S(2)}) collective-permute-start(bf16[32,360]{1,0:T(8,128)(2,1)S(1)} %get-tuple-element.59), channel_id=1, source_target_pairs={{0,4},{4,0},{8,12},{12,8},{1,5},{5,1},{9,13},{13,9},{2,6},{6,2},{1... | collective-permute-start | bytes 69128 | tf_op jit(solution)/shard_map/ppermute | solution.py:224
  (4 other events, 102.3 us)

commit v17 on v14

--- a/solution.py
+++ b/solution.py
@@ -615,10 +615,10 @@
     far_come, near_come = shard_swaps(parts[:3], False), shard_swaps(parts[3:], False)
     third, second = call(functools.partial(sum_rows_kernel, line=0), "sum_far_rows", [shape_of((lines, part))] * 2,
                          own, *far_come)
-    third, second = swap(third, "grp", 3), swap(second, "grp", 2)
+    second, third = swap(second, "grp", 2), swap(third, "grp", 3)
     nearest, own = call(functools.partial(sum_rows_kernel, line=2 * lines), "sum_near_rows",
                         [shape_of((lines, part)), shape_of((lines, part), jnp.float32)], own, *near_come)
-    return call(sum_kernel, "combine", shape_of((steps, rows, part)), own, third, second, swap(nearest, "grp", 1), own_middle)
+    return call(sum_kernel, "combine", shape_of((steps, rows, part)), own, second, third, swap(nearest, "grp", 1), own_middle)
 
 
 def body(*args):

time: 47.4 us -> 48.6 us (1.025)
  waiting for transfers between devices: 15.3 us -> 17.2 us
  starting transfers between devices: 23.9 us -> 23.1 us
    ppermute x9, waiting for transfers between devices: 4.06 us -> 6.13 us  [swap(): return lax.ppermute(value, axes, [(i, i ^ mask) for i in range(size)])]
    ppermute x9, starting transfers between devices: 5.96 us -> 5.22 us  [swap(): return lax.ppermute(value, axes, [(i, i ^ mask) for i in range(size)])]
  transfers between devices with their start and end apart: 24 -> 24, of which waited for: 15 -> 13; matrix products, arithmetic and copies ran while one was open for 0% -> 0% of each run, Pallas kernels for 4% -> 4%
where the time goes in v17:
time: 48.6 us; the launch traced here: 48.5 us
  starting transfers between devices  23.1 us (48%)
  waiting for transfers between devices  17.2 us (35%)
  Pallas kernels  7.95 us (16%)
    ppermute x15, starting transfers between devices, lane_swap(): return lax.ppermute(value, ('sec', 'grp', 'tp'), pairs)  17.9 us
    ppermute x15, waiting for transfers between devices, lane_swap(): return lax.ppermute(value, ('sec', 'grp', 'tp'), pairs)  11.1 us
    ppermute x9, waiting for transfers between devices, swap(): return lax.ppermute(value, axes, [(i, i ^ mask) for i in range(size)])  6.13 us
    ppermute x9, starting transfers between devices, swap(): return lax.ppermute(value, axes, [(i, i ^ mask) for i in range(size)])  5.22 us
    pallas_call x1, Pallas kernels, attention_partial(): pl.pallas_call(attention_kernel, name='attention', out_shape=[shape_of((t...  4.24 us
    pallas_call x8, Pallas kernels, call(): pl.pallas_call(kernel, name=name, out_shape=outs, in_specs=[vmem()] * len...  1.96 us
    pallas_call x1, Pallas kernels, experts(): pl.pallas_call(far_kernel, name='far_columns', out_shape=[shape_of((tps,...  1.17 us
  transfers between devices with their start and end apart: 24, of which 13 were waited for; matrix products, arithmetic and copies ran while one was open for 0% of the time, Pallas kernels for 4%

profile of v17, /device:TPU:0, one launch (start us, length us, event | category | flops | bytes accessed | tf_op | source)
XLA Modules:
  0.0 48.5 jit_solution(6134592068326439516)
XLA Ops:
  0.0 4.2 %attention.1 = (bf16[4,32,384]{2,1,0:T(8,128)(2,1)S(1)}, f32[32,384]{1,0:T(8,128)S(1)}, bf16[32,512]{1,0:T(8,128)(2,1)S(1)}, bf16[2880,512]{1,0:T(8,128)(2,1)S(1)}) custom-call(s32[16]{0:T(128)} %lengths_hbm.1, f32[8]{0:T(128)} %sinks_hbm.1, s32[2,4,16]{2,1,0:T(4,128)} %bitcast.31, f32[2,4,16]{2,1,0:T(4,128)} %bitcast.32, f32[2880]{0:T(1024)} %gain_hbm.1, ...), custom_call_target="tpu_custom_call" | custom-call | tf_op jit(solution)/shard_map/attention/pallas_call | solution.py:408
  5.8 3.8 %collective-permute-start.1 = (bf16[32,384]{1,0:T(8,128)(2,1)S(1)}, bf16[32,384]{1,0:T(8,128)(2,1)S(1)}, u32[]{:S(2)}, u32[]{:S(2)}) collective-permute-start(bf16[32,384]{1,0:T(8,128)(2,1)S(1)} %get-tuple-element.37), channel_id=1, source_target_pairs={{0,3},{1,2},{2,1},{3,0},{4,7},{5,6},{6,5},{7,4},{8,11},{9,10},{10,... | collective-permute-start | bytes 73736 | tf_op jit(solution)/shard_map/ppermute | solution.py:247
  10.0 1.4 %collective-permute-done.1.refs_1_ = bf16[32,384]{1,0:T(8,128)(2,1)S(1)} collective-permute-done((bf16[32,384]{1,0:T(8,128)(2,1)S(1)}, bf16[32,384]{1,0:T(8,128)(2,1)S(1)}, u32[]{:S(2)}, u32[]{:S(2)}) %collective-permute-start.1) | collective-permute-done | bytes 24608 | tf_op jit(solution)/shard_map/ppermute | solution.py:247
  11.4 1.4 %collective-permute-done.2.refs_2_ = bf16[32,384]{1,0:T(8,128)(2,1)S(1)} collective-permute-done((bf16[32,384]{1,0:T(8,128)(2,1)S(1)}, bf16[32,384]{1,0:T(8,128)(2,1)S(1)}, u32[]{:S(2)}, u32[]{:S(2)}) %collective-permute-start.2) | collective-permute-done | bytes 24608 | tf_op jit(solution)/shard_map/ppermute | solution.py:247
  13.2 3.6 %collective-permute-start.4 = (bf16[32,384]{1,0:T(8,128)(2,1)S(1)}, bf16[32,384]{1,0:T(8,128)(2,1)S(1)}, u32[]{:S(2)}, u32[]{:S(2)}) collective-permute-start(bf16[32,384]{1,0:T(8,128)(2,1)S(1)} %sum.1), channel_id=1, source_target_pairs={{0,28},{1,29},{2,30},{3,31},{4,24},{5,25},{6,26},{7,27},{8,20},{9,... | collective-permute-start | bytes 73736 | tf_op jit(solution)/shard_map/ppermute | solution.py:247
  17.2 1.2 %collective-permute-done.4 = bf16[32,384]{1,0:T(8,128)(2,1)S(1)} collective-permute-done((bf16[32,384]{1,0:T(8,128)(2,1)S(1)}, bf16[32,384]{1,0:T(8,128)(2,1)S(1)}, u32[]{:S(2)}, u32[]{:S(2)}) %collective-permute-start.4) | collective-permute-done | bytes 24608 | tf_op jit(solution)/shard_map/ppermute | solution.py:247
  18.4 3.2 %collective-permute-done.5 = bf16[32,384]{1,0:T(8,128)(2,1)S(1)} collective-permute-done((bf16[32,384]{1,0:T(8,128)(2,1)S(1)}, bf16[32,384]{1,0:T(8,128)(2,1)S(1)}, u32[]{:S(2)}, u32[]{:S(2)}) %collective-permute-start.5) | collective-permute-done | bytes 24608 | tf_op jit(solution)/shard_map/ppermute | solution.py:247
  21.6 1.5 %collective-permute-start.7 = (bf16[4,32,384]{2,1,0:T(8,128)(2,1)S(1)}, bf16[4,32,384]{2,1,0:T(8,128)(2,1)S(1)}, u32[]{:S(2)}, u32[]{:S(2)}) collective-permute-start(bf16[4,32,384]{2,1,0:T(8,128)(2,1)S(1)} %pad_maximum_fusion.refs_0_), channel_id=1, source_target_pairs={{0,3},{1,2},{2,1},{3,0},{4,7},{5,6},{6,5},{7,4},{8,11},{9,10},{10,... | collective-permute-start | bytes 294920 | tf_op jit(solution)/shard_map/ppermute | solution.py:247
  23.1 1.8 %collective-permute-start.9 = (bf16[4,32,384]{2,1,0:T(8,128)(2,1)S(1)}, bf16[4,32,384]{2,1,0:T(8,128)(2,1)S(1)}, u32[]{:S(2)}, u32[]{:S(2)}) collective-permute-start(bf16[4,32,384]{2,1,0:T(8,128)(2,1)S(1)} %pad_maximum_fusion.refs_0_), channel_id=1, source_target_pairs={{0,18},{1,16},{2,19},{3,17},{4,21},{5,23},{6,20},{7,22},{8,26},{9,... | collective-permute-start | bytes 294920 | tf_op jit(solution)/shard_map/ppermute | solution.py:247
  24.9 2.4 %collective-permute-done.7.refs_1_ = bf16[4,32,384]{2,1,0:T(8,128)(2,1)S(1)} collective-permute-done((bf16[4,32,384]{2,1,0:T(8,128)(2,1)S(1)}, bf16[4,32,384]{2,1,0:T(8,128)(2,1)S(1)}, u32[]{:S(2)}, u32[]{:S(2)}) %collective-permute-start.7) | collective-permute-done | bytes 98336 | tf_op jit(solution)/shard_map/ppermute | solution.py:247
  27.3 0.8 %collective-permute-done.8.refs_2_ = bf16[4,32,384]{2,1,0:T(8,128)(2,1)S(1)} collective-permute-done((bf16[4,32,384]{2,1,0:T(8,128)(2,1)S(1)}, bf16[4,32,384]{2,1,0:T(8,128)(2,1)S(1)}, u32[]{:S(2)}, u32[]{:S(2)}) %collective-permute-start.8) | collective-permute-done | bytes 98336 | tf_op jit(solution)/shard_map/ppermute | solution.py:247
  29.1 0.6 %near_columns.1 = (bf16[128,1536]{1,0:T(8,128)(2,1)S(1)}, f32[128,180]{1,0:T(8,128)S(1)}, f32[128,180]{1,0:T(8,128)S(1)}, f32[128,128]{1,0:T(8,128)S(1)}) custom-call(f32[1,2880]{1,0:T(1,128)S(1)} %reshape.6.gain_ref, bf16[180,2880]{1,0:T(8,128)(2,1)S(1)} %bitcast.17, bf16[180,2880]{1,0:T(8,128)(2,1)S(1)} %bitcast.19, ...), custom_call_target="tpu_custom_call" | custom-call | flops 132710400 | bytes 3121408 | tf_op jit(solution)/shard_map/near_columns/pallas_call | solution.py:437
  30.1 1.2 %far_columns.1 = (bf16[4,128,360]{2,1,0:T(8,128)(2,1)S(1)}, bf16[128,180]{1,0:T(8,128)(2,1)S(1)}, bf16[128,1536]{1,0:T(8,128)(2,1)S(1)}) custom-call(f32[1,2880]{1,0:T(1,128)S(1)} %reshape.6.gain_ref, bf16[180,2880]{1,0:T(8,128)(2,1)S(1)} %bitcast.18, bf16[180,2880]{1,0:T(8,128)(2,1)S(1)} %bitcast.20, bf16[180,2880]{1,0:T(8,128)(2,1)S(1)} %bitcast.21, ...), custom_call_target="tpu_custom_call" | custom-call | tf_op jit(solution)/shard_map/far_columns/pallas_call | solution.py:573
  31.6 0.6 %own_columns.1 = (f32[4,128,360]{2,1,0:T(8,128)S(1)}, f32[32,360]{1,0:T(8,128)S(1)}) custom-call(bf16[128,180]{1,0:T(8,128)(2,1)S(1)} %get-tuple-element.45.act_ref, bf16[180,2880]{1,0:T(8,128)(2,1)S(1)} %bitcast.22, bf16[128,1536]{1,0:T(8,128)(2,1)S(1)} %get-tuple-element.41.near_x_ref, bf16[128,1536]{1,0:T(8,128)(2,1)S(1)} %get-tuple-element.46.far_x_ref), custom_call_target="tpu_custom_call" | custom-call | flops 66355200 | bytes 737280 | tf_op jit(solution)/shard_map/own_columns/pallas_call | solution.py:583
  32.2 0.9 %collective-permute-done.14.come_ref = bf16[4,128,360]{2,1,0:T(8,128)(2,1)S(1)} collective-permute-done((bf16[4,128,360]{2,1,0:T(8,128)(2,1)S(1)}, bf16[4,128,360]{2,1,0:T(8,128)(2,1)S(1)}, u32[]{:S(2)}, u32[]{:S(2)}) %collective-permute-start.14) | collective-permute-done | bytes 368672 | tf_op jit(solution)/shard_map/ppermute | solution.py:224
  33.1 2.1 %collective-permute-start.18 = (bf16[64,360]{1,0:T(8,128)(2,1)S(1)}, bf16[64,360]{1,0:T(8,128)(2,1)S(1)}, u32[]{:S(2)}, u32[]{:S(2)}) collective-permute-start(bf16[64,360]{1,0:T(8,128)(2,1)S(1)} %get-tuple-element.54), channel_id=1, source_target_pairs={{0,3},{1,2},{2,1},{3,0},{4,7},{5,6},{6,5},{7,4},{8,11},{9,10},{10,... | collective-permute-start | bytes 138248 | tf_op jit(solution)/shard_map/ppermute | solution.py:247
  35.6 0.8 %collective-permute-start.20 = (bf16[64,360]{1,0:T(8,128)(2,1)S(1)}, bf16[64,360]{1,0:T(8,128)(2,1)S(1)}, u32[]{:S(2)}, u32[]{:S(2)}) collective-permute-start(bf16[64,360]{1,0:T(8,128)(2,1)S(1)} %get-tuple-element.56), channel_id=1, source_target_pairs={{0,18},{1,16},{2,19},{3,17},{4,22},{5,20},{6,23},{7,21},{8,26},{9,... | collective-permute-start | bytes 138248 | tf_op jit(solution)/shard_map/ppermute | solution.py:247
  36.4 2.0 %collective-permute-start.15 = (bf16[64,360]{1,0:T(8,128)(2,1)S(1)}, bf16[64,360]{1,0:T(8,128)(2,1)S(1)}, u32[]{:S(2)}, u32[]{:S(2)}) collective-permute-start(bf16[64,360]{1,0:T(8,128)(2,1)S(1)} %get-tuple-element.50), channel_id=1, source_target_pairs={{0,3},{1,2},{2,1},{3,0},{4,7},{5,6},{6,5},{7,4},{8,11},{9,10},{10,... | collective-permute-start | bytes 138248 | tf_op jit(solution)/shard_map/ppermute | solution.py:247
  38.6 1.1 %collective-permute-start.17 = (bf16[64,360]{1,0:T(8,128)(2,1)S(1)}, bf16[64,360]{1,0:T(8,128)(2,1)S(1)}, u32[]{:S(2)}, u32[]{:S(2)}) collective-permute-start(bf16[64,360]{1,0:T(8,128)(2,1)S(1)} %get-tuple-element.52), channel_id=1, source_target_pairs={{0,18},{1,16},{2,19},{3,17},{4,22},{5,20},{6,23},{7,21},{8,26},{9,... | collective-permute-start | bytes 138248 | tf_op jit(solution)/shard_map/ppermute | solution.py:247
  39.7 2.5 %collective-permute-start.21 = (bf16[32,360]{1,0:T(8,128)(2,1)S(1)}, bf16[32,360]{1,0:T(8,128)(2,1)S(1)}, u32[]{:S(2)}, u32[]{:S(2)}) collective-permute-start(bf16[32,360]{1,0:T(8,128)(2,1)S(1)} %get-tuple-element.57), channel_id=1, source_target_pairs={{0,8},{4,12},{8,0},{12,4},{1,9},{5,13},{9,1},{13,5},{2,10},{6,14},... | collective-permute-start | bytes 69128 | tf_op jit(solution)/shard_map/ppermute | solution.py:224
  42.5 0.8 %collective-permute-start.23 = (bf16[32,360]{1,0:T(8,128)(2,1)S(1)}, bf16[32,360]{1,0:T(8,128)(2,1)S(1)}, u32[]{:S(2)}, u32[]{:S(2)}) collective-permute-start(bf16[32,360]{1,0:T(8,128)(2,1)S(1)} %get-tuple-element.59), channel_id=1, source_target_pairs={{0,4},{4,0},{8,12},{12,8},{1,5},{5,1},{9,13},{13,9},{2,6},{6,2},{1... | collective-permute-start | bytes 69128 | tf_op jit(solution)/shard_map/ppermute | solution.py:224
  43.3 1.5 %collective-permute-done.21.refs_1_ = bf16[32,360]{1,0:T(8,128)(2,1)S(1)} collective-permute-done((bf16[32,360]{1,0:T(8,128)(2,1)S(1)}, bf16[32,360]{1,0:T(8,128)(2,1)S(1)}, u32[]{:S(2)}, u32[]{:S(2)}) %collective-permute-start.21) | collective-permute-done | bytes 23072 | tf_op jit(solution)/shard_map/ppermute | solution.py:224
  44.8 3.0 %collective-permute-done.22.refs_2_ = bf16[32,360]{1,0:T(8,128)(2,1)S(1)} collective-permute-done((bf16[32,360]{1,0:T(8,128)(2,1)S(1)}, bf16[32,360]{1,0:T(8,128)(2,1)S(1)}, u32[]{:S(2)}, u32[]{:S(2)}) %collective-permute-start.22) | collective-permute-done | bytes 23072 | tf_op jit(solution)/shard_map/ppermute | solution.py:224
  47.8 0.6 %combine.1 = bf16[2,16,360]{2,1,0:T(8,128)(2,1)} custom-call(f32[32,360]{1,0:T(8,128)S(1)} %get-tuple-element.53.refs_0_, bf16[32,360]{1,0:T(8,128)(2,1)S(1)} %collective-permute-done.21.refs_1_, bf16[32,360]{1,0:T(8,128)(2,1)S(1)} %collective-permute-done.22.refs_2_, bf16[32,360]{1,0:T(8,128)(2,1)S(1)} %collective-permute-done.23.refs_3_, ...), custom_call_target="tpu_custom_call" | custom-call | bytes 184320 | tf_op jit(solution)/shard_map/combine/pallas_call | solution.py:437
  (45 shorter events, 5.3 us)
Async XLA Ops:
  4.3 1.5 %collective-permute-start = (bf16[4,32,384]{2,1,0:T(8,128)(2,1)S(1)}, bf16[4,32,384]{2,1,0:T(8,128)(2,1)S(1)}, u32[]{:S(2)}, u32[]{:S(2)}) collective-permute-start(bf16[4,32,384]{2,1,0:T(8,128)(2,1)S(1)} %get-tuple-element.35), channel_id=1, source_target_pairs={{0,16},{16,0},{1,17},{17,1},{2,18},{18,2},{3,19},{19,3},{4,20},{20... | collective-permute-start | bytes 294920 | tf_op jit(solution)/shard_map/ppermute | solution.py:224
  5.8 5.6 %collective-permute-start.1 = (bf16[32,384]{1,0:T(8,128)(2,1)S(1)}, bf16[32,384]{1,0:T(8,128)(2,1)S(1)}, u32[]{:S(2)}, u32[]{:S(2)}) collective-permute-start(bf16[32,384]{1,0:T(8,128)(2,1)S(1)} %get-tuple-element.37), channel_id=1, source_target_pairs={{0,3},{1,2},{2,1},{3,0},{4,7},{5,6},{6,5},{7,4},{8,11},{9,10},{10,... | collective-permute-start | bytes 73736 | tf_op jit(solution)/shard_map/ppermute | solution.py:247
  9.6 3.3 %collective-permute-start.2 = (bf16[32,384]{1,0:T(8,128)(2,1)S(1)}, bf16[32,384]{1,0:T(8,128)(2,1)S(1)}, u32[]{:S(2)}, u32[]{:S(2)}) collective-permute-start(bf16[32,384]{1,0:T(8,128)(2,1)S(1)} %get-tuple-element.38), channel_id=1, source_target_pairs={{0,17},{1,19},{2,16},{3,18},{4,22},{5,20},{6,23},{7,21},{8,25},{9,... | collective-permute-start | bytes 73736 | tf_op jit(solution)/shard_map/ppermute | solution.py:247
  9.7 3.5 %collective-permute-start.3 = (bf16[32,384]{1,0:T(8,128)(2,1)S(1)}, bf16[32,384]{1,0:T(8,128)(2,1)S(1)}, u32[]{:S(2)}, u32[]{:S(2)}) collective-permute-start(bf16[32,384]{1,0:T(8,128)(2,1)S(1)} %get-tuple-element.39), channel_id=1, source_target_pairs={{0,18},{1,16},{2,19},{3,17},{4,21},{5,23},{6,20},{7,22},{8,26},{9,... | collective-permute-start | bytes 73736 | tf_op jit(solution)/shard_map/ppermute | solution.py:247
  13.2 5.1 %collective-permute-start.4 = (bf16[32,384]{1,0:T(8,128)(2,1)S(1)}, bf16[32,384]{1,0:T(8,128)(2,1)S(1)}, u32[]{:S(2)}, u32[]{:S(2)}) collective-permute-start(bf16[32,384]{1,0:T(8,128)(2,1)S(1)} %sum.1), channel_id=1, source_target_pairs={{0,28},{1,29},{2,30},{3,31},{4,24},{5,25},{6,26},{7,27},{8,20},{9,... | collective-permute-start | bytes 73736 | tf_op jit(solution)/shard_map/ppermute | solution.py:247
  16.8 4.7 %collective-permute-start.5 = (bf16[32,384]{1,0:T(8,128)(2,1)S(1)}, bf16[32,384]{1,0:T(8,128)(2,1)S(1)}, u32[]{:S(2)}, u32[]{:S(2)}) collective-permute-start(bf16[32,384]{1,0:T(8,128)(2,1)S(1)} %sum.1), channel_id=1, source_target_pairs={{0,8},{1,9},{2,10},{3,11},{4,12},{5,13},{6,14},{7,15},{8,0},{9,1},... | collective-permute-start | bytes 73736 | tf_op jit(solution)/shard_map/ppermute | solution.py:247
  16.8 4.7 %collective-permute-start.6 = (bf16[32,384]{1,0:T(8,128)(2,1)S(1)}, bf16[32,384]{1,0:T(8,128)(2,1)S(1)}, u32[]{:S(2)}, u32[]{:S(2)}) collective-permute-start(bf16[32,384]{1,0:T(8,128)(2,1)S(1)} %sum.1), channel_id=1, source_target_pairs={{0,20},{1,21},{2,22},{3,23},{4,16},{5,17},{6,18},{7,19},{8,28},{9,... | collective-permute-start | bytes 73736 | tf_op jit(solution)/shard_map/ppermute | solution.py:247
  21.6 5.7 %collective-permute-start.7 = (bf16[4,32,384]{2,1,0:T(8,128)(2,1)S(1)}, bf16[4,32,384]{2,1,0:T(8,128)(2,1)S(1)}, u32[]{:S(2)}, u32[]{:S(2)}) collective-permute-start(bf16[4,32,384]{2,1,0:T(8,128)(2,1)S(1)} %pad_maximum_fusion.refs_0_), channel_id=1, source_target_pairs={{0,3},{1,2},{2,1},{3,0},{4,7},{5,6},{6,5},{7,4},{8,11},{9,10},{10,... | collective-permute-start | bytes 294920 | tf_op jit(solution)/shard_map/ppermute | solution.py:247
  23.1 5.0 %collective-permute-start.8 = (bf16[4,32,384]{2,1,0:T(8,128)(2,1)S(1)}, bf16[4,32,384]{2,1,0:T(8,128)(2,1)S(1)}, u32[]{:S(2)}, u32[]{:S(2)}) collective-permute-start(bf16[4,32,384]{2,1,0:T(8,128)(2,1)S(1)} %pad_maximum_fusion.refs_0_), channel_id=1, source_target_pairs={{0,17},{1,19},{2,16},{3,18},{4,22},{5,20},{6,23},{7,21},{8,25},{9,... | collective-permute-start | bytes 294920 | tf_op jit(solution)/shard_map/ppermute | solution.py:247
  23.1 5.7 %collective-permute-start.9 = (bf16[4,32,384]{2,1,0:T(8,128)(2,1)S(1)}, bf16[4,32,384]{2,1,0:T(8,128)(2,1)S(1)}, u32[]{:S(2)}, u32[]{:S(2)}) collective-permute-start(bf16[4,32,384]{2,1,0:T(8,128)(2,1)S(1)} %pad_maximum_fusion.refs_0_), channel_id=1, source_target_pairs={{0,18},{1,16},{2,19},{3,17},{4,21},{5,23},{6,20},{7,22},{8,26},{9,... | collective-permute-start | bytes 294920 | tf_op jit(solution)/shard_map/ppermute | solution.py:247
  24.9 4.8 %collective-permute-start.10 = (bf16[4,32,384]{2,1,0:T(8,128)(2,1)S(1)}, bf16[4,32,384]{2,1,0:T(8,128)(2,1)S(1)}, u32[]{:S(2)}, u32[]{:S(2)}) collective-permute-start(bf16[4,32,384]{2,1,0:T(8,128)(2,1)S(1)} %pad_maximum_fusion.refs_0_), channel_id=1, source_target_pairs={{0,16},{16,0},{1,17},{17,1},{2,18},{18,2},{3,19},{19,3},{4,20},{20... | collective-permute-start | bytes 294920 | tf_op jit(solution)/shard_map/ppermute | solution.py:224
  27.3 2.4 %collective-permute-start.11 = (bf16[4,32,384]{2,1,0:T(8,128)(2,1)S(1)}, bf16[4,32,384]{2,1,0:T(8,128)(2,1)S(1)}, u32[]{:S(2)}, u32[]{:S(2)}) collective-permute-start(bf16[4,32,384]{2,1,0:T(8,128)(2,1)S(1)} %collective-permute-done.7.refs_1_), channel_id=1, source_target_pairs={{0,16},{16,0},{1,17},{17,1},{2,18},{18,2},{3,19},{19,3},{4,20},{20... | collective-permute-start | bytes 294920 | tf_op jit(solution)/shard_map/ppermute | solution.py:224
  28.1 1.7 %collective-permute-start.12 = (bf16[4,32,384]{2,1,0:T(8,128)(2,1)S(1)}, bf16[4,32,384]{2,1,0:T(8,128)(2,1)S(1)}, u32[]{:S(2)}, u32[]{:S(2)}) collective-permute-start(bf16[4,32,384]{2,1,0:T(8,128)(2,1)S(1)} %collective-permute-done.8.refs_2_), channel_id=1, source_target_pairs={{0,16},{16,0},{1,17},{17,1},{2,18},{18,2},{3,19},{19,3},{4,20},{20... | collective-permute-start | bytes 294920 | tf_op jit(solution)/shard_map/ppermute | solution.py:224
  28.8 1.3 %collective-permute-start.13 = (bf16[4,32,384]{2,1,0:T(8,128)(2,1)S(1)}, bf16[4,32,384]{2,1,0:T(8,128)(2,1)S(1)}, u32[]{:S(2)}, u32[]{:S(2)}) collective-permute-start(bf16[4,32,384]{2,1,0:T(8,128)(2,1)S(1)} %collective-permute-done.9.refs_3_), channel_id=1, source_target_pairs={{0,16},{16,0},{1,17},{17,1},{2,18},{18,2},{3,19},{19,3},{4,20},{20... | collective-permute-start | bytes 294920 | tf_op jit(solution)/shard_map/ppermute | solution.py:224
  31.3 1.8 %collective-permute-start.14 = (bf16[4,128,360]{2,1,0:T(8,128)(2,1)S(1)}, bf16[4,128,360]{2,1,0:T(8,128)(2,1)S(1)}, u32[]{:S(2)}, u32[]{:S(2)}) collective-permute-start(bf16[4,128,360]{2,1,0:T(8,128)(2,1)S(1)} %get-tuple-element.48), channel_id=1, source_target_pairs={{0,16},{16,0},{1,17},{17,1},{2,18},{18,2},{3,19},{19,3},{4,20},{20... | collective-permute-start | bytes 1105928 | tf_op jit(solution)/shard_map/ppermute | solution.py:224
  33.1 5.4 %collective-permute-start.18 = (bf16[64,360]{1,0:T(8,128)(2,1)S(1)}, bf16[64,360]{1,0:T(8,128)(2,1)S(1)}, u32[]{:S(2)}, u32[]{:S(2)}) collective-permute-start(bf16[64,360]{1,0:T(8,128)(2,1)S(1)} %get-tuple-element.54), channel_id=1, source_target_pairs={{0,3},{1,2},{2,1},{3,0},{4,7},{5,6},{6,5},{7,4},{8,11},{9,10},{10,... | collective-permute-start | bytes 138248 | tf_op jit(solution)/shard_map/ppermute | solution.py:247
  35.2 4.4 %collective-permute-start.19 = (bf16[64,360]{1,0:T(8,128)(2,1)S(1)}, bf16[64,360]{1,0:T(8,128)(2,1)S(1)}, u32[]{:S(2)}, u32[]{:S(2)}) collective-permute-start(bf16[64,360]{1,0:T(8,128)(2,1)S(1)} %get-tuple-element.55), channel_id=1, source_target_pairs={{0,17},{1,19},{2,16},{3,18},{4,21},{5,23},{6,20},{7,22},{8,25},{9,... | collective-permute-start | bytes 138248 | tf_op jit(solution)/shard_map/ppermute | solution.py:247
  35.6 4.0 %collective-permute-start.20 = (bf16[64,360]{1,0:T(8,128)(2,1)S(1)}, bf16[64,360]{1,0:T(8,128)(2,1)S(1)}, u32[]{:S(2)}, u32[]{:S(2)}) collective-permute-start(bf16[64,360]{1,0:T(8,128)(2,1)S(1)} %get-tuple-element.56), channel_id=1, source_target_pairs={{0,18},{1,16},{2,19},{3,17},{4,22},{5,20},{6,23},{7,21},{8,26},{9,... | collective-permute-start | bytes 138248 | tf_op jit(solution)/shard_map/ppermute | solution.py:247
  36.4 6.0 %collective-permute-start.15 = (bf16[64,360]{1,0:T(8,128)(2,1)S(1)}, bf16[64,360]{1,0:T(8,128)(2,1)S(1)}, u32[]{:S(2)}, u32[]{:S(2)}) collective-permute-start(bf16[64,360]{1,0:T(8,128)(2,1)S(1)} %get-tuple-element.50), channel_id=1, source_target_pairs={{0,3},{1,2},{2,1},{3,0},{4,7},{5,6},{6,5},{7,4},{8,11},{9,10},{10,... | collective-permute-start | bytes 138248 | tf_op jit(solution)/shard_map/ppermute | solution.py:247
  38.4 4.0 %collective-permute-start.16 = (bf16[64,360]{1,0:T(8,128)(2,1)S(1)}, bf16[64,360]{1,0:T(8,128)(2,1)S(1)}, u32[]{:S(2)}, u32[]{:S(2)}) collective-permute-start(bf16[64,360]{1,0:T(8,128)(2,1)S(1)} %get-tuple-element.51), channel_id=1, source_target_pairs={{0,17},{1,19},{2,16},{3,18},{4,21},{5,23},{6,20},{7,22},{8,25},{9,... | collective-permute-start | bytes 138248 | tf_op jit(solution)/shard_map/ppermute | solution.py:247
  38.6 3.9 %collective-permute-start.17 = (bf16[64,360]{1,0:T(8,128)(2,1)S(1)}, bf16[64,360]{1,0:T(8,128)(2,1)S(1)}, u32[]{:S(2)}, u32[]{:S(2)}) collective-permute-start(bf16[64,360]{1,0:T(8,128)(2,1)S(1)} %get-tuple-element.52), channel_id=1, source_target_pairs={{0,18},{1,16},{2,19},{3,17},{4,22},{5,20},{6,23},{7,21},{8,26},{9,... | collective-permute-start | bytes 138248 | tf_op jit(solution)/shard_map/ppermute | solution.py:247
  39.7 5.2 %collective-permute-start.21 = (bf16[32,360]{1,0:T(8,128)(2,1)S(1)}, bf16[32,360]{1,0:T(8,128)(2,1)S(1)}, u32[]{:S(2)}, u32[]{:S(2)}) collective-permute-start(bf16[32,360]{1,0:T(8,128)(2,1)S(1)} %get-tuple-element.57), channel_id=1, source_target_pairs={{0,8},{4,12},{8,0},{12,4},{1,9},{5,13},{9,1},{13,5},{2,10},{6,14},... | collective-permute-start | bytes 69128 | tf_op jit(solution)/shard_map/ppermute | solution.py:224
  42.2 5.6 %collective-permute-start.22 = (bf16[32,360]{1,0:T(8,128)(2,1)S(1)}, bf16[32,360]{1,0:T(8,128)(2,1)S(1)}, u32[]{:S(2)}, u32[]{:S(2)}) collective-permute-start(bf16[32,360]{1,0:T(8,128)(2,1)S(1)} %get-tuple-element.58), channel_id=1, source_target_pairs={{0,12},{4,8},{8,4},{12,0},{1,13},{5,9},{9,5},{13,1},{2,14},{6,10},... | collective-permute-start | bytes 69128 | tf_op jit(solution)/shard_map/ppermute | solution.py:224
  42.5 5.3 %collective-permute-start.23 = (bf16[32,360]{1,0:T(8,128)(2,1)S(1)}, bf16[32,360]{1,0:T(8,128)(2,1)S(1)}, u32[]{:S(2)}, u32[]{:S(2)}) collective-permute-start(bf16[32,360]{1,0:T(8,128)(2,1)S(1)} %get-tuple-element.59), channel_id=1, source_target_pairs={{0,4},{4,0},{8,12},{12,8},{1,5},{5,1},{9,13},{13,9},{2,6},{6,2},{1... | collective-permute-start | bytes 69128 | tf_op jit(solution)/shard_map/ppermute | solution.py:224
  (4 other events, 99.7 us)
